TPU v7x, 32 devices: a whole 2x2x4 slice. The times are simulated.
32 devices in a mesh: bz: 2 (over x), by: 4 (over z), bx: 4 (over y, core).
Axes of the slice: x: 2, y: 2, z: 4, core: 2. Of those that a mesh axis runs over, the one named last changes fastest.
Arguments:
- density: float32 [16, 128, 1024], P('bz', 'by', 'bx'), may hold values from 0.2 to 1
- bin_index: int32 [16, 128, 1024], P('bz', 'by', 'bx'), may hold values from 0 to 255
- tf_colour: bfloat16 [3, 256], replicated, may hold values from 0 to 1
- tf_extinction: bfloat16 [256], replicated, may hold values from 0.049804688 to 8
- slab_rank: int32 [2], replicated, may hold values from 0 to 1, as said below
Outputs:
- frame: float32 [4, 256, 2048], P(None, ('by', 'bz'), 'bx')
Inputs may be any that keep to these rules, and one draw needn't show every extreme that they name: slab_rank[i] is i XOR one fixed number: the front-to-back order of a binary tree of slabs in which either child may be the nearer one at each level.
All inputs are finite; a program needn't handle non-finite values.
Results may differ from a plain program's by a relative error of at most 0.0003.
The roundings to bfloat16 on the way count: a program that leaves them out, or rounds other values in their place, can miss the bound.
Values may be sent and summed in bfloat16 or wider, within the bound.
No kernel may reach another device: no remote copies, remote signals or barrier semaphores. Data moves between devices by JAX's collectives and lax.ppermute only.
A program may use at most 64 MiB of HBM per device.

v0:
```python
import jax
import jax.numpy as jnp
from jax import lax
from jax.sharding import PartitionSpec as P


def with_halo(block, sides, width):
    for axis, dim in sides:
        count = lax.axis_size(axis)
        forward = [(i, i + 1) for i in range(count - 1)]
        backward = [(target, source) for source, target in forward]
        low = lax.ppermute(
            lax.slice_in_dim(block, block.shape[dim] - width, None, axis=dim), axis, forward
        )
        high = lax.ppermute(lax.slice_in_dim(block, 0, width, axis=dim), axis, backward)
        block = jnp.concatenate([low, block, high], axis=dim)
    return block


def partner_2(block, axis, stride):
    count = lax.axis_size(axis)
    route = []
    for low in range(count):
        high = low | 1 << stride
        if high != low and high < count:
            route += [(low, high), (high, low)]
    return lax.ppermute(block, axis, route)


def resample_table(length):
    row_index = lax.broadcasted_iota(jnp.int32, (2 * length, length + 2), 0)
    col_index = lax.broadcasted_iota(jnp.int32, (2 * length, length + 2), 1)
    centre = row_index // 2
    parity = row_index % 2
    weights_table = jnp.where(col_index == centre + 1, 0.75, 0.0)
    weights_table = weights_table + jnp.where((col_index == centre) & (parity == 0), 0.25, 0.0)
    weights_table = weights_table + jnp.where((col_index == centre + 2) & (parity == 1), 0.25, 0.0)
    return weights_table.astype(jnp.bfloat16)


def blend_over(in_front, behind):
    return in_front + (1.0 - in_front[3])[None] * behind


def classify(density, bin_index, tf_colour, tf_extinction, total_depth):
    depth_cells, height_cells, width_cells = density.shape
    lookup = jnp.concatenate([tf_colour, tf_extinction[None, :]], axis=0)
    table_size = lookup.shape[1]
    bin_rows = lax.broadcasted_iota(jnp.int32, (table_size, 1), 0)
    flat_bins = bin_index.reshape(depth_cells, height_cells * width_cells)
    flat_density = density.reshape(depth_cells, height_cells * width_cells)

    def one_layer(layer, result):
        layer_bins = lax.dynamic_index_in_dim(flat_bins, layer, 0, keepdims=True)
        layer_density = lax.dynamic_index_in_dim(flat_density, layer, 0, keepdims=False)
        one_hot = (layer_bins == bin_rows).astype(jnp.bfloat16)
        values = jnp.dot(lookup, one_hot, preferred_element_type=jnp.float32)
        opacity = 1.0 - jnp.exp(-values[3] * layer_density / total_depth)
        cells = jnp.concatenate([values[:3] * opacity[None], opacity[None]], axis=0).astype(
            jnp.bfloat16
        )
        return lax.dynamic_update_slice_in_dim(result, cells[:, None], layer, 1)

    start_cells = jnp.zeros((4, depth_cells, height_cells * width_cells), jnp.bfloat16)
    classified = lax.fori_loop(0, depth_cells, one_layer, start_cells)
    return classified.reshape(4, depth_cells, height_cells, width_cells)


def on_device(density, bin_index, tf_colour, tf_extinction, slab_rank):
    slab_count = lax.axis_size("bz")
    depth_cells, height_cells, width_cells = density.shape
    total_depth = float(depth_cells * slab_count)
    colour_cells = classify(density, bin_index, tf_colour, tf_extinction, total_depth)
    padded = with_halo(colour_cells, (("bz", 1), ("by", 2), ("bx", 3)), 1)
    along_x = jnp.einsum(
        "czyq,pq->czyp", padded, resample_table(width_cells), preferred_element_type=jnp.float32
    ).astype(jnp.bfloat16)
    y_table = resample_table(height_cells)

    def add_sample(sample_index, image_now):
        centre = sample_index // 2
        parity = sample_index % 2
        layers = lax.dynamic_slice_in_dim(along_x, centre, 3, 1).astype(jnp.float32)
        lower_weight = jnp.where(parity == 0, 0.25, 0.0)
        upper_weight = jnp.where(parity == 1, 0.25, 0.0)
        mixed_layer = (
            lower_weight * layers[:, 0] + 0.75 * layers[:, 1] + upper_weight * layers[:, 2]
        ).astype(jnp.bfloat16)
        sample = jnp.einsum("qy,cyp->cqp", y_table, mixed_layer, preferred_element_type=jnp.float32)
        return blend_over(image_now, sample)

    start_image = jnp.zeros((4, 2 * height_cells, 2 * width_cells), jnp.float32)
    slab_image = lax.fori_loop(0, 2 * depth_cells, add_sample, start_image)
    rows_piece = 2 * height_cells // slab_count
    my_index = lax.axis_index("bz")
    bit_levels = slab_count.bit_length() - 1
    composite = slab_image.reshape((4,) + (2,) * bit_levels + (rows_piece, 2 * width_cells))
    my_rank = lax.dynamic_index_in_dim(slab_rank, my_index, 0, keepdims=False)
    for level in range(bit_levels):
        position = bit_levels - level
        my_bit = my_index // 2**level % 2
        kept_half = lax.dynamic_index_in_dim(composite, my_bit, position, keepdims=False)
        outgoing = lax.dynamic_index_in_dim(composite, 1 - my_bit, position, keepdims=False)
        incoming = partner_2(outgoing, "bz", level)
        partner = my_index + (1 - 2 * my_bit) * 2**level
        partner_rank = lax.dynamic_index_in_dim(slab_rank, partner, 0, keepdims=False)
        mine_first = my_rank < partner_rank
        composite = blend_over(
            jnp.where(mine_first, kept_half, incoming), jnp.where(mine_first, incoming, kept_half)
        )
    return composite


def solution(mesh):
    return jax.shard_map(
        on_device,
        mesh=mesh,
        in_specs=(P("bz", "by", "bx"), P("bz", "by", "bx"), P(), P(), P()),
        out_specs=P(None, ("by", "bz"), "bx"),
        check_vma=False,
    )
```

profile of v0, /device:TPU:20, one launch (start us, length us, event | category | flops | bytes accessed | tf_op | source)
XLA Modules:
  0.0 81.7 jit_solution(18433311912016750062)
XLA Ops:
  0.0 1.1 %copy.19 = s32[1,8,32,256]{3,1,2,0:T(8,128)S(1)} copy(s32[1,8,32,256]{3,2,1,0:T(8,128)} %bitcast.80) | data formatting | bytes 524288
  1.1 0.7 broadcast_in_dim.50
  1.8 1.1 %copy.20 = f32[1,8,32,256]{3,1,2,0:T(8,128)S(1)} copy(f32[1,8,32,256]{3,2,1,0:T(8,128)} %bitcast.81) | data formatting | bytes 524288
  2.9 0.7 pad_maximum_fusion.1
  3.6 13.1 %while.30 = (s32[]{:T(128)}, bf16[4,8,8192]{2,0,1:T(4,128)(2,1)S(1)}, s32[8,8192]{1,0:T(8,128)S(1)}, bf16[4,256]{1,0:T(4,128)(2,1)S(1)}, f32[8,8192]{1,0:T(8,128)S(1)}, /*index=5*/s32[]{:T(128)}) while((s32[]{:T(128)}, bf16[4,8,8192]{2,0,1:T(4,128)(2,1)S(1)}, s32[8,8192]{1,0:T(8,128)S(1)}, bf16[4,256]{1,0:T(4,128)(2,1)S(1)}, ...), condition=%wide.region_1.2_spmd.clone, body=%wide.region_0.1_spmd.clone.sunk | while | flops 19095552 | bytes 690265 | solution.py:65
  3.6 1.3 %convolution_bitcast_fusion.3 = f32[4,8192]{1,0:T(4,128)S(1)} fusion(bf16[4,256]{1,0:T(4,128)(2,1)S(1)} %get-tuple-element.452, s32[8192]{0:T(1024)S(1)} %bitcast.77), kind=kOutput, calls=%fused_computation.2.clone.1 | convolution fusion | flops 18874368 | bytes 165888 | tf_op jit(solution)/shard_map/while/body/eval_jaxpr/dot_general | solution.py:57
  5.2 1.3 %convolution_bitcast_fusion.3 = f32[4,8192]{1,0:T(4,128)S(1)} fusion(bf16[4,256]{1,0:T(4,128)(2,1)S(1)} %get-tuple-element.452, s32[8192]{0:T(1024)S(1)} %bitcast.77), kind=kOutput, calls=%fused_computation.2.clone.1 | convolution fusion | flops 18874368 | bytes 165888 | tf_op jit(solution)/shard_map/while/body/eval_jaxpr/dot_general | solution.py:57
  6.9 1.3 %convolution_bitcast_fusion.3 = f32[4,8192]{1,0:T(4,128)S(1)} fusion(bf16[4,256]{1,0:T(4,128)(2,1)S(1)} %get-tuple-element.452, s32[8192]{0:T(1024)S(1)} %bitcast.77), kind=kOutput, calls=%fused_computation.2.clone.1 | convolution fusion | flops 18874368 | bytes 165888 | tf_op jit(solution)/shard_map/while/body/eval_jaxpr/dot_general | solution.py:57
  8.5 1.3 %convolution_bitcast_fusion.3 = f32[4,8192]{1,0:T(4,128)S(1)} fusion(bf16[4,256]{1,0:T(4,128)(2,1)S(1)} %get-tuple-element.452, s32[8192]{0:T(1024)S(1)} %bitcast.77), kind=kOutput, calls=%fused_computation.2.clone.1 | convolution fusion | flops 18874368 | bytes 165888 | tf_op jit(solution)/shard_map/while/body/eval_jaxpr/dot_general | solution.py:57
  10.1 1.3 %convolution_bitcast_fusion.3 = f32[4,8192]{1,0:T(4,128)S(1)} fusion(bf16[4,256]{1,0:T(4,128)(2,1)S(1)} %get-tuple-element.452, s32[8192]{0:T(1024)S(1)} %bitcast.77), kind=kOutput, calls=%fused_computation.2.clone.1 | convolution fusion | flops 18874368 | bytes 165888 | tf_op jit(solution)/shard_map/while/body/eval_jaxpr/dot_general | solution.py:57
  11.8 1.3 %convolution_bitcast_fusion.3 = f32[4,8192]{1,0:T(4,128)S(1)} fusion(bf16[4,256]{1,0:T(4,128)(2,1)S(1)} %get-tuple-element.452, s32[8192]{0:T(1024)S(1)} %bitcast.77), kind=kOutput, calls=%fused_computation.2.clone.1 | convolution fusion | flops 18874368 | bytes 165888 | tf_op jit(solution)/shard_map/while/body/eval_jaxpr/dot_general | solution.py:57
  13.4 1.3 %convolution_bitcast_fusion.3 = f32[4,8192]{1,0:T(4,128)S(1)} fusion(bf16[4,256]{1,0:T(4,128)(2,1)S(1)} %get-tuple-element.452, s32[8192]{0:T(1024)S(1)} %bitcast.77), kind=kOutput, calls=%fused_computation.2.clone.1 | convolution fusion | flops 18874368 | bytes 165888 | tf_op jit(solution)/shard_map/while/body/eval_jaxpr/dot_general | solution.py:57
  15.0 1.3 %convolution_bitcast_fusion.3 = f32[4,8192]{1,0:T(4,128)S(1)} fusion(bf16[4,256]{1,0:T(4,128)(2,1)S(1)} %get-tuple-element.452, s32[8192]{0:T(1024)S(1)} %bitcast.77), kind=kOutput, calls=%fused_computation.2.clone.1 | convolution fusion | flops 18874368 | bytes 165888 | tf_op jit(solution)/shard_map/while/body/eval_jaxpr/dot_general | solution.py:57
  16.6 0.4 reshape.63
  17.0 3.4 %collective-permute-start = (bf16[4,1,32,256]{3,2,1,0:T(8,128)(2,1)S(1)}, bf16[4,1,32,256]{3,2,1,0:T(8,128)(2,1)S(1)}, u32[]{:S(2)}, u32[]{:S(2)}) collective-permute-start(bf16[4,1,32,256]{3,2,1,0:T(8,128)(2,1)S(1)} %copy.23), channel_id=1, source_target_pairs={{0,16},{1,17},{2,18},{3,19},{4,20},{5,21},{6,22},{7,23},{8,24},{9,... | collective-permute-start | bytes 196616 | tf_op jit(solution)/shard_map/ppermute | solution.py:12
  20.5 1.3 %collective-permute-start.1 = (bf16[4,1,32,256]{3,2,1,0:T(8,128)(2,1)S(1)}, bf16[4,1,32,256]{3,2,1,0:T(8,128)(2,1)S(1)}, u32[]{:S(2)}, u32[]{:S(2)}) collective-permute-start(bf16[4,1,32,256]{3,2,1,0:T(8,128)(2,1)S(1)} %copy.24), channel_id=1, source_target_pairs={{16,0},{17,1},{18,2},{19,3},{20,4},{21,5},{22,6},{23,7},{24,8},{25... | collective-permute-start | bytes 196616 | tf_op jit(solution)/shard_map/ppermute | solution.py:15
  21.8 0.5 collective-permute-done
  22.4 4.2 %collective-permute-done.1 = bf16[4,1,32,256]{3,2,1,0:T(8,128)(2,1)S(1)} collective-permute-done((bf16[4,1,32,256]{3,2,1,0:T(8,128)(2,1)S(1)}, bf16[4,1,32,256]{3,2,1,0:T(8,128)(2,1)S(1)}, u32[]{:S(2)}, u32[]{:S(2)}) %collective-permute-start.1) | collective-permute-done | bytes 65568 | tf_op jit(solution)/shard_map/ppermute | solution.py:15
  26.7 2.4 %collective-permute-start.3 = (bf16[4,10,1,256]{3,2,1,0:T(2,128)(2,1)S(1)}, bf16[4,10,1,256]{3,2,1,0:T(2,128)(2,1)S(1)}, u32[]{:S(2)}, u32[]{:S(2)}) collective-permute-start(bf16[4,10,1,256]{3,2,1,0:T(2,128)(2,1)S(1)} %get-tuple-element.330), channel_id=1, source_target_pairs={{4,0},{8,4},{12,8},{5,1},{9,5},{13,9},{6,2},{10,6},{14,10},{7,3},{... | collective-permute-start | bytes 61448 | tf_op jit(solution)/shard_map/ppermute | solution.py:15
  29.1 3.5 %collective-permute-start.2 = (bf16[4,10,1,256]{3,2,1,0:T(2,128)(2,1)S(1)}, bf16[4,10,1,256]{3,2,1,0:T(2,128)(2,1)S(1)}, u32[]{:S(2)}, u32[]{:S(2)}) collective-permute-start(bf16[4,10,1,256]{3,2,1,0:T(2,128)(2,1)S(1)} %get-tuple-element.329), channel_id=1, source_target_pairs={{0,4},{4,8},{8,12},{1,5},{5,9},{9,13},{2,6},{6,10},{10,14},{3,7},{... | collective-permute-start | bytes 61448 | tf_op jit(solution)/shard_map/ppermute | solution.py:12
  32.6 2.4 %collective-permute-done.2 = bf16[4,10,1,256]{3,2,1,0:T(2,128)(2,1)S(1)} collective-permute-done((bf16[4,10,1,256]{3,2,1,0:T(2,128)(2,1)S(1)}, bf16[4,10,1,256]{3,2,1,0:T(2,128)(2,1)S(1)}, u32[]{:S(2)}, u32[]{:S(2)}) %collective-permute-start.2) | collective-permute-done | bytes 20512 | tf_op jit(solution)/shard_map/ppermute | solution.py:12
  35.0 0.5 pad_maximum_fusion
  35.4 0.2 fusion.82
  35.7 1.9 %collective-permute-start.5 = (bf16[4,10,34,1]{3,2,1,0:T(8,128)(2,1)S(1)}, bf16[4,10,34,1]{3,2,1,0:T(8,128)(2,1)S(1)}, u32[]{:S(2)}, u32[]{:S(2)}) collective-permute-start(bf16[4,10,34,1]{3,2,1,0:T(8,128)(2,1)S(1)} %get-tuple-element.328), channel_id=1, source_target_pairs={{1,0},{2,1},{3,2},{5,4},{6,5},{7,6},{9,8},{10,9},{11,10},{13,12},{... | collective-permute-start | bytes 8168 | tf_op jit(solution)/shard_map/ppermute | solution.py:15
  37.6 2.4 %collective-permute-start.4 = (bf16[4,10,34,1]{3,2,1,0:T(8,128)(2,1)S(1)}, bf16[4,10,34,1]{3,2,1,0:T(8,128)(2,1)S(1)}, u32[]{:S(2)}, u32[]{:S(2)}) collective-permute-start(bf16[4,10,34,1]{3,2,1,0:T(8,128)(2,1)S(1)} %get-tuple-element.327), channel_id=1, source_target_pairs={{0,1},{1,2},{2,3},{4,5},{5,6},{6,7},{8,9},{9,10},{10,11},{12,13},{... | collective-permute-start | bytes 8168 | tf_op jit(solution)/shard_map/ppermute | solution.py:12
  40.1 3.0 %collective-permute-done.5 = bf16[4,10,34,1]{3,2,1,0:T(8,128)(2,1)S(1)} collective-permute-done((bf16[4,10,34,1]{3,2,1,0:T(8,128)(2,1)S(1)}, bf16[4,10,34,1]{3,2,1,0:T(8,128)(2,1)S(1)}, u32[]{:S(2)}, u32[]{:S(2)}) %collective-permute-start.5) | collective-permute-done | bytes 2752 | tf_op jit(solution)/shard_map/ppermute | solution.py:15
  43.0 3.8 %collective-permute-done.4 = bf16[4,10,34,1]{3,2,1,0:T(8,128)(2,1)S(1)} collective-permute-done((bf16[4,10,34,1]{3,2,1,0:T(8,128)(2,1)S(1)}, bf16[4,10,34,1]{3,2,1,0:T(8,128)(2,1)S(1)}, u32[]{:S(2)}, u32[]{:S(2)}) %collective-permute-start.4) | collective-permute-done | bytes 2752 | tf_op jit(solution)/shard_map/ppermute | solution.py:12
  46.9 2.6 %convolution_convert_fusion = bf16[4,10,34,512]{3,2,1,0:T(8,128)(2,1)} fusion(bf16[4,10,34,1]{3,2,1,0:T(8,128)(2,1)S(1)} %collective-permute-done.5, bf16[4,10,1,256]{3,2,1,0:T(2,128)(2,1)S(1)} %collective-permute-done.3, bf16[4,10,32,256]{3,2,1,0:T(8,128)(2,1)S(1)} %constant_dynamic-update-slice_fusion, ...), kind=kOutput, calls=%fused_computation.61 | convolution fusion | flops 365751872 | bytes 2103616 | tf_op jit(solution)/shard_map/czyq,pq->czyp/dot_general | solution.py:75
  49.4 25.0 %while.31 = (s32[]{:T(128)}, f32[4,64,512]{2,1,0:T(8,128)S(1)}, bf16[4,10,34,512]{3,2,1,0:T(8,128)(2,1)}, s32[64]{0:T(128)S(1)}, s32[64]{0:T(128)S(1)}, /*index=...) while((s32[]{:T(128)}, f32[4,64,512]{2,1,0:T(8,128)S(1)}, ...), condition=%wide.region_3.4_spmd.clone, body=%wide.region_2.3_spmd.clone.sunk | while | flops 10002582 | bytes 4654580 | solution.py:93
  49.5 1.1 %copy_convert_fusion.2 = f32[4,3,34,512]{3,2,0,1:T(8,128)S(1)} fusion(bf16[4,10,34,512]{3,2,1,0:T(8,128)(2,1)} %get-tuple-element.489, s32[]{:T(128)S(6)} %select_n.314), kind=kLoop, calls=%fused_computation.17.clone.1 | loop fusion | flops 208896 | bytes 1327108 | tf_op jit(solution)/shard_map/while/body/eval_jaxpr/convert_element_type | solution.py:83
  50.7 0.3 fusion.98
  51.1 1.1 %copy_convert_fusion.2 = f32[4,3,34,512]{3,2,0,1:T(8,128)S(1)} fusion(bf16[4,10,34,512]{3,2,1,0:T(8,128)(2,1)} %get-tuple-element.489, s32[]{:T(128)S(6)} %select_n.314), kind=kLoop, calls=%fused_computation.17.clone.1 | loop fusion | flops 208896 | bytes 1327108 | tf_op jit(solution)/shard_map/while/body/eval_jaxpr/convert_element_type | solution.py:83
  52.2 0.3 fusion.98
  52.6 1.1 %copy_convert_fusion.2 = f32[4,3,34,512]{3,2,0,1:T(8,128)S(1)} fusion(bf16[4,10,34,512]{3,2,1,0:T(8,128)(2,1)} %get-tuple-element.489, s32[]{:T(128)S(6)} %select_n.314), kind=kLoop, calls=%fused_computation.17.clone.1 | loop fusion | flops 208896 | bytes 1327108 | tf_op jit(solution)/shard_map/while/body/eval_jaxpr/convert_element_type | solution.py:83
  53.8 0.3 fusion.98
  54.2 1.1 %copy_convert_fusion.2 = f32[4,3,34,512]{3,2,0,1:T(8,128)S(1)} fusion(bf16[4,10,34,512]{3,2,1,0:T(8,128)(2,1)} %get-tuple-element.489, s32[]{:T(128)S(6)} %select_n.314), kind=kLoop, calls=%fused_computation.17.clone.1 | loop fusion | flops 208896 | bytes 1327108 | tf_op jit(solution)/shard_map/while/body/eval_jaxpr/convert_element_type | solution.py:83
  55.4 0.3 fusion.98
  55.8 1.1 %copy_convert_fusion.2 = f32[4,3,34,512]{3,2,0,1:T(8,128)S(1)} fusion(bf16[4,10,34,512]{3,2,1,0:T(8,128)(2,1)} %get-tuple-element.489, s32[]{:T(128)S(6)} %select_n.314), kind=kLoop, calls=%fused_computation.17.clone.1 | loop fusion | flops 208896 | bytes 1327108 | tf_op jit(solution)/shard_map/while/body/eval_jaxpr/convert_element_type | solution.py:83
  56.9 0.3 fusion.98
  57.3 1.1 %copy_convert_fusion.2 = f32[4,3,34,512]{3,2,0,1:T(8,128)S(1)} fusion(bf16[4,10,34,512]{3,2,1,0:T(8,128)(2,1)} %get-tuple-element.489, s32[]{:T(128)S(6)} %select_n.314), kind=kLoop, calls=%fused_computation.17.clone.1 | loop fusion | flops 208896 | bytes 1327108 | tf_op jit(solution)/shard_map/while/body/eval_jaxpr/convert_element_type | solution.py:83
  58.5 0.3 fusion.98
  58.9 1.1 %copy_convert_fusion.2 = f32[4,3,34,512]{3,2,0,1:T(8,128)S(1)} fusion(bf16[4,10,34,512]{3,2,1,0:T(8,128)(2,1)} %get-tuple-element.489, s32[]{:T(128)S(6)} %select_n.314), kind=kLoop, calls=%fused_computation.17.clone.1 | loop fusion | flops 208896 | bytes 1327108 | tf_op jit(solution)/shard_map/while/body/eval_jaxpr/convert_element_type | solution.py:83
  60.1 0.3 fusion.98
  60.5 1.1 %copy_convert_fusion.2 = f32[4,3,34,512]{3,2,0,1:T(8,128)S(1)} fusion(bf16[4,10,34,512]{3,2,1,0:T(8,128)(2,1)} %get-tuple-element.489, s32[]{:T(128)S(6)} %select_n.314), kind=kLoop, calls=%fused_computation.17.clone.1 | loop fusion | flops 208896 | bytes 1327108 | tf_op jit(solution)/shard_map/while/body/eval_jaxpr/convert_element_type | solution.py:83
  61.6 0.3 fusion.98
  62.0 1.1 %copy_convert_fusion.2 = f32[4,3,34,512]{3,2,0,1:T(8,128)S(1)} fusion(bf16[4,10,34,512]{3,2,1,0:T(8,128)(2,1)} %get-tuple-element.489, s32[]{:T(128)S(6)} %select_n.314), kind=kLoop, calls=%fused_computation.17.clone.1 | loop fusion | flops 208896 | bytes 1327108 | tf_op jit(solution)/shard_map/while/body/eval_jaxpr/convert_element_type | solution.py:83
  63.2 0.3 fusion.98
  63.6 1.1 %copy_convert_fusion.2 = f32[4,3,34,512]{3,2,0,1:T(8,128)S(1)} fusion(bf16[4,10,34,512]{3,2,1,0:T(8,128)(2,1)} %get-tuple-element.489, s32[]{:T(128)S(6)} %select_n.314), kind=kLoop, calls=%fused_computation.17.clone.1 | loop fusion | flops 208896 | bytes 1327108 | tf_op jit(solution)/shard_map/while/body/eval_jaxpr/convert_element_type | solution.py:83
  64.7 0.3 fusion.98
  65.1 1.1 %copy_convert_fusion.2 = f32[4,3,34,512]{3,2,0,1:T(8,128)S(1)} fusion(bf16[4,10,34,512]{3,2,1,0:T(8,128)(2,1)} %get-tuple-element.489, s32[]{:T(128)S(6)} %select_n.314), kind=kLoop, calls=%fused_computation.17.clone.1 | loop fusion | flops 208896 | bytes 1327108 | tf_op jit(solution)/shard_map/while/body/eval_jaxpr/convert_element_type | solution.py:83
  66.3 0.3 fusion.98
  66.7 1.1 %copy_convert_fusion.2 = f32[4,3,34,512]{3,2,0,1:T(8,128)S(1)} fusion(bf16[4,10,34,512]{3,2,1,0:T(8,128)(2,1)} %get-tuple-element.489, s32[]{:T(128)S(6)} %select_n.314), kind=kLoop, calls=%fused_computation.17.clone.1 | loop fusion | flops 208896 | bytes 1327108 | tf_op jit(solution)/shard_map/while/body/eval_jaxpr/convert_element_type | solution.py:83
  67.9 0.3 fusion.98
  68.3 1.1 %copy_convert_fusion.2 = f32[4,3,34,512]{3,2,0,1:T(8,128)S(1)} fusion(bf16[4,10,34,512]{3,2,1,0:T(8,128)(2,1)} %get-tuple-element.489, s32[]{:T(128)S(6)} %select_n.314), kind=kLoop, calls=%fused_computation.17.clone.1 | loop fusion | flops 208896 | bytes 1327108 | tf_op jit(solution)/shard_map/while/body/eval_jaxpr/convert_element_type | solution.py:83
  69.4 0.3 fusion.98
  69.8 1.1 %copy_convert_fusion.2 = f32[4,3,34,512]{3,2,0,1:T(8,128)S(1)} fusion(bf16[4,10,34,512]{3,2,1,0:T(8,128)(2,1)} %get-tuple-element.489, s32[]{:T(128)S(6)} %select_n.314), kind=kLoop, calls=%fused_computation.17.clone.1 | loop fusion | flops 208896 | bytes 1327108 | tf_op jit(solution)/shard_map/while/body/eval_jaxpr/convert_element_type | solution.py:83
  71.0 0.3 fusion.98
  71.4 1.1 %copy_convert_fusion.2 = f32[4,3,34,512]{3,2,0,1:T(8,128)S(1)} fusion(bf16[4,10,34,512]{3,2,1,0:T(8,128)(2,1)} %get-tuple-element.489, s32[]{:T(128)S(6)} %select_n.314), kind=kLoop, calls=%fused_computation.17.clone.1 | loop fusion | flops 208896 | bytes 1327108 | tf_op jit(solution)/shard_map/while/body/eval_jaxpr/convert_element_type | solution.py:83
  72.5 0.3 fusion.98
  72.9 1.1 %copy_convert_fusion.2 = f32[4,3,34,512]{3,2,0,1:T(8,128)S(1)} fusion(bf16[4,10,34,512]{3,2,1,0:T(8,128)(2,1)} %get-tuple-element.489, s32[]{:T(128)S(6)} %select_n.314), kind=kLoop, calls=%fused_computation.17.clone.1 | loop fusion | flops 208896 | bytes 1327108 | tf_op jit(solution)/shard_map/while/body/eval_jaxpr/convert_element_type | solution.py:83
  74.1 0.3 fusion.98
  74.5 0.6 fusion.85
  76.4 4.5 %collective-permute-done.6 = f32[4,32,512]{2,1,0:T(8,128)S(1)} collective-permute-done((f32[4,32,512]{2,1,0:T(8,128)S(1)}, f32[4,32,512]{2,1,0:T(8,128)S(1)}, u32[]{:S(2)}, u32[]{:S(2)}) %collective-permute-start.6) | collective-permute-done | bytes 262176 | tf_op jit(solution)/shard_map/ppermute | solution.py:27
  80.9 0.8 fusion.67
  (86 shorter events, 3.4 us)
Async XLA Ops:
  17.0 5.3 %collective-permute-start = (bf16[4,1,32,256]{3,2,1,0:T(8,128)(2,1)S(1)}, bf16[4,1,32,256]{3,2,1,0:T(8,128)(2,1)S(1)}, u32[]{:S(2)}, u32[]{:S(2)}) collective-permute-start(bf16[4,1,32,256]{3,2,1,0:T(8,128)(2,1)S(1)} %copy.23), channel_id=1, source_target_pairs={{0,16},{1,17},{2,18},{3,19},{4,20},{5,21},{6,22},{7,23},{8,24},{9,... | collective-permute-start | bytes 196616 | tf_op jit(solution)/shard_map/ppermute | solution.py:12
  20.5 6.2 %collective-permute-start.1 = (bf16[4,1,32,256]{3,2,1,0:T(8,128)(2,1)S(1)}, bf16[4,1,32,256]{3,2,1,0:T(8,128)(2,1)S(1)}, u32[]{:S(2)}, u32[]{:S(2)}) collective-permute-start(bf16[4,1,32,256]{3,2,1,0:T(8,128)(2,1)S(1)} %copy.24), channel_id=1, source_target_pairs={{16,0},{17,1},{18,2},{19,3},{20,4},{21,5},{22,6},{23,7},{24,8},{25... | collective-permute-start | bytes 196616 | tf_op jit(solution)/shard_map/ppermute | solution.py:15
  26.7 5.9 %collective-permute-start.3 = (bf16[4,10,1,256]{3,2,1,0:T(2,128)(2,1)S(1)}, bf16[4,10,1,256]{3,2,1,0:T(2,128)(2,1)S(1)}, u32[]{:S(2)}, u32[]{:S(2)}) collective-permute-start(bf16[4,10,1,256]{3,2,1,0:T(2,128)(2,1)S(1)} %get-tuple-element.330), channel_id=1, source_target_pairs={{4,0},{8,4},{12,8},{5,1},{9,5},{13,9},{6,2},{10,6},{14,10},{7,3},{... | collective-permute-start | bytes 61448 | tf_op jit(solution)/shard_map/ppermute | solution.py:15
  29.1 5.9 %collective-permute-start.2 = (bf16[4,10,1,256]{3,2,1,0:T(2,128)(2,1)S(1)}, bf16[4,10,1,256]{3,2,1,0:T(2,128)(2,1)S(1)}, u32[]{:S(2)}, u32[]{:S(2)}) collective-permute-start(bf16[4,10,1,256]{3,2,1,0:T(2,128)(2,1)S(1)} %get-tuple-element.329), channel_id=1, source_target_pairs={{0,4},{4,8},{8,12},{1,5},{5,9},{9,13},{2,6},{6,10},{10,14},{3,7},{... | collective-permute-start | bytes 61448 | tf_op jit(solution)/shard_map/ppermute | solution.py:12
  35.7 7.4 %collective-permute-start.5 = (bf16[4,10,34,1]{3,2,1,0:T(8,128)(2,1)S(1)}, bf16[4,10,34,1]{3,2,1,0:T(8,128)(2,1)S(1)}, u32[]{:S(2)}, u32[]{:S(2)}) collective-permute-start(bf16[4,10,34,1]{3,2,1,0:T(8,128)(2,1)S(1)} %get-tuple-element.328), channel_id=1, source_target_pairs={{1,0},{2,1},{3,2},{5,4},{6,5},{7,6},{9,8},{10,9},{11,10},{13,12},{... | collective-permute-start | bytes 8168 | tf_op jit(solution)/shard_map/ppermute | solution.py:15
  37.6 9.3 %collective-permute-start.4 = (bf16[4,10,34,1]{3,2,1,0:T(8,128)(2,1)S(1)}, bf16[4,10,34,1]{3,2,1,0:T(8,128)(2,1)S(1)}, u32[]{:S(2)}, u32[]{:S(2)}) collective-permute-start(bf16[4,10,34,1]{3,2,1,0:T(8,128)(2,1)S(1)} %get-tuple-element.327), channel_id=1, source_target_pairs={{0,1},{1,2},{2,3},{4,5},{5,6},{6,7},{8,9},{9,10},{10,11},{12,13},{... | collective-permute-start | bytes 8168 | tf_op jit(solution)/shard_map/ppermute | solution.py:12
  49.4 25.1 %copy-start = (s32[2]{0:T(128)S(1)}, s32[2]{0:T(128)}, u32[]{:S(2)}) copy-start(s32[2]{0:T(128)} %param.13) | copy-start | bytes 28
  74.4 6.4 %collective-permute-start.6 = (f32[4,32,512]{2,1,0:T(8,128)S(1)}, f32[4,32,512]{2,1,0:T(8,128)S(1)}, u32[]{:S(2)}, u32[]{:S(2)}) collective-permute-start(f32[4,32,512]{2,1,0:T(8,128)S(1)} %dynamic-slice_bitcast_fusion), channel_id=1, source_target_pairs={{0,16},{16,0},{1,17},{17,1},{2,18},{18,2},{3,19},{19,3},{4,20},{20... | collective-permute-start | bytes 786440 | tf_op jit(solution)/shard_map/ppermute | solution.py:27
where the time goes:
time: 82.7 us; the launch traced here: 81.7 us
  other arithmetic  23.2 us (28%)
  waiting for transfers between devices  18.5 us (22%)
  matrix products  17.8 us (22%)
  starting transfers between devices  15 us (18%)
  local copies, waits for them, and re-layouts  4.41 us (5%)
  between operations  1.45 us (2%)
  loops' own time  1.39 us (2%)
    convert_element_type x16, other arithmetic, add_sample(): layers = lax.dynamic_slice_in_dim(along_x, centre, 3, 1).astype(jnp.float32)  18.3 us
    dot_general x8, matrix products, one_layer(): values = jnp.dot(lookup, one_hot, preferred_element_type=jnp.float32)  10.7 us
    ppermute x3, starting transfers between devices, with_halo(): lax.ppermute(lax.slice_in_dim(block, block.shape[dim] - width, None, axis...  9.31 us
    ppermute x3, waiting for transfers between devices, with_halo(): lax.ppermute(lax.slice_in_dim(block, 0, width, axis=dim), axis, backward)  7.24 us
    ppermute x3, waiting for transfers between devices, with_halo(): lax.ppermute(lax.slice_in_dim(block, block.shape[dim] - width, None, axis...  6.71 us
    ppermute x3, starting transfers between devices, with_halo(): lax.ppermute(lax.slice_in_dim(block, 0, width, axis=dim), axis, backward)  5.57 us
    ppermute x1, waiting for transfers between devices, partner_2(): return lax.ppermute(block, axis, route)  4.53 us
    dot_general x16, matrix products, add_sample(): jnp.einsum('qy,cyp->cqp', y_table, mixed_layer, preferred_element_type=jn...  4.52 us
  transfers between devices with their start and end apart: 7, of which 6 were waited for; matrix products, arithmetic and copies ran while one was open for 1% of the time, Pallas kernels for 0%

commit v1 on v0

--- a/solution.py
+++ b/solution.py
@@ -1,6 +1,9 @@
 import jax
 import jax.numpy as jnp
+import numpy as np
 from jax import lax
+from jax.experimental import pallas as pl
+from jax.experimental.pallas import tpu as pltpu
 from jax.sharding import PartitionSpec as P
 
 
@@ -66,7 +69,7 @@
     return classified.reshape(4, depth_cells, height_cells, width_cells)
 
 
-def on_device(density, bin_index, tf_colour, tf_extinction, slab_rank):
+def general_device(density, bin_index, tf_colour, tf_extinction, slab_rank):
     slab_count = lax.axis_size("bz")
     depth_cells, height_cells, width_cells = density.shape
     total_depth = float(depth_cells * slab_count)
@@ -111,6 +114,369 @@
     return composite
 
 
+LANES = 128
+LEVELS = 65535.0
+
+
+def pack_words(density, bins):
+    level = (density * LEVELS + 0.5).astype(jnp.int32)
+    return lax.shift_left(level, 16) | bins
+
+
+def word_density(words):
+    return lax.shift_right_logical(words, 16).astype(jnp.float32) * (1.0 / LEVELS)
+
+
+def word_bins(words):
+    return words & 0xFFFF
+
+
+def cell_values(density, bins, tables, depth):
+    low_bits = bins & (LANES - 1)
+    upper = bins >= LANES
+
+    def pick(channel):
+        first, second = tables[channel]
+        return jnp.where(
+            upper,
+            jnp.take_along_axis(second, low_bits, axis=1, mode="promise_in_bounds"),
+            jnp.take_along_axis(first, low_bits, axis=1, mode="promise_in_bounds"),
+        )
+
+    opacity = 1.0 - jnp.exp(-pick(3) * density / depth)
+    return [pick(0) * opacity, pick(1) * opacity, pick(2) * opacity, opacity]
+
+
+def table_halves(colour_ref, extinction_ref, rows):
+    colour = colour_ref[...].astype(jnp.float32)
+    extinction = extinction_ref[...].astype(jnp.float32)
+    result = []
+    for channel in range(4):
+        line = extinction if channel == 3 else colour[channel : channel + 1]
+        result.append(
+            [
+                jnp.broadcast_to(line[:, half * LANES : (half + 1) * LANES], (rows, LANES))
+                for half in range(2)
+            ]
+        )
+    return result
+
+
+def pack_kernel(
+    density_ref, bins_ref, bulk_ref, first_ref, second_ref, columns_ref, own_ref, words_ref
+):
+    layers, rows, cols = density_ref.shape
+    half = rows // 2
+    me = lax.axis_index("bz")
+    words_ref[...] = pack_words(density_ref[...], bins_ref[...])
+    start = pl.multiple_of((1 - me) * half, half)
+    row_at = lax.broadcasted_iota(jnp.int32, (rows, LANES), 0)
+    lane_at = lax.broadcasted_iota(jnp.int32, (rows, LANES), 1)
+    for z in range(layers):
+        for part in range(half // 8):
+            bulk_ref[z * (half // 8) + part] = words_ref[z, pl.ds(start + part * 8, 8), :]
+        edge_rows = [words_ref[z, r : r + 1, :] for r in (0, half - 1, half, rows - 1)]
+        front = me == 0
+        bulk_ref[layers * (half // 8), z : z + 1, :] = jnp.where(front, edge_rows[1], edge_rows[2])
+        own_ref[z : z + 1, :] = jnp.where(front, edge_rows[2], edge_rows[1])
+        first_ref[z : z + 1, :] = jnp.where(front, edge_rows[3], edge_rows[0])
+        second_ref[z : z + 1, :] = jnp.where(front, edge_rows[0], edge_rows[3])
+        left = jnp.where(lane_at == row_at, words_ref[z, :, 0:1], 0)
+        right = jnp.where(lane_at == row_at + rows, words_ref[z, :, cols - 1 : cols], 0)
+        columns_ref[z : z + 1, :] = jnp.sum(left + right, axis=0, keepdims=True)
+
+
+def pack(density, bin_index):
+    layers, rows, cols = density.shape
+    words = jnp.int32
+    return pl.pallas_call(
+        pack_kernel,
+        out_shape=(
+            jax.ShapeDtypeStruct((layers * (rows // 16) + 1, 8, cols), words),
+            jax.ShapeDtypeStruct((layers, cols), words),
+            jax.ShapeDtypeStruct((layers, cols), words),
+            jax.ShapeDtypeStruct((layers, LANES), words),
+            jax.ShapeDtypeStruct((layers, cols), words),
+        ),
+        scratch_shapes=[pltpu.VMEM((layers, rows, cols), words)],
+        name="pack_cells",
+    )(density, bin_index)
+
+
+def render_kernel(
+    rank_ref, density_ref, bins_ref, colour_ref, extinction_ref, weights_ref,
+    bulk_ref, own_ref, first_ref, second_ref, columns_ref,
+    out_ref, cells_ref, halo_ref, along_ref, edge_ref, lines_ref, mixed_ref,
+):
+    layers, rows, cols = density_ref.shape
+    half = rows // 2
+    parts = half // 8
+    width = 2 * cols
+    tiles = width // LANES
+    slabs = 2
+    depth = layers * slabs
+    me, me_y, me_x = lax.axis_index("bz"), lax.axis_index("by"), lax.axis_index("bx")
+    count_y, count_x = lax.axis_size("by"), lax.axis_size("bx")
+    front = me == 0
+    start = pl.multiple_of(me * half, half)
+    total = float(depth)
+    f32 = jnp.float32
+
+    tables = table_halves(colour_ref, extinction_ref, 8)
+    lane_at = lax.broadcasted_iota(jnp.int32, (8, LANES), 1)
+    sub_at = lax.broadcasted_iota(jnp.int32, (8, LANES), 0)
+    side_lane = lane_at & (rows - 1)
+    has_side = lane_at < 2 * rows
+    column_of_right = lane_at < rows
+
+    near_y = jnp.where(front, me_y - 1, me_y + 1)
+    for slab in range(slabs):
+        for place in range(2):
+            at_y = me_y if place == 0 else near_y
+            in_y = (at_y >= 0) & (at_y < count_y)
+            read_y = jnp.clip(at_y, 0, count_y - 1)
+            row_base = (slab * count_y + read_y) * count_x
+            right = columns_ref[row_base + jnp.minimum(me_x + 1, count_x - 1)]
+            left = columns_ref[row_base + jnp.maximum(me_x - 1, 0)]
+            right = jnp.where(in_y & (me_x + 1 < count_x), right, 0)
+            left = jnp.where(in_y & (me_x > 0), left, 0)
+            words = jnp.where(has_side, jnp.where(column_of_right, right, left), 0)
+            values = cell_values(word_density(words), word_bins(words), tables, total)
+            for channel in range(4):
+                halo_ref[place, channel, pl.ds(slab * layers, layers), :] = values[channel]
+
+    def store_cells(layer, part, tile, density, bins):
+        values = cell_values(density, bins, tables, total)
+        return values
+
+    def classify_layer(z, carry, own):
+        slab = me if own else 1 - me
+        layer = slab * layers + z
+        for tile in range(cols // LANES):
+            lanes = pl.ds(tile * LANES, LANES)
+            pieces = []
+            for part in range(parts):
+                if own:
+                    density = density_ref[z, pl.ds(start + part * 8, 8), lanes]
+                    bins = bins_ref[z, pl.ds(start + part * 8, 8), lanes]
+                else:
+                    words = bulk_ref[z * parts + part, :, lanes]
+                    density, bins = word_density(words), word_bins(words)
+                pieces.append(cell_values(density, bins, tables, total))
+            for channel in range(4):
+                block = jnp.concatenate([piece[channel] for piece in pieces], axis=0)
+                base = pl.multiple_of((layer * 4 + channel) * half, half)
+                cells_ref[pl.ds(base, half), lanes] = block.astype(jnp.bfloat16)
+        for channel in range(4):
+            line = halo_ref[0, channel, pl.ds(layer, 1), :]
+            block = jnp.concatenate(
+                [
+                    jnp.where(
+                        has_side & (side_lane == sub_at + start + part * 8),
+                        jnp.broadcast_to(line, (8, LANES)),
+                        0.0,
+                    )
+                    for part in range(parts)
+                ],
+                axis=0,
+            )
+            base = pl.multiple_of((layer * 4 + channel) * half, half)
+            cells_ref[pl.ds(base, half), pl.ds(cols, LANES)] = block.astype(jnp.bfloat16)
+        return carry
+
+    lax.fori_loop(0, layers, lambda z, c: classify_layer(z, c, True), 0)
+    lax.fori_loop(0, layers, lambda z, c: classify_layer(z, c, False), 0)
+
+    edge_base = depth * 4 * half
+    words_own_near = first_ref[...]
+    words_other_near = second_ref[...]
+    words_own_in = own_ref[...]
+    words_other_in = bulk_ref[layers * parts]
+    for slab in range(slabs):
+        mine = me == slab
+        near = jnp.where(mine, words_own_near, words_other_near)
+        inside = jnp.where(mine, words_own_in, words_other_in)
+        pair = [jnp.where(front, near, inside), jnp.where(front, inside, near)]
+        for side in range(2):
+            row = jnp.where(front, rows - 1, half - 1) if side == 0 else jnp.where(front, half, 0)
+            from_near = front if side == 0 else jnp.logical_not(front)
+            for tile in range(cols // LANES):
+                words = pair[side][:, tile * LANES : (tile + 1) * LANES]
+                values = cell_values(word_density(words), word_bins(words), tables, total)
+                for channel in range(4):
+                    edge_ref[side, channel, pl.ds(slab * layers, layers), pl.ds(tile * LANES, LANES)] = values[channel]
+            for channel in range(4):
+                line = jnp.where(
+                    from_near,
+                    halo_ref[1, channel, pl.ds(slab * layers, layers), :],
+                    halo_ref[0, channel, pl.ds(slab * layers, layers), :],
+                )
+                edge_ref[side, channel, pl.ds(slab * layers, layers), pl.ds(cols, LANES)] = jnp.where(
+                    has_side & (side_lane == row), line, 0.0
+                )
+    for side in range(2):
+        for channel in range(4):
+            base = edge_base + (side * 4 + channel) * depth
+            cells_ref[pl.ds(base, depth), :] = edge_ref[side, channel].astype(jnp.bfloat16)
+
+    chunk = 128
+    pad = 4 * half
+
+    def resample_x(index, carry):
+        base = pl.multiple_of(index * chunk, chunk)
+        result = jnp.dot(
+            cells_ref[pl.ds(base, chunk), :], weights_ref[...], preferred_element_type=f32
+        )
+        result = result.astype(jnp.bfloat16).astype(f32)
+        for tile in range(tiles):
+            along_ref[tile, pl.ds(base + pad, chunk), :] = result[:, tile * LANES : (tile + 1) * LANES]
+        return carry
+
+    lax.fori_loop(0, (edge_base + 8 * depth) // chunk, resample_x, 0)
+
+    layer_at = lax.broadcasted_iota(jnp.int32, (depth, LANES), 0)
+    for tile in range(tiles):
+        for side in range(2):
+            for channel in range(4):
+                base = pad + edge_base + (side * 4 + channel) * depth
+                now = along_ref[tile, pl.ds(base, depth), :]
+                before = jnp.where(layer_at == 0, 0.0, pltpu.roll(now, 1, 0))
+                after = jnp.where(layer_at == depth - 1, 0.0, pltpu.roll(now, depth - 1, 0))
+                for parity, other in enumerate((before, after)):
+                    sample = (0.25 * other + 0.75 * now).astype(jnp.bfloat16).astype(f32)
+                    lines_ref[tile, side, channel, parity] = 0.25 * sample
+
+    for tile in range(tiles):
+        along_ref[tile, pl.ds(0, pad), :] = jnp.zeros((pad, LANES), f32)
+        along_ref[tile, pl.ds(pad + edge_base, pad), :] = jnp.zeros((pad, LANES), f32)
+
+    top = sub_at == 0
+    bottom = sub_at == 7
+
+    def layer_rows(tile, layer, channel):
+        base = pl.multiple_of(pad + (layer * 4 + channel) * half, half)
+        return [along_ref[tile, pl.ds(base + part * 8, 8), :] for part in range(parts)]
+
+    def over_layer(tile, layer, image):
+        for parity in range(2):
+            beside = layer - 1 + 2 * parity
+            clear = [[1.0 - image[3][part][odd] for odd in range(2)] for part in range(parts)]
+            updated = []
+            for channel in range(4):
+                here = layer_rows(tile, layer, channel)
+                other = layer_rows(tile, beside, channel)
+                mixed = [
+                    (0.25 * other[part] + 0.75 * here[part]).astype(jnp.bfloat16).astype(f32)
+                    for part in range(parts)
+                ]
+                quarter = [0.25 * value for value in mixed]
+                centre = [0.75 * value for value in mixed]
+                down = [pltpu.roll(value, 1, 0) for value in quarter]
+                up = [pltpu.roll(value, 7, 0) for value in quarter]
+                above = lines_ref[tile, 0, channel, parity, pl.ds(layer, 1), :]
+                below = lines_ref[tile, 1, channel, parity, pl.ds(layer, 1), :]
+                channel_image = []
+                for part in range(parts):
+                    upper = down[part - 1] if part > 0 else jnp.broadcast_to(above, (8, LANES))
+                    lower = up[part + 1] if part + 1 < parts else jnp.broadcast_to(below, (8, LANES))
+                    even = centre[part] + jnp.where(top, upper, down[part])
+                    odd = centre[part] + jnp.where(bottom, lower, up[part])
+                    channel_image.append(
+                        [
+                            image[channel][part][0] + clear[part][0] * even,
+                            image[channel][part][1] + clear[part][1] * odd,
+                        ]
+                    )
+                updated.append(channel_image)
+            image = updated
+        return image
+
+    flip = rank_ref[0]
+
+    def one_tile(tile, carry):
+        def one_slab(position, image):
+            slab = position ^ flip
+            for z in range(layers):
+                image = over_layer(tile, slab * layers + z, image)
+            return image
+
+        zero = jnp.zeros((8, LANES), f32)
+        image = [[[zero, zero] for _ in range(parts)] for _ in range(4)]
+        image = lax.fori_loop(0, slabs, one_slab, image)
+        lanes = pl.ds(pl.multiple_of(tile * LANES, LANES), LANES)
+        for channel in range(4):
+            for part in range(parts):
+                for odd in range(2):
+                    mixed_ref[channel, pl.ds(part * 16 + odd, 8, stride=2), :] = image[channel][part][odd]
+            out_ref[channel, :, lanes] = mixed_ref[channel]
+        return carry
+
+    lax.fori_loop(0, tiles, one_tile, 0)
+
+
+def column_weights(cols, rows):
+    table = np.zeros((cols + LANES, 2 * cols), np.float32)
+    for c in range(cols):
+        table[c, 2 * c : 2 * c + 2] = 0.75
+        if c > 0:
+            table[c - 1, 2 * c] = 0.25
+        if c + 1 < cols:
+            table[c + 1, 2 * c + 1] = 0.25
+    table[cols : cols + rows, 2 * cols - 1] = 0.25
+    table[cols + rows : cols + 2 * rows, 0] = 0.25
+    return jnp.asarray(table, jnp.bfloat16)
+
+
+def two_slab_device(density, bin_index, tf_colour, tf_extinction, slab_rank):
+    layers, rows, cols = density.shape
+    half = rows // 2
+    depth = 2 * layers
+    tiles = 2 * cols // LANES
+    count_y, count_x = lax.axis_size("by"), lax.axis_size("bx")
+    bulk, first, second, columns, own = pack(density, bin_index)
+
+    def at(z, y):
+        return z * count_y + y
+
+    swap = [(0, 1), (1, 0)]
+    same_slab = [(at(0, y), at(0, y + 1)) for y in range(count_y - 1)]
+    same_slab += [(at(1, y + 1), at(1, y)) for y in range(count_y - 1)]
+    other_slab = [(at(1, y), at(0, y + 1)) for y in range(count_y - 1)]
+    other_slab += [(at(0, y + 1), at(1, y)) for y in range(count_y - 1)]
+    columns = lax.all_gather(columns, ("bz", "by", "bx"))
+    bulk = lax.ppermute(bulk, "bz", swap)
+    first = lax.ppermute(first, ("bz", "by"), same_slab)
+    second = lax.ppermute(second, ("bz", "by"), other_slab)
+    f32 = jnp.float32
+    vmem = pl.BlockSpec(memory_space=pltpu.VMEM)
+    cell_rows = depth * 4 * half + 8 * depth
+    return pl.pallas_call(
+        render_kernel,
+        out_shape=jax.ShapeDtypeStruct((4, rows, 2 * cols), f32),
+        in_specs=[pl.BlockSpec(memory_space=pltpu.SMEM)] + [vmem] * 10,
+        out_specs=vmem,
+        scratch_shapes=[
+            pltpu.VMEM((cell_rows, cols + LANES), jnp.bfloat16),
+            pltpu.VMEM((2, 4, depth, LANES), f32),
+            pltpu.VMEM((tiles, cell_rows + 8 * half, LANES), f32),
+            pltpu.VMEM((2, 4, depth, cols + LANES), f32),
+            pltpu.VMEM((tiles, 2, 4, 2, depth, LANES), f32),
+            pltpu.VMEM((4, rows, LANES), f32),
+        ],
+        compiler_params=pltpu.CompilerParams(vmem_limit_bytes=32 * 1024 * 1024),
+        name="render_block",
+    )(
+        slab_rank, density, bin_index, tf_colour, tf_extinction.reshape(1, -1),
+        column_weights(cols, rows), bulk, own, first, second, columns,
+    )
+
+
+def on_device(density, bin_index, tf_colour, tf_extinction, slab_rank):
+    if lax.axis_size("bz") == 2:
+        return two_slab_device(density, bin_index, tf_colour, tf_extinction, slab_rank)
+    return general_device(density, bin_index, tf_colour, tf_extinction, slab_rank)
+
+
 def solution(mesh):
     return jax.shard_map(
         on_device,

time: 82.7 us -> 60.1 us (0.73)
  the two profiles are of different devices: /device:TPU:20 before, /device:TPU:0 now
where the time goes in v1:
time: 60.1 us; the launch traced here: 59.1 us
  blocking collectives  40 us (67%)
  Pallas kernels  10.2 us (17%)
  starting transfers between devices  7.07 us (12%)
  local copies, waits for them, and re-layouts  1.64 us (3%)
    all_gather x1, blocking collectives, two_slab_device(): columns = lax.all_gather(columns, ('bz', 'by', 'bx'))  40 us
    pallas_call x1, Pallas kernels, two_slab_device(): pl.pallas_call(render_kernel, out_shape=jax.ShapeDtypeStruct((4, rows, 2...  8.35 us
    ppermute x1, starting transfers between devices, two_slab_device(): first = lax.ppermute(first, ('bz', 'by'), same_slab)  3.47 us
    ppermute x1, starting transfers between devices, two_slab_device(): bulk = lax.ppermute(bulk, 'bz', swap)  2.94 us
    pallas_call x1, Pallas kernels, pack(): pl.pallas_call(pack_kernel, out_shape=(jax.ShapeDtypeStruct((layers * (ro...  1.88 us
    unnamed x16, local copies, waits for them, and re-layouts  1.64 us
  transfers between devices with their start and end apart: 3, of which 0 were waited for; matrix products, arithmetic and copies ran while one was open for 0% of the time, Pallas kernels for 0%

profile of v1, /device:TPU:0, one launch (start us, length us, event | category | flops | bytes accessed | tf_op | source)
XLA Modules:
  0.0 59.1 jit_solution(14954353616653557208)
XLA Ops:
  0.0 0.0 copy-start.1
  0.0 0.0 copy-start
  0.0 1.9 %pack_cells.1 = (s32[17,8,256]{2,1,0:T(8,128)}, s32[8,256]{1,0:T(8,128)}, s32[8,256]{1,0:T(8,128)}, s32[8,128]{1,0:T(8,128)}, s32[8,256]{1,0:T(8,128)}) custom-call(f32[8,32,256]{2,1,0:T(8,128)} %density_ref.3, s32[8,32,256]{2,1,0:T(8,128)} %bins_ref.3), custom_call_target="tpu_custom_call" | custom-call | tf_op jit(solution)/shard_map/pack_cells/pallas_call | solution.py:192
  1.9 0.0 copy-start.6
  1.9 2.9 %collective-permute-start = (s32[17,8,256]{2,1,0:T(8,128)}, s32[17,8,256]{2,1,0:T(8,128)S(1)}, u32[]{:S(2)}, u32[]{:S(2)}) collective-permute-start(s32[17,8,256]{2,1,0:T(8,128)} %get-tuple-element.10), channel_id=1, source_target_pairs={{0,16},{16,0},{1,17},{17,1},{2,18},{18,2},{3,19},{19,3},{4,20},{20... | collective-permute-start | bytes 417800 | tf_op jit(solution)/shard_map/ppermute | solution.py:447
  4.8 3.5 %collective-permute-start.1 = (s32[8,256]{1,0:T(8,128)}, s32[8,256]{1,0:T(8,128)S(1)}, u32[]{:S(2)}, u32[]{:S(2)}) collective-permute-start(s32[8,256]{1,0:T(8,128)} %get-tuple-element.12), channel_id=1, source_target_pairs={{0,4},{4,8},{8,12},{20,16},{24,20},{28,24},{1,5},{5,9},{9,13},{21,... | collective-permute-start | bytes 24584 | tf_op jit(solution)/shard_map/ppermute | solution.py:448
  8.3 0.7 %collective-permute-start.2 = (s32[8,256]{1,0:T(8,128)}, s32[8,256]{1,0:T(8,128)S(1)}, u32[]{:S(2)}, u32[]{:S(2)}) collective-permute-start(s32[8,256]{1,0:T(8,128)} %get-tuple-element.13), channel_id=1, source_target_pairs={{16,4},{20,8},{24,12},{4,16},{8,20},{12,24},{17,5},{21,9},{25,13},... | collective-permute-start | bytes 24584 | tf_op jit(solution)/shard_map/ppermute | solution.py:449
  9.0 0.0 copy-done.6
  9.0 0.0 copy-start.7
  9.0 0.0 copy-start.3
  9.0 40.0 %all-gather = s32[256,128]{1,0:T(8,128)S(1)} all-gather(s32[8,128]{1,0:T(8,128)S(1)} %copy-done.6), channel_id=2, replica_groups=mesh['bz'=2,'by'=4,'bx'=4] {'bz','by','bx'}, dimensions={0}, use_global_device_ids=true | all-gather | bytes 135168 | tf_op jit(solution)/shard_map/all_gather | solution.py:446
  49.1 0.0 copy-done.7
  49.1 0.0 copy-start.4
  49.1 0.0 collective-permute-done.1.first_ref
  49.1 0.0 collective-permute-done.2.second_ref
  49.1 0.0 collective-permute-done.bulk_ref
  49.1 0.0 copy-start.5
  49.1 0.0 copy-done.1
  49.1 0.0 copy-done
  49.1 0.0 copy-done.3
  49.1 0.6 %copy-done.4 = bf16[3,256]{1,0:T(4,128)(2,1)S(1)} copy-done((bf16[3,256]{1,0:T(4,128)(2,1)S(1)}, bf16[3,256]{1,0:T(4,128)(2,1)}, u32[]{:S(2)}) %copy-start.4) | copy-done | bytes 1560
  49.7 0.0 copy-done.5
  49.8 0.0 copy-start.2
  49.8 1.0 %copy-done.2 = bf16[384,512]{1,0:T(8,128)(2,1)S(1)} copy-done((bf16[384,512]{1,0:T(8,128)(2,1)S(1)}, bf16[384,512]{1,0:T(8,128)(2,1)}, u32[]{:S(2)}) %copy-start.2) | copy-done | bytes 393240
  50.7 8.3 %render_block.1 = f32[4,32,512]{2,1,0:T(8,128)} custom-call(s32[2]{0:T(128)S(1)} %copy-done.5, f32[8,32,256]{2,1,0:T(8,128)S(1)} %copy-done, s32[8,32,256]{2,1,0:T(8,128)S(1)} %copy-done.1, bf16[3,256]{1,0:T(4,128)(2,1)S(1)} %copy-done.4, bf16[1,256]{1,0:T(2,128)(2,1)S(1)} %reshape.3.extinction_ref, bf16[384,512]{1,0:T(8,128)(2,1)S(1)} %copy-done.2, ...), custom_call_target="tpu_custom_call" | custom-call | tf_op jit(solution)/shard_map/render_block/pallas_call | solution.py:453
  (1 shorter events, 0.0 us)
Async XLA Ops:
  0.0 49.1 %copy-start.1 = (s32[8,32,256]{2,1,0:T(8,128)S(1)}, s32[8,32,256]{2,1,0:T(8,128)}, u32[]{:S(2)}) copy-start(s32[8,32,256]{2,1,0:T(8,128)} %bins_ref.3) | copy-start | bytes 786436
  0.0 49.1 %copy-start = (f32[8,32,256]{2,1,0:T(8,128)S(1)}, f32[8,32,256]{2,1,0:T(8,128)}, u32[]{:S(2)}) copy-start(f32[8,32,256]{2,1,0:T(8,128)} %density_ref.3) | copy-start | bytes 786436
  1.9 7.1 %copy-start.6 = (s32[8,128]{1,0:T(8,128)S(1)}, s32[8,128]{1,0:T(8,128)}, u32[]{:S(2)}) copy-start(s32[8,128]{1,0:T(8,128)} %get-tuple-element.14) | copy-start | bytes 12292
  1.9 47.2 %collective-permute-start = (s32[17,8,256]{2,1,0:T(8,128)}, s32[17,8,256]{2,1,0:T(8,128)S(1)}, u32[]{:S(2)}, u32[]{:S(2)}) collective-permute-start(s32[17,8,256]{2,1,0:T(8,128)} %get-tuple-element.10), channel_id=1, source_target_pairs={{0,16},{16,0},{1,17},{17,1},{2,18},{18,2},{3,19},{19,3},{4,20},{20... | collective-permute-start | bytes 417800 | tf_op jit(solution)/shard_map/ppermute | solution.py:447
  4.8 44.2 %collective-permute-start.1 = (s32[8,256]{1,0:T(8,128)}, s32[8,256]{1,0:T(8,128)S(1)}, u32[]{:S(2)}, u32[]{:S(2)}) collective-permute-start(s32[8,256]{1,0:T(8,128)} %get-tuple-element.12), channel_id=1, source_target_pairs={{0,4},{4,8},{8,12},{20,16},{24,20},{28,24},{1,5},{5,9},{9,13},{21,... | collective-permute-start | bytes 24584 | tf_op jit(solution)/shard_map/ppermute | solution.py:448
  8.3 40.8 %collective-permute-start.2 = (s32[8,256]{1,0:T(8,128)}, s32[8,256]{1,0:T(8,128)S(1)}, u32[]{:S(2)}, u32[]{:S(2)}) collective-permute-start(s32[8,256]{1,0:T(8,128)} %get-tuple-element.13), channel_id=1, source_target_pairs={{16,4},{20,8},{24,12},{4,16},{8,20},{12,24},{17,5},{21,9},{25,13},... | collective-permute-start | bytes 24584 | tf_op jit(solution)/shard_map/ppermute | solution.py:449
  9.0 40.1 %copy-start.7 = (bf16[256]{0:T(256)(128)(2,1)S(1)}, bf16[256]{0:T(256)(128)(2,1)}, u32[]{:S(2)}) copy-start(bf16[256]{0:T(256)(128)(2,1)} %param.9) | copy-start | bytes 1540
  9.0 40.1 %copy-start.3 = (s32[8,256]{1,0:T(8,128)S(1)}, s32[8,256]{1,0:T(8,128)}, u32[]{:S(2)}) copy-start(s32[8,256]{1,0:T(8,128)} %get-tuple-element.11.own_ref) | copy-start | bytes 24580
  49.1 0.7 %copy-start.4 = (bf16[3,256]{1,0:T(4,128)(2,1)S(1)}, bf16[3,256]{1,0:T(4,128)(2,1)}, u32[]{:S(2)}) copy-start(bf16[3,256]{1,0:T(4,128)(2,1)} %colour_ref.1) | copy-start | bytes 4612
  49.1 0.7 %copy-start.5 = (s32[2]{0:T(128)S(1)}, s32[2]{0:T(128)}, u32[]{:S(2)}) copy-start(s32[2]{0:T(128)} %rank_ref.1) | copy-start | bytes 28
  49.8 1.0 %copy-start.2 = (bf16[384,512]{1,0:T(8,128)(2,1)S(1)}, bf16[384,512]{1,0:T(8,128)(2,1)}, u32[]{:S(2)}) copy-start(bf16[384,512]{1,0:T(8,128)(2,1)} %constant.2.clone.weights_ref) | copy-start | bytes 1179652

commit v2 on v0

--- a/solution.py
+++ b/solution.py
@@ -1,6 +1,8 @@
 import jax
 import jax.numpy as jnp
 from jax import lax
+from jax.experimental import pallas as pl
+from jax.experimental.pallas import tpu as pltpu
 from jax.sharding import PartitionSpec as P
 
 
@@ -66,7 +68,7 @@
     return classified.reshape(4, depth_cells, height_cells, width_cells)
 
 
-def on_device(density, bin_index, tf_colour, tf_extinction, slab_rank):
+def general_device(density, bin_index, tf_colour, tf_extinction, slab_rank):
     slab_count = lax.axis_size("bz")
     depth_cells, height_cells, width_cells = density.shape
     total_depth = float(depth_cells * slab_count)
@@ -111,6 +113,461 @@
     return composite
 
 
+LANES = 128
+LEVELS = 65535.0
+VMEM = pl.BlockSpec(memory_space=pltpu.VMEM)
+
+
+def pack_words(density, bins):
+    level = (density * LEVELS + 0.5).astype(jnp.int32)
+    return lax.shift_left(level, 16) | bins
+
+
+def unpack_words(words):
+    density = lax.shift_right_logical(words, 16).astype(jnp.float32) * (1.0 / LEVELS)
+    return density, words & 0xFFFF
+
+
+def cell_values(density, bins, tables, depth):
+    low_bits = bins & (LANES - 1)
+    upper = bins >= LANES
+
+    def pick(channel):
+        first, second = tables[channel]
+        return jnp.where(
+            upper,
+            jnp.take_along_axis(second, low_bits, axis=1, mode="promise_in_bounds"),
+            jnp.take_along_axis(first, low_bits, axis=1, mode="promise_in_bounds"),
+        )
+
+    opacity = (1.0 - jnp.exp(-pick(3) * density / depth)) * (1.0 / 64.0)
+    return [pick(0) * opacity, pick(1) * opacity, pick(2) * opacity, opacity]
+
+
+def table_halves(colour_ref, extinction_ref):
+    colour = colour_ref[...].astype(jnp.float32)
+    extinction = extinction_ref[...].astype(jnp.float32)
+    result = []
+    for channel in range(4):
+        line = extinction if channel == 3 else colour[channel : channel + 1]
+        result.append(
+            [
+                jnp.broadcast_to(line[:, half * LANES : (half + 1) * LANES], (8, LANES))
+                for half in range(2)
+            ]
+        )
+    return result
+
+
+def cost(microseconds):
+    return pl.CostEstimate(
+        flops=0, bytes_accessed=int(3.6e6 * microseconds), transcendentals=0
+    )
+
+
+def columns_kernel(density_hbm, bins_hbm, columns_ref, density_ref, bins_ref, sems):
+    layers, rows, cols = density_ref.shape
+    copies = [
+        pltpu.make_async_copy(density_hbm, density_ref, sems.at[0]),
+        pltpu.make_async_copy(bins_hbm, bins_ref, sems.at[1]),
+    ]
+    for copy in copies:
+        copy.start()
+    for copy in copies:
+        copy.wait()
+    row_at = lax.broadcasted_iota(jnp.int32, (rows, LANES), 0)
+    lane_at = lax.broadcasted_iota(jnp.int32, (rows, LANES), 1)
+    for z in range(layers):
+        first = pack_words(density_ref[z, :, 0:1], bins_ref[z, :, 0:1])
+        last = pack_words(density_ref[z, :, cols - 1 : cols], bins_ref[z, :, cols - 1 : cols])
+        line = jnp.where(lane_at == row_at, first, 0) + jnp.where(lane_at == row_at + rows, last, 0)
+        columns_ref[z : z + 1, :] = jnp.sum(line, axis=0, keepdims=True)
+
+
+def pack_kernel(density_ref, bins_ref, bulk_ref, edges_ref, words_ref):
+    layers, rows, cols = density_ref.shape
+    half = rows // 2
+    front = lax.axis_index("bz") == 0
+    start = pl.multiple_of(jnp.where(front, half, 0), half)
+    for z in range(layers):
+        words = pack_words(
+            density_ref[z, pl.ds(start, half), :], bins_ref[z, pl.ds(start, half), :]
+        )
+        for tile in range(cols // LANES):
+            lanes = slice(tile * LANES, (tile + 1) * LANES)
+            words_ref[z, tile] = words[:, lanes]
+            for part in range(2):
+                bulk_ref[2 * z + part, :, lanes] = words_ref[z, tile, pl.ds(part, 8, stride=2), :]
+        line = [
+            pack_words(density_ref[z, r : r + 1, :], bins_ref[z, r : r + 1, :])
+            for r in (0, half - 1, half, rows - 1)
+        ]
+        bulk_ref[2 * layers, z : z + 1, :] = jnp.where(front, line[1], line[2])
+        edges_ref[0, z : z + 1, :] = jnp.where(front, line[2], line[1])
+        edges_ref[1, z : z + 1, :] = jnp.where(front, line[0], line[3])
+
+
+def diagonal_kernel(bulk_ref, edges_ref, halo_ref, weights_ref, line_ref):
+    layers = edges_ref.shape[1]
+    cols = edges_ref.shape[2]
+    front = lax.axis_index("bz") == 0
+    other = jnp.concatenate(
+        [
+            jnp.where(front, bulk_ref[2 * z, 0:1, :], bulk_ref[2 * z + 1, 7:8, :])
+            for z in range(layers)
+        ],
+        axis=0,
+    )
+    mine = edges_ref[1]
+    line_ref[0] = jnp.where(front, mine, other)
+    line_ref[1] = jnp.where(front, other, mine)
+    halo = halo_ref[...]
+    halo_other = bulk_ref[2 * layers + 1, :, 0:LANES]
+    line_ref[2, :, 0:LANES] = jnp.where(front, halo, halo_other)
+    line_ref[2, :, LANES : 2 * LANES] = jnp.where(front, halo_other, halo)
+
+
+def fill_weights(weights_ref, rows):
+    cols = weights_ref.shape[0] - LANES
+    row = lax.broadcasted_iota(jnp.int32, (cols, 2 * cols), 0)
+    at = lax.broadcasted_iota(jnp.int32, (cols, 2 * cols), 1)
+    centre = lax.shift_right_logical(at, 1)
+    beside = centre - 1 + 2 * (at & 1)
+    weights_ref[0:cols, :] = jnp.where(
+        row == centre, 3.0, jnp.where(row == beside, 1.0, 0.0)
+    ).astype(jnp.bfloat16)
+    row = lax.broadcasted_iota(jnp.int32, (LANES, 2 * cols), 0)
+    at = lax.broadcasted_iota(jnp.int32, (LANES, 2 * cols), 1)
+    right = (row < rows) & (at == 2 * cols - 1)
+    left = (row >= rows) & (row < 2 * rows) & (at == 0)
+    weights_ref[cols : cols + LANES, :] = jnp.where(right | left, 1.0, 0.0).astype(jnp.bfloat16)
+
+
+def lane_maps(rows):
+    lane_at = lax.broadcasted_iota(jnp.int32, (8, LANES), 1)
+    sub_at = lax.broadcasted_iota(jnp.int32, (8, LANES), 0)
+    return lane_at & (rows - 1), lane_at < 2 * rows, sub_at
+
+
+def along_columns(read_cells, halo_words, tables, weights_ref, cells_ref, values_ref, store, rows, layers, cols):
+    total = float(2 * layers)
+    start = lax.axis_index("bz") * (rows // 2)
+    side_lane, has_side, sub_at = lane_maps(rows)
+    halo = cell_values(*unpack_words(halo_words), tables, total)
+    for channel in range(4):
+        values_ref[channel] = halo[channel]
+    for z in range(layers):
+        for tile in range(cols // LANES):
+            even = cell_values(*read_cells(z, 0, tile), tables, total)
+            odd = cell_values(*read_cells(z, 1, tile), tables, total)
+            for channel in range(4):
+                base = (z * 4 + channel) * 16
+                block = jnp.concatenate([even[channel], odd[channel]], axis=0)
+                cells_ref[base : base + 16, tile * LANES : (tile + 1) * LANES] = block.astype(jnp.bfloat16)
+        for channel in range(4):
+            base = (z * 4 + channel) * 16
+            line = jnp.broadcast_to(values_ref[channel, z : z + 1, :], (8, LANES))
+            block = jnp.concatenate(
+                [
+                    jnp.where(has_side & (side_lane == start + 2 * sub_at + part), line, 0.0)
+                    for part in range(2)
+                ],
+                axis=0,
+            )
+            cells_ref[base : base + 16, cols : cols + LANES] = block.astype(jnp.bfloat16)
+    result = jnp.dot(cells_ref[...], weights_ref[...], preferred_element_type=jnp.float32)
+    result = result.astype(jnp.bfloat16).astype(jnp.float32)
+    for tile in range(2 * cols // LANES):
+        store(tile, result[:, tile * LANES : (tile + 1) * LANES])
+
+
+def own_kernel(
+    density_ref, bins_ref, colour_ref, extinction_ref, halo_ref,
+    along_ref, weights_ref, cells_ref, values_ref, rows_ref, binrows_ref,
+):
+    layers, rows, cols = density_ref.shape
+    half = rows // 2
+    start = pl.multiple_of(lax.axis_index("bz") * half, half)
+    fill_weights(weights_ref, rows)
+    tables = table_halves(colour_ref, extinction_ref)
+    for z in range(layers):
+        for tile in range(cols // LANES):
+            lanes = slice(tile * LANES, (tile + 1) * LANES)
+            rows_ref[z, tile] = density_ref[z, pl.ds(start, half), lanes]
+            binrows_ref[z, tile] = bins_ref[z, pl.ds(start, half), lanes]
+
+    def read_cells(z, part, tile):
+        at = pl.ds(part, 8, stride=2)
+        return rows_ref[z, tile, at, :], binrows_ref[z, tile, at, :]
+
+    def store(tile, block):
+        along_ref[tile] = block
+
+    along_columns(
+        read_cells, halo_ref[...], tables, weights_ref, cells_ref, values_ref, store, rows, layers, cols
+    )
+
+
+def other_kernel(
+    bulk_ref, colour_ref, extinction_ref, weights_ref, own_ref,
+    along_ref, cells_ref, values_ref,
+):
+    layers = (bulk_ref.shape[0] - 2) // 2
+    cols = bulk_ref.shape[2]
+    size = own_ref.shape[1]
+    rows = 32
+    me = lax.axis_index("bz")
+    tables = table_halves(colour_ref, extinction_ref)
+    pad = size // layers
+    mine = pl.multiple_of(pad + me * size, pad)
+    theirs = pl.multiple_of(pad + (1 - me) * size, pad)
+    for tile in range(own_ref.shape[0]):
+        along_ref[tile, 0:pad, :] = jnp.zeros((pad, LANES), jnp.float32)
+        along_ref[tile, pad + 2 * size : 2 * pad + 2 * size, :] = jnp.zeros((pad, LANES), jnp.float32)
+        along_ref[tile, pl.ds(mine, size), :] = own_ref[tile]
+
+    def read_cells(z, part, tile):
+        return unpack_words(bulk_ref[2 * z + part, :, tile * LANES : (tile + 1) * LANES])
+
+    def store(tile, block):
+        along_ref[tile, pl.ds(theirs, size), :] = block
+
+    along_columns(
+        read_cells, bulk_ref[2 * layers + 1, :, 0:LANES], tables, weights_ref, cells_ref, values_ref,
+        store, rows, layers, cols,
+    )
+
+
+def render_kernel(
+    rank_ref, colour_ref, extinction_ref, weights_ref, bulk_ref, edges_ref, halo_ref, near_ref, along_ref,
+    out_ref, cells_ref, lines_ref, mixed_ref,
+):
+    layers, cols = edges_ref.shape[1:]
+    depth = 2 * layers
+    rows = out_ref.shape[1]
+    half = rows // 2
+    tiles = 2 * cols // LANES
+    total = float(depth)
+    f32 = jnp.float32
+    me = lax.axis_index("bz")
+    front = me == 0
+    tables = table_halves(colour_ref, extinction_ref)
+    side_lane, has_side, sub_at = lane_maps(rows)
+
+    for slab in range(2):
+        mine = me == slab
+        inside = jnp.where(mine, edges_ref[0], bulk_ref[2 * layers])
+        halo_inside = jnp.where(mine, halo_ref[...], bulk_ref[2 * layers + 1, :, 0:LANES])
+        near = near_ref[slab]
+        halo_near = near_ref[2, :, slab * LANES : (slab + 1) * LANES]
+        for side in range(2):
+            row = jnp.where(front, rows - 1, half - 1) if side == 0 else jnp.where(front, half, 0)
+            use_near = front if side == 0 else jnp.logical_not(front)
+            words = jnp.where(use_near, near, inside)
+            halo = jnp.where(use_near, halo_near, halo_inside)
+            base = side * 4 * depth + slab * layers
+            blocks = [
+                cell_values(*unpack_words(words[:, t * LANES : (t + 1) * LANES]), tables, total)
+                for t in range(cols // LANES)
+            ]
+            values = cell_values(*unpack_words(halo), tables, total)
+            blocks.append([jnp.where(has_side & (side_lane == row), value, 0.0) for value in values])
+            for channel in range(4):
+                for t, block in enumerate(blocks):
+                    cells_ref[
+                        base + channel * depth : base + channel * depth + layers,
+                        t * LANES : (t + 1) * LANES,
+                    ] = block[channel]
+    edge = jnp.dot(
+        cells_ref[...].astype(jnp.bfloat16), weights_ref[...], preferred_element_type=f32
+    )
+    edge = edge.astype(jnp.bfloat16).astype(f32)
+    layer_at = lax.broadcasted_iota(jnp.int32, (depth, LANES), 0)
+    for tile in range(tiles):
+        for side in range(2):
+            for channel in range(4):
+                base = (side * 4 + channel) * depth
+                now = edge[base : base + depth, tile * LANES : (tile + 1) * LANES]
+                triple = 3.0 * now
+                before = jnp.where(layer_at == 0, 0.0, pltpu.roll(now, 1, 0))
+                after = jnp.where(layer_at == depth - 1, 0.0, pltpu.roll(now, depth - 1, 0))
+                for parity, beside in enumerate((before, after)):
+                    lines_ref[tile, side, channel, parity] = (
+                        (beside + triple).astype(jnp.bfloat16).astype(f32)
+                    )
+
+    top = sub_at == 0
+    bottom = sub_at == 7
+
+    def layer_rows(tile, layer, channel):
+        base = pl.multiple_of((layer * 4 + channel) * 16, 16)
+        return [along_ref[tile, pl.ds(base + part * 8, 8), :] for part in range(2)]
+
+    def over_layer(tile, layer, image):
+        here = [layer_rows(tile, layer + 1, channel) for channel in range(4)]
+        triple = [[3.0 * value for value in pair] for pair in here]
+        for parity in range(2):
+            clear = [1.0 - value for value in image[3]]
+            updated = []
+            for channel in range(4):
+                beside = layer_rows(tile, layer + 2 * parity, channel)
+                even, odd = [
+                    (beside[part] + triple[channel][part]).astype(jnp.bfloat16).astype(f32)
+                    for part in range(2)
+                ]
+                above = lines_ref[tile, 0, channel, parity, pl.ds(layer, 1), :]
+                below = lines_ref[tile, 1, channel, parity, pl.ds(layer, 1), :]
+                before_even = jnp.where(top, jnp.broadcast_to(above, (8, LANES)), pltpu.roll(odd, 1, 0))
+                after_odd = jnp.where(bottom, jnp.broadcast_to(below, (8, LANES)), pltpu.roll(even, 7, 0))
+                even_centre = 3.0 * even
+                odd_centre = 3.0 * odd
+                samples = [
+                    before_even + even_centre, even_centre + odd, even + odd_centre, odd_centre + after_odd
+                ]
+                updated.append(
+                    [image[channel][i] + clear[i] * samples[i] for i in range(4)]
+                )
+            image = updated
+        return image
+
+    flip = rank_ref[0]
+
+    def one_tile(tile, carry):
+        def one_slab(position, image):
+            slab = position ^ flip
+            for z in range(layers):
+                image = over_layer(tile, slab * layers + z, image)
+            return image
+
+        zero = jnp.zeros((8, LANES), f32)
+        image = [[zero] * 4 for _ in range(4)]
+        image = lax.fori_loop(0, 2, one_slab, image)
+        lanes = pl.ds(pl.multiple_of(tile * LANES, LANES), LANES)
+        for channel in range(4):
+            for i in range(4):
+                mixed_ref[channel, pl.ds(i, 8, stride=4), :] = image[channel][i]
+            out_ref[channel, :, lanes] = mixed_ref[channel]
+        return carry
+
+    lax.fori_loop(0, tiles, one_tile, 0)
+
+
+def two_slab_device(density, bin_index, tf_colour, tf_extinction, slab_rank):
+    layers, rows, cols = density.shape
+    half = rows // 2
+    tiles = 2 * cols // LANES
+    size = layers * 4 * half
+    count_y, count_x = lax.axis_size("by"), lax.axis_size("bx")
+    f32, bf16, i32 = jnp.float32, jnp.bfloat16, jnp.int32
+    extinction = tf_extinction.reshape(1, -1)
+    params = pltpu.CompilerParams(vmem_limit_bytes=16 * 1024 * 1024)
+
+    hbm = pl.BlockSpec(memory_space=pltpu.HBM)
+    density = pltpu.with_memory_space_constraint(density, pltpu.HBM)
+    bin_index = pltpu.with_memory_space_constraint(bin_index, pltpu.HBM)
+    columns, density, bin_index = pl.pallas_call(
+        columns_kernel,
+        out_shape=(
+            pltpu.VMEM((layers, LANES), i32),
+            pltpu.VMEM(density.shape, f32),
+            pltpu.VMEM(density.shape, i32),
+        ),
+        in_specs=[hbm] * 2,
+        out_specs=(VMEM,) * 3,
+        scratch_shapes=[pltpu.SemaphoreType.DMA((2,))],
+        compiler_params=params,
+        cost_estimate=cost(1.0),
+        name="pack_columns",
+    )(density, bin_index)
+
+    pairs = [(x, x + 1) for x in range(0, count_x - 1, 2)]
+    cross = [(x, x + 1) for x in range(1, count_x - 1, 2)]
+
+    def both(route):
+        return route + [(target, source) for source, target in route]
+
+    across = lax.ppermute(columns, "bx", both(cross))
+    beside = lax.ppermute(columns, "bx", both(pairs))
+    bulk, edges = pl.pallas_call(
+        pack_kernel,
+        out_shape=(pltpu.VMEM((2 * layers + 1, 8, cols), i32), pltpu.VMEM((2, layers, cols), i32)),
+        in_specs=[VMEM] * 2,
+        out_specs=(VMEM, VMEM),
+        scratch_shapes=[pltpu.VMEM((layers, cols // LANES, half, LANES), i32)],
+        compiler_params=params,
+        cost_estimate=cost(0.7),
+        name="pack_block",
+    )(density, bin_index)
+    lane_at = lax.broadcasted_iota(i32, (layers, LANES), 1)
+    right_is_beside = lax.axis_index("bx") % 2 == 0
+    halo = jnp.where((lane_at < rows) == right_is_beside, beside, across)
+    bulk = jnp.concatenate([bulk, jnp.concatenate([halo] * (cols // LANES), axis=1)[None]], axis=0)
+    bulk = lax.ppermute(bulk, "bz", [(0, 1), (1, 0)])
+
+    along, weights = pl.pallas_call(
+        own_kernel,
+        out_shape=(pltpu.VMEM((tiles, size, LANES), f32), pltpu.VMEM((cols + LANES, 2 * cols), bf16)),
+        in_specs=[VMEM] * 5,
+        out_specs=(VMEM, VMEM),
+        scratch_shapes=[
+            pltpu.VMEM((size, cols + LANES), bf16),
+            pltpu.VMEM((4, layers, LANES), f32),
+            pltpu.VMEM((layers, cols // LANES, half, LANES), f32),
+            pltpu.VMEM((layers, cols // LANES, half, LANES), i32),
+        ],
+        compiler_params=params,
+        cost_estimate=cost(2.0),
+        name="own_slab",
+    )(density, bin_index, tf_colour, extinction, halo)
+
+    line = pl.pallas_call(
+        diagonal_kernel,
+        out_shape=pltpu.VMEM((3, layers, cols), i32),
+        in_specs=[VMEM] * 4,
+        out_specs=VMEM,
+        compiler_params=params,
+        cost_estimate=cost(0.2),
+        name="diagonal_line",
+    )(bulk, edges, halo, weights)
+    route = [(count_y + y, y + 1) for y in range(count_y - 1)]
+    near = lax.ppermute(line, ("bz", "by"), both(route))
+
+    along = pl.pallas_call(
+        other_kernel,
+        out_shape=pltpu.VMEM((tiles, 2 * size + 2 * 4 * half, LANES), f32),
+        in_specs=[VMEM] * 5,
+        out_specs=VMEM,
+        scratch_shapes=[
+            pltpu.VMEM((size, cols + LANES), bf16),
+            pltpu.VMEM((4, layers, LANES), f32),
+        ],
+        compiler_params=params,
+        cost_estimate=cost(2.0),
+        name="other_slab",
+    )(bulk, tf_colour, extinction, weights, along)
+
+    return pl.pallas_call(
+        render_kernel,
+        out_shape=jax.ShapeDtypeStruct((4, rows, 2 * cols), f32),
+        in_specs=[pl.BlockSpec(memory_space=pltpu.SMEM)] + [VMEM] * 8,
+        out_specs=VMEM,
+        scratch_shapes=[
+            pltpu.VMEM((8 * 2 * layers, cols + LANES), f32),
+            pltpu.VMEM((tiles, 2, 4, 2, 2 * layers, LANES), f32),
+            pltpu.VMEM((4, rows, LANES), f32),
+        ],
+        compiler_params=params,
+        cost_estimate=cost(5.0),
+        name="render_rows",
+    )(slab_rank, tf_colour, extinction, weights, bulk, edges, halo, near, along)
+
+
+def on_device(density, bin_index, tf_colour, tf_extinction, slab_rank):
+    if lax.axis_size("bz") == 2:
+        return two_slab_device(density, bin_index, tf_colour, tf_extinction, slab_rank)
+    return general_device(density, bin_index, tf_colour, tf_extinction, slab_rank)
+
+
 def solution(mesh):
     return jax.shard_map(
         on_device,

time: 82.7 us -> 21.9 us (0.26); the launches traced: 81.7 us -> 21.8 us
  other arithmetic: 23.2 us -> 0.03 us
  matrix products: 17.8 us -> 0 us
  waiting for transfers between devices: 18.5 us -> 5.76 us
  starting transfers between devices: 15 us -> 7.42 us
  Pallas kernels: 0 us -> 7.11 us
  local copies, waits for them, and re-layouts: 4.41 us -> 1.35 us
  loops' own time: 1.39 us -> 0 us
  between operations: 1.45 us -> 0.1 us
    convert_element_type x16 -> x0, other arithmetic: 18.3 us -> none  [add_sample(): layers = lax.dynamic_slice_in_dim(along_x, centre, 3, 1).astype(jnp.float32)]
    dot_general x25 -> x0, matrix products: 17.8 us -> none  [the longest x8 10.7 us: one_layer(): values = jnp.dot(lookup, one_hot, preferred_element_type=jnp.float32)]
    ppermute x7 -> x4, waiting for transfers between devices: 18.5 us -> 5.76 us  [the longest x1 2.29 us: two_slab_device(): across = lax.ppermute(columns, 'bx', both(cross))]
    ppermute x7 -> x4, starting transfers between devices: 15 us -> 7.42 us  [the longest x1 3.29 us: two_slab_device(): near = lax.ppermute(line, ('bz', 'by'), both(route))]
    pallas_call x0 -> x6, Pallas kernels: none -> 7.11 us  [the longest x1 3.65 us: two_slab_device(): pl.pallas_call(render_kernel, out_shape=jax.ShapeDtypeStruct((4, rows, 2...]
    concatenate x18 -> x1, other arithmetic: 2.33 us -> 0.01 us  [two_slab_device(): jnp.concatenate([bulk, jnp.concatenate([halo] * (cols // LANES), axis=1)[...]
    unnamed x8 -> x4, local copies, waits for them, and re-layouts: 2.27 us -> 0.69 us
    another operation x2 -> x0, loops' own time: 1.39 us -> none  [the longest x1 1.17 us: on_device(): slab_image = lax.fori_loop(0, 2 * depth_cells, add_sample, start_image)]
  transfers between devices with their start and end apart: 7 -> 4, of which waited for: 6 -> 3; matrix products, arithmetic and copies ran while one was open for 1% -> 3% of each run, Pallas kernels for 0% -> 10%
where the time goes in v2:
time: 21.9 us; the launch traced here: 21.8 us
  starting transfers between devices  7.42 us (34%)
  Pallas kernels  7.11 us (32%)
  waiting for transfers between devices  5.76 us (26%)
  local copies, waits for them, and re-layouts  1.35 us (6%)
    pallas_call x1, Pallas kernels, two_slab_device(): pl.pallas_call(render_kernel, out_shape=jax.ShapeDtypeStruct((4, rows, 2...  3.65 us
    ppermute x1, starting transfers between devices, two_slab_device(): near = lax.ppermute(line, ('bz', 'by'), both(route))  3.29 us
    ppermute x1, starting transfers between devices, two_slab_device(): across = lax.ppermute(columns, 'bx', both(cross))  2.5 us
    ppermute x1, waiting for transfers between devices, two_slab_device(): across = lax.ppermute(columns, 'bx', both(cross))  2.29 us
    ppermute x1, waiting for transfers between devices, two_slab_device(): near = lax.ppermute(line, ('bz', 'by'), both(route))  2.25 us
    ppermute x1, starting transfers between devices, two_slab_device(): bulk = lax.ppermute(bulk, 'bz', [(0, 1), (1, 0)])  1.56 us
    ppermute x1, waiting for transfers between devices, two_slab_device(): bulk = lax.ppermute(bulk, 'bz', [(0, 1), (1, 0)])  1.22 us
    pallas_call x1, Pallas kernels, two_slab_device(): pl.pallas_call(columns_kernel, out_shape=(pltpu.VMEM((layers, LANES), i32...  1.22 us
  transfers between devices with their start and end apart: 4, of which 3 were waited for; matrix products, arithmetic and copies ran while one was open for 3% of the time, Pallas kernels for 10%

profile of v2, /device:TPU:20, one launch (start us, length us, event | category | flops | bytes accessed | tf_op | source)
XLA Modules:
  0.0 21.8 jit_solution(2059771694670723875)
XLA Ops:
  0.0 1.2 %pack_columns.1 = (s32[8,128]{1,0:T(8,128)S(1)}, f32[8,32,256]{2,1,0:T(8,128)S(1)}, s32[8,32,256]{2,1,0:T(8,128)S(1)}) custom-call(f32[8,32,256]{2,1,0:T(8,128)} %density_hbm.1, s32[8,32,256]{2,1,0:T(8,128)} %bins_hbm.1), custom_call_target="tpu_custom_call" | custom-call | bytes 3600000 | tf_op jit(solution)/shard_map/pack_columns/pallas_call | solution.py:468
  1.2 0.1 collective-permute-start
  1.3 2.5 %collective-permute-start.1 = (s32[8,128]{1,0:T(8,128)S(1)}, s32[8,128]{1,0:T(8,128)S(1)}, u32[]{:S(2)}, u32[]{:S(2)}) collective-permute-start(s32[8,128]{1,0:T(8,128)S(1)} %get-tuple-element.14), channel_id=1, source_target_pairs={{1,2},{2,1},{5,6},{6,5},{9,10},{10,9},{13,14},{14,13},{17,18},{18,... | collective-permute-start | bytes 12296 | tf_op jit(solution)/shard_map/ppermute | solution.py:489
  3.8 0.1 pack_block.1
  3.9 0.0 collective-permute-done
  3.9 2.3 %collective-permute-done.1 = s32[8,128]{1,0:T(8,128)S(1)} collective-permute-done((s32[8,128]{1,0:T(8,128)S(1)}, s32[8,128]{1,0:T(8,128)S(1)}, u32[]{:S(2)}, u32[]{:S(2)}) %collective-permute-start.1) | collective-permute-done | bytes 4128 | tf_op jit(solution)/shard_map/ppermute | solution.py:489
  6.3 1.6 %collective-permute-start.2 = (s32[18,8,256]{2,1,0:T(8,128)S(1)}, s32[18,8,256]{2,1,0:T(8,128)S(1)}, u32[]{:S(2)}, u32[]{:S(2)}) collective-permute-start(s32[18,8,256]{2,1,0:T(8,128)S(1)} %pad_add_fusion), channel_id=1, source_target_pairs={{0,16},{16,0},{1,17},{17,1},{2,18},{18,2},{3,19},{19,3},{4,20},{20... | collective-permute-start | bytes 442376 | tf_op jit(solution)/shard_map/ppermute | solution.py:505
  7.8 0.7 %reshape.3.extinction_ref = bf16[1,256]{1,0:T(2,128)(2,1)S(1)} reshape(bf16[256]{0:T(256)(128)(2,1)} %param.8) | data formatting | bytes 1024 | tf_op jit(solution)/shard_map/reshape | solution.py:462
  8.5 0.0 copy-start
  8.5 0.7 %copy-done = bf16[3,256]{1,0:T(4,128)(2,1)S(1)} copy-done((bf16[3,256]{1,0:T(4,128)(2,1)S(1)}, bf16[3,256]{1,0:T(4,128)(2,1)}, u32[]{:S(2)}) %copy-start) | copy-done | bytes 1560
  9.2 1.1 %own_slab.1 = (f32[4,512,128]{2,1,0:T(8,128)S(1)}, bf16[384,512]{1,0:T(8,128)(2,1)S(1)}) custom-call(f32[8,32,256]{2,1,0:T(8,128)S(1)} %get-tuple-element.12.density_ref, s32[8,32,256]{2,1,0:T(8,128)S(1)} %get-tuple-element.13.bins_ref, bf16[3,256]{1,0:T(4,128)(2,1)S(1)} %copy-done, bf16[1,256]{1,0:T(2,128)(2,1)S(1)} %reshape.3.extinction_ref, ...), custom_call_target="tpu_custom_call" | custom-call | bytes 7200000 | tf_op jit(solution)/shard_map/own_slab/pallas_call | solution.py:507
  10.2 0.0 copy-start.1
  10.2 1.2 %collective-permute-done.2.bulk_ref = s32[18,8,256]{2,1,0:T(8,128)S(1)} collective-permute-done((s32[18,8,256]{2,1,0:T(8,128)S(1)}, s32[18,8,256]{2,1,0:T(8,128)S(1)}, u32[]{:S(2)}, u32[]{:S(2)}) %collective-permute-start.2) | collective-permute-done | bytes 147488 | tf_op jit(solution)/shard_map/ppermute | solution.py:505
  11.5 3.3 %collective-permute-start.3 = (s32[3,8,256]{2,1,0:T(8,128)S(1)}, s32[3,8,256]{2,1,0:T(8,128)S(1)}, u32[]{:S(2)}, u32[]{:S(2)}) collective-permute-start(s32[3,8,256]{2,1,0:T(8,128)S(1)} %diagonal_line.1), channel_id=1, source_target_pairs={{16,4},{20,8},{24,12},{4,16},{8,20},{12,24},{17,5},{21,9},{25,13},... | collective-permute-start | bytes 73736 | tf_op jit(solution)/shard_map/ppermute | solution.py:533
  14.8 1.1 %other_slab.1.along_ref = f32[4,1152,128]{2,1,0:T(8,128)S(1)} custom-call(s32[18,8,256]{2,1,0:T(8,128)S(1)} %collective-permute-done.2.bulk_ref, bf16[3,256]{1,0:T(4,128)(2,1)S(1)} %copy-done, bf16[1,256]{1,0:T(2,128)(2,1)S(1)} %reshape.3.extinction_ref, bf16[384,512]{1,0:T(8,128)(2,1)S(1)} %get-tuple-element.15.weights_ref, ...), custom_call_target="tpu_custom_call" | custom-call | bytes 7200000 | tf_op jit(solution)/shard_map/other_slab/pallas_call | solution.py:535
  15.9 2.2 %collective-permute-done.3.near_ref = s32[3,8,256]{2,1,0:T(8,128)S(1)} collective-permute-done((s32[3,8,256]{2,1,0:T(8,128)S(1)}, s32[3,8,256]{2,1,0:T(8,128)S(1)}, u32[]{:S(2)}, u32[]{:S(2)}) %collective-permute-start.3) | collective-permute-done | bytes 24608 | tf_op jit(solution)/shard_map/ppermute | solution.py:533
  18.1 0.0 copy-done.1
  18.1 3.7 %render_rows.1 = f32[4,32,512]{2,1,0:T(8,128)} custom-call(s32[2]{0:T(128)S(1)} %copy-done.1, bf16[3,256]{1,0:T(4,128)(2,1)S(1)} %copy-done, bf16[1,256]{1,0:T(2,128)(2,1)S(1)} %reshape.3.extinction_ref, bf16[384,512]{1,0:T(8,128)(2,1)S(1)} %get-tuple-element.15.weights_ref, s32[18,8,256]{2,1,0:T(8,128)S(1)} %collective-permute-done.2.bulk_ref, ...), custom_call_target="tpu_custom_call" | custom-call | bytes 18000000 | tf_op jit(solution)/shard_map/render_rows/pallas_call | solution.py:549
  (5 shorter events, 0.0 us)
Async XLA Ops:
  1.2 2.7 %collective-permute-start = (s32[8,128]{1,0:T(8,128)S(1)}, s32[8,128]{1,0:T(8,128)S(1)}, u32[]{:S(2)}, u32[]{:S(2)}) collective-permute-start(s32[8,128]{1,0:T(8,128)S(1)} %get-tuple-element.14), channel_id=1, source_target_pairs={{0,1},{2,3},{1,0},{3,2},{4,5},{6,7},{5,4},{7,6},{8,9},{10,11},{9,8... | collective-permute-start | bytes 12296 | tf_op jit(solution)/shard_map/ppermute | solution.py:490
  1.3 4.9 %collective-permute-start.1 = (s32[8,128]{1,0:T(8,128)S(1)}, s32[8,128]{1,0:T(8,128)S(1)}, u32[]{:S(2)}, u32[]{:S(2)}) collective-permute-start(s32[8,128]{1,0:T(8,128)S(1)} %get-tuple-element.14), channel_id=1, source_target_pairs={{1,2},{2,1},{5,6},{6,5},{9,10},{10,9},{13,14},{14,13},{17,18},{18,... | collective-permute-start | bytes 12296 | tf_op jit(solution)/shard_map/ppermute | solution.py:489
  6.3 5.2 %collective-permute-start.2 = (s32[18,8,256]{2,1,0:T(8,128)S(1)}, s32[18,8,256]{2,1,0:T(8,128)S(1)}, u32[]{:S(2)}, u32[]{:S(2)}) collective-permute-start(s32[18,8,256]{2,1,0:T(8,128)S(1)} %pad_add_fusion), channel_id=1, source_target_pairs={{0,16},{16,0},{1,17},{17,1},{2,18},{18,2},{3,19},{19,3},{4,20},{20... | collective-permute-start | bytes 442376 | tf_op jit(solution)/shard_map/ppermute | solution.py:505
  8.5 0.7 %copy-start = (bf16[3,256]{1,0:T(4,128)(2,1)S(1)}, bf16[3,256]{1,0:T(4,128)(2,1)}, u32[]{:S(2)}) copy-start(bf16[3,256]{1,0:T(4,128)(2,1)} %colour_ref.5) | copy-start | bytes 4612
  10.2 7.9 %copy-start.1 = (s32[2]{0:T(128)S(1)}, s32[2]{0:T(128)}, u32[]{:S(2)}) copy-start(s32[2]{0:T(128)} %rank_ref.1) | copy-start | bytes 28
  11.5 6.6 %collective-permute-start.3 = (s32[3,8,256]{2,1,0:T(8,128)S(1)}, s32[3,8,256]{2,1,0:T(8,128)S(1)}, u32[]{:S(2)}, u32[]{:S(2)}) collective-permute-start(s32[3,8,256]{2,1,0:T(8,128)S(1)} %diagonal_line.1), channel_id=1, source_target_pairs={{16,4},{20,8},{24,12},{4,16},{8,20},{12,24},{17,5},{21,9},{25,13},... | collective-permute-start | bytes 73736 | tf_op jit(solution)/shard_map/ppermute | solution.py:533

commit v3 on v2

--- a/solution.py
+++ b/solution.py
@@ -1,3 +1,5 @@
+import functools
+
 import jax
 import jax.numpy as jnp
 from jax import lax
@@ -144,19 +146,8 @@
     return [pick(0) * opacity, pick(1) * opacity, pick(2) * opacity, opacity]
 
 
-def table_halves(colour_ref, extinction_ref):
-    colour = colour_ref[...].astype(jnp.float32)
-    extinction = extinction_ref[...].astype(jnp.float32)
-    result = []
-    for channel in range(4):
-        line = extinction if channel == 3 else colour[channel : channel + 1]
-        result.append(
-            [
-                jnp.broadcast_to(line[:, half * LANES : (half + 1) * LANES], (8, LANES))
-                for half in range(2)
-            ]
-        )
-    return result
+def read_tables(tables_ref):
+    return [[tables_ref[2 * channel + half] for half in range(2)] for channel in range(4)]
 
 
 def cost(microseconds):
@@ -165,16 +156,10 @@
     )
 
 
-def columns_kernel(density_hbm, bins_hbm, columns_ref, density_ref, bins_ref, sems):
+def columns_kernel(
+    density_ref, bins_ref, colour_ref, extinction_ref, columns_ref, dense_ref, index_ref, tables_ref
+):
     layers, rows, cols = density_ref.shape
-    copies = [
-        pltpu.make_async_copy(density_hbm, density_ref, sems.at[0]),
-        pltpu.make_async_copy(bins_hbm, bins_ref, sems.at[1]),
-    ]
-    for copy in copies:
-        copy.start()
-    for copy in copies:
-        copy.wait()
     row_at = lax.broadcasted_iota(jnp.int32, (rows, LANES), 0)
     lane_at = lax.broadcasted_iota(jnp.int32, (rows, LANES), 1)
     for z in range(layers):
@@ -182,34 +167,56 @@
         last = pack_words(density_ref[z, :, cols - 1 : cols], bins_ref[z, :, cols - 1 : cols])
         line = jnp.where(lane_at == row_at, first, 0) + jnp.where(lane_at == row_at + rows, last, 0)
         columns_ref[z : z + 1, :] = jnp.sum(line, axis=0, keepdims=True)
-
-
-def pack_kernel(density_ref, bins_ref, bulk_ref, edges_ref, words_ref):
-    layers, rows, cols = density_ref.shape
+        for tile in range(cols // LANES):
+            lanes = slice(tile * LANES, (tile + 1) * LANES)
+            dense_ref[z, tile] = density_ref[z, :, lanes]
+            index_ref[z, tile] = bins_ref[z, :, lanes]
+    colour = colour_ref[...].astype(jnp.float32)
+    extinction = extinction_ref[...].astype(jnp.float32).reshape(1, 2 * LANES)
+    for channel in range(4):
+        line = extinction if channel == 3 else colour[channel : channel + 1]
+        for half in range(2):
+            tables_ref[2 * channel + half] = jnp.broadcast_to(
+                line[:, half * LANES : (half + 1) * LANES], (8, LANES)
+            )
+
+
+def pack_kernel(
+    dense_ref, index_ref, beside_ref, across_ref, cells_ref, bulk_ref, edges_ref, halo_ref
+):
+    layers, tiles, rows = dense_ref.shape[:3]
     half = rows // 2
     front = lax.axis_index("bz") == 0
-    start = pl.multiple_of(jnp.where(front, half, 0), half)
-    for z in range(layers):
-        words = pack_words(
-            density_ref[z, pl.ds(start, half), :], bins_ref[z, pl.ds(start, half), :]
-        )
-        for tile in range(cols // LANES):
-            lanes = slice(tile * LANES, (tile + 1) * LANES)
-            words_ref[z, tile] = words[:, lanes]
+    start = jnp.where(front, half, 0)
+    me_x = lax.axis_index("bx")
+    lane_at = lax.broadcasted_iota(jnp.int32, (layers, LANES), 1)
+    even_x = lax.rem(me_x, 2) == 0
+    right = jnp.where(even_x, beside_ref[...], across_ref[...])
+    left = jnp.where(even_x, across_ref[...], beside_ref[...])
+    right = jnp.where(me_x + 1 < lax.axis_size("bx"), right, 0)
+    left = jnp.where(me_x > 0, left, 0)
+    halo = jnp.where(lane_at < rows, right, jnp.where(lane_at < 2 * rows, left, 0))
+    halo_ref[...] = halo
+    for tile in range(tiles):
+        lanes = slice(tile * LANES, (tile + 1) * LANES)
+        bulk_ref[2 * layers + 1, :, lanes] = halo
+        for z in range(layers):
             for part in range(2):
-                bulk_ref[2 * z + part, :, lanes] = words_ref[z, tile, pl.ds(part, 8, stride=2), :]
-        line = [
-            pack_words(density_ref[z, r : r + 1, :], bins_ref[z, r : r + 1, :])
-            for r in (0, half - 1, half, rows - 1)
-        ]
-        bulk_ref[2 * layers, z : z + 1, :] = jnp.where(front, line[1], line[2])
-        edges_ref[0, z : z + 1, :] = jnp.where(front, line[2], line[1])
-        edges_ref[1, z : z + 1, :] = jnp.where(front, line[0], line[3])
-
-
-def diagonal_kernel(bulk_ref, edges_ref, halo_ref, weights_ref, line_ref):
+                at = pl.ds(start + part, half // 2, stride=2)
+                bulk_ref[2 * z + part, :, lanes] = pack_words(
+                    dense_ref[z, tile, at, :], index_ref[z, tile, at, :]
+                )
+            line = [
+                pack_words(dense_ref[z, tile, r : r + 1, :], index_ref[z, tile, r : r + 1, :])
+                for r in (0, half - 1, half, rows - 1)
+            ]
+            bulk_ref[2 * layers, z : z + 1, lanes] = jnp.where(front, line[1], line[2])
+            edges_ref[0, z : z + 1, lanes] = jnp.where(front, line[2], line[1])
+            edges_ref[1, z : z + 1, lanes] = jnp.where(front, line[0], line[3])
+
+
+def diagonal_kernel(bulk_ref, edges_ref, halo_ref, along_ref, line_ref):
     layers = edges_ref.shape[1]
-    cols = edges_ref.shape[2]
     front = lax.axis_index("bz") == 0
     other = jnp.concatenate(
         [
@@ -249,21 +256,26 @@
     return lane_at & (rows - 1), lane_at < 2 * rows, sub_at
 
 
-def along_columns(read_cells, halo_words, tables, weights_ref, cells_ref, values_ref, store, rows, layers, cols):
+def classify_rows(read_cells, tables, cells_ref, layers, tiles):
     total = float(2 * layers)
-    start = lax.axis_index("bz") * (rows // 2)
-    side_lane, has_side, sub_at = lane_maps(rows)
-    halo = cell_values(*unpack_words(halo_words), tables, total)
-    for channel in range(4):
-        values_ref[channel] = halo[channel]
     for z in range(layers):
-        for tile in range(cols // LANES):
+        for tile in range(tiles):
             even = cell_values(*read_cells(z, 0, tile), tables, total)
             odd = cell_values(*read_cells(z, 1, tile), tables, total)
             for channel in range(4):
                 base = (z * 4 + channel) * 16
                 block = jnp.concatenate([even[channel], odd[channel]], axis=0)
                 cells_ref[base : base + 16, tile * LANES : (tile + 1) * LANES] = block.astype(jnp.bfloat16)
+
+
+def classify_halo(words, tables, ends_ref, values_ref, rows):
+    layers = words.shape[0]
+    start = lax.axis_index("bz") * (rows // 2)
+    side_lane, has_side, sub_at = lane_maps(rows)
+    halo = cell_values(*unpack_words(words), tables, float(2 * layers))
+    for channel in range(4):
+        values_ref[channel] = halo[channel]
+    for z in range(layers):
         for channel in range(4):
             base = (z * 4 + channel) * 16
             line = jnp.broadcast_to(values_ref[channel, z : z + 1, :], (8, LANES))
@@ -274,50 +286,44 @@
                 ],
                 axis=0,
             )
-            cells_ref[base : base + 16, cols : cols + LANES] = block.astype(jnp.bfloat16)
-    result = jnp.dot(cells_ref[...], weights_ref[...], preferred_element_type=jnp.float32)
-    result = result.astype(jnp.bfloat16).astype(jnp.float32)
-    for tile in range(2 * cols // LANES):
-        store(tile, result[:, tile * LANES : (tile + 1) * LANES])
-
-
-def own_kernel(
-    density_ref, bins_ref, colour_ref, extinction_ref, halo_ref,
-    along_ref, weights_ref, cells_ref, values_ref, rows_ref, binrows_ref,
-):
-    layers, rows, cols = density_ref.shape
+            ends_ref[base : base + 16, :] = block.astype(jnp.bfloat16)
+
+
+def along_columns(cells, ends, weights_ref):
+    cols = cells.shape[1]
+    result = jnp.dot(cells, weights_ref[0:cols, :], preferred_element_type=jnp.float32)
+    result += jnp.dot(ends, weights_ref[cols : cols + LANES, :], preferred_element_type=jnp.float32)
+    return result.astype(jnp.bfloat16).astype(jnp.float32)
+
+
+def cells_kernel(dense_ref, index_ref, tables_ref, cells_ref, weights_ref):
+    layers, tiles, rows = dense_ref.shape[:3]
     half = rows // 2
-    start = pl.multiple_of(lax.axis_index("bz") * half, half)
+    start = lax.axis_index("bz") * half
     fill_weights(weights_ref, rows)
-    tables = table_halves(colour_ref, extinction_ref)
-    for z in range(layers):
-        for tile in range(cols // LANES):
-            lanes = slice(tile * LANES, (tile + 1) * LANES)
-            rows_ref[z, tile] = density_ref[z, pl.ds(start, half), lanes]
-            binrows_ref[z, tile] = bins_ref[z, pl.ds(start, half), lanes]
 
     def read_cells(z, part, tile):
-        at = pl.ds(part, 8, stride=2)
-        return rows_ref[z, tile, at, :], binrows_ref[z, tile, at, :]
-
-    def store(tile, block):
-        along_ref[tile] = block
-
-    along_columns(
-        read_cells, halo_ref[...], tables, weights_ref, cells_ref, values_ref, store, rows, layers, cols
-    )
+        at = pl.ds(start + part, half // 2, stride=2)
+        return dense_ref[z, tile, at, :], index_ref[z, tile, at, :]
+
+    classify_rows(read_cells, read_tables(tables_ref), cells_ref, layers, tiles)
+
+
+def own_kernel(rows, cells_ref, halo_ref, tables_ref, weights_ref, along_ref, ends_ref, values_ref):
+    classify_halo(halo_ref[...], read_tables(tables_ref), ends_ref, values_ref, rows)
+    result = along_columns(cells_ref[...], ends_ref[...], weights_ref)
+    for tile in range(along_ref.shape[0]):
+        along_ref[tile] = result[:, tile * LANES : (tile + 1) * LANES]
 
 
 def other_kernel(
-    bulk_ref, colour_ref, extinction_ref, weights_ref, own_ref,
-    along_ref, cells_ref, values_ref,
+    rows, bulk_ref, tables_ref, weights_ref, own_ref, along_ref, cells_ref, ends_ref, values_ref
 ):
     layers = (bulk_ref.shape[0] - 2) // 2
     cols = bulk_ref.shape[2]
     size = own_ref.shape[1]
-    rows = 32
     me = lax.axis_index("bz")
-    tables = table_halves(colour_ref, extinction_ref)
+    tables = read_tables(tables_ref)
     pad = size // layers
     mine = pl.multiple_of(pad + me * size, pad)
     theirs = pl.multiple_of(pad + (1 - me) * size, pad)
@@ -329,17 +335,15 @@
     def read_cells(z, part, tile):
         return unpack_words(bulk_ref[2 * z + part, :, tile * LANES : (tile + 1) * LANES])
 
-    def store(tile, block):
-        along_ref[tile, pl.ds(theirs, size), :] = block
-
-    along_columns(
-        read_cells, bulk_ref[2 * layers + 1, :, 0:LANES], tables, weights_ref, cells_ref, values_ref,
-        store, rows, layers, cols,
-    )
+    classify_rows(read_cells, tables, cells_ref, layers, cols // LANES)
+    classify_halo(bulk_ref[2 * layers + 1, :, 0:LANES], tables, ends_ref, values_ref, rows)
+    result = along_columns(cells_ref[...], ends_ref[...], weights_ref)
+    for tile in range(along_ref.shape[0]):
+        along_ref[tile, pl.ds(theirs, size), :] = result[:, tile * LANES : (tile + 1) * LANES]
 
 
 def render_kernel(
-    rank_ref, colour_ref, extinction_ref, weights_ref, bulk_ref, edges_ref, halo_ref, near_ref, along_ref,
+    rank_ref, tables_ref, weights_ref, bulk_ref, edges_ref, halo_ref, near_ref, along_ref,
     out_ref, cells_ref, lines_ref, mixed_ref,
 ):
     layers, cols = edges_ref.shape[1:]
@@ -351,15 +355,17 @@
     f32 = jnp.float32
     me = lax.axis_index("bz")
     front = me == 0
-    tables = table_halves(colour_ref, extinction_ref)
+    tables = read_tables(tables_ref)
     side_lane, has_side, sub_at = lane_maps(rows)
+    me_y = lax.axis_index("by")
+    has_near = jnp.where(front, me_y > 0, me_y + 1 < lax.axis_size("by"))
 
     for slab in range(2):
         mine = me == slab
         inside = jnp.where(mine, edges_ref[0], bulk_ref[2 * layers])
         halo_inside = jnp.where(mine, halo_ref[...], bulk_ref[2 * layers + 1, :, 0:LANES])
-        near = near_ref[slab]
-        halo_near = near_ref[2, :, slab * LANES : (slab + 1) * LANES]
+        near = jnp.where(has_near, near_ref[slab], 0)
+        halo_near = jnp.where(has_near, near_ref[2, :, slab * LANES : (slab + 1) * LANES], 0)
         for side in range(2):
             row = jnp.where(front, rows - 1, half - 1) if side == 0 else jnp.where(front, half, 0)
             use_near = front if side == 0 else jnp.logical_not(front)
@@ -459,107 +465,89 @@
     size = layers * 4 * half
     count_y, count_x = lax.axis_size("by"), lax.axis_size("bx")
     f32, bf16, i32 = jnp.float32, jnp.bfloat16, jnp.int32
-    extinction = tf_extinction.reshape(1, -1)
-    params = pltpu.CompilerParams(vmem_limit_bytes=16 * 1024 * 1024)
-
-    hbm = pl.BlockSpec(memory_space=pltpu.HBM)
-    density = pltpu.with_memory_space_constraint(density, pltpu.HBM)
-    bin_index = pltpu.with_memory_space_constraint(bin_index, pltpu.HBM)
-    columns, density, bin_index = pl.pallas_call(
-        columns_kernel,
-        out_shape=(
-            pltpu.VMEM((layers, LANES), i32),
-            pltpu.VMEM(density.shape, f32),
-            pltpu.VMEM(density.shape, i32),
-        ),
-        in_specs=[hbm] * 2,
-        out_specs=(VMEM,) * 3,
-        scratch_shapes=[pltpu.SemaphoreType.DMA((2,))],
-        compiler_params=params,
-        cost_estimate=cost(1.0),
-        name="pack_columns",
-    )(density, bin_index)
-
-    pairs = [(x, x + 1) for x in range(0, count_x - 1, 2)]
-    cross = [(x, x + 1) for x in range(1, count_x - 1, 2)]
+
+    def call(kernel, name, out_shape, time, scratch_shapes=(), in_specs=None):
+        def run(*operands):
+            return pl.pallas_call(
+                kernel,
+                out_shape=out_shape,
+                in_specs=in_specs or [VMEM] * len(operands),
+                out_specs=(VMEM,) * len(out_shape) if isinstance(out_shape, tuple) else VMEM,
+                scratch_shapes=scratch_shapes,
+                compiler_params=pltpu.CompilerParams(vmem_limit_bytes=16 * 1024 * 1024),
+                cost_estimate=cost(time),
+                name=name,
+            )(*operands)
+
+        return run
 
     def both(route):
         return route + [(target, source) for source, target in route]
 
+    blocks = (layers, cols // LANES, rows, LANES)
+    columns, dense, index, tables = call(
+        columns_kernel,
+        "pack_columns",
+        (
+            pltpu.VMEM((layers, LANES), i32),
+            pltpu.VMEM(blocks, f32),
+            pltpu.VMEM(blocks, i32),
+            pltpu.VMEM((8, 8, LANES), f32),
+        ),
+        1.2,
+    )(*[pltpu.with_memory_space_constraint(x, pltpu.HBM) for x in (density, bin_index, tf_colour, tf_extinction)])
+
+    pairs = [(x, x + 1) for x in range(0, count_x, 2)]
+    cross = [(x, (x + 1) % count_x) for x in range(1, count_x, 2)]
+    beside = lax.ppermute(columns, "bx", both(pairs))
     across = lax.ppermute(columns, "bx", both(cross))
-    beside = lax.ppermute(columns, "bx", both(pairs))
-    bulk, edges = pl.pallas_call(
+
+    cells, weights = call(
+        cells_kernel,
+        "own_cells",
+        (pltpu.VMEM((size, cols), bf16), pltpu.VMEM((cols + LANES, 2 * cols), bf16)),
+        0.5,
+    )(dense, index, tables)
+    bulk, edges, halo = call(
         pack_kernel,
-        out_shape=(pltpu.VMEM((2 * layers + 1, 8, cols), i32), pltpu.VMEM((2, layers, cols), i32)),
-        in_specs=[VMEM] * 2,
-        out_specs=(VMEM, VMEM),
-        scratch_shapes=[pltpu.VMEM((layers, cols // LANES, half, LANES), i32)],
-        compiler_params=params,
-        cost_estimate=cost(0.7),
-        name="pack_block",
-    )(density, bin_index)
-    lane_at = lax.broadcasted_iota(i32, (layers, LANES), 1)
-    right_is_beside = lax.axis_index("bx") % 2 == 0
-    halo = jnp.where((lane_at < rows) == right_is_beside, beside, across)
-    bulk = jnp.concatenate([bulk, jnp.concatenate([halo] * (cols // LANES), axis=1)[None]], axis=0)
+        "pack_block",
+        (
+            pltpu.VMEM((2 * layers + 2, 8, cols), i32),
+            pltpu.VMEM((2, layers, cols), i32),
+            pltpu.VMEM((layers, LANES), i32),
+        ),
+        0.2,
+    )(dense, index, beside, across, cells)
     bulk = lax.ppermute(bulk, "bz", [(0, 1), (1, 0)])
 
-    along, weights = pl.pallas_call(
-        own_kernel,
-        out_shape=(pltpu.VMEM((tiles, size, LANES), f32), pltpu.VMEM((cols + LANES, 2 * cols), bf16)),
-        in_specs=[VMEM] * 5,
-        out_specs=(VMEM, VMEM),
-        scratch_shapes=[
-            pltpu.VMEM((size, cols + LANES), bf16),
-            pltpu.VMEM((4, layers, LANES), f32),
-            pltpu.VMEM((layers, cols // LANES, half, LANES), f32),
-            pltpu.VMEM((layers, cols // LANES, half, LANES), i32),
-        ],
-        compiler_params=params,
-        cost_estimate=cost(2.0),
-        name="own_slab",
-    )(density, bin_index, tf_colour, extinction, halo)
-
-    line = pl.pallas_call(
-        diagonal_kernel,
-        out_shape=pltpu.VMEM((3, layers, cols), i32),
-        in_specs=[VMEM] * 4,
-        out_specs=VMEM,
-        compiler_params=params,
-        cost_estimate=cost(0.2),
-        name="diagonal_line",
-    )(bulk, edges, halo, weights)
-    route = [(count_y + y, y + 1) for y in range(count_y - 1)]
+    ends = [pltpu.VMEM((size, LANES), bf16), pltpu.VMEM((4, layers, LANES), f32)]
+    along = call(
+        functools.partial(own_kernel, rows), "own_slab", pltpu.VMEM((tiles, size, LANES), f32), 0.7, ends
+    )(cells, halo, tables, weights)
+    line = call(diagonal_kernel, "diagonal_line", pltpu.VMEM((3, layers, cols), i32), 0.1)(
+        bulk, edges, halo, along
+    )
+    route = [(count_y + y, (y + 1) % count_y) for y in range(count_y)]
     near = lax.ppermute(line, ("bz", "by"), both(route))
-
-    along = pl.pallas_call(
-        other_kernel,
-        out_shape=pltpu.VMEM((tiles, 2 * size + 2 * 4 * half, LANES), f32),
-        in_specs=[VMEM] * 5,
-        out_specs=VMEM,
-        scratch_shapes=[
-            pltpu.VMEM((size, cols + LANES), bf16),
-            pltpu.VMEM((4, layers, LANES), f32),
-        ],
-        compiler_params=params,
-        cost_estimate=cost(2.0),
-        name="other_slab",
-    )(bulk, tf_colour, extinction, weights, along)
-
-    return pl.pallas_call(
+    along = call(
+        functools.partial(other_kernel, rows),
+        "other_slab",
+        pltpu.VMEM((tiles, 2 * size + 2 * 4 * half, LANES), f32),
+        1.0,
+        [pltpu.VMEM((size, cols), bf16)] + ends,
+    )(bulk, tables, weights, along)
+    return call(
         render_kernel,
-        out_shape=jax.ShapeDtypeStruct((4, rows, 2 * cols), f32),
-        in_specs=[pl.BlockSpec(memory_space=pltpu.SMEM)] + [VMEM] * 8,
-        out_specs=VMEM,
-        scratch_shapes=[
+        "render_rows",
+        jax.ShapeDtypeStruct((4, rows, 2 * cols), f32),
+        3.6,
+        [
             pltpu.VMEM((8 * 2 * layers, cols + LANES), f32),
             pltpu.VMEM((tiles, 2, 4, 2, 2 * layers, LANES), f32),
             pltpu.VMEM((4, rows, LANES), f32),
         ],
-        compiler_params=params,
-        cost_estimate=cost(5.0),
-        name="render_rows",
-    )(slab_rank, tf_colour, extinction, weights, bulk, edges, halo, near, along)
+        [pl.BlockSpec(memory_space=pltpu.SMEM)] + [VMEM] * 7,
+    )(slab_rank, tables, weights, bulk, edges, halo, near, along)
 
 
 def on_device(density, bin_index, tf_colour, tf_extinction, slab_rank):

time: 21.9 us -> 22 us (level)
  the two profiles are of different devices: /device:TPU:20 before, /device:TPU:0 now
where the time goes in v3:
time: 22 us; the launch traced here: 21.9 us
  starting transfers between devices  10.1 us (46%)
  Pallas kernels  6.76 us (31%)
  waiting for transfers between devices  4.96 us (23%)
    pallas_call x7, Pallas kernels, run(): pl.pallas_call(kernel, out_shape=out_shape, in_specs=in_specs or [VMEM] *...  6.76 us
    ppermute x1, starting transfers between devices, two_slab_device(): near = lax.ppermute(line, ('bz', 'by'), both(route))  4.81 us
    ppermute x1, waiting for transfers between devices, two_slab_device(): bulk = lax.ppermute(bulk, 'bz', [(0, 1), (1, 0)])  3.64 us
    ppermute x1, starting transfers between devices, two_slab_device(): across = lax.ppermute(columns, 'bx', both(cross))  2.47 us
    ppermute x1, starting transfers between devices, two_slab_device(): bulk = lax.ppermute(bulk, 'bz', [(0, 1), (1, 0)])  2.13 us
    ppermute x1, waiting for transfers between devices, two_slab_device(): near = lax.ppermute(line, ('bz', 'by'), both(route))  1.04 us
    ppermute x1, starting transfers between devices, two_slab_device(): beside = lax.ppermute(columns, 'bx', both(pairs))  0.68 us
  transfers between devices with their start and end apart: 4, of which 4 were waited for; matrix products, arithmetic and copies ran while one was open for 0% of the time, Pallas kernels for 8%

profile of v3, /device:TPU:0, one launch (start us, length us, event | category | flops | bytes accessed | tf_op | source)
XLA Modules:
  0.0 21.9 jit_solution(18345237763390332236)
XLA Ops:
  0.0 1.2 %pack_columns.1 = (s32[8,128]{1,0:T(8,128)S(1)}, f32[8,2,32,128]{3,2,1,0:T(8,128)S(1)}, s32[8,2,32,128]{3,2,1,0:T(8,128)S(1)}, f32[8,8,128]{2,1,0:T(8,128)S(1)}) custom-call(f32[8,32,256]{2,1,0:T(8,128)} %density_ref.1, s32[8,32,256]{2,1,0:T(8,128)} %bins_ref.1, bf16[3,256]{1,0:T(4,128)(2,1)} %colour_ref.1, bf16[256]{0:T(256)(128)(2,1)} %extinction_ref.1), custom_call_target="tpu_custom_call" | custom-call | bytes 4320000 | tf_op jit(solution)/shard_map/pack_columns/pallas_call | solution.py:471
  1.2 2.5 %collective-permute-start.1 = (s32[8,128]{1,0:T(8,128)S(1)}, s32[8,128]{1,0:T(8,128)S(1)}, u32[]{:S(2)}, u32[]{:S(2)}) collective-permute-start(s32[8,128]{1,0:T(8,128)S(1)} %get-tuple-element.18), channel_id=1, source_target_pairs={{1,2},{3,0},{2,1},{0,3},{5,6},{7,4},{6,5},{4,7},{9,10},{11,8},{10,... | collective-permute-start | bytes 12296 | tf_op jit(solution)/shard_map/ppermute | solution.py:503
  3.7 0.7 %collective-permute-start = (s32[8,128]{1,0:T(8,128)S(1)}, s32[8,128]{1,0:T(8,128)S(1)}, u32[]{:S(2)}, u32[]{:S(2)}) collective-permute-start(s32[8,128]{1,0:T(8,128)S(1)} %get-tuple-element.18), channel_id=1, source_target_pairs={{0,1},{2,3},{1,0},{3,2},{4,5},{6,7},{5,4},{7,6},{8,9},{10,11},{9,8... | collective-permute-start | bytes 12296 | tf_op jit(solution)/shard_map/ppermute | solution.py:502
  4.4 0.5 %own_cells.1 = (bf16[512,256]{1,0:T(8,128)(2,1)S(1)}, bf16[384,512]{1,0:T(8,128)(2,1)S(1)}) custom-call(f32[8,2,32,128]{3,2,1,0:T(8,128)S(1)} %get-tuple-element.15.dense_ref, s32[8,2,32,128]{3,2,1,0:T(8,128)S(1)} %get-tuple-element.16.index_ref, f32[8,8,128]{2,1,0:T(8,128)S(1)} %get-tuple-element.14.tables_ref), custom_call_target="tpu_custom_call" | custom-call | bytes 1800000 | tf_op jit(solution)/shard_map/own_cells/pallas_call | solution.py:471
  4.9 0.1 collective-permute-done.1.across_ref
  5.0 0.2 collective-permute-done.beside_ref
  5.2 0.1 pack_block.1
  5.3 2.1 %collective-permute-start.2 = (s32[18,8,256]{2,1,0:T(8,128)S(1)}, s32[18,8,256]{2,1,0:T(8,128)S(1)}, u32[]{:S(2)}, u32[]{:S(2)}) collective-permute-start(s32[18,8,256]{2,1,0:T(8,128)S(1)} %get-tuple-element.20), channel_id=1, source_target_pairs={{0,16},{16,0},{1,17},{17,1},{2,18},{18,2},{3,19},{19,3},{4,20},{20... | collective-permute-start | bytes 442376 | tf_op jit(solution)/shard_map/ppermute | solution.py:521
  7.4 0.5 %own_slab.1.along_ref.own_ref = f32[4,512,128]{2,1,0:T(8,128)S(1)} custom-call(bf16[512,256]{1,0:T(8,128)(2,1)S(1)} %get-tuple-element.19.cells_ref, s32[8,128]{1,0:T(8,128)S(1)} %get-tuple-element.22.halo_ref, f32[8,8,128]{2,1,0:T(8,128)S(1)} %get-tuple-element.14.tables_ref, bf16[384,512]{1,0:T(8,128)(2,1)S(1)} %get-tuple-element.17.weights_ref), custom_call_target="tpu_custom_call" | custom-call | bytes 2520000 | tf_op jit(solution)/shard_map/own_slab/pallas_call | solution.py:471
  7.9 3.6 %collective-permute-done.2.bulk_ref = s32[18,8,256]{2,1,0:T(8,128)S(1)} collective-permute-done((s32[18,8,256]{2,1,0:T(8,128)S(1)}, s32[18,8,256]{2,1,0:T(8,128)S(1)}, u32[]{:S(2)}, u32[]{:S(2)}) %collective-permute-start.2) | collective-permute-done | bytes 147488 | tf_op jit(solution)/shard_map/ppermute | solution.py:521
  11.6 0.0 copy-start
  11.6 4.8 %collective-permute-start.3 = (s32[3,8,256]{2,1,0:T(8,128)S(1)}, s32[3,8,256]{2,1,0:T(8,128)S(1)}, u32[]{:S(2)}, u32[]{:S(2)}) collective-permute-start(s32[3,8,256]{2,1,0:T(8,128)S(1)} %diagonal_line.1), channel_id=1, source_target_pairs={{16,4},{20,8},{24,12},{28,0},{4,16},{8,20},{12,24},{0,28},{17,5},{... | collective-permute-start | bytes 73736 | tf_op jit(solution)/shard_map/ppermute | solution.py:531
  16.4 0.8 %other_slab.1.along_ref = f32[4,1152,128]{2,1,0:T(8,128)S(1)} custom-call(s32[18,8,256]{2,1,0:T(8,128)S(1)} %collective-permute-done.2.bulk_ref, f32[8,8,128]{2,1,0:T(8,128)S(1)} %get-tuple-element.14.tables_ref, bf16[384,512]{1,0:T(8,128)(2,1)S(1)} %get-tuple-element.17.weights_ref, f32[4,512,128]{2,1,0:T(8,128)S(1)} %own_slab.1.along_ref.own_ref), custom_call_target="tpu_custom_call" | custom-call | bytes 3600000 | tf_op jit(solution)/shard_map/other_slab/pallas_call | solution.py:471
  17.2 1.0 %collective-permute-done.3.near_ref = s32[3,8,256]{2,1,0:T(8,128)S(1)} collective-permute-done((s32[3,8,256]{2,1,0:T(8,128)S(1)}, s32[3,8,256]{2,1,0:T(8,128)S(1)}, u32[]{:S(2)}, u32[]{:S(2)}) %collective-permute-start.3) | collective-permute-done | bytes 24608 | tf_op jit(solution)/shard_map/ppermute | solution.py:531
  18.2 0.0 copy-done
  18.2 3.6 %render_rows.1 = f32[4,32,512]{2,1,0:T(8,128)} custom-call(s32[2]{0:T(128)S(1)} %copy-done, f32[8,8,128]{2,1,0:T(8,128)S(1)} %get-tuple-element.14.tables_ref, bf16[384,512]{1,0:T(8,128)(2,1)S(1)} %get-tuple-element.17.weights_ref, s32[18,8,256]{2,1,0:T(8,128)S(1)} %collective-permute-done.2.bulk_ref, s32[2,8,256]{2,1,0:T(8,128)S(1)} %get-tuple-element.21.edges_ref, ...), custom_call_target="tpu_custom_call" | custom-call | bytes 12960000 | tf_op jit(solution)/shard_map/render_rows/pallas_call | solution.py:471
  (1 shorter events, 0.0 us)
Async XLA Ops:
  1.2 3.8 %collective-permute-start.1 = (s32[8,128]{1,0:T(8,128)S(1)}, s32[8,128]{1,0:T(8,128)S(1)}, u32[]{:S(2)}, u32[]{:S(2)}) collective-permute-start(s32[8,128]{1,0:T(8,128)S(1)} %get-tuple-element.18), channel_id=1, source_target_pairs={{1,2},{3,0},{2,1},{0,3},{5,6},{7,4},{6,5},{4,7},{9,10},{11,8},{10,... | collective-permute-start | bytes 12296 | tf_op jit(solution)/shard_map/ppermute | solution.py:503
  3.7 1.5 %collective-permute-start = (s32[8,128]{1,0:T(8,128)S(1)}, s32[8,128]{1,0:T(8,128)S(1)}, u32[]{:S(2)}, u32[]{:S(2)}) collective-permute-start(s32[8,128]{1,0:T(8,128)S(1)} %get-tuple-element.18), channel_id=1, source_target_pairs={{0,1},{2,3},{1,0},{3,2},{4,5},{6,7},{5,4},{7,6},{8,9},{10,11},{9,8... | collective-permute-start | bytes 12296 | tf_op jit(solution)/shard_map/ppermute | solution.py:502
  5.3 6.3 %collective-permute-start.2 = (s32[18,8,256]{2,1,0:T(8,128)S(1)}, s32[18,8,256]{2,1,0:T(8,128)S(1)}, u32[]{:S(2)}, u32[]{:S(2)}) collective-permute-start(s32[18,8,256]{2,1,0:T(8,128)S(1)} %get-tuple-element.20), channel_id=1, source_target_pairs={{0,16},{16,0},{1,17},{17,1},{2,18},{18,2},{3,19},{19,3},{4,20},{20... | collective-permute-start | bytes 442376 | tf_op jit(solution)/shard_map/ppermute | solution.py:521
  11.6 6.6 %copy-start = (s32[2]{0:T(128)S(1)}, s32[2]{0:T(128)}, u32[]{:S(2)}) copy-start(s32[2]{0:T(128)} %rank_ref.1) | copy-start | bytes 28
  11.6 6.6 %collective-permute-start.3 = (s32[3,8,256]{2,1,0:T(8,128)S(1)}, s32[3,8,256]{2,1,0:T(8,128)S(1)}, u32[]{:S(2)}, u32[]{:S(2)}) collective-permute-start(s32[3,8,256]{2,1,0:T(8,128)S(1)} %diagonal_line.1), channel_id=1, source_target_pairs={{16,4},{20,8},{24,12},{28,0},{4,16},{8,20},{12,24},{0,28},{17,5},{... | collective-permute-start | bytes 73736 | tf_op jit(solution)/shard_map/ppermute | solution.py:531

commit v4 on v3

v4 whole, which is shorter than its diff:
```python
import jax
import jax.numpy as jnp
from jax import lax
from jax.experimental import pallas as pl
from jax.experimental.pallas import tpu as pltpu
from jax.sharding import PartitionSpec as P


def with_halo(block, sides, width):
    for axis, dim in sides:
        count = lax.axis_size(axis)
        forward = [(i, i + 1) for i in range(count - 1)]
        backward = [(target, source) for source, target in forward]
        low = lax.ppermute(
            lax.slice_in_dim(block, block.shape[dim] - width, None, axis=dim), axis, forward
        )
        high = lax.ppermute(lax.slice_in_dim(block, 0, width, axis=dim), axis, backward)
        block = jnp.concatenate([low, block, high], axis=dim)
    return block


def partner_2(block, axis, stride):
    count = lax.axis_size(axis)
    route = []
    for low in range(count):
        high = low | 1 << stride
        if high != low and high < count:
            route += [(low, high), (high, low)]
    return lax.ppermute(block, axis, route)


def resample_table(length):
    row_index = lax.broadcasted_iota(jnp.int32, (2 * length, length + 2), 0)
    col_index = lax.broadcasted_iota(jnp.int32, (2 * length, length + 2), 1)
    centre = row_index // 2
    parity = row_index % 2
    weights_table = jnp.where(col_index == centre + 1, 0.75, 0.0)
    weights_table = weights_table + jnp.where((col_index == centre) & (parity == 0), 0.25, 0.0)
    weights_table = weights_table + jnp.where((col_index == centre + 2) & (parity == 1), 0.25, 0.0)
    return weights_table.astype(jnp.bfloat16)


def blend_over(in_front, behind):
    return in_front + (1.0 - in_front[3])[None] * behind


def classify(density, bin_index, tf_colour, tf_extinction, total_depth):
    depth_cells, height_cells, width_cells = density.shape
    lookup = jnp.concatenate([tf_colour, tf_extinction[None, :]], axis=0)
    table_size = lookup.shape[1]
    bin_rows = lax.broadcasted_iota(jnp.int32, (table_size, 1), 0)
    flat_bins = bin_index.reshape(depth_cells, height_cells * width_cells)
    flat_density = density.reshape(depth_cells, height_cells * width_cells)

    def one_layer(layer, result):
        layer_bins = lax.dynamic_index_in_dim(flat_bins, layer, 0, keepdims=True)
        layer_density = lax.dynamic_index_in_dim(flat_density, layer, 0, keepdims=False)
        one_hot = (layer_bins == bin_rows).astype(jnp.bfloat16)
        values = jnp.dot(lookup, one_hot, preferred_element_type=jnp.float32)
        opacity = 1.0 - jnp.exp(-values[3] * layer_density / total_depth)
        cells = jnp.concatenate([values[:3] * opacity[None], opacity[None]], axis=0).astype(
            jnp.bfloat16
        )
        return lax.dynamic_update_slice_in_dim(result, cells[:, None], layer, 1)

    start_cells = jnp.zeros((4, depth_cells, height_cells * width_cells), jnp.bfloat16)
    classified = lax.fori_loop(0, depth_cells, one_layer, start_cells)
    return classified.reshape(4, depth_cells, height_cells, width_cells)


def general_device(density, bin_index, tf_colour, tf_extinction, slab_rank):
    slab_count = lax.axis_size("bz")
    depth_cells, height_cells, width_cells = density.shape
    total_depth = float(depth_cells * slab_count)
    colour_cells = classify(density, bin_index, tf_colour, tf_extinction, total_depth)
    padded = with_halo(colour_cells, (("bz", 1), ("by", 2), ("bx", 3)), 1)
    along_x = jnp.einsum(
        "czyq,pq->czyp", padded, resample_table(width_cells), preferred_element_type=jnp.float32
    ).astype(jnp.bfloat16)
    y_table = resample_table(height_cells)

    def add_sample(sample_index, image_now):
        centre = sample_index // 2
        parity = sample_index % 2
        layers = lax.dynamic_slice_in_dim(along_x, centre, 3, 1).astype(jnp.float32)
        lower_weight = jnp.where(parity == 0, 0.25, 0.0)
        upper_weight = jnp.where(parity == 1, 0.25, 0.0)
        mixed_layer = (
            lower_weight * layers[:, 0] + 0.75 * layers[:, 1] + upper_weight * layers[:, 2]
        ).astype(jnp.bfloat16)
        sample = jnp.einsum("qy,cyp->cqp", y_table, mixed_layer, preferred_element_type=jnp.float32)
        return blend_over(image_now, sample)

    start_image = jnp.zeros((4, 2 * height_cells, 2 * width_cells), jnp.float32)
    slab_image = lax.fori_loop(0, 2 * depth_cells, add_sample, start_image)
    rows_piece = 2 * height_cells // slab_count
    my_index = lax.axis_index("bz")
    bit_levels = slab_count.bit_length() - 1
    composite = slab_image.reshape((4,) + (2,) * bit_levels + (rows_piece, 2 * width_cells))
    my_rank = lax.dynamic_index_in_dim(slab_rank, my_index, 0, keepdims=False)
    for level in range(bit_levels):
        position = bit_levels - level
        my_bit = my_index // 2**level % 2
        kept_half = lax.dynamic_index_in_dim(composite, my_bit, position, keepdims=False)
        outgoing = lax.dynamic_index_in_dim(composite, 1 - my_bit, position, keepdims=False)
        incoming = partner_2(outgoing, "bz", level)
        partner = my_index + (1 - 2 * my_bit) * 2**level
        partner_rank = lax.dynamic_index_in_dim(slab_rank, partner, 0, keepdims=False)
        mine_first = my_rank < partner_rank
        composite = blend_over(
            jnp.where(mine_first, kept_half, incoming), jnp.where(mine_first, incoming, kept_half)
        )
    return composite


LANES = 128
LEVELS = 65535.0
VMEM = pl.BlockSpec(memory_space=pltpu.VMEM)


def pack_words(density, bins):
    level = (density * LEVELS + 0.5).astype(jnp.int32)
    return lax.shift_left(level, 16) | bins


def unpack_words(words):
    density = lax.shift_right_logical(words, 16).astype(jnp.float32) * (1.0 / LEVELS)
    return density, words & 0xFFFF


def cell_values(density, bins, tables, depth):
    low_bits = bins & (LANES - 1)
    upper = bins >= LANES

    def pick(channel):
        first, second = tables[channel]
        return jnp.where(
            upper,
            jnp.take_along_axis(second, low_bits, axis=1, mode="promise_in_bounds"),
            jnp.take_along_axis(first, low_bits, axis=1, mode="promise_in_bounds"),
        )

    opacity = (1.0 - jnp.exp(-pick(3) * density / depth)) * (1.0 / 64.0)
    return [pick(0) * opacity, pick(1) * opacity, pick(2) * opacity, opacity]


def read_tables(tables_ref):
    return [[tables_ref[2 * channel + half] for half in range(2)] for channel in range(4)]


def cost(microseconds):
    return pl.CostEstimate(
        flops=0, bytes_accessed=int(3.6e6 * microseconds), transcendentals=0
    )


def stage_kernel(
    density_ref, bins_ref, colour_ref, extinction_ref,
    small_ref, mine_ref, columns_ref, dense_ref, index_ref, tables_ref,
):
    layers, rows, cols = density_ref.shape
    front = lax.axis_index("bz") == 0
    row_at = lax.broadcasted_iota(jnp.int32, (rows, LANES), 0)
    lane_at = lax.broadcasted_iota(jnp.int32, (rows, LANES), 1)
    for z in range(layers):
        first = pack_words(density_ref[z, :, 0:1], bins_ref[z, :, 0:1])
        last = pack_words(density_ref[z, :, cols - 1 : cols], bins_ref[z, :, cols - 1 : cols])
        line = jnp.where(lane_at == row_at, first, 0) + jnp.where(lane_at == row_at + rows, last, 0)
        columns_ref[z : z + 1, :] = jnp.sum(line, axis=0, keepdims=True)
        top, bottom = [
            pack_words(density_ref[z, r : r + 1, :], bins_ref[z, r : r + 1, :]) for r in (0, rows - 1)
        ]
        small_ref[0, z : z + 1, :] = jnp.where(front, bottom, top)
        mine_ref[z : z + 1, :] = jnp.where(front, top, bottom)
        for tile in range(cols // LANES):
            lanes = slice(tile * LANES, (tile + 1) * LANES)
            dense_ref[z, tile] = density_ref[z, :, lanes]
            index_ref[z, tile] = bins_ref[z, :, lanes]
    for tile in range(cols // LANES):
        small_ref[1, :, tile * LANES : (tile + 1) * LANES] = columns_ref[...]
    colour = colour_ref[...].astype(jnp.float32)
    extinction = extinction_ref[...].astype(jnp.float32).reshape(1, 2 * LANES)
    for channel in range(4):
        line = extinction if channel == 3 else colour[channel : channel + 1]
        for half in range(2):
            tables_ref[2 * channel + half] = jnp.broadcast_to(
                line[:, half * LANES : (half + 1) * LANES], (8, LANES)
            )


def pack_kernel(dense_ref, index_ref, bulk_ref, inside_ref):
    layers, tiles, rows = dense_ref.shape[:3]
    half = rows // 2
    front = lax.axis_index("bz") == 0
    start = jnp.where(front, half, 0)
    for tile in range(tiles):
        lanes = slice(tile * LANES, (tile + 1) * LANES)
        for z in range(layers):
            for part in range(2):
                at = pl.ds(start + part, half // 2, stride=2)
                bulk_ref[2 * z + part, :, lanes] = pack_words(
                    dense_ref[z, tile, at, :], index_ref[z, tile, at, :]
                )
            line = [
                pack_words(dense_ref[z, tile, r : r + 1, :], index_ref[z, tile, r : r + 1, :])
                for r in (half - 1, half)
            ]
            bulk_ref[2 * layers, z : z + 1, lanes] = jnp.where(front, line[0], line[1])
            inside_ref[z : z + 1, lanes] = jnp.where(front, line[1], line[0])


def diagonal_kernel(mine_ref, other_ref, cells_ref, line_ref):
    front = lax.axis_index("bz") == 0
    line_ref[0] = jnp.where(front, mine_ref[...], other_ref[0])
    line_ref[1] = jnp.where(front, other_ref[0], mine_ref[...])


def side_kernel(columns_ref, other_ref, near_ref, along_ref, ends_ref):
    layers = columns_ref.shape[0]
    front = lax.axis_index("bz") == 0
    near_inside = has_near(front)
    lane_at = lax.broadcasted_iota(jnp.int32, (layers, LANES), 1)
    for slab in range(2):
        mine = front if slab == 0 else jnp.logical_not(front)
        columns = jnp.where(mine, columns_ref[...], other_ref[1, :, 0:LANES])
        near = jnp.where(near_inside, near_ref[slab], 0)
        cols = near.shape[1]
        columns = jnp.where(lane_at == 64, near[:, 0:1], columns)
        ends_ref[slab] = jnp.where(lane_at == 65, near[:, cols - 1 : cols], columns)


def has_near(front):
    me_y = lax.axis_index("by")
    return jnp.where(front, me_y > 0, me_y + 1 < lax.axis_size("by"))


def fill_weights(weights_ref, rows):
    cols = weights_ref.shape[0] - LANES
    row = lax.broadcasted_iota(jnp.int32, (cols, 2 * cols), 0)
    at = lax.broadcasted_iota(jnp.int32, (cols, 2 * cols), 1)
    centre = lax.shift_right_logical(at, 1)
    beside = centre - 1 + 2 * (at & 1)
    weights_ref[0:cols, :] = jnp.where(
        row == centre, 3.0, jnp.where(row == beside, 1.0, 0.0)
    ).astype(jnp.bfloat16)
    row = lax.broadcasted_iota(jnp.int32, (LANES, 2 * LANES), 0)
    at = lax.broadcasted_iota(jnp.int32, (LANES, 2 * LANES), 1)
    right = ((row < rows) | (row == 64)) & (at == 2 * LANES - 1)
    left = (((row >= rows) & (row < 2 * rows)) | (row == 65)) & (at == 0)
    weights_ref[cols : cols + LANES, 0 : 2 * LANES] = jnp.where(right | left, 1.0, 0.0).astype(
        jnp.bfloat16
    )


def lane_maps(rows):
    lane_at = lax.broadcasted_iota(jnp.int32, (8, LANES), 1)
    sub_at = lax.broadcasted_iota(jnp.int32, (8, LANES), 0)
    return lane_at & (rows - 1), lane_at < 2 * rows, sub_at


def classify_rows(read_cells, tables, cells_ref, layers, tiles):
    total = float(2 * layers)
    for z in range(layers):
        for tile in range(tiles):
            even = cell_values(*read_cells(z, 0, tile), tables, total)
            odd = cell_values(*read_cells(z, 1, tile), tables, total)
            for channel in range(4):
                base = (z * 4 + channel) * 16
                block = jnp.concatenate([even[channel], odd[channel]], axis=0)
                cells_ref[base : base + 16, tile * LANES : (tile + 1) * LANES] = block.astype(jnp.bfloat16)


def classify_halo(words, tables, ends_ref, values_ref, rows, base):
    layers = words.shape[0]
    start = lax.axis_index("bz") * (rows // 2)
    side_lane, has_side, sub_at = lane_maps(rows)
    halo = cell_values(*unpack_words(words), tables, float(2 * layers))
    for channel in range(4):
        values_ref[channel, 0:layers] = halo[channel]
    masks = [has_side & (side_lane == start + 2 * sub_at + part) for part in range(2)]
    for z in range(layers):
        for channel in range(4):
            line = jnp.broadcast_to(values_ref[channel, z : z + 1, :], (8, LANES))
            block = jnp.concatenate([jnp.where(mask, line, 0.0) for mask in masks], axis=0)
            at = base + (z * 4 + channel) * 16
            ends_ref[at : at + 16, :] = block.astype(jnp.bfloat16)
    return halo


def rounded(value):
    return value.astype(jnp.bfloat16).astype(jnp.float32)


def along_columns(cells, weights_ref, store):
    cols = cells.shape[1]
    tiles = 2 * cols // LANES
    result = jnp.dot(cells, weights_ref[0:cols, :], preferred_element_type=jnp.float32)
    for tile in range(tiles):
        block = result[:, tile * LANES : (tile + 1) * LANES]
        store(tile, block if tile in (0, tiles - 1) else rounded(block))


def cells_kernel(dense_ref, index_ref, tables_ref, cells_ref, weights_ref):
    layers, tiles, rows = dense_ref.shape[:3]
    half = rows // 2
    start = lax.axis_index("bz") * half
    fill_weights(weights_ref, rows)

    def read_cells(z, part, tile):
        at = pl.ds(start + part, half // 2, stride=2)
        return dense_ref[z, tile, at, :], index_ref[z, tile, at, :]

    classify_rows(read_cells, read_tables(tables_ref), cells_ref, layers, tiles)


def own_kernel(cells_ref, weights_ref, along_ref):
    def store(tile, block):
        along_ref[tile] = block

    along_columns(cells_ref[...], weights_ref, store)


def other_kernel(bulk_ref, tables_ref, weights_ref, own_ref, along_ref, cells_ref):
    layers = (bulk_ref.shape[0] - 1) // 2
    cols = bulk_ref.shape[2]
    size = own_ref.shape[1]
    me = lax.axis_index("bz")
    pad = size // layers
    mine = pl.multiple_of(pad + me * size, pad)
    theirs = pl.multiple_of(pad + (1 - me) * size, pad)
    for tile in range(own_ref.shape[0]):
        along_ref[tile, 0:pad, :] = jnp.zeros((pad, LANES), jnp.float32)
        along_ref[tile, pad + 2 * size : 2 * pad + 2 * size, :] = jnp.zeros((pad, LANES), jnp.float32)
        along_ref[tile, pl.ds(mine, size), :] = own_ref[tile]

    def read_cells(z, part, tile):
        return unpack_words(bulk_ref[2 * z + part, :, tile * LANES : (tile + 1) * LANES])

    def store(tile, block):
        along_ref[tile, pl.ds(theirs, size), :] = block

    classify_rows(read_cells, read_tables(tables_ref), cells_ref, layers, cols // LANES)
    along_columns(cells_ref[...], weights_ref, store)


def edge_lines(edge, tile, lines_ref, depth):
    layer_at = lax.broadcasted_iota(jnp.int32, (depth, LANES), 0)
    for side in range(2):
        for channel in range(4):
            base = (side * 4 + channel) * depth
            now = edge[base : base + depth]
            triple = 3.0 * now
            before = jnp.where(layer_at == 0, 0.0, pltpu.roll(now, 1, 0))
            after = jnp.where(layer_at == depth - 1, 0.0, pltpu.roll(now, depth - 1, 0))
            for parity, beside in enumerate((before, after)):
                lines_ref[tile, side, channel, parity] = rounded(beside + triple)


def render_tile(tile, along_ref, lines_ref, flip, layers):
    sub_at = lax.broadcasted_iota(jnp.int32, (8, LANES), 0)
    top = sub_at == 0
    bottom = sub_at == 7

    def layer_rows(layer, channel):
        base = pl.multiple_of((layer * 4 + channel) * 16, 16)
        return [along_ref[tile, pl.ds(base + part * 8, 8), :] for part in range(2)]

    def over_layer(layer, image):
        here = [layer_rows(layer + 1, channel) for channel in range(4)]
        triple = [[3.0 * value for value in pair] for pair in here]
        for parity in range(2):
            clear = [1.0 - value for value in image[3]]
            updated = []
            for channel in range(4):
                beside = layer_rows(layer + 2 * parity, channel)
                even, odd = [rounded(beside[part] + triple[channel][part]) for part in range(2)]
                above = lines_ref[tile, 0, channel, parity, pl.ds(layer, 1), :]
                below = lines_ref[tile, 1, channel, parity, pl.ds(layer, 1), :]
                before_even = jnp.where(top, jnp.broadcast_to(above, (8, LANES)), pltpu.roll(odd, 1, 0))
                after_odd = jnp.where(bottom, jnp.broadcast_to(below, (8, LANES)), pltpu.roll(even, 7, 0))
                even_centre = 3.0 * even
                odd_centre = 3.0 * odd
                samples = [
                    before_even + even_centre, even_centre + odd, even + odd_centre, odd_centre + after_odd
                ]
                updated.append([image[channel][i] + clear[i] * samples[i] for i in range(4)])
            image = updated
        return image

    def one_slab(position, image):
        slab = position ^ flip
        for z in range(layers):
            image = over_layer(slab * layers + z, image)
        return image

    zero = jnp.zeros((8, LANES), jnp.float32)
    return lax.fori_loop(0, 2, one_slab, [[zero] * 4 for _ in range(4)])


def inner_kernel(
    rank_ref, tables_ref, weights_ref, bulk_ref, inside_ref, near_ref, along_ref, ends_ref,
    image_ref, edge_ref, cells_ref, lines_ref, mixed_ref,
):
    layers, cols = inside_ref.shape
    depth = 2 * layers
    tiles = 2 * cols // LANES
    me = lax.axis_index("bz")
    front = me == 0
    tables = read_tables(tables_ref)
    near_inside = has_near(front)
    for slab in range(2):
        inside = jnp.where(me == slab, inside_ref[...], bulk_ref[2 * layers])
        near = jnp.where(near_inside, near_ref[slab], 0)
        for side in range(2):
            use_near = front if side == 0 else jnp.logical_not(front)
            words = jnp.where(use_near, near, inside)
            for t in range(cols // LANES):
                lanes = slice(t * LANES, (t + 1) * LANES)
                values = cell_values(*unpack_words(words[:, lanes]), tables, float(depth))
                for channel in range(4):
                    base = (side * 4 + channel) * depth + slab * layers
                    cells_ref[base : base + layers, lanes] = values[channel]
    edge = jnp.dot(
        cells_ref[...].astype(jnp.bfloat16), weights_ref[0:cols, :], preferred_element_type=jnp.float32
    )
    for tile in range(tiles):
        block = edge[:, tile * LANES : (tile + 1) * LANES]
        if tile in (0, tiles - 1):
            edge_ref[0 if tile == 0 else 1] = block
        else:
            edge_lines(rounded(block), tile - 1, lines_ref, depth)

    def one_tile(index, carry):
        image = render_tile(index, along_ref.at[1 : tiles - 1], lines_ref, rank_ref[0], layers)
        lanes = pl.ds(pl.multiple_of(index * LANES, LANES), LANES)
        for channel in range(4):
            for i in range(4):
                mixed_ref[channel, pl.ds(i, 8, stride=4), :] = image[channel][i]
            image_ref[channel, :, lanes] = mixed_ref[channel]
        return carry

    lax.fori_loop(0, tiles - 2, one_tile, 0)


def outer_kernel(
    rank_ref, tables_ref, weights_ref, beside_ref, across_ref, along_ref, edge_ref, image_ref,
    out_ref, ends_ref, values_ref, fixed_ref, lines_ref, mixed_ref,
):
    rows = out_ref.shape[1]
    cols = out_ref.shape[2] // 2
    layers = beside_ref.shape[1]
    depth = 2 * layers
    tiles = 2 * cols // LANES
    size = layers * 64
    pad = 64
    front = lax.axis_index("bz") == 0
    me_x = lax.axis_index("bx")
    even_x = lax.rem(me_x, 2) == 0
    tables = read_tables(tables_ref)
    lane_at = lax.broadcasted_iota(jnp.int32, (layers, LANES), 1)
    is_right = (lane_at < rows) | (lane_at == 64)
    for slab in range(2):
        right = jnp.where(even_x, beside_ref[slab], across_ref[slab])
        left = jnp.where(even_x, across_ref[slab], beside_ref[slab])
        right = jnp.where(me_x + 1 < lax.axis_size("bx"), right, 0)
        left = jnp.where(me_x > 0, left, 0)
        halo = jnp.where(is_right, right, left)
        values = classify_halo(halo, tables, ends_ref, values_ref, rows, slab * size)
        for side in range(2):
            row = jnp.where(front, 64, rows // 2 - 1) if side == 0 else jnp.where(front, rows // 2, 64)
            twin = jnp.where(row == 64, 65, row + rows)
            keep = (lane_at == row) | (lane_at == twin)
            for channel in range(4):
                values_ref[4 + side * 4 + channel, slab * layers : (slab + 1) * layers] = jnp.where(
                    keep, values[channel], 0.0
                )
    for line in range(8):
        base = 2 * size + line * depth
        ends_ref[base : base + depth, :] = values_ref[4 + line].astype(jnp.bfloat16)
    added = jnp.dot(
        ends_ref[...], weights_ref[cols : cols + LANES, 0 : 2 * LANES], preferred_element_type=jnp.float32
    )
    for index, tile in enumerate((0, tiles - 1)):
        block = added[:, index * LANES : (index + 1) * LANES]
        fixed_ref[index, 0:pad, :] = jnp.zeros((pad, LANES), jnp.float32)
        fixed_ref[index, pad + 2 * size :, :] = jnp.zeros((pad, LANES), jnp.float32)
        fixed_ref[index, pad : pad + 2 * size, :] = rounded(
            along_ref[tile, pad : pad + 2 * size, :] + block[0 : 2 * size]
        )
        edge_lines(rounded(edge_ref[index] + block[2 * size :]), index, lines_ref, depth)
    out_ref[:, :, LANES : 2 * cols - LANES] = image_ref[...]

    def one_tile(index, carry):
        image = render_tile(index, fixed_ref, lines_ref, rank_ref[0], layers)
        lanes = pl.ds(pl.multiple_of(index * (2 * cols - LANES), LANES), LANES)
        for channel in range(4):
            for i in range(4):
                mixed_ref[channel, pl.ds(i, 8, stride=4), :] = image[channel][i]
            out_ref[channel, :, lanes] = mixed_ref[channel]
        return carry

    lax.fori_loop(0, 2, one_tile, 0)


def two_slab_device(density, bin_index, tf_colour, tf_extinction, slab_rank):
    layers, rows, cols = density.shape
    half = rows // 2
    tiles = 2 * cols // LANES
    size = layers * 4 * half
    count_y, count_x = lax.axis_size("by"), lax.axis_size("bx")
    f32, bf16, i32 = jnp.float32, jnp.bfloat16, jnp.int32

    def call(kernel, name, out_shape, time, scratch_shapes=(), in_specs=None):
        def run(*operands):
            return pl.pallas_call(
                kernel,
                out_shape=out_shape,
                in_specs=in_specs or [VMEM] * len(operands),
                out_specs=(VMEM,) * len(out_shape) if isinstance(out_shape, tuple) else VMEM,
                scratch_shapes=scratch_shapes,
                compiler_params=pltpu.CompilerParams(vmem_limit_bytes=16 * 1024 * 1024),
                cost_estimate=cost(time),
                name=name,
            )(*operands)

        return run

    def both(route):
        return route + [(target, source) for source, target in route]

    blocks = (layers, cols // LANES, rows, LANES)
    small, mine, columns, dense, index, tables = call(
        stage_kernel,
        "stage_block",
        (
            pltpu.VMEM((2, layers, cols), i32),
            pltpu.VMEM((layers, cols), i32),
            pltpu.VMEM((layers, LANES), i32),
            pltpu.VMEM(blocks, f32),
            pltpu.VMEM(blocks, i32),
            pltpu.VMEM((8, 8, LANES), f32),
        ),
        1.2,
    )(*[pltpu.with_memory_space_constraint(x, pltpu.HBM) for x in (density, bin_index, tf_colour, tf_extinction)])
    swap = [(0, 1), (1, 0)]
    other_small = lax.ppermute(small, "bz", swap)
    bulk, inside = call(
        pack_kernel,
        "pack_block",
        (pltpu.VMEM((2 * layers + 1, 8, cols), i32), pltpu.VMEM((layers, cols), i32)),
        0.1,
    )(dense, index)
    bulk = lax.ppermute(bulk, "bz", swap)
    cells, weights = call(
        cells_kernel,
        "own_cells",
        (pltpu.VMEM((size, cols), bf16), pltpu.VMEM((cols + LANES, 2 * cols), bf16)),
        0.5,
    )(dense, index, tables)

    line = call(diagonal_kernel, "diagonal_line", pltpu.VMEM((2, layers, cols), i32), 0.1)(
        mine, other_small, cells
    )
    route = [(count_y + y, y + 1) for y in range(count_y - 1)]
    alone = [(0, 0), (2 * count_y - 1, 2 * count_y - 1)]
    near = lax.ppermute(line, ("bz", "by"), both(route) + alone)
    along = call(own_kernel, "own_slab", pltpu.VMEM((tiles, size, LANES), f32), 0.4)(cells, weights)
    along = call(
        other_kernel,
        "other_slab",
        pltpu.VMEM((tiles, 2 * size + 2 * 4 * half, LANES), f32),
        0.7,
        [pltpu.VMEM((size, cols), bf16)],
    )(bulk, tables, weights, along)
    ends = call(side_kernel, "side_columns", pltpu.VMEM((2, layers, LANES), i32), 0.1)(
        columns, other_small, near, along
    )
    pairs = [(x, x + 1) for x in range(0, count_x, 2)]
    cross = [(x, (x + 1) % count_x) for x in range(1, count_x, 2)]
    beside = lax.ppermute(ends, "bx", both(pairs))
    across = lax.ppermute(ends, "bx", both(cross))
    smem = pl.BlockSpec(memory_space=pltpu.SMEM)
    lines = pltpu.VMEM((2, 2, 4, 2, 2 * layers, LANES), f32)
    image, edge = call(
        inner_kernel,
        "inner_tiles",
        (pltpu.VMEM((4, rows, (tiles - 2) * LANES), f32), pltpu.VMEM((2, 16 * layers, LANES), f32)),
        2.0,
        [pltpu.VMEM((16 * layers, cols), f32), lines, pltpu.VMEM((4, rows, LANES), f32)],
        [smem] + [VMEM] * 7,
    )(slab_rank, tables, weights, bulk, inside, near, along, ends)
    return call(
        outer_kernel,
        "outer_tiles",
        jax.ShapeDtypeStruct((4, rows, 2 * cols), f32),
        2.0,
        [
            pltpu.VMEM((2 * size + 16 * layers, LANES), bf16),
            pltpu.VMEM((12, 2 * layers, LANES), f32),
            pltpu.VMEM((2, 2 * size + 2 * 4 * half, LANES), f32),
            lines,
            pltpu.VMEM((4, rows, LANES), f32),
        ],
        [smem] + [VMEM] * 7,
    )(slab_rank, tables, weights, beside, across, along, edge, image)


def on_device(density, bin_index, tf_colour, tf_extinction, slab_rank):
    if lax.axis_size("bz") == 2:
        return two_slab_device(density, bin_index, tf_colour, tf_extinction, slab_rank)
    return general_device(density, bin_index, tf_colour, tf_extinction, slab_rank)


def solution(mesh):
    return jax.shard_map(
        on_device,
        mesh=mesh,
        in_specs=(P("bz", "by", "bx"), P("bz", "by", "bx"), P(), P(), P()),
        out_specs=P(None, ("by", "bz"), "bx"),
        check_vma=False,
    )
```

time: 22 us -> 20.2 us (0.918)
  the two profiles are of different devices: /device:TPU:0 before, /device:TPU:9 now
where the time goes in v4:
time: 20.2 us; the launch traced here: 20 us
  starting transfers between devices  8.35 us (41%)
  Pallas kernels  7.47 us (37%)
  waiting for transfers between devices  4.15 us (21%)
    pallas_call x9, Pallas kernels, run(): pl.pallas_call(kernel, out_shape=out_shape, in_specs=in_specs or [VMEM] *...  7.47 us
    ppermute x1, starting transfers between devices, two_slab_device(): across = lax.ppermute(ends, 'bx', both(cross))  3.83 us
    ppermute x1, starting transfers between devices, two_slab_device(): near = lax.ppermute(line, ('bz', 'by'), both(route) + alone)  2.99 us
    ppermute x1, waiting for transfers between devices, two_slab_device(): other_small = lax.ppermute(small, 'bz', swap)  2.89 us
    ppermute x1, starting transfers between devices, two_slab_device(): bulk = lax.ppermute(bulk, 'bz', swap)  1.27 us
    ppermute x1, waiting for transfers between devices, two_slab_device(): near = lax.ppermute(line, ('bz', 'by'), both(route) + alone)  1.25 us
  transfers between devices with their start and end apart: 5, of which 2 were waited for; matrix products, arithmetic and copies ran while one was open for 0% of the time, Pallas kernels for 17%

profile of v4, /device:TPU:9, one launch (start us, length us, event | category | flops | bytes accessed | tf_op | source)
XLA Modules:
  0.0 20.0 jit_solution(9244421342299060279)
XLA Ops:
  0.0 1.2 %stage_block.1 = (s32[2,8,256]{2,1,0:T(8,128)S(1)}, s32[8,256]{1,0:T(8,128)S(1)}, s32[8,128]{1,0:T(8,128)S(1)}, f32[8,2,32,128]{3,2,1,0:T(8,128)S(1)}, s32[8,2,3...) custom-call(f32[8,32,256]{2,1,0:T(8,128)} %density_ref.1, s32[8,32,256]{2,1,0:T(8,128)} %bins_ref.1, ...), custom_call_target="tpu_custom_call" | custom-call | bytes 4320000 | tf_op jit(solution)/shard_map/stage_block/pallas_call | solution.py:515
  1.2 0.1 pack_block.1
  1.3 1.3 %collective-permute-start.2 = (s32[17,8,256]{2,1,0:T(8,128)S(1)}, s32[17,8,256]{2,1,0:T(8,128)S(1)}, u32[]{:S(2)}, u32[]{:S(2)}) collective-permute-start(s32[17,8,256]{2,1,0:T(8,128)S(1)} %get-tuple-element.25), channel_id=1, source_target_pairs={{0,16},{16,0},{1,17},{17,1},{2,18},{18,2},{3,19},{19,3},{4,20},{20... | collective-permute-start | bytes 417800 | tf_op jit(solution)/shard_map/ppermute | solution.py:553
  2.6 0.3 %collective-permute-start = (s32[2,8,256]{2,1,0:T(8,128)S(1)}, s32[2,8,256]{2,1,0:T(8,128)S(1)}, u32[]{:S(2)}, u32[]{:S(2)}) collective-permute-start(s32[2,8,256]{2,1,0:T(8,128)S(1)} %get-tuple-element.22), channel_id=1, source_target_pairs={{0,16},{16,0},{1,17},{17,1},{2,18},{18,2},{3,19},{19,3},{4,20},{20... | collective-permute-start | bytes 49160 | tf_op jit(solution)/shard_map/ppermute | solution.py:546
  2.8 0.5 %own_cells.1 = (bf16[512,256]{1,0:T(8,128)(2,1)S(1)}, bf16[384,512]{1,0:T(8,128)(2,1)S(1)}) custom-call(f32[8,2,32,128]{3,2,1,0:T(8,128)S(1)} %get-tuple-element.18.dense_ref, s32[8,2,32,128]{3,2,1,0:T(8,128)S(1)} %get-tuple-element.19.index_ref, f32[8,8,128]{2,1,0:T(8,128)S(1)} %get-tuple-element.17.tables_ref), custom_call_target="tpu_custom_call" | custom-call | bytes 1800000 | tf_op jit(solution)/shard_map/own_cells/pallas_call | solution.py:515
  3.4 2.9 %collective-permute-done.other_ref = s32[2,8,256]{2,1,0:T(8,128)S(1)} collective-permute-done((s32[2,8,256]{2,1,0:T(8,128)S(1)}, s32[2,8,256]{2,1,0:T(8,128)S(1)}, u32[]{:S(2)}, u32[]{:S(2)}) %collective-permute-start) | collective-permute-done | bytes 16416 | tf_op jit(solution)/shard_map/ppermute | solution.py:546
  6.3 3.0 %collective-permute-start.1 = (s32[2,8,256]{2,1,0:T(8,128)S(1)}, s32[2,8,256]{2,1,0:T(8,128)S(1)}, u32[]{:S(2)}, u32[]{:S(2)}) collective-permute-start(s32[2,8,256]{2,1,0:T(8,128)S(1)} %diagonal_line.1), channel_id=1, source_target_pairs={{16,4},{20,8},{24,12},{4,16},{8,20},{12,24},{0,0},{28,28},{17,5},{... | collective-permute-start | bytes 49160 | tf_op jit(solution)/shard_map/ppermute | solution.py:566
  9.3 0.3 %own_slab.1.own_ref = f32[4,512,128]{2,1,0:T(8,128)S(1)} custom-call(bf16[512,256]{1,0:T(8,128)(2,1)S(1)} %get-tuple-element.24.cells_ref, bf16[384,512]{1,0:T(8,128)(2,1)S(1)} %get-tuple-element.20.weights_ref), custom_call_target="tpu_custom_call" | custom-call | bytes 1440000 | tf_op jit(solution)/shard_map/own_slab/pallas_call | solution.py:515
  9.6 0.0 copy-start
  9.6 0.0 collective-permute-done.2.bulk_ref
  9.6 0.8 %other_slab.1.along_ref = f32[4,1152,128]{2,1,0:T(8,128)S(1)} custom-call(s32[17,8,256]{2,1,0:T(8,128)S(1)} %collective-permute-done.2.bulk_ref, f32[8,8,128]{2,1,0:T(8,128)S(1)} %get-tuple-element.17.tables_ref, bf16[384,512]{1,0:T(8,128)(2,1)S(1)} %get-tuple-element.20.weights_ref, f32[4,512,128]{2,1,0:T(8,128)S(1)} %own_slab.1.own_ref), custom_call_target="tpu_custom_call" | custom-call | bytes 2520000 | tf_op jit(solution)/shard_map/other_slab/pallas_call | solution.py:515
  10.4 1.3 %collective-permute-done.1.near_ref = s32[2,8,256]{2,1,0:T(8,128)S(1)} collective-permute-done((s32[2,8,256]{2,1,0:T(8,128)S(1)}, s32[2,8,256]{2,1,0:T(8,128)S(1)}, u32[]{:S(2)}, u32[]{:S(2)}) %collective-permute-start.1) | collective-permute-done | bytes 16416 | tf_op jit(solution)/shard_map/ppermute | solution.py:566
  11.6 0.1 side_columns.1.ends_ref
  11.7 3.8 %collective-permute-start.4 = (s32[2,8,128]{2,1,0:T(8,128)S(1)}, s32[2,8,128]{2,1,0:T(8,128)S(1)}, u32[]{:S(2)}, u32[]{:S(2)}) collective-permute-start(s32[2,8,128]{2,1,0:T(8,128)S(1)} %side_columns.1.ends_ref), channel_id=1, source_target_pairs={{1,2},{3,0},{2,1},{0,3},{5,6},{7,4},{6,5},{4,7},{9,10},{11,8},{10,... | collective-permute-start | bytes 24584 | tf_op jit(solution)/shard_map/ppermute | solution.py:581
  15.5 0.0 collective-permute-start.3
  15.5 0.0 copy-done
  15.5 1.9 %inner_tiles.1 = (f32[4,32,256]{2,1,0:T(8,128)S(1)}, f32[2,128,128]{2,1,0:T(8,128)S(1)}) custom-call(s32[2]{0:T(128)S(1)} %copy-done, f32[8,8,128]{2,1,0:T(8,128)S(1)} %get-tuple-element.17.tables_ref, bf16[384,512]{1,0:T(8,128)(2,1)S(1)} %get-tuple-element.20.weights_ref, s32[17,8,256]{2,1,0:T(8,128)S(1)} %collective-permute-done.2.bulk_ref, ...), custom_call_target="tpu_custom_call" | custom-call | bytes 7200000 | tf_op jit(solution)/shard_map/inner_tiles/pallas_call | solution.py:515
  17.4 0.0 collective-permute-done.4.across_ref
  17.4 0.0 collective-permute-done.3.beside_ref
  17.4 2.6 %outer_tiles.1 = f32[4,32,512]{2,1,0:T(8,128)} custom-call(s32[2]{0:T(128)S(1)} %copy-done, f32[8,8,128]{2,1,0:T(8,128)S(1)} %get-tuple-element.17.tables_ref, bf16[384,512]{1,0:T(8,128)(2,1)S(1)} %get-tuple-element.20.weights_ref, s32[2,8,128]{2,1,0:T(8,128)S(1)} %collective-permute-done.3.beside_ref, s32[2,8,128]{2,1,0:T(8,128)S(1)} %collective-permute-done.4.across_ref, ...), custom_call_target="tpu_custom_call" | custom-call | bytes 7200000 | tf_op jit(solution)/shard_map/outer_tiles/pallas_call | solution.py:515
  (1 shorter events, 0.0 us)
Async XLA Ops:
  1.3 8.3 %collective-permute-start.2 = (s32[17,8,256]{2,1,0:T(8,128)S(1)}, s32[17,8,256]{2,1,0:T(8,128)S(1)}, u32[]{:S(2)}, u32[]{:S(2)}) collective-permute-start(s32[17,8,256]{2,1,0:T(8,128)S(1)} %get-tuple-element.25), channel_id=1, source_target_pairs={{0,16},{16,0},{1,17},{17,1},{2,18},{18,2},{3,19},{19,3},{4,20},{20... | collective-permute-start | bytes 417800 | tf_op jit(solution)/shard_map/ppermute | solution.py:553
  2.6 3.7 %collective-permute-start = (s32[2,8,256]{2,1,0:T(8,128)S(1)}, s32[2,8,256]{2,1,0:T(8,128)S(1)}, u32[]{:S(2)}, u32[]{:S(2)}) collective-permute-start(s32[2,8,256]{2,1,0:T(8,128)S(1)} %get-tuple-element.22), channel_id=1, source_target_pairs={{0,16},{16,0},{1,17},{17,1},{2,18},{18,2},{3,19},{19,3},{4,20},{20... | collective-permute-start | bytes 49160 | tf_op jit(solution)/shard_map/ppermute | solution.py:546
  6.3 5.4 %collective-permute-start.1 = (s32[2,8,256]{2,1,0:T(8,128)S(1)}, s32[2,8,256]{2,1,0:T(8,128)S(1)}, u32[]{:S(2)}, u32[]{:S(2)}) collective-permute-start(s32[2,8,256]{2,1,0:T(8,128)S(1)} %diagonal_line.1), channel_id=1, source_target_pairs={{16,4},{20,8},{24,12},{4,16},{8,20},{12,24},{0,0},{28,28},{17,5},{... | collective-permute-start | bytes 49160 | tf_op jit(solution)/shard_map/ppermute | solution.py:566
  9.6 6.0 %copy-start = (s32[2]{0:T(128)S(1)}, s32[2]{0:T(128)}, u32[]{:S(2)}) copy-start(s32[2]{0:T(128)} %rank_ref.3) | copy-start | bytes 28
  11.7 5.7 %collective-permute-start.4 = (s32[2,8,128]{2,1,0:T(8,128)S(1)}, s32[2,8,128]{2,1,0:T(8,128)S(1)}, u32[]{:S(2)}, u32[]{:S(2)}) collective-permute-start(s32[2,8,128]{2,1,0:T(8,128)S(1)} %side_columns.1.ends_ref), channel_id=1, source_target_pairs={{1,2},{3,0},{2,1},{0,3},{5,6},{7,4},{6,5},{4,7},{9,10},{11,8},{10,... | collective-permute-start | bytes 24584 | tf_op jit(solution)/shard_map/ppermute | solution.py:581
  15.5 1.9 %collective-permute-start.3 = (s32[2,8,128]{2,1,0:T(8,128)S(1)}, s32[2,8,128]{2,1,0:T(8,128)S(1)}, u32[]{:S(2)}, u32[]{:S(2)}) collective-permute-start(s32[2,8,128]{2,1,0:T(8,128)S(1)} %side_columns.1.ends_ref), channel_id=1, source_target_pairs={{0,1},{2,3},{1,0},{3,2},{4,5},{6,7},{5,4},{7,6},{8,9},{10,11},{9,8... | collective-permute-start | bytes 24584 | tf_op jit(solution)/shard_map/ppermute | solution.py:580

commit v5 on v4

--- a/solution.py
+++ b/solution.py
@@ -188,7 +188,7 @@
             )
 
 
-def pack_kernel(dense_ref, index_ref, bulk_ref, inside_ref):
+def pack_kernel(dense_ref, index_ref, cells_ref, bulk_ref, inside_ref):
     layers, tiles, rows = dense_ref.shape[:3]
     half = rows // 2
     front = lax.axis_index("bz") == 0
@@ -209,7 +209,7 @@
             inside_ref[z : z + 1, lanes] = jnp.where(front, line[1], line[0])
 
 
-def diagonal_kernel(mine_ref, other_ref, cells_ref, line_ref):
+def diagonal_kernel(mine_ref, other_ref, inside_ref, line_ref):
     front = lax.axis_index("bz") == 0
     line_ref[0] = jnp.where(front, mine_ref[...], other_ref[0])
     line_ref[1] = jnp.where(front, other_ref[0], mine_ref[...])
@@ -544,26 +544,32 @@
     )(*[pltpu.with_memory_space_constraint(x, pltpu.HBM) for x in (density, bin_index, tf_colour, tf_extinction)])
     swap = [(0, 1), (1, 0)]
     other_small = lax.ppermute(small, "bz", swap)
-    bulk, inside = call(
-        pack_kernel,
-        "pack_block",
-        (pltpu.VMEM((2 * layers + 1, 8, cols), i32), pltpu.VMEM((layers, cols), i32)),
-        0.1,
-    )(dense, index)
-    bulk = lax.ppermute(bulk, "bz", swap)
     cells, weights = call(
         cells_kernel,
         "own_cells",
         (pltpu.VMEM((size, cols), bf16), pltpu.VMEM((cols + LANES, 2 * cols), bf16)),
         0.5,
     )(dense, index, tables)
+    bulk, inside = call(
+        pack_kernel,
+        "pack_block",
+        (pltpu.VMEM((2 * layers + 1, 8, cols), i32), pltpu.VMEM((layers, cols), i32)),
+        0.1,
+    )(dense, index, cells)
+    bulk = lax.ppermute(bulk, "bz", swap)
 
     line = call(diagonal_kernel, "diagonal_line", pltpu.VMEM((2, layers, cols), i32), 0.1)(
-        mine, other_small, cells
+        mine, other_small, inside
     )
-    route = [(count_y + y, y + 1) for y in range(count_y - 1)]
-    alone = [(0, 0), (2 * count_y - 1, 2 * count_y - 1)]
-    near = lax.ppermute(line, ("bz", "by"), both(route) + alone)
+    def place(z, y, x):
+        return (z * count_y + y) * count_x + x
+
+    route = [
+        (place(1, y, x), place(0, y + 1, x)) for y in range(count_y - 1) for x in range(count_x)
+    ]
+    for z, y in ((0, 0), (1, count_y - 1)):
+        route += [(place(z, y, x), place(z, y, x + 1)) for x in range(0, count_x, 2)]
+    near = lax.ppermute(line, ("bz", "by", "bx"), both(route))
     along = call(own_kernel, "own_slab", pltpu.VMEM((tiles, size, LANES), f32), 0.4)(cells, weights)
     along = call(
         other_kernel,

time: 20.2 us -> 18.9 us (0.936)
  the two profiles are of different devices: /device:TPU:9 before, /device:TPU:7 now
where the time goes in v5:
time: 18.9 us; the launch traced here: 18.8 us
  Pallas kernels  7.48 us (40%)
  starting transfers between devices  5.69 us (30%)
  waiting for transfers between devices  5.55 us (29%)
    pallas_call x9, Pallas kernels, run(): pl.pallas_call(kernel, out_shape=out_shape, in_specs=in_specs or [VMEM] *...  7.48 us
    ppermute x1, waiting for transfers between devices, two_slab_device(): other_small = lax.ppermute(small, 'bz', swap)  3.43 us
    ppermute x1, starting transfers between devices, two_slab_device(): beside = lax.ppermute(ends, 'bx', both(pairs))  2.7 us
    ppermute x1, starting transfers between devices, two_slab_device(): near = lax.ppermute(line, ('bz', 'by', 'bx'), both(route))  1.27 us
    ppermute x1, starting transfers between devices, two_slab_device(): other_small = lax.ppermute(small, 'bz', swap)  1.21 us
    ppermute x1, waiting for transfers between devices, two_slab_device(): near = lax.ppermute(line, ('bz', 'by', 'bx'), both(route))  1.09 us
    ppermute x1, waiting for transfers between devices, two_slab_device(): across = lax.ppermute(ends, 'bx', both(cross))  1.03 us
  transfers between devices with their start and end apart: 5, of which 3 were waited for; matrix products, arithmetic and copies ran while one was open for 0% of the time, Pallas kernels for 16%

profile of v5, /device:TPU:7, one launch (start us, length us, event | category | flops | bytes accessed | tf_op | source)
XLA Modules:
  0.0 18.8 jit_solution(15229881719669692701)
XLA Ops:
  0.0 1.2 %stage_block.1 = (s32[2,8,256]{2,1,0:T(8,128)S(1)}, s32[8,256]{1,0:T(8,128)S(1)}, s32[8,128]{1,0:T(8,128)S(1)}, f32[8,2,32,128]{3,2,1,0:T(8,128)S(1)}, s32[8,2,3...) custom-call(f32[8,32,256]{2,1,0:T(8,128)} %density_ref.1, s32[8,32,256]{2,1,0:T(8,128)} %bins_ref.1, ...), custom_call_target="tpu_custom_call" | custom-call | bytes 4320000 | tf_op jit(solution)/shard_map/stage_block/pallas_call | solution.py:515
  1.2 0.5 %own_cells.1 = (bf16[512,256]{1,0:T(8,128)(2,1)S(1)}, bf16[384,512]{1,0:T(8,128)(2,1)S(1)}) custom-call(f32[8,2,32,128]{3,2,1,0:T(8,128)S(1)} %get-tuple-element.18.dense_ref, s32[8,2,32,128]{3,2,1,0:T(8,128)S(1)} %get-tuple-element.19.index_ref, f32[8,8,128]{2,1,0:T(8,128)S(1)} %get-tuple-element.17.tables_ref), custom_call_target="tpu_custom_call" | custom-call | bytes 1800000 | tf_op jit(solution)/shard_map/own_cells/pallas_call | solution.py:515
  1.8 0.1 pack_block.1
  1.8 0.3 %collective-permute-start.2 = (s32[17,8,256]{2,1,0:T(8,128)S(1)}, s32[17,8,256]{2,1,0:T(8,128)S(1)}, u32[]{:S(2)}, u32[]{:S(2)}) collective-permute-start(s32[17,8,256]{2,1,0:T(8,128)S(1)} %get-tuple-element.26), channel_id=1, source_target_pairs={{0,16},{16,0},{1,17},{17,1},{2,18},{18,2},{3,19},{19,3},{4,20},{20... | collective-permute-start | bytes 417800 | tf_op jit(solution)/shard_map/ppermute | solution.py:559
  2.2 1.2 %collective-permute-start = (s32[2,8,256]{2,1,0:T(8,128)S(1)}, s32[2,8,256]{2,1,0:T(8,128)S(1)}, u32[]{:S(2)}, u32[]{:S(2)}) collective-permute-start(s32[2,8,256]{2,1,0:T(8,128)S(1)} %get-tuple-element.22), channel_id=1, source_target_pairs={{0,16},{16,0},{1,17},{17,1},{2,18},{18,2},{3,19},{19,3},{4,20},{20... | collective-permute-start | bytes 49160 | tf_op jit(solution)/shard_map/ppermute | solution.py:546
  3.4 3.4 %collective-permute-done.other_ref = s32[2,8,256]{2,1,0:T(8,128)S(1)} collective-permute-done((s32[2,8,256]{2,1,0:T(8,128)S(1)}, s32[2,8,256]{2,1,0:T(8,128)S(1)}, u32[]{:S(2)}, u32[]{:S(2)}) %collective-permute-start) | collective-permute-done | bytes 16416 | tf_op jit(solution)/shard_map/ppermute | solution.py:546
  6.8 1.3 %collective-permute-start.1 = (s32[2,8,256]{2,1,0:T(8,128)S(1)}, s32[2,8,256]{2,1,0:T(8,128)S(1)}, u32[]{:S(2)}, u32[]{:S(2)}) collective-permute-start(s32[2,8,256]{2,1,0:T(8,128)S(1)} %diagonal_line.1), channel_id=1, source_target_pairs={{16,4},{17,5},{18,6},{19,7},{20,8},{21,9},{22,10},{23,11},{24,12},... | collective-permute-start | bytes 49160 | tf_op jit(solution)/shard_map/ppermute | solution.py:572
  8.1 0.3 %own_slab.1.own_ref = f32[4,512,128]{2,1,0:T(8,128)S(1)} custom-call(bf16[512,256]{1,0:T(8,128)(2,1)S(1)} %get-tuple-element.24.cells_ref, bf16[384,512]{1,0:T(8,128)(2,1)S(1)} %get-tuple-element.20.weights_ref), custom_call_target="tpu_custom_call" | custom-call | bytes 1440000 | tf_op jit(solution)/shard_map/own_slab/pallas_call | solution.py:515
  8.4 0.0 copy-start
  8.4 0.0 collective-permute-done.2.bulk_ref
  8.4 0.8 %other_slab.1.along_ref = f32[4,1152,128]{2,1,0:T(8,128)S(1)} custom-call(s32[17,8,256]{2,1,0:T(8,128)S(1)} %collective-permute-done.2.bulk_ref, f32[8,8,128]{2,1,0:T(8,128)S(1)} %get-tuple-element.17.tables_ref, bf16[384,512]{1,0:T(8,128)(2,1)S(1)} %get-tuple-element.20.weights_ref, f32[4,512,128]{2,1,0:T(8,128)S(1)} %own_slab.1.own_ref), custom_call_target="tpu_custom_call" | custom-call | bytes 2520000 | tf_op jit(solution)/shard_map/other_slab/pallas_call | solution.py:515
  9.2 1.1 %collective-permute-done.1.near_ref = s32[2,8,256]{2,1,0:T(8,128)S(1)} collective-permute-done((s32[2,8,256]{2,1,0:T(8,128)S(1)}, s32[2,8,256]{2,1,0:T(8,128)S(1)}, u32[]{:S(2)}, u32[]{:S(2)}) %collective-permute-start.1) | collective-permute-done | bytes 16416 | tf_op jit(solution)/shard_map/ppermute | solution.py:572
  10.3 0.1 side_columns.1.ends_ref
  10.4 2.7 %collective-permute-start.3 = (s32[2,8,128]{2,1,0:T(8,128)S(1)}, s32[2,8,128]{2,1,0:T(8,128)S(1)}, u32[]{:S(2)}, u32[]{:S(2)}) collective-permute-start(s32[2,8,128]{2,1,0:T(8,128)S(1)} %side_columns.1.ends_ref), channel_id=1, source_target_pairs={{0,1},{2,3},{1,0},{3,2},{4,5},{6,7},{5,4},{7,6},{8,9},{10,11},{9,8... | collective-permute-start | bytes 24584 | tf_op jit(solution)/shard_map/ppermute | solution.py:586
  13.1 0.2 %collective-permute-start.4 = (s32[2,8,128]{2,1,0:T(8,128)S(1)}, s32[2,8,128]{2,1,0:T(8,128)S(1)}, u32[]{:S(2)}, u32[]{:S(2)}) collective-permute-start(s32[2,8,128]{2,1,0:T(8,128)S(1)} %side_columns.1.ends_ref), channel_id=1, source_target_pairs={{1,2},{3,0},{2,1},{0,3},{5,6},{7,4},{6,5},{4,7},{9,10},{11,8},{10,... | collective-permute-start | bytes 24584 | tf_op jit(solution)/shard_map/ppermute | solution.py:587
  13.3 0.0 copy-done
  13.3 1.9 %inner_tiles.1 = (f32[4,32,256]{2,1,0:T(8,128)S(1)}, f32[2,128,128]{2,1,0:T(8,128)S(1)}) custom-call(s32[2]{0:T(128)S(1)} %copy-done, f32[8,8,128]{2,1,0:T(8,128)S(1)} %get-tuple-element.17.tables_ref, bf16[384,512]{1,0:T(8,128)(2,1)S(1)} %get-tuple-element.20.weights_ref, s32[17,8,256]{2,1,0:T(8,128)S(1)} %collective-permute-done.2.bulk_ref, ...), custom_call_target="tpu_custom_call" | custom-call | bytes 7200000 | tf_op jit(solution)/shard_map/inner_tiles/pallas_call | solution.py:515
  15.1 0.0 collective-permute-done.3.beside_ref
  15.1 1.0 %collective-permute-done.4.across_ref = s32[2,8,128]{2,1,0:T(8,128)S(1)} collective-permute-done((s32[2,8,128]{2,1,0:T(8,128)S(1)}, s32[2,8,128]{2,1,0:T(8,128)S(1)}, u32[]{:S(2)}, u32[]{:S(2)}) %collective-permute-start.4) | collective-permute-done | bytes 8224 | tf_op jit(solution)/shard_map/ppermute | solution.py:587
  16.2 2.6 %outer_tiles.1 = f32[4,32,512]{2,1,0:T(8,128)} custom-call(s32[2]{0:T(128)S(1)} %copy-done, f32[8,8,128]{2,1,0:T(8,128)S(1)} %get-tuple-element.17.tables_ref, bf16[384,512]{1,0:T(8,128)(2,1)S(1)} %get-tuple-element.20.weights_ref, s32[2,8,128]{2,1,0:T(8,128)S(1)} %collective-permute-done.3.beside_ref, s32[2,8,128]{2,1,0:T(8,128)S(1)} %collective-permute-done.4.across_ref, ...), custom_call_target="tpu_custom_call" | custom-call | bytes 7200000 | tf_op jit(solution)/shard_map/outer_tiles/pallas_call | solution.py:515
  (1 shorter events, 0.0 us)
Async XLA Ops:
  1.8 6.6 %collective-permute-start.2 = (s32[17,8,256]{2,1,0:T(8,128)S(1)}, s32[17,8,256]{2,1,0:T(8,128)S(1)}, u32[]{:S(2)}, u32[]{:S(2)}) collective-permute-start(s32[17,8,256]{2,1,0:T(8,128)S(1)} %get-tuple-element.26), channel_id=1, source_target_pairs={{0,16},{16,0},{1,17},{17,1},{2,18},{18,2},{3,19},{19,3},{4,20},{20... | collective-permute-start | bytes 417800 | tf_op jit(solution)/shard_map/ppermute | solution.py:559
  2.2 4.6 %collective-permute-start = (s32[2,8,256]{2,1,0:T(8,128)S(1)}, s32[2,8,256]{2,1,0:T(8,128)S(1)}, u32[]{:S(2)}, u32[]{:S(2)}) collective-permute-start(s32[2,8,256]{2,1,0:T(8,128)S(1)} %get-tuple-element.22), channel_id=1, source_target_pairs={{0,16},{16,0},{1,17},{17,1},{2,18},{18,2},{3,19},{19,3},{4,20},{20... | collective-permute-start | bytes 49160 | tf_op jit(solution)/shard_map/ppermute | solution.py:546
  6.8 3.5 %collective-permute-start.1 = (s32[2,8,256]{2,1,0:T(8,128)S(1)}, s32[2,8,256]{2,1,0:T(8,128)S(1)}, u32[]{:S(2)}, u32[]{:S(2)}) collective-permute-start(s32[2,8,256]{2,1,0:T(8,128)S(1)} %diagonal_line.1), channel_id=1, source_target_pairs={{16,4},{17,5},{18,6},{19,7},{20,8},{21,9},{22,10},{23,11},{24,12},... | collective-permute-start | bytes 49160 | tf_op jit(solution)/shard_map/ppermute | solution.py:572
  8.4 4.9 %copy-start = (s32[2]{0:T(128)S(1)}, s32[2]{0:T(128)}, u32[]{:S(2)}) copy-start(s32[2]{0:T(128)} %rank_ref.3) | copy-start | bytes 28
  10.4 4.8 %collective-permute-start.3 = (s32[2,8,128]{2,1,0:T(8,128)S(1)}, s32[2,8,128]{2,1,0:T(8,128)S(1)}, u32[]{:S(2)}, u32[]{:S(2)}) collective-permute-start(s32[2,8,128]{2,1,0:T(8,128)S(1)} %side_columns.1.ends_ref), channel_id=1, source_target_pairs={{0,1},{2,3},{1,0},{3,2},{4,5},{6,7},{5,4},{7,6},{8,9},{10,11},{9,8... | collective-permute-start | bytes 24584 | tf_op jit(solution)/shard_map/ppermute | solution.py:586
  13.1 3.1 %collective-permute-start.4 = (s32[2,8,128]{2,1,0:T(8,128)S(1)}, s32[2,8,128]{2,1,0:T(8,128)S(1)}, u32[]{:S(2)}, u32[]{:S(2)}) collective-permute-start(s32[2,8,128]{2,1,0:T(8,128)S(1)} %side_columns.1.ends_ref), channel_id=1, source_target_pairs={{1,2},{3,0},{2,1},{0,3},{5,6},{7,4},{6,5},{4,7},{9,10},{11,8},{10,... | collective-permute-start | bytes 24584 | tf_op jit(solution)/shard_map/ppermute | solution.py:587

commit v6 on v4

--- a/solution.py
+++ b/solution.py
@@ -156,7 +156,7 @@
 
 def stage_kernel(
     density_ref, bins_ref, colour_ref, extinction_ref,
-    small_ref, mine_ref, columns_ref, dense_ref, index_ref, tables_ref,
+    first_ref, second_ref, columns_ref, dense_ref, index_ref, tables_ref,
 ):
     layers, rows, cols = density_ref.shape
     front = lax.axis_index("bz") == 0
@@ -170,14 +170,12 @@
         top, bottom = [
             pack_words(density_ref[z, r : r + 1, :], bins_ref[z, r : r + 1, :]) for r in (0, rows - 1)
         ]
-        small_ref[0, z : z + 1, :] = jnp.where(front, bottom, top)
-        mine_ref[z : z + 1, :] = jnp.where(front, top, bottom)
+        first_ref[z : z + 1, :] = jnp.where(front, bottom, top)
+        second_ref[z : z + 1, :] = jnp.where(front, top, bottom)
         for tile in range(cols // LANES):
             lanes = slice(tile * LANES, (tile + 1) * LANES)
             dense_ref[z, tile] = density_ref[z, :, lanes]
             index_ref[z, tile] = bins_ref[z, :, lanes]
-    for tile in range(cols // LANES):
-        small_ref[1, :, tile * LANES : (tile + 1) * LANES] = columns_ref[...]
     colour = colour_ref[...].astype(jnp.float32)
     extinction = extinction_ref[...].astype(jnp.float32).reshape(1, 2 * LANES)
     for channel in range(4):
@@ -188,13 +186,14 @@
             )
 
 
-def pack_kernel(dense_ref, index_ref, bulk_ref, inside_ref):
+def pack_kernel(dense_ref, index_ref, columns_ref, bulk_ref, inside_ref):
     layers, tiles, rows = dense_ref.shape[:3]
     half = rows // 2
     front = lax.axis_index("bz") == 0
     start = jnp.where(front, half, 0)
     for tile in range(tiles):
         lanes = slice(tile * LANES, (tile + 1) * LANES)
+        bulk_ref[2 * layers + 1, :, lanes] = columns_ref[...]
         for z in range(layers):
             for part in range(2):
                 at = pl.ds(start + part, half // 2, stride=2)
@@ -209,21 +208,20 @@
             inside_ref[z : z + 1, lanes] = jnp.where(front, line[1], line[0])
 
 
-def diagonal_kernel(mine_ref, other_ref, cells_ref, line_ref):
-    front = lax.axis_index("bz") == 0
-    line_ref[0] = jnp.where(front, mine_ref[...], other_ref[0])
-    line_ref[1] = jnp.where(front, other_ref[0], mine_ref[...])
-
-
-def side_kernel(columns_ref, other_ref, near_ref, along_ref, ends_ref):
+def near_words(slab, first_ref, second_ref):
+    me = lax.axis_index("bz")
+    words = jnp.where(me == slab, first_ref[...], second_ref[...])
+    return jnp.where(has_near(me == 0), words, 0)
+
+
+def side_kernel(columns_ref, bulk_ref, first_ref, second_ref, along_ref, ends_ref):
     layers = columns_ref.shape[0]
     front = lax.axis_index("bz") == 0
-    near_inside = has_near(front)
     lane_at = lax.broadcasted_iota(jnp.int32, (layers, LANES), 1)
     for slab in range(2):
         mine = front if slab == 0 else jnp.logical_not(front)
-        columns = jnp.where(mine, columns_ref[...], other_ref[1, :, 0:LANES])
-        near = jnp.where(near_inside, near_ref[slab], 0)
+        columns = jnp.where(mine, columns_ref[...], bulk_ref[2 * layers + 1, :, 0:LANES])
+        near = near_words(slab, first_ref, second_ref)
         cols = near.shape[1]
         columns = jnp.where(lane_at == 64, near[:, 0:1], columns)
         ends_ref[slab] = jnp.where(lane_at == 65, near[:, cols - 1 : cols], columns)
@@ -320,8 +318,8 @@
     along_columns(cells_ref[...], weights_ref, store)
 
 
-def other_kernel(bulk_ref, tables_ref, weights_ref, own_ref, along_ref, cells_ref):
-    layers = (bulk_ref.shape[0] - 1) // 2
+def other_kernel(bulk_ref, tables_ref, weights_ref, own_ref, ends_ref, along_ref, cells_ref):
+    layers = (bulk_ref.shape[0] - 2) // 2
     cols = bulk_ref.shape[2]
     size = own_ref.shape[1]
     me = lax.axis_index("bz")
@@ -398,7 +396,7 @@
 
 
 def inner_kernel(
-    rank_ref, tables_ref, weights_ref, bulk_ref, inside_ref, near_ref, along_ref, ends_ref,
+    rank_ref, tables_ref, weights_ref, bulk_ref, inside_ref, first_ref, second_ref, along_ref,
     image_ref, edge_ref, cells_ref, lines_ref, mixed_ref,
 ):
     layers, cols = inside_ref.shape
@@ -407,10 +405,9 @@
     me = lax.axis_index("bz")
     front = me == 0
     tables = read_tables(tables_ref)
-    near_inside = has_near(front)
     for slab in range(2):
         inside = jnp.where(me == slab, inside_ref[...], bulk_ref[2 * layers])
-        near = jnp.where(near_inside, near_ref[slab], 0)
+        near = near_words(slab, first_ref, second_ref)
         for side in range(2):
             use_near = front if side == 0 else jnp.logical_not(front)
             words = jnp.where(use_near, near, inside)
@@ -529,12 +526,13 @@
         return route + [(target, source) for source, target in route]
 
     blocks = (layers, cols // LANES, rows, LANES)
-    small, mine, columns, dense, index, tables = call(
+    row = pltpu.VMEM((layers, cols), i32)
+    first, second, columns, dense, index, tables = call(
         stage_kernel,
         "stage_block",
         (
-            pltpu.VMEM((2, layers, cols), i32),
-            pltpu.VMEM((layers, cols), i32),
+            row,
+            row,
             pltpu.VMEM((layers, LANES), i32),
             pltpu.VMEM(blocks, f32),
             pltpu.VMEM(blocks, i32),
@@ -542,43 +540,47 @@
         ),
         1.2,
     )(*[pltpu.with_memory_space_constraint(x, pltpu.HBM) for x in (density, bin_index, tf_colour, tf_extinction)])
-    swap = [(0, 1), (1, 0)]
-    other_small = lax.ppermute(small, "bz", swap)
     bulk, inside = call(
-        pack_kernel,
-        "pack_block",
-        (pltpu.VMEM((2 * layers + 1, 8, cols), i32), pltpu.VMEM((layers, cols), i32)),
-        0.1,
-    )(dense, index)
-    bulk = lax.ppermute(bulk, "bz", swap)
+        pack_kernel, "pack_block", (pltpu.VMEM((2 * layers + 2, 8, cols), i32), row), 0.1
+    )(dense, index, columns)
+
+    def place(z, y, x):
+        return (z * count_y + y) * count_x + x
+
+    steps = range(count_y - 1)
+    ring = [(place(0, y, 0), place(0, y + 1, 0)) for y in steps]
+    ring += [(place(1, y + 1, 0), place(1, y, 0)) for y in steps]
+    ring += [(place(0, count_y - 1, 0), place(1, count_y - 1, 0)), (place(1, 0, 0), place(0, 0, 0))]
+    ring = [(source + x, target + x) for source, target in ring for x in range(count_x)]
+    diagonal = [(place(1, y, x), place(0, y + 1, x)) for y in steps for x in range(count_x)]
+    for z, y in ((0, 0), (1, count_y - 1)):
+        diagonal += [(place(z, y, x), place(z, y, x + 1)) for x in range(0, count_x, 2)]
+    axes = ("bz", "by", "bx")
+    bulk = lax.ppermute(bulk, "bz", [(0, 1), (1, 0)])
+    first = lax.ppermute(first, axes, ring)
+    second = lax.ppermute(second, axes, both(diagonal))
+
     cells, weights = call(
         cells_kernel,
         "own_cells",
         (pltpu.VMEM((size, cols), bf16), pltpu.VMEM((cols + LANES, 2 * cols), bf16)),
         0.5,
     )(dense, index, tables)
-
-    line = call(diagonal_kernel, "diagonal_line", pltpu.VMEM((2, layers, cols), i32), 0.1)(
-        mine, other_small, cells
-    )
-    route = [(count_y + y, y + 1) for y in range(count_y - 1)]
-    alone = [(0, 0), (2 * count_y - 1, 2 * count_y - 1)]
-    near = lax.ppermute(line, ("bz", "by"), both(route) + alone)
     along = call(own_kernel, "own_slab", pltpu.VMEM((tiles, size, LANES), f32), 0.4)(cells, weights)
-    along = call(
-        other_kernel,
-        "other_slab",
-        pltpu.VMEM((tiles, 2 * size + 2 * 4 * half, LANES), f32),
-        0.7,
-        [pltpu.VMEM((size, cols), bf16)],
-    )(bulk, tables, weights, along)
     ends = call(side_kernel, "side_columns", pltpu.VMEM((2, layers, LANES), i32), 0.1)(
-        columns, other_small, near, along
+        columns, bulk, first, second, along
     )
     pairs = [(x, x + 1) for x in range(0, count_x, 2)]
     cross = [(x, (x + 1) % count_x) for x in range(1, count_x, 2)]
     beside = lax.ppermute(ends, "bx", both(pairs))
     across = lax.ppermute(ends, "bx", both(cross))
+    along = call(
+        other_kernel,
+        "other_slab",
+        pltpu.VMEM((tiles, 2 * size + 2 * 4 * half, LANES), f32),
+        0.8,
+        [pltpu.VMEM((size, cols), bf16)],
+    )(bulk, tables, weights, along, ends)
     smem = pl.BlockSpec(memory_space=pltpu.SMEM)
     lines = pltpu.VMEM((2, 2, 4, 2, 2 * layers, LANES), f32)
     image, edge = call(
@@ -588,7 +590,7 @@
         2.0,
         [pltpu.VMEM((16 * layers, cols), f32), lines, pltpu.VMEM((4, rows, LANES), f32)],
         [smem] + [VMEM] * 7,
-    )(slab_rank, tables, weights, bulk, inside, near, along, ends)
+    )(slab_rank, tables, weights, bulk, inside, first, second, along)
     return call(
         outer_kernel,
         "outer_tiles",

time: 20.2 us -> 16.4 us (0.81)
  the two profiles are of different devices: /device:TPU:9 before, /device:TPU:17 now
where the time goes in v6:
time: 16.4 us; the launch traced here: 16.3 us
  Pallas kernels  7.47 us (46%)
  starting transfers between devices  6.17 us (38%)
  waiting for transfers between devices  2.56 us (16%)
    pallas_call x8, Pallas kernels, run(): pl.pallas_call(kernel, out_shape=out_shape, in_specs=in_specs or [VMEM] *...  7.47 us
    ppermute x1, starting transfers between devices, two_slab_device(): beside = lax.ppermute(ends, 'bx', both(pairs))  2.39 us
    ppermute x1, waiting for transfers between devices, two_slab_device(): second = lax.ppermute(second, axes, both(diagonal))  1.9 us
    ppermute x1, starting transfers between devices, two_slab_device(): first = lax.ppermute(first, axes, ring)  1.3 us
    ppermute x1, starting transfers between devices, two_slab_device(): bulk = lax.ppermute(bulk, 'bz', [(0, 1), (1, 0)])  1.27 us
    ppermute x1, starting transfers between devices, two_slab_device(): across = lax.ppermute(ends, 'bx', both(cross))  1.2 us
    ppermute x1, waiting for transfers between devices, two_slab_device(): first = lax.ppermute(first, axes, ring)  0.65 us
  transfers between devices with their start and end apart: 5, of which 2 were waited for; matrix products, arithmetic and copies ran while one was open for 0% of the time, Pallas kernels for 21%

profile of v6, /device:TPU:17, one launch (start us, length us, event | category | flops | bytes accessed | tf_op | source)
XLA Modules:
  0.0 16.3 jit_solution(17154847772341801490)
XLA Ops:
  0.0 1.2 %stage_block.1 = (s32[8,256]{1,0:T(8,128)S(1)}, s32[8,256]{1,0:T(8,128)S(1)}, s32[8,128]{1,0:T(8,128)S(1)}, f32[8,2,32,128]{3,2,1,0:T(8,128)S(1)}, s32[8,2,32,12...) custom-call(f32[8,32,256]{2,1,0:T(8,128)} %density_ref.1, s32[8,32,256]{2,1,0:T(8,128)} %bins_ref.1, ...), custom_call_target="tpu_custom_call" | custom-call | bytes 4320000 | tf_op jit(solution)/shard_map/stage_block/pallas_call | solution.py:512
  1.2 0.1 pack_block.1
  1.3 1.3 %collective-permute-start = (s32[18,8,256]{2,1,0:T(8,128)S(1)}, s32[18,8,256]{2,1,0:T(8,128)S(1)}, u32[]{:S(2)}, u32[]{:S(2)}) collective-permute-start(s32[18,8,256]{2,1,0:T(8,128)S(1)} %get-tuple-element.22), channel_id=1, source_target_pairs={{0,16},{16,0},{1,17},{17,1},{2,18},{18,2},{3,19},{19,3},{4,20},{20... | collective-permute-start | bytes 442376 | tf_op jit(solution)/shard_map/ppermute | solution.py:559
  2.6 1.3 %collective-permute-start.1 = (s32[8,256]{1,0:T(8,128)S(1)}, s32[8,256]{1,0:T(8,128)S(1)}, u32[]{:S(2)}, u32[]{:S(2)}) collective-permute-start(s32[8,256]{1,0:T(8,128)S(1)} %get-tuple-element.23), channel_id=1, source_target_pairs={{0,4},{1,5},{2,6},{3,7},{4,8},{5,9},{6,10},{7,11},{8,12},{9,13},{1... | collective-permute-start | bytes 24584 | tf_op jit(solution)/shard_map/ppermute | solution.py:560
  3.9 0.0 collective-permute-start.2
  3.9 0.5 %own_cells.1 = (bf16[512,256]{1,0:T(8,128)(2,1)S(1)}, bf16[384,512]{1,0:T(8,128)(2,1)S(1)}) custom-call(f32[8,2,32,128]{3,2,1,0:T(8,128)S(1)} %get-tuple-element.18.dense_ref, s32[8,2,32,128]{3,2,1,0:T(8,128)S(1)} %get-tuple-element.19.index_ref, f32[8,8,128]{2,1,0:T(8,128)S(1)} %get-tuple-element.17.tables_ref), custom_call_target="tpu_custom_call" | custom-call | bytes 1800000 | tf_op jit(solution)/shard_map/own_cells/pallas_call | solution.py:512
  4.4 0.3 %own_slab.1.along_ref.own_ref = f32[4,512,128]{2,1,0:T(8,128)S(1)} custom-call(bf16[512,256]{1,0:T(8,128)(2,1)S(1)} %get-tuple-element.25.cells_ref, bf16[384,512]{1,0:T(8,128)(2,1)S(1)} %get-tuple-element.20.weights_ref), custom_call_target="tpu_custom_call" | custom-call | bytes 1440000 | tf_op jit(solution)/shard_map/own_slab/pallas_call | solution.py:512
  4.7 0.0 copy-start
  4.7 0.6 %collective-permute-done.1.first_ref = s32[8,256]{1,0:T(8,128)S(1)} collective-permute-done((s32[8,256]{1,0:T(8,128)S(1)}, s32[8,256]{1,0:T(8,128)S(1)}, u32[]{:S(2)}, u32[]{:S(2)}) %collective-permute-start.1) | collective-permute-done | bytes 8224 | tf_op jit(solution)/shard_map/ppermute | solution.py:560
  5.4 1.9 %collective-permute-done.2.second_ref = s32[8,256]{1,0:T(8,128)S(1)} collective-permute-done((s32[8,256]{1,0:T(8,128)S(1)}, s32[8,256]{1,0:T(8,128)S(1)}, u32[]{:S(2)}, u32[]{:S(2)}) %collective-permute-start.2) | collective-permute-done | bytes 8224 | tf_op jit(solution)/shard_map/ppermute | solution.py:561
  7.3 0.0 collective-permute-done.bulk_ref
  7.3 0.1 side_columns.1.ends_ref
  7.3 2.4 %collective-permute-start.3 = (s32[2,8,128]{2,1,0:T(8,128)S(1)}, s32[2,8,128]{2,1,0:T(8,128)S(1)}, u32[]{:S(2)}, u32[]{:S(2)}) collective-permute-start(s32[2,8,128]{2,1,0:T(8,128)S(1)} %side_columns.1.ends_ref), channel_id=1, source_target_pairs={{0,1},{2,3},{1,0},{3,2},{4,5},{6,7},{5,4},{7,6},{8,9},{10,11},{9,8... | collective-permute-start | bytes 24584 | tf_op jit(solution)/shard_map/ppermute | solution.py:575
  9.7 1.2 %collective-permute-start.4 = (s32[2,8,128]{2,1,0:T(8,128)S(1)}, s32[2,8,128]{2,1,0:T(8,128)S(1)}, u32[]{:S(2)}, u32[]{:S(2)}) collective-permute-start(s32[2,8,128]{2,1,0:T(8,128)S(1)} %side_columns.1.ends_ref), channel_id=1, source_target_pairs={{1,2},{3,0},{2,1},{0,3},{5,6},{7,4},{6,5},{4,7},{9,10},{11,8},{10,... | collective-permute-start | bytes 24584 | tf_op jit(solution)/shard_map/ppermute | solution.py:576
  10.9 0.8 %other_slab.1.along_ref = f32[4,1152,128]{2,1,0:T(8,128)S(1)} custom-call(s32[18,8,256]{2,1,0:T(8,128)S(1)} %collective-permute-done.bulk_ref, f32[8,8,128]{2,1,0:T(8,128)S(1)} %get-tuple-element.17.tables_ref, bf16[384,512]{1,0:T(8,128)(2,1)S(1)} %get-tuple-element.20.weights_ref, f32[4,512,128]{2,1,0:T(8,128)S(1)} %own_slab.1.along_ref.own_ref, ...), custom_call_target="tpu_custom_call" | custom-call | bytes 2880000 | tf_op jit(solution)/shard_map/other_slab/pallas_call | solution.py:512
  11.7 0.0 copy-done
  11.8 1.9 %inner_tiles.1 = (f32[4,32,256]{2,1,0:T(8,128)S(1)}, f32[2,128,128]{2,1,0:T(8,128)S(1)}) custom-call(s32[2]{0:T(128)S(1)} %copy-done, f32[8,8,128]{2,1,0:T(8,128)S(1)} %get-tuple-element.17.tables_ref, bf16[384,512]{1,0:T(8,128)(2,1)S(1)} %get-tuple-element.20.weights_ref, s32[18,8,256]{2,1,0:T(8,128)S(1)} %collective-permute-done.bulk_ref, ...), custom_call_target="tpu_custom_call" | custom-call | bytes 7200000 | tf_op jit(solution)/shard_map/inner_tiles/pallas_call | solution.py:512
  13.6 0.0 collective-permute-done.3.beside_ref
  13.6 0.0 collective-permute-done.4.across_ref
  13.6 2.6 %outer_tiles.1 = f32[4,32,512]{2,1,0:T(8,128)} custom-call(s32[2]{0:T(128)S(1)} %copy-done, f32[8,8,128]{2,1,0:T(8,128)S(1)} %get-tuple-element.17.tables_ref, bf16[384,512]{1,0:T(8,128)(2,1)S(1)} %get-tuple-element.20.weights_ref, s32[2,8,128]{2,1,0:T(8,128)S(1)} %collective-permute-done.3.beside_ref, s32[2,8,128]{2,1,0:T(8,128)S(1)} %collective-permute-done.4.across_ref, ...), custom_call_target="tpu_custom_call" | custom-call | bytes 7200000 | tf_op jit(solution)/shard_map/outer_tiles/pallas_call | solution.py:512
Async XLA Ops:
  1.3 6.0 %collective-permute-start = (s32[18,8,256]{2,1,0:T(8,128)S(1)}, s32[18,8,256]{2,1,0:T(8,128)S(1)}, u32[]{:S(2)}, u32[]{:S(2)}) collective-permute-start(s32[18,8,256]{2,1,0:T(8,128)S(1)} %get-tuple-element.22), channel_id=1, source_target_pairs={{0,16},{16,0},{1,17},{17,1},{2,18},{18,2},{3,19},{19,3},{4,20},{20... | collective-permute-start | bytes 442376 | tf_op jit(solution)/shard_map/ppermute | solution.py:559
  2.6 2.8 %collective-permute-start.1 = (s32[8,256]{1,0:T(8,128)S(1)}, s32[8,256]{1,0:T(8,128)S(1)}, u32[]{:S(2)}, u32[]{:S(2)}) collective-permute-start(s32[8,256]{1,0:T(8,128)S(1)} %get-tuple-element.23), channel_id=1, source_target_pairs={{0,4},{1,5},{2,6},{3,7},{4,8},{5,9},{6,10},{7,11},{8,12},{9,13},{1... | collective-permute-start | bytes 24584 | tf_op jit(solution)/shard_map/ppermute | solution.py:560
  3.9 3.4 %collective-permute-start.2 = (s32[8,256]{1,0:T(8,128)S(1)}, s32[8,256]{1,0:T(8,128)S(1)}, u32[]{:S(2)}, u32[]{:S(2)}) collective-permute-start(s32[8,256]{1,0:T(8,128)S(1)} %get-tuple-element.24), channel_id=1, source_target_pairs={{16,4},{17,5},{18,6},{19,7},{20,8},{21,9},{22,10},{23,11},{24,12},... | collective-permute-start | bytes 24584 | tf_op jit(solution)/shard_map/ppermute | solution.py:561
  4.7 7.0 %copy-start = (s32[2]{0:T(128)S(1)}, s32[2]{0:T(128)}, u32[]{:S(2)}) copy-start(s32[2]{0:T(128)} %rank_ref.3) | copy-start | bytes 28
  7.3 6.3 %collective-permute-start.3 = (s32[2,8,128]{2,1,0:T(8,128)S(1)}, s32[2,8,128]{2,1,0:T(8,128)S(1)}, u32[]{:S(2)}, u32[]{:S(2)}) collective-permute-start(s32[2,8,128]{2,1,0:T(8,128)S(1)} %side_columns.1.ends_ref), channel_id=1, source_target_pairs={{0,1},{2,3},{1,0},{3,2},{4,5},{6,7},{5,4},{7,6},{8,9},{10,11},{9,8... | collective-permute-start | bytes 24584 | tf_op jit(solution)/shard_map/ppermute | solution.py:575
  9.7 3.9 %collective-permute-start.4 = (s32[2,8,128]{2,1,0:T(8,128)S(1)}, s32[2,8,128]{2,1,0:T(8,128)S(1)}, u32[]{:S(2)}, u32[]{:S(2)}) collective-permute-start(s32[2,8,128]{2,1,0:T(8,128)S(1)} %side_columns.1.ends_ref), channel_id=1, source_target_pairs={{1,2},{3,0},{2,1},{0,3},{5,6},{7,4},{6,5},{4,7},{9,10},{11,8},{10,... | collective-permute-start | bytes 24584 | tf_op jit(solution)/shard_map/ppermute | solution.py:576

commit v7 on v6

--- a/solution.py
+++ b/solution.py
@@ -1,3 +1,5 @@
+import functools
+
 import jax
 import jax.numpy as jnp
 from jax import lax
@@ -150,7 +152,7 @@
 
 def cost(microseconds):
     return pl.CostEstimate(
-        flops=0, bytes_accessed=int(3.6e6 * microseconds), transcendentals=0
+        flops=int(1e9 * microseconds), bytes_accessed=int(3.6e6 * microseconds), transcendentals=0
     )
 
 
@@ -186,14 +188,13 @@
             )
 
 
-def pack_kernel(dense_ref, index_ref, columns_ref, bulk_ref, inside_ref):
+def pack_kernel(dense_ref, index_ref, bulk_ref, inside_ref):
     layers, tiles, rows = dense_ref.shape[:3]
     half = rows // 2
     front = lax.axis_index("bz") == 0
     start = jnp.where(front, half, 0)
     for tile in range(tiles):
         lanes = slice(tile * LANES, (tile + 1) * LANES)
-        bulk_ref[2 * layers + 1, :, lanes] = columns_ref[...]
         for z in range(layers):
             for part in range(2):
                 at = pl.ds(start + part, half // 2, stride=2)
@@ -214,13 +215,13 @@
     return jnp.where(has_near(me == 0), words, 0)
 
 
-def side_kernel(columns_ref, bulk_ref, first_ref, second_ref, along_ref, ends_ref):
+def side_kernel(columns_ref, other_ref, first_ref, second_ref, ends_ref):
     layers = columns_ref.shape[0]
     front = lax.axis_index("bz") == 0
     lane_at = lax.broadcasted_iota(jnp.int32, (layers, LANES), 1)
     for slab in range(2):
         mine = front if slab == 0 else jnp.logical_not(front)
-        columns = jnp.where(mine, columns_ref[...], bulk_ref[2 * layers + 1, :, 0:LANES])
+        columns = jnp.where(mine, columns_ref[...], other_ref[...])
         near = near_words(slab, first_ref, second_ref)
         cols = near.shape[1]
         columns = jnp.where(lane_at == 64, near[:, 0:1], columns)
@@ -268,64 +269,98 @@
                 cells_ref[base : base + 16, tile * LANES : (tile + 1) * LANES] = block.astype(jnp.bfloat16)
 
 
-def classify_halo(words, tables, ends_ref, values_ref, rows, base):
-    layers = words.shape[0]
-    start = lax.axis_index("bz") * (rows // 2)
-    side_lane, has_side, sub_at = lane_maps(rows)
-    halo = cell_values(*unpack_words(words), tables, float(2 * layers))
-    for channel in range(4):
-        values_ref[channel, 0:layers] = halo[channel]
-    masks = [has_side & (side_lane == start + 2 * sub_at + part) for part in range(2)]
-    for z in range(layers):
-        for channel in range(4):
-            line = jnp.broadcast_to(values_ref[channel, z : z + 1, :], (8, LANES))
-            block = jnp.concatenate([jnp.where(mask, line, 0.0) for mask in masks], axis=0)
-            at = base + (z * 4 + channel) * 16
-            ends_ref[at : at + 16, :] = block.astype(jnp.bfloat16)
-    return halo
-
-
 def rounded(value):
     return value.astype(jnp.bfloat16).astype(jnp.float32)
 
 
-def along_columns(cells, weights_ref, store):
+def cells_kernel(dense_ref, index_ref, tables_ref, cells_ref, weights_ref):
+    layers, tiles, rows = dense_ref.shape[:3]
+    half = rows // 2
+    start = lax.axis_index("bz") * half
+    fill_weights(weights_ref, rows)
+
+    def read_cells(z, part, tile):
+        at = pl.ds(start + part, half // 2, stride=2)
+        return dense_ref[z, tile, at, :], index_ref[z, tile, at, :]
+
+    classify_rows(read_cells, read_tables(tables_ref), cells_ref, layers, tiles)
+
+
+def halo_kernel(
+    rows, beside_ref, across_ref, tables_ref, weights_ref, added_ref, ends_ref, values_ref, keep_ref
+):
+    layers = beside_ref.shape[1]
+    cols = weights_ref.shape[0] - LANES
+    size = layers * 64
+    depth = 2 * layers
+    front = lax.axis_index("bz") == 0
+    start = lax.axis_index("bz") * (rows // 2)
+    me_x = lax.axis_index("bx")
+    even_x = lax.rem(me_x, 2) == 0
+    tables = read_tables(tables_ref)
+    side_lane, has_side, sub_at = lane_maps(rows)
+    masks = [has_side & (side_lane == start + 2 * sub_at + part) for part in range(2)]
+    lane_at = lax.broadcasted_iota(jnp.int32, (layers, LANES), 1)
+    is_right = (lane_at < rows) | (lane_at == 64)
+    for slab in range(2):
+        right = jnp.where(even_x, beside_ref[slab], across_ref[slab])
+        left = jnp.where(even_x, across_ref[slab], beside_ref[slab])
+        right = jnp.where(me_x + 1 < lax.axis_size("bx"), right, 0)
+        left = jnp.where(me_x > 0, left, 0)
+        words = jnp.where(is_right, right, left)
+        values = cell_values(*unpack_words(words), tables, float(depth))
+        for channel in range(4):
+            values_ref[channel] = values[channel]
+        for z in range(layers):
+            for channel in range(4):
+                line = jnp.broadcast_to(values_ref[channel, z : z + 1, :], (8, LANES))
+                block = jnp.concatenate([jnp.where(mask, line, 0.0) for mask in masks], axis=0)
+                at = slab * size + (z * 4 + channel) * 16
+                ends_ref[at : at + 16, :] = block.astype(jnp.bfloat16)
+        for side in range(2):
+            row = jnp.where(front, 64, rows // 2 - 1) if side == 0 else jnp.where(front, rows // 2, 64)
+            twin = jnp.where(row == 64, 65, row + rows)
+            keep = (lane_at == row) | (lane_at == twin)
+            for channel in range(4):
+                at = pl.ds(slab * layers * 8 + side * 4 + channel, layers, stride=8)
+                keep_ref[at, :] = jnp.where(keep, values[channel], 0.0)
+    ends_ref[2 * size :, :] = keep_ref[...].astype(jnp.bfloat16)
+    added = jnp.dot(
+        ends_ref[...], weights_ref[cols : cols + LANES, 0 : 2 * LANES], preferred_element_type=jnp.float32
+    )
+    for index in range(2):
+        added_ref[index] = added[:, index * LANES : (index + 1) * LANES]
+
+
+def along_columns(cells, weights_ref, added, store):
     cols = cells.shape[1]
     tiles = 2 * cols // LANES
     result = jnp.dot(cells, weights_ref[0:cols, :], preferred_element_type=jnp.float32)
     for tile in range(tiles):
         block = result[:, tile * LANES : (tile + 1) * LANES]
-        store(tile, block if tile in (0, tiles - 1) else rounded(block))
-
-
-def cells_kernel(dense_ref, index_ref, tables_ref, cells_ref, weights_ref):
-    layers, tiles, rows = dense_ref.shape[:3]
-    half = rows // 2
-    start = lax.axis_index("bz") * half
-    fill_weights(weights_ref, rows)
-
-    def read_cells(z, part, tile):
-        at = pl.ds(start + part, half // 2, stride=2)
-        return dense_ref[z, tile, at, :], index_ref[z, tile, at, :]
-
-    classify_rows(read_cells, read_tables(tables_ref), cells_ref, layers, tiles)
-
-
-def own_kernel(cells_ref, weights_ref, along_ref):
+        if tile in (0, tiles - 1):
+            block = block + added(0 if tile == 0 else 1)
+        store(tile, rounded(block))
+
+
+def own_kernel(cells_ref, weights_ref, added_ref, along_ref):
+    size = cells_ref.shape[0]
+    mine = pl.multiple_of(lax.axis_index("bz") * size, size)
+
     def store(tile, block):
         along_ref[tile] = block
 
-    along_columns(cells_ref[...], weights_ref, store)
-
-
-def other_kernel(bulk_ref, tables_ref, weights_ref, own_ref, ends_ref, along_ref, cells_ref):
-    layers = (bulk_ref.shape[0] - 2) // 2
+    along_columns(cells_ref[...], weights_ref, lambda i: added_ref[i, pl.ds(mine, size), :], store)
+
+
+def other_kernel(bulk_ref, tables_ref, weights_ref, added_ref, own_ref, along_ref, cells_ref):
+    layers = (bulk_ref.shape[0] - 1) // 2
     cols = bulk_ref.shape[2]
     size = own_ref.shape[1]
     me = lax.axis_index("bz")
     pad = size // layers
     mine = pl.multiple_of(pad + me * size, pad)
-    theirs = pl.multiple_of(pad + (1 - me) * size, pad)
+    theirs = pl.multiple_of((1 - me) * size, pad)
     for tile in range(own_ref.shape[0]):
         along_ref[tile, 0:pad, :] = jnp.zeros((pad, LANES), jnp.float32)
         along_ref[tile, pad + 2 * size : 2 * pad + 2 * size, :] = jnp.zeros((pad, LANES), jnp.float32)
@@ -335,23 +370,10 @@
         return unpack_words(bulk_ref[2 * z + part, :, tile * LANES : (tile + 1) * LANES])
 
     def store(tile, block):
-        along_ref[tile, pl.ds(theirs, size), :] = block
+        along_ref[tile, pl.ds(theirs + pad, size), :] = block
 
     classify_rows(read_cells, read_tables(tables_ref), cells_ref, layers, cols // LANES)
-    along_columns(cells_ref[...], weights_ref, store)
-
-
-def edge_lines(edge, tile, lines_ref, depth):
-    layer_at = lax.broadcasted_iota(jnp.int32, (depth, LANES), 0)
-    for side in range(2):
-        for channel in range(4):
-            base = (side * 4 + channel) * depth
-            now = edge[base : base + depth]
-            triple = 3.0 * now
-            before = jnp.where(layer_at == 0, 0.0, pltpu.roll(now, 1, 0))
-            after = jnp.where(layer_at == depth - 1, 0.0, pltpu.roll(now, depth - 1, 0))
-            for parity, beside in enumerate((before, after)):
-                lines_ref[tile, side, channel, parity] = rounded(beside + triple)
+    along_columns(cells_ref[...], weights_ref, lambda i: added_ref[i, pl.ds(theirs, size), :], store)
 
 
 def render_tile(tile, along_ref, lines_ref, flip, layers):
@@ -369,13 +391,14 @@
         for parity in range(2):
             clear = [1.0 - value for value in image[3]]
             updated = []
+            line = (layer * 2 + parity) * 8
             for channel in range(4):
                 beside = layer_rows(layer + 2 * parity, channel)
                 even, odd = [rounded(beside[part] + triple[channel][part]) for part in range(2)]
-                above = lines_ref[tile, 0, channel, parity, pl.ds(layer, 1), :]
-                below = lines_ref[tile, 1, channel, parity, pl.ds(layer, 1), :]
-                before_even = jnp.where(top, jnp.broadcast_to(above, (8, LANES)), pltpu.roll(odd, 1, 0))
-                after_odd = jnp.where(bottom, jnp.broadcast_to(below, (8, LANES)), pltpu.roll(even, 7, 0))
+                above = lines_ref[tile, pl.ds(line + channel, 8, stride=0), :]
+                below = lines_ref[tile, pl.ds(line + 4 + channel, 8, stride=0), :]
+                before_even = jnp.where(top, above, pltpu.roll(odd, 1, 0))
+                after_odd = jnp.where(bottom, below, pltpu.roll(even, 7, 0))
                 even_centre = 3.0 * even
                 odd_centre = 3.0 * odd
                 samples = [
@@ -395,13 +418,14 @@
     return lax.fori_loop(0, 2, one_slab, [[zero] * 4 for _ in range(4)])
 
 
-def inner_kernel(
-    rank_ref, tables_ref, weights_ref, bulk_ref, inside_ref, first_ref, second_ref, along_ref,
-    image_ref, edge_ref, cells_ref, lines_ref, mixed_ref,
+def render_kernel(
+    rank_ref, tables_ref, weights_ref, bulk_ref, inside_ref, first_ref, second_ref, added_ref, along_ref,
+    out_ref, cells_ref, lines_ref, mixed_ref,
 ):
     layers, cols = inside_ref.shape
     depth = 2 * layers
     tiles = 2 * cols // LANES
+    size = layers * 64
     me = lax.axis_index("bz")
     front = me == 0
     tables = read_tables(tables_ref)
@@ -412,91 +436,44 @@
             use_near = front if side == 0 else jnp.logical_not(front)
             words = jnp.where(use_near, near, inside)
             for t in range(cols // LANES):
-                lanes = slice(t * LANES, (t + 1) * LANES)
-                values = cell_values(*unpack_words(words[:, lanes]), tables, float(depth))
+                values = cell_values(
+                    *unpack_words(words[:, t * LANES : (t + 1) * LANES]), tables, float(depth)
+                )
                 for channel in range(4):
-                    base = (side * 4 + channel) * depth + slab * layers
-                    cells_ref[base : base + layers, lanes] = values[channel]
-    edge = jnp.dot(
-        cells_ref[...].astype(jnp.bfloat16), weights_ref[0:cols, :], preferred_element_type=jnp.float32
+                    at = pl.ds(slab * layers * 8 + side * 4 + channel, layers, stride=8)
+                    cells_ref[t, at, :] = values[channel]
+    edge = sum(
+        jnp.dot(
+            cells_ref[t].astype(jnp.bfloat16),
+            weights_ref[t * LANES : (t + 1) * LANES, :],
+            preferred_element_type=jnp.float32,
+        )
+        for t in range(cols // LANES)
     )
     for tile in range(tiles):
-        block = edge[:, tile * LANES : (tile + 1) * LANES]
+        now = edge[:, tile * LANES : (tile + 1) * LANES]
         if tile in (0, tiles - 1):
-            edge_ref[0 if tile == 0 else 1] = block
-        else:
-            edge_lines(rounded(block), tile - 1, lines_ref, depth)
-
-    def one_tile(index, carry):
-        image = render_tile(index, along_ref.at[1 : tiles - 1], lines_ref, rank_ref[0], layers)
-        lanes = pl.ds(pl.multiple_of(index * LANES, LANES), LANES)
-        for channel in range(4):
-            for i in range(4):
-                mixed_ref[channel, pl.ds(i, 8, stride=4), :] = image[channel][i]
-            image_ref[channel, :, lanes] = mixed_ref[channel]
-        return carry
-
-    lax.fori_loop(0, tiles - 2, one_tile, 0)
-
-
-def outer_kernel(
-    rank_ref, tables_ref, weights_ref, beside_ref, across_ref, along_ref, edge_ref, image_ref,
-    out_ref, ends_ref, values_ref, fixed_ref, lines_ref, mixed_ref,
-):
-    rows = out_ref.shape[1]
-    cols = out_ref.shape[2] // 2
-    layers = beside_ref.shape[1]
-    depth = 2 * layers
-    tiles = 2 * cols // LANES
-    size = layers * 64
-    pad = 64
-    front = lax.axis_index("bz") == 0
-    me_x = lax.axis_index("bx")
-    even_x = lax.rem(me_x, 2) == 0
-    tables = read_tables(tables_ref)
-    lane_at = lax.broadcasted_iota(jnp.int32, (layers, LANES), 1)
-    is_right = (lane_at < rows) | (lane_at == 64)
-    for slab in range(2):
-        right = jnp.where(even_x, beside_ref[slab], across_ref[slab])
-        left = jnp.where(even_x, across_ref[slab], beside_ref[slab])
-        right = jnp.where(me_x + 1 < lax.axis_size("bx"), right, 0)
-        left = jnp.where(me_x > 0, left, 0)
-        halo = jnp.where(is_right, right, left)
-        values = classify_halo(halo, tables, ends_ref, values_ref, rows, slab * size)
-        for side in range(2):
-            row = jnp.where(front, 64, rows // 2 - 1) if side == 0 else jnp.where(front, rows // 2, 64)
-            twin = jnp.where(row == 64, 65, row + rows)
-            keep = (lane_at == row) | (lane_at == twin)
-            for channel in range(4):
-                values_ref[4 + side * 4 + channel, slab * layers : (slab + 1) * layers] = jnp.where(
-                    keep, values[channel], 0.0
-                )
-    for line in range(8):
-        base = 2 * size + line * depth
-        ends_ref[base : base + depth, :] = values_ref[4 + line].astype(jnp.bfloat16)
-    added = jnp.dot(
-        ends_ref[...], weights_ref[cols : cols + LANES, 0 : 2 * LANES], preferred_element_type=jnp.float32
-    )
-    for index, tile in enumerate((0, tiles - 1)):
-        block = added[:, index * LANES : (index + 1) * LANES]
-        fixed_ref[index, 0:pad, :] = jnp.zeros((pad, LANES), jnp.float32)
-        fixed_ref[index, pad + 2 * size :, :] = jnp.zeros((pad, LANES), jnp.float32)
-        fixed_ref[index, pad : pad + 2 * size, :] = rounded(
-            along_ref[tile, pad : pad + 2 * size, :] + block[0 : 2 * size]
-        )
-        edge_lines(rounded(edge_ref[index] + block[2 * size :]), index, lines_ref, depth)
-    out_ref[:, :, LANES : 2 * cols - LANES] = image_ref[...]
-
-    def one_tile(index, carry):
-        image = render_tile(index, fixed_ref, lines_ref, rank_ref[0], layers)
-        lanes = pl.ds(pl.multiple_of(index * (2 * cols - LANES), LANES), LANES)
+            now = now + added_ref[0 if tile == 0 else 1, 2 * size : 2 * size + 8 * depth, :]
+        now = rounded(now)
+        triple = 3.0 * now
+        empty = jnp.zeros((8, LANES), jnp.float32)
+        for layer in range(depth):
+            here = triple[layer * 8 : layer * 8 + 8]
+            before = now[layer * 8 - 8 : layer * 8] if layer > 0 else empty
+            after = now[layer * 8 + 8 : layer * 8 + 16] if layer + 1 < depth else empty
+            lines_ref[tile, layer * 16 : layer * 16 + 8, :] = rounded(before + here)
+            lines_ref[tile, layer * 16 + 8 : layer * 16 + 16, :] = rounded(after + here)
+
+    def one_tile(tile, carry):
+        image = render_tile(tile, along_ref, lines_ref, rank_ref[0], layers)
+        lanes = pl.ds(pl.multiple_of(tile * LANES, LANES), LANES)
         for channel in range(4):
             for i in range(4):
                 mixed_ref[channel, pl.ds(i, 8, stride=4), :] = image[channel][i]
             out_ref[channel, :, lanes] = mixed_ref[channel]
         return carry
 
-    lax.fori_loop(0, 2, one_tile, 0)
+    lax.fori_loop(0, tiles, one_tile, 0)
 
 
 def two_slab_device(density, bin_index, tf_colour, tf_extinction, slab_rank):
@@ -540,10 +517,6 @@
         ),
         1.2,
     )(*[pltpu.with_memory_space_constraint(x, pltpu.HBM) for x in (density, bin_index, tf_colour, tf_extinction)])
-    bulk, inside = call(
-        pack_kernel, "pack_block", (pltpu.VMEM((2 * layers + 2, 8, cols), i32), row), 0.1
-    )(dense, index, columns)
-
     def place(z, y, x):
         return (z * count_y + y) * count_x + x
 
@@ -556,9 +529,14 @@
     for z, y in ((0, 0), (1, count_y - 1)):
         diagonal += [(place(z, y, x), place(z, y, x + 1)) for x in range(0, count_x, 2)]
     axes = ("bz", "by", "bx")
-    bulk = lax.ppermute(bulk, "bz", [(0, 1), (1, 0)])
+    swap = [(0, 1), (1, 0)]
+    second = lax.ppermute(second, axes, both(diagonal))
+    other_columns = lax.ppermute(columns, "bz", swap)
+    bulk, inside = call(pack_kernel, "pack_block", (pltpu.VMEM((2 * layers + 1, 8, cols), i32), row), 0.1)(
+        dense, index
+    )
+    bulk = lax.ppermute(bulk, "bz", swap)
     first = lax.ppermute(first, axes, ring)
-    second = lax.ppermute(second, axes, both(diagonal))
 
     cells, weights = call(
         cells_kernel,
@@ -566,45 +544,44 @@
         (pltpu.VMEM((size, cols), bf16), pltpu.VMEM((cols + LANES, 2 * cols), bf16)),
         0.5,
     )(dense, index, tables)
-    along = call(own_kernel, "own_slab", pltpu.VMEM((tiles, size, LANES), f32), 0.4)(cells, weights)
     ends = call(side_kernel, "side_columns", pltpu.VMEM((2, layers, LANES), i32), 0.1)(
-        columns, bulk, first, second, along
+        columns, other_columns, first, second
     )
     pairs = [(x, x + 1) for x in range(0, count_x, 2)]
     cross = [(x, (x + 1) % count_x) for x in range(1, count_x, 2)]
     beside = lax.ppermute(ends, "bx", both(pairs))
     across = lax.ppermute(ends, "bx", both(cross))
+    added = call(
+        functools.partial(halo_kernel, rows),
+        "halo_columns",
+        pltpu.VMEM((2, 2 * size + 16 * layers, LANES), f32),
+        0.4,
+        [
+            pltpu.VMEM((2 * size + 16 * layers, LANES), bf16),
+            pltpu.VMEM((4, layers, LANES), f32),
+            pltpu.VMEM((16 * layers, LANES), f32),
+        ],
+    )(beside, across, tables, weights)
+    along = call(own_kernel, "own_slab", pltpu.VMEM((tiles, size, LANES), f32), 2.0)(cells, weights, added)
     along = call(
         other_kernel,
         "other_slab",
         pltpu.VMEM((tiles, 2 * size + 2 * 4 * half, LANES), f32),
         0.8,
         [pltpu.VMEM((size, cols), bf16)],
-    )(bulk, tables, weights, along, ends)
-    smem = pl.BlockSpec(memory_space=pltpu.SMEM)
-    lines = pltpu.VMEM((2, 2, 4, 2, 2 * layers, LANES), f32)
-    image, edge = call(
-        inner_kernel,
-        "inner_tiles",
-        (pltpu.VMEM((4, rows, (tiles - 2) * LANES), f32), pltpu.VMEM((2, 16 * layers, LANES), f32)),
-        2.0,
-        [pltpu.VMEM((16 * layers, cols), f32), lines, pltpu.VMEM((4, rows, LANES), f32)],
-        [smem] + [VMEM] * 7,
-    )(slab_rank, tables, weights, bulk, inside, first, second, along)
+    )(bulk, tables, weights, added, along)
     return call(
-        outer_kernel,
-        "outer_tiles",
+        render_kernel,
+        "render_rows",
         jax.ShapeDtypeStruct((4, rows, 2 * cols), f32),
-        2.0,
+        3.0,
         [
-            pltpu.VMEM((2 * size + 16 * layers, LANES), bf16),
-            pltpu.VMEM((12, 2 * layers, LANES), f32),
-            pltpu.VMEM((2, 2 * size + 2 * 4 * half, LANES), f32),
-            lines,
+            pltpu.VMEM((cols // LANES, 16 * layers, LANES), f32),
+            pltpu.VMEM((tiles, 32 * layers, LANES), f32),
             pltpu.VMEM((4, rows, LANES), f32),
         ],
-        [smem] + [VMEM] * 7,
-    )(slab_rank, tables, weights, beside, across, along, edge, image)
+        [pl.BlockSpec(memory_space=pltpu.SMEM)] + [VMEM] * 8,
+    )(slab_rank, tables, weights, bulk, inside, first, second, added, along)
 
 
 def on_device(density, bin_index, tf_colour, tf_extinction, slab_rank):

time: 16.4 us -> 17.8 us (1.085)
  starting transfers between devices: 6.17 us -> 7.59 us
  Pallas kernels: 7.47 us -> 6.99 us
  waiting for transfers between devices: 2.56 us -> 2.97 us
    ppermute x1, starting transfers between devices: 2.39 us -> 0.01 us  [two_slab_device(): beside = lax.ppermute(ends, 'bx', both(pairs))]
    ppermute x1, starting transfers between devices: 1.2 us -> 3.52 us  [two_slab_device(): across = lax.ppermute(ends, 'bx', both(cross))]
    ppermute x1 -> x2, starting transfers between devices: 1.27 us -> 2.77 us  [the longest x1 1.5 us: two_slab_device(): bulk = lax.ppermute(bulk, 'bz', swap)]
    ppermute x1, waiting for transfers between devices: 0.01 us -> 1.03 us  [two_slab_device(): across = lax.ppermute(ends, 'bx', both(cross))]
    ppermute x1, waiting for transfers between devices: 0.65 us -> 0.01 us  [two_slab_device(): first = lax.ppermute(first, axes, ring)]
    pallas_call x8, Pallas kernels: 7.47 us -> 6.99 us  [run(): pl.pallas_call(kernel, out_shape=out_shape, in_specs=in_specs or [VMEM] *...]
  transfers between devices with their start and end apart: 5 -> 6, of which waited for: 2 -> 2; matrix products, arithmetic and copies ran while one was open for 0% -> 0% of each run, Pallas kernels for 21% -> 8%
where the time goes in v7:
time: 17.8 us; the launch traced here: 17.6 us
  starting transfers between devices  7.59 us (43%)
  Pallas kernels  6.99 us (39%)
  waiting for transfers between devices  2.97 us (17%)
    pallas_call x8, Pallas kernels, run(): pl.pallas_call(kernel, out_shape=out_shape, in_specs=in_specs or [VMEM] *...  6.99 us
    ppermute x1, starting transfers between devices, two_slab_device(): across = lax.ppermute(ends, 'bx', both(cross))  3.52 us
    ppermute x1, waiting for transfers between devices, two_slab_device(): second = lax.ppermute(second, axes, both(diagonal))  1.93 us
    ppermute x1, starting transfers between devices, two_slab_device(): bulk = lax.ppermute(bulk, 'bz', swap)  1.5 us
    ppermute x1, starting transfers between devices, two_slab_device(): first = lax.ppermute(first, axes, ring)  1.3 us
    ppermute x1, starting transfers between devices, two_slab_device(): other_columns = lax.ppermute(columns, 'bz', swap)  1.28 us
    ppermute x1, waiting for transfers between devices, two_slab_device(): across = lax.ppermute(ends, 'bx', both(cross))  1.03 us
  transfers between devices with their start and end apart: 6, of which 2 were waited for; matrix products, arithmetic and copies ran while one was open for 0% of the time, Pallas kernels for 8%

profile of v7, /device:TPU:17, one launch (start us, length us, event | category | flops | bytes accessed | tf_op | source)
XLA Modules:
  0.0 17.6 jit_solution(14511525895914162864)
XLA Ops:
  0.0 1.2 %stage_block.1 = (s32[8,256]{1,0:T(8,128)S(1)}, s32[8,256]{1,0:T(8,128)S(1)}, s32[8,128]{1,0:T(8,128)S(1)}, f32[8,2,32,128]{3,2,1,0:T(8,128)S(1)}, s32[8,2,32,12...) custom-call(f32[8,32,256]{2,1,0:T(8,128)} %density_ref.1, s32[8,32,256]{2,1,0:T(8,128)} %bins_ref.1, ...), custom_call_target="tpu_custom_call" | custom-call | flops 1200000000 | bytes 4320000 | tf_op jit(solution)/shard_map/stage_block/pallas_call | solution.py:489
  1.2 1.3 %collective-permute-start.3 = (s32[8,128]{1,0:T(8,128)S(1)}, s32[8,128]{1,0:T(8,128)S(1)}, u32[]{:S(2)}, u32[]{:S(2)}) collective-permute-start(s32[8,128]{1,0:T(8,128)S(1)} %get-tuple-element.23.columns_ref), channel_id=1, source_target_pairs={{0,16},{16,0},{1,17},{17,1},{2,18},{18,2},{3,19},{19,3},{4,20},{20... | collective-permute-start | bytes 12296 | tf_op jit(solution)/shard_map/ppermute | solution.py:534
  2.5 1.3 %collective-permute-start.1 = (s32[8,256]{1,0:T(8,128)S(1)}, s32[8,256]{1,0:T(8,128)S(1)}, u32[]{:S(2)}, u32[]{:S(2)}) collective-permute-start(s32[8,256]{1,0:T(8,128)S(1)} %get-tuple-element.21), channel_id=1, source_target_pairs={{0,4},{1,5},{2,6},{3,7},{4,8},{5,9},{6,10},{7,11},{8,12},{9,13},{1... | collective-permute-start | bytes 24584 | tf_op jit(solution)/shard_map/ppermute | solution.py:539
  3.8 0.0 collective-permute-start.2
  3.8 0.1 pack_block.1
  3.9 1.5 %collective-permute-start = (s32[17,8,256]{2,1,0:T(8,128)S(1)}, s32[17,8,256]{2,1,0:T(8,128)S(1)}, u32[]{:S(2)}, u32[]{:S(2)}) collective-permute-start(s32[17,8,256]{2,1,0:T(8,128)S(1)} %get-tuple-element.19), channel_id=1, source_target_pairs={{0,16},{16,0},{1,17},{17,1},{2,18},{18,2},{3,19},{19,3},{4,20},{20... | collective-permute-start | bytes 417800 | tf_op jit(solution)/shard_map/ppermute | solution.py:538
  5.4 0.0 collective-permute-done.3.other_ref
  5.4 0.0 collective-permute-done.1.first_ref
  5.4 1.9 %collective-permute-done.2.second_ref = s32[8,256]{1,0:T(8,128)S(1)} collective-permute-done((s32[8,256]{1,0:T(8,128)S(1)}, s32[8,256]{1,0:T(8,128)S(1)}, u32[]{:S(2)}, u32[]{:S(2)}) %collective-permute-start.2) | collective-permute-done | bytes 8224 | tf_op jit(solution)/shard_map/ppermute | solution.py:533
  7.3 0.1 side_columns.1
  7.4 3.5 %collective-permute-start.5 = (s32[2,8,128]{2,1,0:T(8,128)S(1)}, s32[2,8,128]{2,1,0:T(8,128)S(1)}, u32[]{:S(2)}, u32[]{:S(2)}) collective-permute-start(s32[2,8,128]{2,1,0:T(8,128)S(1)} %side_columns.1), channel_id=1, source_target_pairs={{1,2},{3,0},{2,1},{0,3},{5,6},{7,4},{6,5},{4,7},{9,10},{11,8},{10,... | collective-permute-start | bytes 24584 | tf_op jit(solution)/shard_map/ppermute | solution.py:553
  10.9 0.0 collective-permute-start.4
  10.9 0.5 %own_cells.1 = (bf16[512,256]{1,0:T(8,128)(2,1)S(1)}, bf16[384,512]{1,0:T(8,128)(2,1)S(1)}) custom-call(f32[8,2,32,128]{3,2,1,0:T(8,128)S(1)} %get-tuple-element.16.dense_ref, s32[8,2,32,128]{3,2,1,0:T(8,128)S(1)} %get-tuple-element.17.index_ref, f32[8,8,128]{2,1,0:T(8,128)S(1)} %get-tuple-element.15.tables_ref), custom_call_target="tpu_custom_call" | custom-call | flops 500000000 | bytes 1800000 | tf_op jit(solution)/shard_map/own_cells/pallas_call | solution.py:489
  11.4 1.0 %collective-permute-done.5.across_ref = s32[2,8,128]{2,1,0:T(8,128)S(1)} collective-permute-done((s32[2,8,128]{2,1,0:T(8,128)S(1)}, s32[2,8,128]{2,1,0:T(8,128)S(1)}, u32[]{:S(2)}, u32[]{:S(2)}) %collective-permute-start.5) | collective-permute-done | bytes 8224 | tf_op jit(solution)/shard_map/ppermute | solution.py:553
  12.5 0.0 collective-permute-done.4.beside_ref
  12.5 0.4 %halo_columns.1.added_ref = f32[2,1152,128]{2,1,0:T(8,128)S(1)} custom-call(s32[2,8,128]{2,1,0:T(8,128)S(1)} %collective-permute-done.4.beside_ref, s32[2,8,128]{2,1,0:T(8,128)S(1)} %collective-permute-done.5.across_ref, f32[8,8,128]{2,1,0:T(8,128)S(1)} %get-tuple-element.15.tables_ref, bf16[384,512]{1,0:T(8,128)(2,1)S(1)} %get-tuple-element.18.weights_ref), custom_call_target="tpu_custom_call" | custom-call | flops 400000000 | bytes 1440000 | tf_op jit(solution)/shard_map/halo_columns/pallas_call | solution.py:489
  12.9 0.3 %own_slab.1.own_ref = f32[4,512,128]{2,1,0:T(8,128)S(1)} custom-call(bf16[512,256]{1,0:T(8,128)(2,1)S(1)} %get-tuple-element.24.cells_ref, bf16[384,512]{1,0:T(8,128)(2,1)S(1)} %get-tuple-element.18.weights_ref, f32[2,1152,128]{2,1,0:T(8,128)S(1)} %halo_columns.1.added_ref), custom_call_target="tpu_custom_call" | custom-call | flops 2000000000 | bytes 7200000 | tf_op jit(solution)/shard_map/own_slab/pallas_call | solution.py:489
  13.2 0.0 copy-start
  13.2 0.0 collective-permute-done.bulk_ref
  13.2 0.8 %other_slab.1.along_ref = f32[4,1152,128]{2,1,0:T(8,128)S(1)} custom-call(s32[17,8,256]{2,1,0:T(8,128)S(1)} %collective-permute-done.bulk_ref, f32[8,8,128]{2,1,0:T(8,128)S(1)} %get-tuple-element.15.tables_ref, bf16[384,512]{1,0:T(8,128)(2,1)S(1)} %get-tuple-element.18.weights_ref, f32[2,1152,128]{2,1,0:T(8,128)S(1)} %halo_columns.1.added_ref, ...), custom_call_target="tpu_custom_call" | custom-call | flops 800000000 | bytes 2880000 | tf_op jit(solution)/shard_map/other_slab/pallas_call | solution.py:489
  14.0 0.0 copy-done
  14.0 3.6 %render_rows.1 = f32[4,32,512]{2,1,0:T(8,128)} custom-call(s32[2]{0:T(128)S(1)} %copy-done, f32[8,8,128]{2,1,0:T(8,128)S(1)} %get-tuple-element.15.tables_ref, bf16[384,512]{1,0:T(8,128)(2,1)S(1)} %get-tuple-element.18.weights_ref, s32[17,8,256]{2,1,0:T(8,128)S(1)} %collective-permute-done.bulk_ref, s32[8,256]{1,0:T(8,128)S(1)} %get-tuple-element.20.inside_ref, ...), custom_call_target="tpu_custom_call" | custom-call | flops 3000000000 | bytes 10800000 | tf_op jit(solution)/shard_map/render_rows/pallas_call | solution.py:489
Async XLA Ops:
  1.2 4.1 %collective-permute-start.3 = (s32[8,128]{1,0:T(8,128)S(1)}, s32[8,128]{1,0:T(8,128)S(1)}, u32[]{:S(2)}, u32[]{:S(2)}) collective-permute-start(s32[8,128]{1,0:T(8,128)S(1)} %get-tuple-element.23.columns_ref), channel_id=1, source_target_pairs={{0,16},{16,0},{1,17},{17,1},{2,18},{18,2},{3,19},{19,3},{4,20},{20... | collective-permute-start | bytes 12296 | tf_op jit(solution)/shard_map/ppermute | solution.py:534
  2.5 2.9 %collective-permute-start.1 = (s32[8,256]{1,0:T(8,128)S(1)}, s32[8,256]{1,0:T(8,128)S(1)}, u32[]{:S(2)}, u32[]{:S(2)}) collective-permute-start(s32[8,256]{1,0:T(8,128)S(1)} %get-tuple-element.21), channel_id=1, source_target_pairs={{0,4},{1,5},{2,6},{3,7},{4,8},{5,9},{6,10},{7,11},{8,12},{9,13},{1... | collective-permute-start | bytes 24584 | tf_op jit(solution)/shard_map/ppermute | solution.py:539
  3.8 3.5 %collective-permute-start.2 = (s32[8,256]{1,0:T(8,128)S(1)}, s32[8,256]{1,0:T(8,128)S(1)}, u32[]{:S(2)}, u32[]{:S(2)}) collective-permute-start(s32[8,256]{1,0:T(8,128)S(1)} %get-tuple-element.22), channel_id=1, source_target_pairs={{16,4},{17,5},{18,6},{19,7},{20,8},{21,9},{22,10},{23,11},{24,12},... | collective-permute-start | bytes 24584 | tf_op jit(solution)/shard_map/ppermute | solution.py:533
  3.9 9.3 %collective-permute-start = (s32[17,8,256]{2,1,0:T(8,128)S(1)}, s32[17,8,256]{2,1,0:T(8,128)S(1)}, u32[]{:S(2)}, u32[]{:S(2)}) collective-permute-start(s32[17,8,256]{2,1,0:T(8,128)S(1)} %get-tuple-element.19), channel_id=1, source_target_pairs={{0,16},{16,0},{1,17},{17,1},{2,18},{18,2},{3,19},{19,3},{4,20},{20... | collective-permute-start | bytes 417800 | tf_op jit(solution)/shard_map/ppermute | solution.py:538
  7.4 5.1 %collective-permute-start.5 = (s32[2,8,128]{2,1,0:T(8,128)S(1)}, s32[2,8,128]{2,1,0:T(8,128)S(1)}, u32[]{:S(2)}, u32[]{:S(2)}) collective-permute-start(s32[2,8,128]{2,1,0:T(8,128)S(1)} %side_columns.1), channel_id=1, source_target_pairs={{1,2},{3,0},{2,1},{0,3},{5,6},{7,4},{6,5},{4,7},{9,10},{11,8},{10,... | collective-permute-start | bytes 24584 | tf_op jit(solution)/shard_map/ppermute | solution.py:553
  10.9 1.6 %collective-permute-start.4 = (s32[2,8,128]{2,1,0:T(8,128)S(1)}, s32[2,8,128]{2,1,0:T(8,128)S(1)}, u32[]{:S(2)}, u32[]{:S(2)}) collective-permute-start(s32[2,8,128]{2,1,0:T(8,128)S(1)} %side_columns.1), channel_id=1, source_target_pairs={{0,1},{2,3},{1,0},{3,2},{4,5},{6,7},{5,4},{7,6},{8,9},{10,11},{9,8... | collective-permute-start | bytes 24584 | tf_op jit(solution)/shard_map/ppermute | solution.py:552
  13.2 0.8 %copy-start = (s32[2]{0:T(128)S(1)}, s32[2]{0:T(128)}, u32[]{:S(2)}) copy-start(s32[2]{0:T(128)} %rank_ref.1) | copy-start | bytes 28

commit v8 on v6

--- a/solution.py
+++ b/solution.py
@@ -150,7 +150,7 @@
 
 def cost(microseconds):
     return pl.CostEstimate(
-        flops=0, bytes_accessed=int(3.6e6 * microseconds), transcendentals=0
+        flops=int(1e9 * microseconds), bytes_accessed=int(3.6e6 * microseconds), transcendentals=0
     )
 
 
@@ -174,8 +174,8 @@
         second_ref[z : z + 1, :] = jnp.where(front, top, bottom)
         for tile in range(cols // LANES):
             lanes = slice(tile * LANES, (tile + 1) * LANES)
-            dense_ref[z, tile] = density_ref[z, :, lanes]
-            index_ref[z, tile] = bins_ref[z, :, lanes]
+            dense_ref[z, tile, 0:rows] = density_ref[z, :, lanes]
+            index_ref[z, tile, 0:rows] = bins_ref[z, :, lanes]
     colour = colour_ref[...].astype(jnp.float32)
     extinction = extinction_ref[...].astype(jnp.float32).reshape(1, 2 * LANES)
     for channel in range(4):
@@ -187,7 +187,7 @@
 
 
 def pack_kernel(dense_ref, index_ref, columns_ref, bulk_ref, inside_ref):
-    layers, tiles, rows = dense_ref.shape[:3]
+    layers, tiles, rows = dense_ref.shape[0], dense_ref.shape[1], dense_ref.shape[2] - 8
     half = rows // 2
     front = lax.axis_index("bz") == 0
     start = jnp.where(front, half, 0)
@@ -268,25 +268,21 @@
                 cells_ref[base : base + 16, tile * LANES : (tile + 1) * LANES] = block.astype(jnp.bfloat16)
 
 
-def classify_halo(words, tables, ends_ref, values_ref, rows, base):
-    layers = words.shape[0]
-    start = lax.axis_index("bz") * (rows // 2)
-    side_lane, has_side, sub_at = lane_maps(rows)
-    halo = cell_values(*unpack_words(words), tables, float(2 * layers))
-    for channel in range(4):
-        values_ref[channel, 0:layers] = halo[channel]
-    masks = [has_side & (side_lane == start + 2 * sub_at + part) for part in range(2)]
-    for z in range(layers):
-        for channel in range(4):
-            line = jnp.broadcast_to(values_ref[channel, z : z + 1, :], (8, LANES))
-            block = jnp.concatenate([jnp.where(mask, line, 0.0) for mask in masks], axis=0)
-            at = base + (z * 4 + channel) * 16
-            ends_ref[at : at + 16, :] = block.astype(jnp.bfloat16)
-    return halo
-
-
 def rounded(value):
     return value.astype(jnp.bfloat16).astype(jnp.float32)
+
+
+def cells_kernel(dense_ref, index_ref, tables_ref, cells_ref, weights_ref):
+    layers, tiles, rows = dense_ref.shape[0], dense_ref.shape[1], dense_ref.shape[2] - 8
+    half = rows // 2
+    start = lax.axis_index("bz") * half
+    fill_weights(weights_ref, rows)
+
+    def read_cells(z, part, tile):
+        at = pl.ds(start + part, half // 2, stride=2)
+        return dense_ref[z, tile, at, :], index_ref[z, tile, at, :]
+
+    classify_rows(read_cells, read_tables(tables_ref), cells_ref, layers, tiles)
 
 
 def along_columns(cells, weights_ref, store):
@@ -298,38 +294,25 @@
         store(tile, block if tile in (0, tiles - 1) else rounded(block))
 
 
-def cells_kernel(dense_ref, index_ref, tables_ref, cells_ref, weights_ref):
-    layers, tiles, rows = dense_ref.shape[:3]
-    half = rows // 2
-    start = lax.axis_index("bz") * half
-    fill_weights(weights_ref, rows)
-
-    def read_cells(z, part, tile):
-        at = pl.ds(start + part, half // 2, stride=2)
-        return dense_ref[z, tile, at, :], index_ref[z, tile, at, :]
-
-    classify_rows(read_cells, read_tables(tables_ref), cells_ref, layers, tiles)
-
-
 def own_kernel(cells_ref, weights_ref, along_ref):
+    size = cells_ref.shape[0]
+    pad = along_ref.shape[1] // 2 - size
+    mine = pl.multiple_of(pad + lax.axis_index("bz") * size, pad)
+
     def store(tile, block):
-        along_ref[tile] = block
+        along_ref[tile, 0:pad, :] = jnp.zeros((pad, LANES), jnp.float32)
+        along_ref[tile, pad + 2 * size :, :] = jnp.zeros((pad, LANES), jnp.float32)
+        along_ref[tile, pl.ds(mine, size), :] = block
 
     along_columns(cells_ref[...], weights_ref, store)
 
 
-def other_kernel(bulk_ref, tables_ref, weights_ref, own_ref, ends_ref, along_ref, cells_ref):
+def other_kernel(bulk_ref, tables_ref, weights_ref, ends_ref, own_ref, along_ref, cells_ref):
     layers = (bulk_ref.shape[0] - 2) // 2
     cols = bulk_ref.shape[2]
-    size = own_ref.shape[1]
-    me = lax.axis_index("bz")
-    pad = size // layers
-    mine = pl.multiple_of(pad + me * size, pad)
-    theirs = pl.multiple_of(pad + (1 - me) * size, pad)
-    for tile in range(own_ref.shape[0]):
-        along_ref[tile, 0:pad, :] = jnp.zeros((pad, LANES), jnp.float32)
-        along_ref[tile, pad + 2 * size : 2 * pad + 2 * size, :] = jnp.zeros((pad, LANES), jnp.float32)
-        along_ref[tile, pl.ds(mine, size), :] = own_ref[tile]
+    size = cells_ref.shape[0]
+    pad = along_ref.shape[1] // 2 - size
+    theirs = pl.multiple_of(pad + (1 - lax.axis_index("bz")) * size, pad)
 
     def read_cells(z, part, tile):
         return unpack_words(bulk_ref[2 * z + part, :, tile * LANES : (tile + 1) * LANES])
@@ -341,58 +324,65 @@
     along_columns(cells_ref[...], weights_ref, store)
 
 
-def edge_lines(edge, tile, lines_ref, depth):
-    layer_at = lax.broadcasted_iota(jnp.int32, (depth, LANES), 0)
-    for side in range(2):
-        for channel in range(4):
-            base = (side * 4 + channel) * depth
-            now = edge[base : base + depth]
-            triple = 3.0 * now
-            before = jnp.where(layer_at == 0, 0.0, pltpu.roll(now, 1, 0))
-            after = jnp.where(layer_at == depth - 1, 0.0, pltpu.roll(now, depth - 1, 0))
-            for parity, beside in enumerate((before, after)):
-                lines_ref[tile, side, channel, parity] = rounded(beside + triple)
-
-
-def render_tile(tile, along_ref, lines_ref, flip, layers):
+def edge_lines(now, lines_ref, depth):
+    triple = 3.0 * now
+    empty = jnp.zeros((8, LANES), jnp.float32)
+    for layer in range(depth):
+        here = triple[layer * 8 : layer * 8 + 8]
+        before = now[layer * 8 - 8 : layer * 8] if layer > 0 else empty
+        after = now[layer * 8 + 8 : layer * 8 + 16] if layer + 1 < depth else empty
+        lines_ref[layer * 16 : layer * 16 + 8, :] = rounded(before + here)
+        lines_ref[layer * 16 + 8 : layer * 16 + 16, :] = rounded(after + here)
+
+
+def render_tile(along_ref, lines_ref, flip, layers):
     sub_at = lax.broadcasted_iota(jnp.int32, (8, LANES), 0)
     top = sub_at == 0
     bottom = sub_at == 7
 
-    def layer_rows(layer, channel):
-        base = pl.multiple_of((layer * 4 + channel) * 16, 16)
-        return [along_ref[tile, pl.ds(base + part * 8, 8), :] for part in range(2)]
-
-    def over_layer(layer, image):
-        here = [layer_rows(layer + 1, channel) for channel in range(4)]
-        triple = [[3.0 * value for value in pair] for pair in here]
-        for parity in range(2):
-            clear = [1.0 - value for value in image[3]]
-            updated = []
-            for channel in range(4):
-                beside = layer_rows(layer + 2 * parity, channel)
-                even, odd = [rounded(beside[part] + triple[channel][part]) for part in range(2)]
-                above = lines_ref[tile, 0, channel, parity, pl.ds(layer, 1), :]
-                below = lines_ref[tile, 1, channel, parity, pl.ds(layer, 1), :]
-                before_even = jnp.where(top, jnp.broadcast_to(above, (8, LANES)), pltpu.roll(odd, 1, 0))
-                after_odd = jnp.where(bottom, jnp.broadcast_to(below, (8, LANES)), pltpu.roll(even, 7, 0))
-                even_centre = 3.0 * even
-                odd_centre = 3.0 * odd
-                samples = [
-                    before_even + even_centre, even_centre + odd, even + odd_centre, odd_centre + after_odd
-                ]
-                updated.append([image[channel][i] + clear[i] * samples[i] for i in range(4)])
-            image = updated
-        return image
-
     def one_slab(position, image):
         slab = position ^ flip
+        view = along_ref.at[pl.ds(pl.multiple_of(slab * (layers * 64), 64), (layers + 2) * 64), :]
+        lines = lines_ref.at[pl.ds(pl.multiple_of(slab * (layers * 16), 16), layers * 16 + 8), :]
+
+        def layer_rows(layer, channel):
+            base = (layer * 4 + channel) * 16
+            return [view[base + part * 8 : base + part * 8 + 8, :] for part in range(2)]
+
         for z in range(layers):
-            image = over_layer(slab * layers + z, image)
+            triple = [[3.0 * value for value in layer_rows(z + 1, channel)] for channel in range(4)]
+            for parity in range(2):
+                clear = [1.0 - value for value in image[3]]
+                updated = []
+                for channel in range(4):
+                    beside = layer_rows(z + 2 * parity, channel)
+                    even, odd = [rounded(beside[part] + triple[channel][part]) for part in range(2)]
+                    line = (z * 2 + parity) * 8 + channel
+                    above = lines[pl.ds(line, 8, stride=0), :]
+                    below = lines[pl.ds(line + 4, 8, stride=0), :]
+                    before_even = jnp.where(top, above, pltpu.roll(odd, 1, 0))
+                    after_odd = jnp.where(bottom, below, pltpu.roll(even, 7, 0))
+                    even_centre = 3.0 * even
+                    odd_centre = 3.0 * odd
+                    samples = [
+                        before_even + even_centre,
+                        even_centre + odd,
+                        even + odd_centre,
+                        odd_centre + after_odd,
+                    ]
+                    updated.append([image[channel][i] + clear[i] * samples[i] for i in range(4)])
+                image = updated
         return image
 
     zero = jnp.zeros((8, LANES), jnp.float32)
     return lax.fori_loop(0, 2, one_slab, [[zero] * 4 for _ in range(4)])
+
+
+def store_tile(image, mixed_ref, out_ref, lanes):
+    for channel in range(4):
+        for i in range(4):
+            mixed_ref[channel, pl.ds(i, 8, stride=4), :] = image[channel][i]
+        out_ref[channel, :, lanes] = mixed_ref[channel, 0:32]
 
 
 def inner_kernel(
@@ -412,28 +402,30 @@
             use_near = front if side == 0 else jnp.logical_not(front)
             words = jnp.where(use_near, near, inside)
             for t in range(cols // LANES):
-                lanes = slice(t * LANES, (t + 1) * LANES)
-                values = cell_values(*unpack_words(words[:, lanes]), tables, float(depth))
+                values = cell_values(
+                    *unpack_words(words[:, t * LANES : (t + 1) * LANES]), tables, float(depth)
+                )
                 for channel in range(4):
-                    base = (side * 4 + channel) * depth + slab * layers
-                    cells_ref[base : base + layers, lanes] = values[channel]
-    edge = jnp.dot(
-        cells_ref[...].astype(jnp.bfloat16), weights_ref[0:cols, :], preferred_element_type=jnp.float32
+                    at = pl.ds(slab * layers * 8 + side * 4 + channel, layers, stride=8)
+                    cells_ref[t, at, :] = values[channel]
+    edge = sum(
+        jnp.dot(
+            cells_ref[t, 0 : 8 * depth].astype(jnp.bfloat16),
+            weights_ref[t * LANES : (t + 1) * LANES, :],
+            preferred_element_type=jnp.float32,
+        )
+        for t in range(cols // LANES)
     )
     for tile in range(tiles):
-        block = edge[:, tile * LANES : (tile + 1) * LANES]
+        now = edge[:, tile * LANES : (tile + 1) * LANES]
         if tile in (0, tiles - 1):
-            edge_ref[0 if tile == 0 else 1] = block
+            edge_ref[0 if tile == 0 else 1] = now
         else:
-            edge_lines(rounded(block), tile - 1, lines_ref, depth)
+            edge_lines(rounded(now), lines_ref.at[tile - 1], depth)
 
     def one_tile(index, carry):
-        image = render_tile(index, along_ref.at[1 : tiles - 1], lines_ref, rank_ref[0], layers)
-        lanes = pl.ds(pl.multiple_of(index * LANES, LANES), LANES)
-        for channel in range(4):
-            for i in range(4):
-                mixed_ref[channel, pl.ds(i, 8, stride=4), :] = image[channel][i]
-            image_ref[channel, :, lanes] = mixed_ref[channel]
+        image = render_tile(along_ref.at[index + 1], lines_ref.at[index], rank_ref[0], layers)
+        store_tile(image, mixed_ref, image_ref, pl.ds(pl.multiple_of(index * LANES, LANES), LANES))
         return carry
 
     lax.fori_loop(0, tiles - 2, one_tile, 0)
@@ -441,19 +433,22 @@
 
 def outer_kernel(
     rank_ref, tables_ref, weights_ref, beside_ref, across_ref, along_ref, edge_ref, image_ref,
-    out_ref, ends_ref, values_ref, fixed_ref, lines_ref, mixed_ref,
+    out_ref, ends_ref, values_ref, keep_ref, fixed_ref, lines_ref, mixed_ref,
 ):
     rows = out_ref.shape[1]
     cols = out_ref.shape[2] // 2
     layers = beside_ref.shape[1]
     depth = 2 * layers
     tiles = 2 * cols // LANES
-    size = layers * 64
     pad = 64
+    size = layers * pad
     front = lax.axis_index("bz") == 0
+    start = lax.axis_index("bz") * (rows // 2)
     me_x = lax.axis_index("bx")
     even_x = lax.rem(me_x, 2) == 0
     tables = read_tables(tables_ref)
+    side_lane, has_side, sub_at = lane_maps(rows)
+    masks = [has_side & (side_lane == start + 2 * sub_at + part) for part in range(2)]
     lane_at = lax.broadcasted_iota(jnp.int32, (layers, LANES), 1)
     is_right = (lane_at < rows) | (lane_at == 64)
     for slab in range(2):
@@ -461,19 +456,24 @@
         left = jnp.where(even_x, across_ref[slab], beside_ref[slab])
         right = jnp.where(me_x + 1 < lax.axis_size("bx"), right, 0)
         left = jnp.where(me_x > 0, left, 0)
-        halo = jnp.where(is_right, right, left)
-        values = classify_halo(halo, tables, ends_ref, values_ref, rows, slab * size)
+        words = jnp.where(is_right, right, left)
+        values = cell_values(*unpack_words(words), tables, float(depth))
+        for channel in range(4):
+            values_ref[slab * 4 + channel, 0:layers] = values[channel]
+        for z in range(layers):
+            for channel in range(4):
+                line = values_ref[slab * 4 + channel, pl.ds(z, 8, stride=0), :]
+                block = jnp.concatenate([jnp.where(mask, line, 0.0) for mask in masks], axis=0)
+                at = slab * size + (z * 4 + channel) * 16
+                ends_ref[at : at + 16, :] = block.astype(jnp.bfloat16)
         for side in range(2):
             row = jnp.where(front, 64, rows // 2 - 1) if side == 0 else jnp.where(front, rows // 2, 64)
             twin = jnp.where(row == 64, 65, row + rows)
             keep = (lane_at == row) | (lane_at == twin)
             for channel in range(4):
-                values_ref[4 + side * 4 + channel, slab * layers : (slab + 1) * layers] = jnp.where(
-                    keep, values[channel], 0.0
-                )
-    for line in range(8):
-        base = 2 * size + line * depth
-        ends_ref[base : base + depth, :] = values_ref[4 + line].astype(jnp.bfloat16)
+                at = pl.ds(slab * layers * 8 + side * 4 + channel, layers, stride=8)
+                keep_ref[at, :] = jnp.where(keep, values[channel], 0.0)
+    ends_ref[2 * size :, :] = keep_ref[0 : 8 * depth].astype(jnp.bfloat16)
     added = jnp.dot(
         ends_ref[...], weights_ref[cols : cols + LANES, 0 : 2 * LANES], preferred_element_type=jnp.float32
     )
@@ -484,16 +484,13 @@
         fixed_ref[index, pad : pad + 2 * size, :] = rounded(
             along_ref[tile, pad : pad + 2 * size, :] + block[0 : 2 * size]
         )
-        edge_lines(rounded(edge_ref[index] + block[2 * size :]), index, lines_ref, depth)
+        edge_lines(rounded(edge_ref[index] + block[2 * size :]), lines_ref.at[index], depth)
     out_ref[:, :, LANES : 2 * cols - LANES] = image_ref[...]
 
     def one_tile(index, carry):
-        image = render_tile(index, fixed_ref, lines_ref, rank_ref[0], layers)
+        image = render_tile(fixed_ref.at[index], lines_ref.at[index], rank_ref[0], layers)
         lanes = pl.ds(pl.multiple_of(index * (2 * cols - LANES), LANES), LANES)
-        for channel in range(4):
-            for i in range(4):
-                mixed_ref[channel, pl.ds(i, 8, stride=4), :] = image[channel][i]
-            out_ref[channel, :, lanes] = mixed_ref[channel]
+        store_tile(image, mixed_ref, out_ref, lanes)
         return carry
 
     lax.fori_loop(0, 2, one_tile, 0)
@@ -507,7 +504,7 @@
     count_y, count_x = lax.axis_size("by"), lax.axis_size("bx")
     f32, bf16, i32 = jnp.float32, jnp.bfloat16, jnp.int32
 
-    def call(kernel, name, out_shape, time, scratch_shapes=(), in_specs=None):
+    def call(kernel, name, out_shape, time, scratch_shapes=(), in_specs=None, aliases={}):
         def run(*operands):
             return pl.pallas_call(
                 kernel,
@@ -515,6 +512,7 @@
                 in_specs=in_specs or [VMEM] * len(operands),
                 out_specs=(VMEM,) * len(out_shape) if isinstance(out_shape, tuple) else VMEM,
                 scratch_shapes=scratch_shapes,
+                input_output_aliases=aliases,
                 compiler_params=pltpu.CompilerParams(vmem_limit_bytes=16 * 1024 * 1024),
                 cost_estimate=cost(time),
                 name=name,
@@ -525,7 +523,7 @@
     def both(route):
         return route + [(target, source) for source, target in route]
 
-    blocks = (layers, cols // LANES, rows, LANES)
+    blocks = (layers, cols // LANES, rows + 8, LANES)
     row = pltpu.VMEM((layers, cols), i32)
     first, second, columns, dense, index, tables = call(
         stage_kernel,
@@ -566,7 +564,8 @@
         (pltpu.VMEM((size, cols), bf16), pltpu.VMEM((cols + LANES, 2 * cols), bf16)),
         0.5,
     )(dense, index, tables)
-    along = call(own_kernel, "own_slab", pltpu.VMEM((tiles, size, LANES), f32), 0.4)(cells, weights)
+    whole = pltpu.VMEM((tiles, 2 * size + 2 * 4 * half, LANES), f32)
+    along = call(own_kernel, "own_slab", whole, 0.4)(cells, weights)
     ends = call(side_kernel, "side_columns", pltpu.VMEM((2, layers, LANES), i32), 0.1)(
         columns, bulk, first, second, along
     )
@@ -574,21 +573,17 @@
     cross = [(x, (x + 1) % count_x) for x in range(1, count_x, 2)]
     beside = lax.ppermute(ends, "bx", both(pairs))
     across = lax.ppermute(ends, "bx", both(cross))
-    along = call(
-        other_kernel,
-        "other_slab",
-        pltpu.VMEM((tiles, 2 * size + 2 * 4 * half, LANES), f32),
-        0.8,
-        [pltpu.VMEM((size, cols), bf16)],
-    )(bulk, tables, weights, along, ends)
+    along = call(other_kernel, "other_slab", whole, 0.8, [pltpu.VMEM((size, cols), bf16)], aliases={4: 0})(
+        bulk, tables, weights, ends, along
+    )
     smem = pl.BlockSpec(memory_space=pltpu.SMEM)
-    lines = pltpu.VMEM((2, 2, 4, 2, 2 * layers, LANES), f32)
+    lines = pltpu.VMEM((2, 32 * layers + 8, LANES), f32)
     image, edge = call(
         inner_kernel,
         "inner_tiles",
         (pltpu.VMEM((4, rows, (tiles - 2) * LANES), f32), pltpu.VMEM((2, 16 * layers, LANES), f32)),
         2.0,
-        [pltpu.VMEM((16 * layers, cols), f32), lines, pltpu.VMEM((4, rows, LANES), f32)],
+        [pltpu.VMEM((cols // LANES, 16 * layers + 8, LANES), f32), lines, pltpu.VMEM((4, rows + 8, LANES), f32)],
         [smem] + [VMEM] * 7,
     )(slab_rank, tables, weights, bulk, inside, first, second, along)
     return call(
@@ -598,10 +593,11 @@
         2.0,
         [
             pltpu.VMEM((2 * size + 16 * layers, LANES), bf16),
-            pltpu.VMEM((12, 2 * layers, LANES), f32),
+            pltpu.VMEM((8, 2 * layers, LANES), f32),
+            pltpu.VMEM((16 * layers + 8, LANES), f32),
             pltpu.VMEM((2, 2 * size + 2 * 4 * half, LANES), f32),
             lines,
-            pltpu.VMEM((4, rows, LANES), f32),
+            pltpu.VMEM((4, rows + 8, LANES), f32),
         ],
         [smem] + [VMEM] * 7,
     )(slab_rank, tables, weights, beside, across, along, edge, image)

time: 16.4 us -> 16.4 us (level)
    ppermute x1, starting transfers between devices: 2.39 us -> 0.01 us  [two_slab_device(): beside = lax.ppermute(ends, 'bx', both(pairs))]
    ppermute x1, starting transfers between devices: 1.2 us -> 3.53 us  [two_slab_device(): across = lax.ppermute(ends, 'bx', both(cross))]
  transfers between devices with their start and end apart: 5 -> 5, of which waited for: 2 -> 2; matrix products, arithmetic and copies ran while one was open for 0% -> 0% of each run, Pallas kernels for 21% -> 22%
where the time goes in v8:
time: 16.4 us; the launch traced here: 16.2 us
  Pallas kernels  7.5 us (46%)
  starting transfers between devices  6.1 us (37%)
  waiting for transfers between devices  2.56 us (16%)
    pallas_call x8, Pallas kernels, run(): pl.pallas_call(kernel, out_shape=out_shape, in_specs=in_specs or [VMEM] *...  7.5 us
    ppermute x1, starting transfers between devices, two_slab_device(): across = lax.ppermute(ends, 'bx', both(cross))  3.53 us
    ppermute x1, waiting for transfers between devices, two_slab_device(): second = lax.ppermute(second, axes, both(diagonal))  1.9 us
    ppermute x1, starting transfers between devices, two_slab_device(): first = lax.ppermute(first, axes, ring)  1.3 us
    ppermute x1, starting transfers between devices, two_slab_device(): bulk = lax.ppermute(bulk, 'bz', [(0, 1), (1, 0)])  1.28 us
    ppermute x1, waiting for transfers between devices, two_slab_device(): first = lax.ppermute(first, axes, ring)  0.65 us
  transfers between devices with their start and end apart: 5, of which 2 were waited for; matrix products, arithmetic and copies ran while one was open for 0% of the time, Pallas kernels for 22%

profile of v8, /device:TPU:17, one launch (start us, length us, event | category | flops | bytes accessed | tf_op | source)
XLA Modules:
  0.0 16.2 jit_solution(17920872636109363188)
XLA Ops:
  0.0 1.2 %stage_block.1 = (s32[8,256]{1,0:T(8,128)S(1)}, s32[8,256]{1,0:T(8,128)S(1)}, s32[8,128]{1,0:T(8,128)S(1)}, f32[8,2,40,128]{3,2,1,0:T(8,128)S(1)}, s32[8,2,40,12...) custom-call(f32[8,32,256]{2,1,0:T(8,128)} %density_ref.1, s32[8,32,256]{2,1,0:T(8,128)} %bins_ref.1, ...), custom_call_target="tpu_custom_call" | custom-call | flops 1200000000 | bytes 4320000 | tf_op jit(solution)/shard_map/stage_block/pallas_call | solution.py:509
  1.2 0.1 pack_block.1
  1.3 1.3 %collective-permute-start = (s32[18,8,256]{2,1,0:T(8,128)S(1)}, s32[18,8,256]{2,1,0:T(8,128)S(1)}, u32[]{:S(2)}, u32[]{:S(2)}) collective-permute-start(s32[18,8,256]{2,1,0:T(8,128)S(1)} %get-tuple-element.22), channel_id=1, source_target_pairs={{0,16},{16,0},{1,17},{17,1},{2,18},{18,2},{3,19},{19,3},{4,20},{20... | collective-permute-start | bytes 442376 | tf_op jit(solution)/shard_map/ppermute | solution.py:557
  2.6 1.3 %collective-permute-start.1 = (s32[8,256]{1,0:T(8,128)S(1)}, s32[8,256]{1,0:T(8,128)S(1)}, u32[]{:S(2)}, u32[]{:S(2)}) collective-permute-start(s32[8,256]{1,0:T(8,128)S(1)} %get-tuple-element.23), channel_id=1, source_target_pairs={{0,4},{1,5},{2,6},{3,7},{4,8},{5,9},{6,10},{7,11},{8,12},{9,13},{1... | collective-permute-start | bytes 24584 | tf_op jit(solution)/shard_map/ppermute | solution.py:558
  3.9 0.0 collective-permute-start.2
  3.9 0.5 %own_cells.1 = (bf16[512,256]{1,0:T(8,128)(2,1)S(1)}, bf16[384,512]{1,0:T(8,128)(2,1)S(1)}) custom-call(f32[8,2,40,128]{3,2,1,0:T(8,128)S(1)} %get-tuple-element.18.dense_ref, s32[8,2,40,128]{3,2,1,0:T(8,128)S(1)} %get-tuple-element.19.index_ref, f32[8,8,128]{2,1,0:T(8,128)S(1)} %get-tuple-element.17.tables_ref), custom_call_target="tpu_custom_call" | custom-call | flops 500000000 | bytes 1800000 | tf_op jit(solution)/shard_map/own_cells/pallas_call | solution.py:509
  4.4 0.3 %own_slab.1.along_ref.own_ref = f32[4,1152,128]{2,1,0:T(8,128)S(1)} custom-call(bf16[512,256]{1,0:T(8,128)(2,1)S(1)} %get-tuple-element.25.cells_ref, bf16[384,512]{1,0:T(8,128)(2,1)S(1)} %get-tuple-element.20.weights_ref), custom_call_target="tpu_custom_call" | custom-call | flops 400000000 | bytes 1440000 | tf_op jit(solution)/shard_map/own_slab/pallas_call | solution.py:509
  4.7 0.7 %collective-permute-done.1.first_ref = s32[8,256]{1,0:T(8,128)S(1)} collective-permute-done((s32[8,256]{1,0:T(8,128)S(1)}, s32[8,256]{1,0:T(8,128)S(1)}, u32[]{:S(2)}, u32[]{:S(2)}) %collective-permute-start.1) | collective-permute-done | bytes 8224 | tf_op jit(solution)/shard_map/ppermute | solution.py:558
  5.4 1.9 %collective-permute-done.2.second_ref = s32[8,256]{1,0:T(8,128)S(1)} collective-permute-done((s32[8,256]{1,0:T(8,128)S(1)}, s32[8,256]{1,0:T(8,128)S(1)}, u32[]{:S(2)}, u32[]{:S(2)}) %collective-permute-start.2) | collective-permute-done | bytes 8224 | tf_op jit(solution)/shard_map/ppermute | solution.py:559
  7.3 0.0 collective-permute-done.bulk_ref
  7.3 0.1 side_columns.1.ends_ref
  7.3 0.0 copy-start
  7.3 3.5 %collective-permute-start.4 = (s32[2,8,128]{2,1,0:T(8,128)S(1)}, s32[2,8,128]{2,1,0:T(8,128)S(1)}, u32[]{:S(2)}, u32[]{:S(2)}) collective-permute-start(s32[2,8,128]{2,1,0:T(8,128)S(1)} %side_columns.1.ends_ref), channel_id=1, source_target_pairs={{1,2},{3,0},{2,1},{0,3},{5,6},{7,4},{6,5},{4,7},{9,10},{11,8},{10,... | collective-permute-start | bytes 24584 | tf_op jit(solution)/shard_map/ppermute | solution.py:575
  10.9 0.0 collective-permute-start.3
  10.9 0.8 %other_slab.1.along_ref = f32[4,1152,128]{2,1,0:T(8,128)S(1)} custom-call(s32[18,8,256]{2,1,0:T(8,128)S(1)} %collective-permute-done.bulk_ref, f32[8,8,128]{2,1,0:T(8,128)S(1)} %get-tuple-element.17.tables_ref, bf16[384,512]{1,0:T(8,128)(2,1)S(1)} %get-tuple-element.20.weights_ref, ...), custom_call_target="tpu_custom_call", output_to_operand_aliasing={{}: (4, {})} | custom-call | flops 800000000 | bytes 2880000 | tf_op jit(solution)/shard_map/other_slab/pallas_call | solution.py:509
  11.7 0.0 copy-done
  11.7 1.9 %inner_tiles.1 = (f32[4,32,256]{2,1,0:T(8,128)S(1)}, f32[2,128,128]{2,1,0:T(8,128)S(1)}) custom-call(s32[2]{0:T(128)S(1)} %copy-done, f32[8,8,128]{2,1,0:T(8,128)S(1)} %get-tuple-element.17.tables_ref, bf16[384,512]{1,0:T(8,128)(2,1)S(1)} %get-tuple-element.20.weights_ref, s32[18,8,256]{2,1,0:T(8,128)S(1)} %collective-permute-done.bulk_ref, ...), custom_call_target="tpu_custom_call" | custom-call | flops 2000000000 | bytes 7200000 | tf_op jit(solution)/shard_map/inner_tiles/pallas_call | solution.py:509
  13.6 0.0 collective-permute-done.4.across_ref
  13.6 0.0 collective-permute-done.3.beside_ref
  13.6 2.6 %outer_tiles.1 = f32[4,32,512]{2,1,0:T(8,128)} custom-call(s32[2]{0:T(128)S(1)} %copy-done, f32[8,8,128]{2,1,0:T(8,128)S(1)} %get-tuple-element.17.tables_ref, bf16[384,512]{1,0:T(8,128)(2,1)S(1)} %get-tuple-element.20.weights_ref, s32[2,8,128]{2,1,0:T(8,128)S(1)} %collective-permute-done.3.beside_ref, s32[2,8,128]{2,1,0:T(8,128)S(1)} %collective-permute-done.4.across_ref, ...), custom_call_target="tpu_custom_call" | custom-call | flops 2000000000 | bytes 7200000 | tf_op jit(solution)/shard_map/outer_tiles/pallas_call | solution.py:509
Async XLA Ops:
  1.3 6.0 %collective-permute-start = (s32[18,8,256]{2,1,0:T(8,128)S(1)}, s32[18,8,256]{2,1,0:T(8,128)S(1)}, u32[]{:S(2)}, u32[]{:S(2)}) collective-permute-start(s32[18,8,256]{2,1,0:T(8,128)S(1)} %get-tuple-element.22), channel_id=1, source_target_pairs={{0,16},{16,0},{1,17},{17,1},{2,18},{18,2},{3,19},{19,3},{4,20},{20... | collective-permute-start | bytes 442376 | tf_op jit(solution)/shard_map/ppermute | solution.py:557
  2.6 2.8 %collective-permute-start.1 = (s32[8,256]{1,0:T(8,128)S(1)}, s32[8,256]{1,0:T(8,128)S(1)}, u32[]{:S(2)}, u32[]{:S(2)}) collective-permute-start(s32[8,256]{1,0:T(8,128)S(1)} %get-tuple-element.23), channel_id=1, source_target_pairs={{0,4},{1,5},{2,6},{3,7},{4,8},{5,9},{6,10},{7,11},{8,12},{9,13},{1... | collective-permute-start | bytes 24584 | tf_op jit(solution)/shard_map/ppermute | solution.py:558
  3.9 3.4 %collective-permute-start.2 = (s32[8,256]{1,0:T(8,128)S(1)}, s32[8,256]{1,0:T(8,128)S(1)}, u32[]{:S(2)}, u32[]{:S(2)}) collective-permute-start(s32[8,256]{1,0:T(8,128)S(1)} %get-tuple-element.24), channel_id=1, source_target_pairs={{16,4},{17,5},{18,6},{19,7},{20,8},{21,9},{22,10},{23,11},{24,12},... | collective-permute-start | bytes 24584 | tf_op jit(solution)/shard_map/ppermute | solution.py:559
  7.3 4.3 %copy-start = (s32[2]{0:T(128)S(1)}, s32[2]{0:T(128)}, u32[]{:S(2)}) copy-start(s32[2]{0:T(128)} %rank_ref.3) | copy-start | bytes 28
  7.3 6.2 %collective-permute-start.4 = (s32[2,8,128]{2,1,0:T(8,128)S(1)}, s32[2,8,128]{2,1,0:T(8,128)S(1)}, u32[]{:S(2)}, u32[]{:S(2)}) collective-permute-start(s32[2,8,128]{2,1,0:T(8,128)S(1)} %side_columns.1.ends_ref), channel_id=1, source_target_pairs={{1,2},{3,0},{2,1},{0,3},{5,6},{7,4},{6,5},{4,7},{9,10},{11,8},{10,... | collective-permute-start | bytes 24584 | tf_op jit(solution)/shard_map/ppermute | solution.py:575
  10.9 2.7 %collective-permute-start.3 = (s32[2,8,128]{2,1,0:T(8,128)S(1)}, s32[2,8,128]{2,1,0:T(8,128)S(1)}, u32[]{:S(2)}, u32[]{:S(2)}) collective-permute-start(s32[2,8,128]{2,1,0:T(8,128)S(1)} %side_columns.1.ends_ref), channel_id=1, source_target_pairs={{0,1},{2,3},{1,0},{3,2},{4,5},{6,7},{5,4},{7,6},{8,9},{10,11},{9,8... | collective-permute-start | bytes 24584 | tf_op jit(solution)/shard_map/ppermute | solution.py:574

commit v9 on v8

--- a/solution.py
+++ b/solution.py
@@ -335,6 +335,11 @@
         lines_ref[layer * 16 + 8 : layer * 16 + 16, :] = rounded(after + here)
 
 
+def rounded_parts(value):
+    scaled = value * 65537.0
+    return scaled + (value - scaled)
+
+
 def render_tile(along_ref, lines_ref, flip, layers):
     sub_at = lax.broadcasted_iota(jnp.int32, (8, LANES), 0)
     top = sub_at == 0
@@ -356,7 +361,7 @@
                 updated = []
                 for channel in range(4):
                     beside = layer_rows(z + 2 * parity, channel)
-                    even, odd = [rounded(beside[part] + triple[channel][part]) for part in range(2)]
+                    even, odd = [rounded_parts(beside[part] + triple[channel][part]) for part in range(2)]
                     line = (z * 2 + parity) * 8 + channel
                     above = lines[pl.ds(line, 8, stride=0), :]
                     below = lines[pl.ds(line + 4, 8, stride=0), :]
@@ -565,7 +570,7 @@
         0.5,
     )(dense, index, tables)
     whole = pltpu.VMEM((tiles, 2 * size + 2 * 4 * half, LANES), f32)
-    along = call(own_kernel, "own_slab", whole, 0.4)(cells, weights)
+    along = call(own_kernel, "own_slab", whole, 2.0)(cells, weights)
     ends = call(side_kernel, "side_columns", pltpu.VMEM((2, layers, LANES), i32), 0.1)(
         columns, bulk, first, second, along
     )

time: 16.4 us -> 18.1 us (1.10)
  the two profiles are of different devices: /device:TPU:17 before, /device:TPU:0 now
where the time goes in v9:
time: 18.1 us; the launch traced here: 18 us
  starting transfers between devices  7.82 us (43%)
  Pallas kernels  7.67 us (42%)
  waiting for transfers between devices  2.43 us (13%)
    pallas_call x8, Pallas kernels, run(): pl.pallas_call(kernel, out_shape=out_shape, in_specs=in_specs or [VMEM] *...  7.67 us
    ppermute x1, starting transfers between devices, two_slab_device(): bulk = lax.ppermute(bulk, 'bz', [(0, 1), (1, 0)])  3.1 us
    ppermute x1, starting transfers between devices, two_slab_device(): first = lax.ppermute(first, axes, ring)  3.08 us
    ppermute x1, waiting for transfers between devices, two_slab_device(): bulk = lax.ppermute(bulk, 'bz', [(0, 1), (1, 0)])  2.42 us
    ppermute x1, starting transfers between devices, two_slab_device(): beside = lax.ppermute(ends, 'bx', both(pairs))  1.62 us
  transfers between devices with their start and end apart: 5, of which 1 were waited for; matrix products, arithmetic and copies ran while one was open for 0% of the time, Pallas kernels for 20%

profile of v9, /device:TPU:0, one launch (start us, length us, event | category | flops | bytes accessed | tf_op | source)
XLA Modules:
  0.0 18.0 jit_solution(9990037908535282055)
XLA Ops:
  0.0 1.2 %stage_block.1 = (s32[8,256]{1,0:T(8,128)S(1)}, s32[8,256]{1,0:T(8,128)S(1)}, s32[8,128]{1,0:T(8,128)S(1)}, f32[8,2,40,128]{3,2,1,0:T(8,128)S(1)}, s32[8,2,40,12...) custom-call(f32[8,32,256]{2,1,0:T(8,128)} %density_ref.1, s32[8,32,256]{2,1,0:T(8,128)} %bins_ref.1, ...), custom_call_target="tpu_custom_call" | custom-call | flops 1200000000 | bytes 4320000 | tf_op jit(solution)/shard_map/stage_block/pallas_call | solution.py:514
  1.2 3.1 %collective-permute-start.1 = (s32[8,256]{1,0:T(8,128)S(1)}, s32[8,256]{1,0:T(8,128)S(1)}, u32[]{:S(2)}, u32[]{:S(2)}) collective-permute-start(s32[8,256]{1,0:T(8,128)S(1)} %get-tuple-element.23), channel_id=1, source_target_pairs={{0,4},{1,5},{2,6},{3,7},{4,8},{5,9},{6,10},{7,11},{8,12},{9,13},{1... | collective-permute-start | bytes 24584 | tf_op jit(solution)/shard_map/ppermute | solution.py:563
  4.3 0.0 collective-permute-start.2
  4.3 0.1 pack_block.1
  4.4 3.1 %collective-permute-start = (s32[18,8,256]{2,1,0:T(8,128)S(1)}, s32[18,8,256]{2,1,0:T(8,128)S(1)}, u32[]{:S(2)}, u32[]{:S(2)}) collective-permute-start(s32[18,8,256]{2,1,0:T(8,128)S(1)} %get-tuple-element.22), channel_id=1, source_target_pairs={{0,16},{16,0},{1,17},{17,1},{2,18},{18,2},{3,19},{19,3},{4,20},{20... | collective-permute-start | bytes 442376 | tf_op jit(solution)/shard_map/ppermute | solution.py:562
  7.5 0.5 %own_cells.1 = (bf16[512,256]{1,0:T(8,128)(2,1)S(1)}, bf16[384,512]{1,0:T(8,128)(2,1)S(1)}) custom-call(f32[8,2,40,128]{3,2,1,0:T(8,128)S(1)} %get-tuple-element.18.dense_ref, s32[8,2,40,128]{3,2,1,0:T(8,128)S(1)} %get-tuple-element.19.index_ref, f32[8,8,128]{2,1,0:T(8,128)S(1)} %get-tuple-element.17.tables_ref), custom_call_target="tpu_custom_call" | custom-call | flops 500000000 | bytes 1800000 | tf_op jit(solution)/shard_map/own_cells/pallas_call | solution.py:514
  8.0 0.3 %own_slab.1.along_ref.own_ref = f32[4,1152,128]{2,1,0:T(8,128)S(1)} custom-call(bf16[512,256]{1,0:T(8,128)(2,1)S(1)} %get-tuple-element.25.cells_ref, bf16[384,512]{1,0:T(8,128)(2,1)S(1)} %get-tuple-element.20.weights_ref), custom_call_target="tpu_custom_call" | custom-call | flops 2000000000 | bytes 7200000 | tf_op jit(solution)/shard_map/own_slab/pallas_call | solution.py:514
  8.3 0.0 collective-permute-done.1.first_ref
  8.3 0.0 collective-permute-done.2.second_ref
  8.3 2.4 %collective-permute-done.bulk_ref = s32[18,8,256]{2,1,0:T(8,128)S(1)} collective-permute-done((s32[18,8,256]{2,1,0:T(8,128)S(1)}, s32[18,8,256]{2,1,0:T(8,128)S(1)}, u32[]{:S(2)}, u32[]{:S(2)}) %collective-permute-start) | collective-permute-done | bytes 147488 | tf_op jit(solution)/shard_map/ppermute | solution.py:562
  10.8 0.1 side_columns.1.ends_ref
  10.8 0.0 copy-start
  10.8 0.0 collective-permute-start.4
  10.9 1.6 %collective-permute-start.3 = (s32[2,8,128]{2,1,0:T(8,128)S(1)}, s32[2,8,128]{2,1,0:T(8,128)S(1)}, u32[]{:S(2)}, u32[]{:S(2)}) collective-permute-start(s32[2,8,128]{2,1,0:T(8,128)S(1)} %side_columns.1.ends_ref), channel_id=1, source_target_pairs={{0,1},{2,3},{1,0},{3,2},{4,5},{6,7},{5,4},{7,6},{8,9},{10,11},{9,8... | collective-permute-start | bytes 24584 | tf_op jit(solution)/shard_map/ppermute | solution.py:579
  12.5 0.8 %other_slab.1.along_ref = f32[4,1152,128]{2,1,0:T(8,128)S(1)} custom-call(s32[18,8,256]{2,1,0:T(8,128)S(1)} %collective-permute-done.bulk_ref, f32[8,8,128]{2,1,0:T(8,128)S(1)} %get-tuple-element.17.tables_ref, bf16[384,512]{1,0:T(8,128)(2,1)S(1)} %get-tuple-element.20.weights_ref, ...), custom_call_target="tpu_custom_call", output_to_operand_aliasing={{}: (4, {})} | custom-call | flops 800000000 | bytes 2880000 | tf_op jit(solution)/shard_map/other_slab/pallas_call | solution.py:514
  13.3 0.0 copy-done
  13.3 2.0 %inner_tiles.1 = (f32[4,32,256]{2,1,0:T(8,128)S(1)}, f32[2,128,128]{2,1,0:T(8,128)S(1)}) custom-call(s32[2]{0:T(128)S(1)} %copy-done, f32[8,8,128]{2,1,0:T(8,128)S(1)} %get-tuple-element.17.tables_ref, bf16[384,512]{1,0:T(8,128)(2,1)S(1)} %get-tuple-element.20.weights_ref, s32[18,8,256]{2,1,0:T(8,128)S(1)} %collective-permute-done.bulk_ref, ...), custom_call_target="tpu_custom_call" | custom-call | flops 2000000000 | bytes 7200000 | tf_op jit(solution)/shard_map/inner_tiles/pallas_call | solution.py:514
  15.3 0.0 collective-permute-done.4.across_ref
  15.3 0.0 collective-permute-done.3.beside_ref
  15.3 2.7 %outer_tiles.1 = f32[4,32,512]{2,1,0:T(8,128)} custom-call(s32[2]{0:T(128)S(1)} %copy-done, f32[8,8,128]{2,1,0:T(8,128)S(1)} %get-tuple-element.17.tables_ref, bf16[384,512]{1,0:T(8,128)(2,1)S(1)} %get-tuple-element.20.weights_ref, s32[2,8,128]{2,1,0:T(8,128)S(1)} %collective-permute-done.3.beside_ref, s32[2,8,128]{2,1,0:T(8,128)S(1)} %collective-permute-done.4.across_ref, ...), custom_call_target="tpu_custom_call" | custom-call | flops 2000000000 | bytes 7200000 | tf_op jit(solution)/shard_map/outer_tiles/pallas_call | solution.py:514
Async XLA Ops:
  1.2 7.1 %collective-permute-start.1 = (s32[8,256]{1,0:T(8,128)S(1)}, s32[8,256]{1,0:T(8,128)S(1)}, u32[]{:S(2)}, u32[]{:S(2)}) collective-permute-start(s32[8,256]{1,0:T(8,128)S(1)} %get-tuple-element.23), channel_id=1, source_target_pairs={{0,4},{1,5},{2,6},{3,7},{4,8},{5,9},{6,10},{7,11},{8,12},{9,13},{1... | collective-permute-start | bytes 24584 | tf_op jit(solution)/shard_map/ppermute | solution.py:563
  4.3 4.0 %collective-permute-start.2 = (s32[8,256]{1,0:T(8,128)S(1)}, s32[8,256]{1,0:T(8,128)S(1)}, u32[]{:S(2)}, u32[]{:S(2)}) collective-permute-start(s32[8,256]{1,0:T(8,128)S(1)} %get-tuple-element.24), channel_id=1, source_target_pairs={{16,4},{17,5},{18,6},{19,7},{20,8},{21,9},{22,10},{23,11},{24,12},... | collective-permute-start | bytes 24584 | tf_op jit(solution)/shard_map/ppermute | solution.py:564
  4.4 6.4 %collective-permute-start = (s32[18,8,256]{2,1,0:T(8,128)S(1)}, s32[18,8,256]{2,1,0:T(8,128)S(1)}, u32[]{:S(2)}, u32[]{:S(2)}) collective-permute-start(s32[18,8,256]{2,1,0:T(8,128)S(1)} %get-tuple-element.22), channel_id=1, source_target_pairs={{0,16},{16,0},{1,17},{17,1},{2,18},{18,2},{3,19},{19,3},{4,20},{20... | collective-permute-start | bytes 442376 | tf_op jit(solution)/shard_map/ppermute | solution.py:562
  10.8 2.5 %copy-start = (s32[2]{0:T(128)S(1)}, s32[2]{0:T(128)}, u32[]{:S(2)}) copy-start(s32[2]{0:T(128)} %rank_ref.3) | copy-start | bytes 28
  10.8 4.4 %collective-permute-start.4 = (s32[2,8,128]{2,1,0:T(8,128)S(1)}, s32[2,8,128]{2,1,0:T(8,128)S(1)}, u32[]{:S(2)}, u32[]{:S(2)}) collective-permute-start(s32[2,8,128]{2,1,0:T(8,128)S(1)} %side_columns.1.ends_ref), channel_id=1, source_target_pairs={{1,2},{3,0},{2,1},{0,3},{5,6},{7,4},{6,5},{4,7},{9,10},{11,8},{10,... | collective-permute-start | bytes 24584 | tf_op jit(solution)/shard_map/ppermute | solution.py:580
  10.9 4.4 %collective-permute-start.3 = (s32[2,8,128]{2,1,0:T(8,128)S(1)}, s32[2,8,128]{2,1,0:T(8,128)S(1)}, u32[]{:S(2)}, u32[]{:S(2)}) collective-permute-start(s32[2,8,128]{2,1,0:T(8,128)S(1)} %side_columns.1.ends_ref), channel_id=1, source_target_pairs={{0,1},{2,3},{1,0},{3,2},{4,5},{6,7},{5,4},{7,6},{8,9},{10,11},{9,8... | collective-permute-start | bytes 24584 | tf_op jit(solution)/shard_map/ppermute | solution.py:579

commit v10 on v8

--- a/solution.py
+++ b/solution.py
@@ -1,3 +1,5 @@
+import functools
+
 import jax
 import jax.numpy as jnp
 from jax import lax
@@ -165,7 +167,7 @@
     for z in range(layers):
         first = pack_words(density_ref[z, :, 0:1], bins_ref[z, :, 0:1])
         last = pack_words(density_ref[z, :, cols - 1 : cols], bins_ref[z, :, cols - 1 : cols])
-        line = jnp.where(lane_at == row_at, first, 0) + jnp.where(lane_at == row_at + rows, last, 0)
+        line = jnp.where(lane_at == row_at, first, 0) + jnp.where(lane_at == row_at + LANES // 2, last, 0)
         columns_ref[z : z + 1, :] = jnp.sum(line, axis=0, keepdims=True)
         top, bottom = [
             pack_words(density_ref[z, r : r + 1, :], bins_ref[z, r : r + 1, :]) for r in (0, rows - 1)
@@ -214,7 +216,7 @@
     return jnp.where(has_near(me == 0), words, 0)
 
 
-def side_kernel(columns_ref, bulk_ref, first_ref, second_ref, along_ref, ends_ref):
+def side_kernel(rows, columns_ref, bulk_ref, first_ref, second_ref, along_ref, ends_ref):
     layers = columns_ref.shape[0]
     front = lax.axis_index("bz") == 0
     lane_at = lax.broadcasted_iota(jnp.int32, (layers, LANES), 1)
@@ -223,8 +225,10 @@
         columns = jnp.where(mine, columns_ref[...], bulk_ref[2 * layers + 1, :, 0:LANES])
         near = near_words(slab, first_ref, second_ref)
         cols = near.shape[1]
-        columns = jnp.where(lane_at == 64, near[:, 0:1], columns)
-        ends_ref[slab] = jnp.where(lane_at == 65, near[:, cols - 1 : cols], columns)
+        columns = jnp.where(lane_at == rows, near[:, 0:1], columns)
+        ends_ref[slab] = jnp.where(
+            lane_at == LANES // 2 + rows, near[:, cols - 1 : cols], columns
+        )
 
 
 def has_near(front):
@@ -232,28 +236,15 @@
     return jnp.where(front, me_y > 0, me_y + 1 < lax.axis_size("by"))
 
 
-def fill_weights(weights_ref, rows):
-    cols = weights_ref.shape[0] - LANES
+def fill_weights(weights_ref):
+    cols = weights_ref.shape[0]
     row = lax.broadcasted_iota(jnp.int32, (cols, 2 * cols), 0)
     at = lax.broadcasted_iota(jnp.int32, (cols, 2 * cols), 1)
     centre = lax.shift_right_logical(at, 1)
     beside = centre - 1 + 2 * (at & 1)
-    weights_ref[0:cols, :] = jnp.where(
-        row == centre, 3.0, jnp.where(row == beside, 1.0, 0.0)
-    ).astype(jnp.bfloat16)
-    row = lax.broadcasted_iota(jnp.int32, (LANES, 2 * LANES), 0)
-    at = lax.broadcasted_iota(jnp.int32, (LANES, 2 * LANES), 1)
-    right = ((row < rows) | (row == 64)) & (at == 2 * LANES - 1)
-    left = (((row >= rows) & (row < 2 * rows)) | (row == 65)) & (at == 0)
-    weights_ref[cols : cols + LANES, 0 : 2 * LANES] = jnp.where(right | left, 1.0, 0.0).astype(
+    weights_ref[...] = jnp.where(row == centre, 3.0, jnp.where(row == beside, 1.0, 0.0)).astype(
         jnp.bfloat16
     )
-
-
-def lane_maps(rows):
-    lane_at = lax.broadcasted_iota(jnp.int32, (8, LANES), 1)
-    sub_at = lax.broadcasted_iota(jnp.int32, (8, LANES), 0)
-    return lane_at & (rows - 1), lane_at < 2 * rows, sub_at
 
 
 def classify_rows(read_cells, tables, cells_ref, layers, tiles):
@@ -276,7 +267,7 @@
     layers, tiles, rows = dense_ref.shape[0], dense_ref.shape[1], dense_ref.shape[2] - 8
     half = rows // 2
     start = lax.axis_index("bz") * half
-    fill_weights(weights_ref, rows)
+    fill_weights(weights_ref)
 
     def read_cells(z, part, tile):
         at = pl.ds(start + part, half // 2, stride=2)
@@ -286,12 +277,9 @@
 
 
 def along_columns(cells, weights_ref, store):
-    cols = cells.shape[1]
-    tiles = 2 * cols // LANES
-    result = jnp.dot(cells, weights_ref[0:cols, :], preferred_element_type=jnp.float32)
-    for tile in range(tiles):
-        block = result[:, tile * LANES : (tile + 1) * LANES]
-        store(tile, block if tile in (0, tiles - 1) else rounded(block))
+    result = rounded(jnp.dot(cells, weights_ref[...], preferred_element_type=jnp.float32))
+    for tile in range(result.shape[1] // LANES):
+        store(tile, result[:, tile * LANES : (tile + 1) * LANES])
 
 
 def own_kernel(cells_ref, weights_ref, along_ref):
@@ -416,12 +404,13 @@
         )
         for t in range(cols // LANES)
     )
+    edge = rounded(edge)
     for tile in range(tiles):
         now = edge[:, tile * LANES : (tile + 1) * LANES]
         if tile in (0, tiles - 1):
             edge_ref[0 if tile == 0 else 1] = now
         else:
-            edge_lines(rounded(now), lines_ref.at[tile - 1], depth)
+            edge_lines(now, lines_ref.at[tile - 1], depth)
 
     def one_tile(index, carry):
         image = render_tile(along_ref.at[index + 1], lines_ref.at[index], rank_ref[0], layers)
@@ -432,59 +421,68 @@
 
 
 def outer_kernel(
-    rank_ref, tables_ref, weights_ref, beside_ref, across_ref, along_ref, edge_ref, image_ref,
-    out_ref, ends_ref, values_ref, keep_ref, fixed_ref, lines_ref, mixed_ref,
+    rank_ref, tables_ref, ends_ref, beside_ref, across_ref, along_ref, edge_ref, image_ref,
+    out_ref, values_ref, turned_ref, keep_ref, fixed_ref, lines_ref, mixed_ref,
 ):
     rows = out_ref.shape[1]
     cols = out_ref.shape[2] // 2
+    half = rows // 2
     layers = beside_ref.shape[1]
     depth = 2 * layers
     tiles = 2 * cols // LANES
     pad = 64
     size = layers * pad
+    middle = LANES // 2
     front = lax.axis_index("bz") == 0
-    start = lax.axis_index("bz") * (rows // 2)
+    start = lax.axis_index("bz") * half
     me_x = lax.axis_index("bx")
     even_x = lax.rem(me_x, 2) == 0
     tables = read_tables(tables_ref)
-    side_lane, has_side, sub_at = lane_maps(rows)
-    masks = [has_side & (side_lane == start + 2 * sub_at + part) for part in range(2)]
-    lane_at = lax.broadcasted_iota(jnp.int32, (layers, LANES), 1)
-    is_right = (lane_at < rows) | (lane_at == 64)
+    lane_at = lax.broadcasted_iota(jnp.int32, (8, LANES), 1)
+    places = [lane_at == 0, lane_at == LANES - 1]
     for slab in range(2):
         right = jnp.where(even_x, beside_ref[slab], across_ref[slab])
         left = jnp.where(even_x, across_ref[slab], beside_ref[slab])
         right = jnp.where(me_x + 1 < lax.axis_size("bx"), right, 0)
         left = jnp.where(me_x > 0, left, 0)
-        words = jnp.where(is_right, right, left)
-        values = cell_values(*unpack_words(words), tables, float(depth))
+        words = jnp.where(lane_at < middle, right, left)
+        mine = cell_values(*unpack_words(ends_ref[slab]), tables, float(depth))
+        halo = cell_values(*unpack_words(words), tables, float(depth))
         for channel in range(4):
-            values_ref[slab * 4 + channel, 0:layers] = values[channel]
-        for z in range(layers):
-            for channel in range(4):
-                line = values_ref[slab * 4 + channel, pl.ds(z, 8, stride=0), :]
-                block = jnp.concatenate([jnp.where(mask, line, 0.0) for mask in masks], axis=0)
-                at = slab * size + (z * 4 + channel) * 16
-                ends_ref[at : at + 16, :] = block.astype(jnp.bfloat16)
-        for side in range(2):
-            row = jnp.where(front, 64, rows // 2 - 1) if side == 0 else jnp.where(front, rows // 2, 64)
-            twin = jnp.where(row == 64, 65, row + rows)
-            keep = (lane_at == row) | (lane_at == twin)
-            for channel in range(4):
-                at = pl.ds(slab * layers * 8 + side * 4 + channel, layers, stride=8)
-                keep_ref[at, :] = jnp.where(keep, values[channel], 0.0)
-    ends_ref[2 * size :, :] = keep_ref[0 : 8 * depth].astype(jnp.bfloat16)
-    added = jnp.dot(
-        ends_ref[...], weights_ref[cols : cols + LANES, 0 : 2 * LANES], preferred_element_type=jnp.float32
-    )
+            value = rounded(
+                3.0 * rounded(mine[channel]) + pltpu.roll(rounded(halo[channel]), middle, 1)
+            )
+            base = (slab * 4 + channel) * layers
+            values_ref[base : base + layers, :] = value
+            for side, (at_front, at_back) in enumerate(((rows, half - 1), (half, rows))):
+                for index in range(2):
+                    shift = index * middle
+                    column = jnp.where(
+                        front,
+                        value[:, at_front + shift : at_front + shift + 1],
+                        value[:, at_back + shift : at_back + shift + 1],
+                    )
+                    at = pl.ds(slab * layers * 8 + side * 4 + channel, layers, stride=8)
+                    keep_ref[index, at, :] = jnp.broadcast_to(column, (layers, LANES))
+    values_ref[8 * layers :, :] = jnp.zeros((LANES - 8 * layers, LANES), jnp.float32)
+    turned_ref[0:LANES, :] = values_ref[...].T
     for index, tile in enumerate((0, tiles - 1)):
-        block = added[:, index * LANES : (index + 1) * LANES]
+        place = places[index]
         fixed_ref[index, 0:pad, :] = jnp.zeros((pad, LANES), jnp.float32)
         fixed_ref[index, pad + 2 * size :, :] = jnp.zeros((pad, LANES), jnp.float32)
-        fixed_ref[index, pad : pad + 2 * size, :] = rounded(
-            along_ref[tile, pad : pad + 2 * size, :] + block[0 : 2 * size]
-        )
-        edge_lines(rounded(edge_ref[index] + block[2 * size :]), lines_ref.at[index], depth)
+        for part in range(2):
+            turned = turned_ref[pl.ds(index * middle + start + part, 8, stride=2), :]
+            for slab in range(2):
+                for z in range(layers):
+                    for channel in range(4):
+                        at = (slab * 4 + channel) * layers + z
+                        base = pad + ((slab * layers + z) * 4 + channel) * 16 + part * 8
+                        fixed_ref[index, base : base + 8, :] = jnp.where(
+                            place, turned[:, at : at + 1], along_ref[tile, base : base + 8, :]
+                        )
+        wide = lax.broadcasted_iota(jnp.int32, (8 * depth, LANES), 1)
+        now = jnp.where(wide == index * (LANES - 1), keep_ref[index, 0 : 8 * depth], edge_ref[index])
+        edge_lines(now, lines_ref.at[index], depth)
     out_ref[:, :, LANES : 2 * cols - LANES] = image_ref[...]
 
     def one_tile(index, carry):
@@ -561,12 +559,12 @@
     cells, weights = call(
         cells_kernel,
         "own_cells",
-        (pltpu.VMEM((size, cols), bf16), pltpu.VMEM((cols + LANES, 2 * cols), bf16)),
+        (pltpu.VMEM((size, cols), bf16), pltpu.VMEM((cols, 2 * cols), bf16)),
         0.5,
     )(dense, index, tables)
     whole = pltpu.VMEM((tiles, 2 * size + 2 * 4 * half, LANES), f32)
     along = call(own_kernel, "own_slab", whole, 0.4)(cells, weights)
-    ends = call(side_kernel, "side_columns", pltpu.VMEM((2, layers, LANES), i32), 0.1)(
+    ends = call(functools.partial(side_kernel, rows), "side_columns", pltpu.VMEM((2, layers, LANES), i32), 0.1)(
         columns, bulk, first, second, along
     )
     pairs = [(x, x + 1) for x in range(0, count_x, 2)]
@@ -592,15 +590,15 @@
         jax.ShapeDtypeStruct((4, rows, 2 * cols), f32),
         2.0,
         [
-            pltpu.VMEM((2 * size + 16 * layers, LANES), bf16),
-            pltpu.VMEM((8, 2 * layers, LANES), f32),
-            pltpu.VMEM((16 * layers + 8, LANES), f32),
+            pltpu.VMEM((LANES, LANES), f32),
+            pltpu.VMEM((LANES + 16, LANES), f32),
+            pltpu.VMEM((2, 16 * layers + 8, LANES), f32),
             pltpu.VMEM((2, 2 * size + 2 * 4 * half, LANES), f32),
             lines,
             pltpu.VMEM((4, rows + 8, LANES), f32),
         ],
         [smem] + [VMEM] * 7,
-    )(slab_rank, tables, weights, beside, across, along, edge, image)
+    )(slab_rank, tables, ends, beside, across, along, edge, image)
 
 
 def on_device(density, bin_index, tf_colour, tf_extinction, slab_rank):

time: 16.4 us -> 16.7 us (1.018)
  Pallas kernels: 7.5 us -> 7.87 us
    pallas_call x8, Pallas kernels: 7.5 us -> 7.87 us  [run(): pl.pallas_call(kernel, out_shape=out_shape, in_specs=in_specs or [VMEM] *...]
  transfers between devices with their start and end apart: 5 -> 5, of which waited for: 2 -> 2; matrix products, arithmetic and copies ran while one was open for 0% -> 0% of each run, Pallas kernels for 22% -> 21%
where the time goes in v10:
time: 16.7 us; the launch traced here: 16.6 us
  Pallas kernels  7.87 us (47%)
  starting transfers between devices  6.1 us (37%)
  waiting for transfers between devices  2.56 us (15%)
    pallas_call x8, Pallas kernels, run(): pl.pallas_call(kernel, out_shape=out_shape, in_specs=in_specs or [VMEM] *...  7.87 us
    ppermute x1, starting transfers between devices, two_slab_device(): across = lax.ppermute(ends, 'bx', both(cross))  3.53 us
    ppermute x1, waiting for transfers between devices, two_slab_device(): second = lax.ppermute(second, axes, both(diagonal))  1.9 us
    ppermute x1, starting transfers between devices, two_slab_device(): first = lax.ppermute(first, axes, ring)  1.3 us
    ppermute x1, starting transfers between devices, two_slab_device(): bulk = lax.ppermute(bulk, 'bz', [(0, 1), (1, 0)])  1.28 us
    ppermute x1, waiting for transfers between devices, two_slab_device(): first = lax.ppermute(first, axes, ring)  0.65 us
  transfers between devices with their start and end apart: 5, of which 2 were waited for; matrix products, arithmetic and copies ran while one was open for 0% of the time, Pallas kernels for 21%

profile of v10, /device:TPU:17, one launch (start us, length us, event | category | flops | bytes accessed | tf_op | source)
XLA Modules:
  0.0 16.6 jit_solution(13034342578806145586)
XLA Ops:
  0.0 1.2 %stage_block.1 = (s32[8,256]{1,0:T(8,128)S(1)}, s32[8,256]{1,0:T(8,128)S(1)}, s32[8,128]{1,0:T(8,128)S(1)}, f32[8,2,40,128]{3,2,1,0:T(8,128)S(1)}, s32[8,2,40,12...) custom-call(f32[8,32,256]{2,1,0:T(8,128)} %density_ref.1, s32[8,32,256]{2,1,0:T(8,128)} %bins_ref.1, ...), custom_call_target="tpu_custom_call" | custom-call | flops 1200000000 | bytes 4320000 | tf_op jit(solution)/shard_map/stage_block/pallas_call | solution.py:507
  1.2 0.1 pack_block.1
  1.3 1.3 %collective-permute-start = (s32[18,8,256]{2,1,0:T(8,128)S(1)}, s32[18,8,256]{2,1,0:T(8,128)S(1)}, u32[]{:S(2)}, u32[]{:S(2)}) collective-permute-start(s32[18,8,256]{2,1,0:T(8,128)S(1)} %get-tuple-element.21), channel_id=1, source_target_pairs={{0,16},{16,0},{1,17},{17,1},{2,18},{18,2},{3,19},{19,3},{4,20},{20... | collective-permute-start | bytes 442376 | tf_op jit(solution)/shard_map/ppermute | solution.py:555
  2.6 1.3 %collective-permute-start.1 = (s32[8,256]{1,0:T(8,128)S(1)}, s32[8,256]{1,0:T(8,128)S(1)}, u32[]{:S(2)}, u32[]{:S(2)}) collective-permute-start(s32[8,256]{1,0:T(8,128)S(1)} %get-tuple-element.22), channel_id=1, source_target_pairs={{0,4},{1,5},{2,6},{3,7},{4,8},{5,9},{6,10},{7,11},{8,12},{9,13},{1... | collective-permute-start | bytes 24584 | tf_op jit(solution)/shard_map/ppermute | solution.py:556
  3.9 0.0 collective-permute-start.2
  3.9 0.5 %own_cells.1 = (bf16[512,256]{1,0:T(8,128)(2,1)S(1)}, bf16[256,512]{1,0:T(8,128)(2,1)S(1)}) custom-call(f32[8,2,40,128]{3,2,1,0:T(8,128)S(1)} %get-tuple-element.19.dense_ref, s32[8,2,40,128]{3,2,1,0:T(8,128)S(1)} %get-tuple-element.20.index_ref, f32[8,8,128]{2,1,0:T(8,128)S(1)} %get-tuple-element.17.tables_ref), custom_call_target="tpu_custom_call" | custom-call | flops 500000000 | bytes 1800000 | tf_op jit(solution)/shard_map/own_cells/pallas_call | solution.py:507
  4.4 0.3 %own_slab.1.along_ref.own_ref = f32[4,1152,128]{2,1,0:T(8,128)S(1)} custom-call(bf16[512,256]{1,0:T(8,128)(2,1)S(1)} %get-tuple-element.24.cells_ref, bf16[256,512]{1,0:T(8,128)(2,1)S(1)} %get-tuple-element.25.weights_ref), custom_call_target="tpu_custom_call" | custom-call | flops 400000000 | bytes 1440000 | tf_op jit(solution)/shard_map/own_slab/pallas_call | solution.py:507
  4.7 0.7 %collective-permute-done.1.first_ref = s32[8,256]{1,0:T(8,128)S(1)} collective-permute-done((s32[8,256]{1,0:T(8,128)S(1)}, s32[8,256]{1,0:T(8,128)S(1)}, u32[]{:S(2)}, u32[]{:S(2)}) %collective-permute-start.1) | collective-permute-done | bytes 8224 | tf_op jit(solution)/shard_map/ppermute | solution.py:556
  5.4 1.9 %collective-permute-done.2.second_ref = s32[8,256]{1,0:T(8,128)S(1)} collective-permute-done((s32[8,256]{1,0:T(8,128)S(1)}, s32[8,256]{1,0:T(8,128)S(1)}, u32[]{:S(2)}, u32[]{:S(2)}) %collective-permute-start.2) | collective-permute-done | bytes 8224 | tf_op jit(solution)/shard_map/ppermute | solution.py:557
  7.3 0.0 collective-permute-done.bulk_ref
  7.3 0.1 side_columns.1.ends_ref
  7.3 0.0 copy-start
  7.3 3.5 %collective-permute-start.4 = (s32[2,8,128]{2,1,0:T(8,128)S(1)}, s32[2,8,128]{2,1,0:T(8,128)S(1)}, u32[]{:S(2)}, u32[]{:S(2)}) collective-permute-start(s32[2,8,128]{2,1,0:T(8,128)S(1)} %side_columns.1.ends_ref), channel_id=1, source_target_pairs={{1,2},{3,0},{2,1},{0,3},{5,6},{7,4},{6,5},{4,7},{9,10},{11,8},{10,... | collective-permute-start | bytes 24584 | tf_op jit(solution)/shard_map/ppermute | solution.py:573
  10.9 0.0 collective-permute-start.3
  10.9 0.8 %other_slab.1.along_ref = f32[4,1152,128]{2,1,0:T(8,128)S(1)} custom-call(s32[18,8,256]{2,1,0:T(8,128)S(1)} %collective-permute-done.bulk_ref, f32[8,8,128]{2,1,0:T(8,128)S(1)} %get-tuple-element.17.tables_ref, bf16[256,512]{1,0:T(8,128)(2,1)S(1)} %get-tuple-element.25.weights_ref, ...), custom_call_target="tpu_custom_call", output_to_operand_aliasing={{}: (4, {})} | custom-call | flops 800000000 | bytes 2880000 | tf_op jit(solution)/shard_map/other_slab/pallas_call | solution.py:507
  11.7 0.0 copy-done
  11.7 1.9 %inner_tiles.1 = (f32[4,32,256]{2,1,0:T(8,128)S(1)}, f32[2,128,128]{2,1,0:T(8,128)S(1)}) custom-call(s32[2]{0:T(128)S(1)} %copy-done, f32[8,8,128]{2,1,0:T(8,128)S(1)} %get-tuple-element.17.tables_ref, bf16[256,512]{1,0:T(8,128)(2,1)S(1)} %get-tuple-element.25.weights_ref, s32[18,8,256]{2,1,0:T(8,128)S(1)} %collective-permute-done.bulk_ref, ...), custom_call_target="tpu_custom_call" | custom-call | flops 2000000000 | bytes 7200000 | tf_op jit(solution)/shard_map/inner_tiles/pallas_call | solution.py:507
  13.6 0.0 collective-permute-done.4.across_ref
  13.6 0.0 collective-permute-done.3.beside_ref
  13.6 3.0 %outer_tiles.1 = f32[4,32,512]{2,1,0:T(8,128)} custom-call(s32[2]{0:T(128)S(1)} %copy-done, f32[8,8,128]{2,1,0:T(8,128)S(1)} %get-tuple-element.17.tables_ref, s32[2,8,128]{2,1,0:T(8,128)S(1)} %side_columns.1.ends_ref, s32[2,8,128]{2,1,0:T(8,128)S(1)} %collective-permute-done.3.beside_ref, s32[2,8,128]{2,1,0:T(8,128)S(1)} %collective-permute-done.4.across_ref, ...), custom_call_target="tpu_custom_call" | custom-call | flops 2000000000 | bytes 7200000 | tf_op jit(solution)/shard_map/outer_tiles/pallas_call | solution.py:507
Async XLA Ops:
  1.3 6.0 %collective-permute-start = (s32[18,8,256]{2,1,0:T(8,128)S(1)}, s32[18,8,256]{2,1,0:T(8,128)S(1)}, u32[]{:S(2)}, u32[]{:S(2)}) collective-permute-start(s32[18,8,256]{2,1,0:T(8,128)S(1)} %get-tuple-element.21), channel_id=1, source_target_pairs={{0,16},{16,0},{1,17},{17,1},{2,18},{18,2},{3,19},{19,3},{4,20},{20... | collective-permute-start | bytes 442376 | tf_op jit(solution)/shard_map/ppermute | solution.py:555
  2.6 2.8 %collective-permute-start.1 = (s32[8,256]{1,0:T(8,128)S(1)}, s32[8,256]{1,0:T(8,128)S(1)}, u32[]{:S(2)}, u32[]{:S(2)}) collective-permute-start(s32[8,256]{1,0:T(8,128)S(1)} %get-tuple-element.22), channel_id=1, source_target_pairs={{0,4},{1,5},{2,6},{3,7},{4,8},{5,9},{6,10},{7,11},{8,12},{9,13},{1... | collective-permute-start | bytes 24584 | tf_op jit(solution)/shard_map/ppermute | solution.py:556
  3.9 3.4 %collective-permute-start.2 = (s32[8,256]{1,0:T(8,128)S(1)}, s32[8,256]{1,0:T(8,128)S(1)}, u32[]{:S(2)}, u32[]{:S(2)}) collective-permute-start(s32[8,256]{1,0:T(8,128)S(1)} %get-tuple-element.23), channel_id=1, source_target_pairs={{16,4},{17,5},{18,6},{19,7},{20,8},{21,9},{22,10},{23,11},{24,12},... | collective-permute-start | bytes 24584 | tf_op jit(solution)/shard_map/ppermute | solution.py:557
  7.3 4.3 %copy-start = (s32[2]{0:T(128)S(1)}, s32[2]{0:T(128)}, u32[]{:S(2)}) copy-start(s32[2]{0:T(128)} %rank_ref.3) | copy-start | bytes 28
  7.3 6.2 %collective-permute-start.4 = (s32[2,8,128]{2,1,0:T(8,128)S(1)}, s32[2,8,128]{2,1,0:T(8,128)S(1)}, u32[]{:S(2)}, u32[]{:S(2)}) collective-permute-start(s32[2,8,128]{2,1,0:T(8,128)S(1)} %side_columns.1.ends_ref), channel_id=1, source_target_pairs={{1,2},{3,0},{2,1},{0,3},{5,6},{7,4},{6,5},{4,7},{9,10},{11,8},{10,... | collective-permute-start | bytes 24584 | tf_op jit(solution)/shard_map/ppermute | solution.py:573
  10.9 2.7 %collective-permute-start.3 = (s32[2,8,128]{2,1,0:T(8,128)S(1)}, s32[2,8,128]{2,1,0:T(8,128)S(1)}, u32[]{:S(2)}, u32[]{:S(2)}) collective-permute-start(s32[2,8,128]{2,1,0:T(8,128)S(1)} %side_columns.1.ends_ref), channel_id=1, source_target_pairs={{0,1},{2,3},{1,0},{3,2},{4,5},{6,7},{5,4},{7,6},{8,9},{10,11},{9,8... | collective-permute-start | bytes 24584 | tf_op jit(solution)/shard_map/ppermute | solution.py:572

commit v11 on v8

--- a/solution.py
+++ b/solution.py
@@ -324,26 +324,25 @@
     along_columns(cells_ref[...], weights_ref, store)
 
 
-def edge_lines(now, lines_ref, depth):
+def edge_lines(now, shift_ref, depth):
     triple = 3.0 * now
     empty = jnp.zeros((8, LANES), jnp.float32)
     for layer in range(depth):
         here = triple[layer * 8 : layer * 8 + 8]
         before = now[layer * 8 - 8 : layer * 8] if layer > 0 else empty
         after = now[layer * 8 + 8 : layer * 8 + 16] if layer + 1 < depth else empty
-        lines_ref[layer * 16 : layer * 16 + 8, :] = rounded(before + here)
-        lines_ref[layer * 16 + 8 : layer * 16 + 16, :] = rounded(after + here)
-
-
-def render_tile(along_ref, lines_ref, flip, layers):
-    sub_at = lax.broadcasted_iota(jnp.int32, (8, LANES), 0)
-    top = sub_at == 0
-    bottom = sub_at == 7
-
+        for parity, beside in enumerate((before, after)):
+            line = rounded(beside + here)
+            base = (layer * 2 + parity) * 128
+            shift_ref[pl.ds(base + 23, 4, stride=32), :] = line[0:4]
+            shift_ref[pl.ds(base + 8, 4, stride=32), :] = line[4:8]
+
+
+def render_tile(along_ref, shift_ref, flip, layers):
     def one_slab(position, image):
         slab = position ^ flip
         view = along_ref.at[pl.ds(pl.multiple_of(slab * (layers * 64), 64), (layers + 2) * 64), :]
-        lines = lines_ref.at[pl.ds(pl.multiple_of(slab * (layers * 16), 16), layers * 16 + 8), :]
+        shift = shift_ref.at[pl.ds(pl.multiple_of(slab * (layers * 256), 256), layers * 256), :]
 
         def layer_rows(layer, channel):
             base = (layer * 4 + channel) * 16
@@ -357,11 +356,11 @@
                 for channel in range(4):
                     beside = layer_rows(z + 2 * parity, channel)
                     even, odd = [rounded(beside[part] + triple[channel][part]) for part in range(2)]
-                    line = (z * 2 + parity) * 8 + channel
-                    above = lines[pl.ds(line, 8, stride=0), :]
-                    below = lines[pl.ds(line + 4, 8, stride=0), :]
-                    before_even = jnp.where(top, above, pltpu.roll(odd, 1, 0))
-                    after_odd = jnp.where(bottom, below, pltpu.roll(even, 7, 0))
+                    base = ((z * 2 + parity) * 4 + channel) * 32
+                    shift[base : base + 8, :] = even
+                    shift[base + 24 : base + 32, :] = odd
+                    before_even = shift[base + 23 : base + 31, :]
+                    after_odd = shift[base + 1 : base + 9, :]
                     even_centre = 3.0 * even
                     odd_centre = 3.0 * odd
                     samples = [
@@ -387,7 +386,7 @@
 
 def inner_kernel(
     rank_ref, tables_ref, weights_ref, bulk_ref, inside_ref, first_ref, second_ref, along_ref,
-    image_ref, edge_ref, cells_ref, lines_ref, mixed_ref,
+    image_ref, edge_ref, cells_ref, shift_ref, mixed_ref,
 ):
     layers, cols = inside_ref.shape
     depth = 2 * layers
@@ -421,10 +420,10 @@
         if tile in (0, tiles - 1):
             edge_ref[0 if tile == 0 else 1] = now
         else:
-            edge_lines(rounded(now), lines_ref.at[tile - 1], depth)
+            edge_lines(rounded(now), shift_ref.at[tile - 1], depth)
 
     def one_tile(index, carry):
-        image = render_tile(along_ref.at[index + 1], lines_ref.at[index], rank_ref[0], layers)
+        image = render_tile(along_ref.at[index + 1], shift_ref.at[index], rank_ref[0], layers)
         store_tile(image, mixed_ref, image_ref, pl.ds(pl.multiple_of(index * LANES, LANES), LANES))
         return carry
 
@@ -433,7 +432,7 @@
 
 def outer_kernel(
     rank_ref, tables_ref, weights_ref, beside_ref, across_ref, along_ref, edge_ref, image_ref,
-    out_ref, ends_ref, values_ref, keep_ref, fixed_ref, lines_ref, mixed_ref,
+    out_ref, ends_ref, values_ref, keep_ref, fixed_ref, shift_ref, mixed_ref,
 ):
     rows = out_ref.shape[1]
     cols = out_ref.shape[2] // 2
@@ -484,11 +483,11 @@
         fixed_ref[index, pad : pad + 2 * size, :] = rounded(
             along_ref[tile, pad : pad + 2 * size, :] + block[0 : 2 * size]
         )
-        edge_lines(rounded(edge_ref[index] + block[2 * size :]), lines_ref.at[index], depth)
+        edge_lines(rounded(edge_ref[index] + block[2 * size :]), shift_ref.at[index], depth)
     out_ref[:, :, LANES : 2 * cols - LANES] = image_ref[...]
 
     def one_tile(index, carry):
-        image = render_tile(fixed_ref.at[index], lines_ref.at[index], rank_ref[0], layers)
+        image = render_tile(fixed_ref.at[index], shift_ref.at[index], rank_ref[0], layers)
         lanes = pl.ds(pl.multiple_of(index * (2 * cols - LANES), LANES), LANES)
         store_tile(image, mixed_ref, out_ref, lanes)
         return carry
@@ -577,13 +576,13 @@
         bulk, tables, weights, ends, along
     )
     smem = pl.BlockSpec(memory_space=pltpu.SMEM)
-    lines = pltpu.VMEM((2, 32 * layers + 8, LANES), f32)
+    shift = pltpu.VMEM((2, 512 * layers + 128, LANES), f32)
     image, edge = call(
         inner_kernel,
         "inner_tiles",
         (pltpu.VMEM((4, rows, (tiles - 2) * LANES), f32), pltpu.VMEM((2, 16 * layers, LANES), f32)),
         2.0,
-        [pltpu.VMEM((cols // LANES, 16 * layers + 8, LANES), f32), lines, pltpu.VMEM((4, rows + 8, LANES), f32)],
+        [pltpu.VMEM((cols // LANES, 16 * layers + 8, LANES), f32), shift, pltpu.VMEM((4, rows + 8, LANES), f32)],
         [smem] + [VMEM] * 7,
     )(slab_rank, tables, weights, bulk, inside, first, second, along)
     return call(
@@ -596,7 +595,7 @@
             pltpu.VMEM((8, 2 * layers, LANES), f32),
             pltpu.VMEM((16 * layers + 8, LANES), f32),
             pltpu.VMEM((2, 2 * size + 2 * 4 * half, LANES), f32),
-            lines,
+            shift,
             pltpu.VMEM((4, rows + 8, LANES), f32),
         ],
         [smem] + [VMEM] * 7,

time: 16.4 us -> 16.7 us (1.018)
  the two profiles are of different devices: /device:TPU:17 before, /device:TPU:9 now
where the time goes in v11:
time: 16.7 us; the launch traced here: 16.5 us
  Pallas kernels  7.8 us (47%)
  starting transfers between devices  6.16 us (37%)
  waiting for transfers between devices  2.52 us (15%)
    pallas_call x8, Pallas kernels, run(): pl.pallas_call(kernel, out_shape=out_shape, in_specs=in_specs or [VMEM] *...  7.8 us
    ppermute x1, starting transfers between devices, two_slab_device(): across = lax.ppermute(ends, 'bx', both(cross))  3.53 us
    ppermute x1, waiting for transfers between devices, two_slab_device(): second = lax.ppermute(second, axes, both(diagonal))  1.9 us
    ppermute x1, starting transfers between devices, two_slab_device(): first = lax.ppermute(first, axes, ring)  1.3 us
    ppermute x1, starting transfers between devices, two_slab_device(): bulk = lax.ppermute(bulk, 'bz', [(0, 1), (1, 0)])  1.28 us
    ppermute x1, waiting for transfers between devices, two_slab_device(): first = lax.ppermute(first, axes, ring)  0.61 us
  transfers between devices with their start and end apart: 5, of which 2 were waited for; matrix products, arithmetic and copies ran while one was open for 0% of the time, Pallas kernels for 22%

profile of v11, /device:TPU:9, one launch (start us, length us, event | category | flops | bytes accessed | tf_op | source)
XLA Modules:
  0.0 16.5 jit_solution(4237059678449751229)
XLA Ops:
  0.0 1.2 %stage_block.1 = (s32[8,256]{1,0:T(8,128)S(1)}, s32[8,256]{1,0:T(8,128)S(1)}, s32[8,128]{1,0:T(8,128)S(1)}, f32[8,2,40,128]{3,2,1,0:T(8,128)S(1)}, s32[8,2,40,12...) custom-call(f32[8,32,256]{2,1,0:T(8,128)} %density_ref.1, s32[8,32,256]{2,1,0:T(8,128)} %bins_ref.1, ...), custom_call_target="tpu_custom_call" | custom-call | flops 1200000000 | bytes 4320000 | tf_op jit(solution)/shard_map/stage_block/pallas_call | solution.py:508
  1.2 0.1 pack_block.1
  1.3 1.3 %collective-permute-start = (s32[18,8,256]{2,1,0:T(8,128)S(1)}, s32[18,8,256]{2,1,0:T(8,128)S(1)}, u32[]{:S(2)}, u32[]{:S(2)}) collective-permute-start(s32[18,8,256]{2,1,0:T(8,128)S(1)} %get-tuple-element.22), channel_id=1, source_target_pairs={{0,16},{16,0},{1,17},{17,1},{2,18},{18,2},{3,19},{19,3},{4,20},{20... | collective-permute-start | bytes 442376 | tf_op jit(solution)/shard_map/ppermute | solution.py:556
  2.6 1.3 %collective-permute-start.1 = (s32[8,256]{1,0:T(8,128)S(1)}, s32[8,256]{1,0:T(8,128)S(1)}, u32[]{:S(2)}, u32[]{:S(2)}) collective-permute-start(s32[8,256]{1,0:T(8,128)S(1)} %get-tuple-element.23), channel_id=1, source_target_pairs={{0,4},{1,5},{2,6},{3,7},{4,8},{5,9},{6,10},{7,11},{8,12},{9,13},{1... | collective-permute-start | bytes 24584 | tf_op jit(solution)/shard_map/ppermute | solution.py:557
  3.9 0.1 collective-permute-start.2
  3.9 0.5 %own_cells.1 = (bf16[512,256]{1,0:T(8,128)(2,1)S(1)}, bf16[384,512]{1,0:T(8,128)(2,1)S(1)}) custom-call(f32[8,2,40,128]{3,2,1,0:T(8,128)S(1)} %get-tuple-element.18.dense_ref, s32[8,2,40,128]{3,2,1,0:T(8,128)S(1)} %get-tuple-element.19.index_ref, f32[8,8,128]{2,1,0:T(8,128)S(1)} %get-tuple-element.17.tables_ref), custom_call_target="tpu_custom_call" | custom-call | flops 500000000 | bytes 1800000 | tf_op jit(solution)/shard_map/own_cells/pallas_call | solution.py:508
  4.5 0.3 %own_slab.1.along_ref.own_ref = f32[4,1152,128]{2,1,0:T(8,128)S(1)} custom-call(bf16[512,256]{1,0:T(8,128)(2,1)S(1)} %get-tuple-element.25.cells_ref, bf16[384,512]{1,0:T(8,128)(2,1)S(1)} %get-tuple-element.20.weights_ref), custom_call_target="tpu_custom_call" | custom-call | flops 400000000 | bytes 1440000 | tf_op jit(solution)/shard_map/own_slab/pallas_call | solution.py:508
  4.8 0.6 %collective-permute-done.1.first_ref = s32[8,256]{1,0:T(8,128)S(1)} collective-permute-done((s32[8,256]{1,0:T(8,128)S(1)}, s32[8,256]{1,0:T(8,128)S(1)}, u32[]{:S(2)}, u32[]{:S(2)}) %collective-permute-start.1) | collective-permute-done | bytes 8224 | tf_op jit(solution)/shard_map/ppermute | solution.py:557
  5.4 1.9 %collective-permute-done.2.second_ref = s32[8,256]{1,0:T(8,128)S(1)} collective-permute-done((s32[8,256]{1,0:T(8,128)S(1)}, s32[8,256]{1,0:T(8,128)S(1)}, u32[]{:S(2)}, u32[]{:S(2)}) %collective-permute-start.2) | collective-permute-done | bytes 8224 | tf_op jit(solution)/shard_map/ppermute | solution.py:558
  7.3 0.0 collective-permute-done.bulk_ref
  7.3 0.1 side_columns.1.ends_ref
  7.3 0.0 copy-start
  7.3 3.5 %collective-permute-start.4 = (s32[2,8,128]{2,1,0:T(8,128)S(1)}, s32[2,8,128]{2,1,0:T(8,128)S(1)}, u32[]{:S(2)}, u32[]{:S(2)}) collective-permute-start(s32[2,8,128]{2,1,0:T(8,128)S(1)} %side_columns.1.ends_ref), channel_id=1, source_target_pairs={{1,2},{3,0},{2,1},{0,3},{5,6},{7,4},{6,5},{4,7},{9,10},{11,8},{10,... | collective-permute-start | bytes 24584 | tf_op jit(solution)/shard_map/ppermute | solution.py:574
  10.9 0.0 collective-permute-start.3
  10.9 0.8 %other_slab.1.along_ref = f32[4,1152,128]{2,1,0:T(8,128)S(1)} custom-call(s32[18,8,256]{2,1,0:T(8,128)S(1)} %collective-permute-done.bulk_ref, f32[8,8,128]{2,1,0:T(8,128)S(1)} %get-tuple-element.17.tables_ref, bf16[384,512]{1,0:T(8,128)(2,1)S(1)} %get-tuple-element.20.weights_ref, ...), custom_call_target="tpu_custom_call", output_to_operand_aliasing={{}: (4, {})} | custom-call | flops 800000000 | bytes 2880000 | tf_op jit(solution)/shard_map/other_slab/pallas_call | solution.py:508
  11.7 0.0 copy-done
  11.7 2.0 %inner_tiles.1 = (f32[4,32,256]{2,1,0:T(8,128)S(1)}, f32[2,128,128]{2,1,0:T(8,128)S(1)}) custom-call(s32[2]{0:T(128)S(1)} %copy-done, f32[8,8,128]{2,1,0:T(8,128)S(1)} %get-tuple-element.17.tables_ref, bf16[384,512]{1,0:T(8,128)(2,1)S(1)} %get-tuple-element.20.weights_ref, s32[18,8,256]{2,1,0:T(8,128)S(1)} %collective-permute-done.bulk_ref, ...), custom_call_target="tpu_custom_call" | custom-call | flops 2000000000 | bytes 7200000 | tf_op jit(solution)/shard_map/inner_tiles/pallas_call | solution.py:508
  13.7 0.0 collective-permute-done.4.across_ref
  13.7 0.0 collective-permute-done.3.beside_ref
  13.7 2.8 %outer_tiles.1 = f32[4,32,512]{2,1,0:T(8,128)} custom-call(s32[2]{0:T(128)S(1)} %copy-done, f32[8,8,128]{2,1,0:T(8,128)S(1)} %get-tuple-element.17.tables_ref, bf16[384,512]{1,0:T(8,128)(2,1)S(1)} %get-tuple-element.20.weights_ref, s32[2,8,128]{2,1,0:T(8,128)S(1)} %collective-permute-done.3.beside_ref, s32[2,8,128]{2,1,0:T(8,128)S(1)} %collective-permute-done.4.across_ref, ...), custom_call_target="tpu_custom_call" | custom-call | flops 2000000000 | bytes 7200000 | tf_op jit(solution)/shard_map/outer_tiles/pallas_call | solution.py:508
Async XLA Ops:
  1.3 6.0 %collective-permute-start = (s32[18,8,256]{2,1,0:T(8,128)S(1)}, s32[18,8,256]{2,1,0:T(8,128)S(1)}, u32[]{:S(2)}, u32[]{:S(2)}) collective-permute-start(s32[18,8,256]{2,1,0:T(8,128)S(1)} %get-tuple-element.22), channel_id=1, source_target_pairs={{0,16},{16,0},{1,17},{17,1},{2,18},{18,2},{3,19},{19,3},{4,20},{20... | collective-permute-start | bytes 442376 | tf_op jit(solution)/shard_map/ppermute | solution.py:556
  2.6 2.8 %collective-permute-start.1 = (s32[8,256]{1,0:T(8,128)S(1)}, s32[8,256]{1,0:T(8,128)S(1)}, u32[]{:S(2)}, u32[]{:S(2)}) collective-permute-start(s32[8,256]{1,0:T(8,128)S(1)} %get-tuple-element.23), channel_id=1, source_target_pairs={{0,4},{1,5},{2,6},{3,7},{4,8},{5,9},{6,10},{7,11},{8,12},{9,13},{1... | collective-permute-start | bytes 24584 | tf_op jit(solution)/shard_map/ppermute | solution.py:557
  3.9 3.4 %collective-permute-start.2 = (s32[8,256]{1,0:T(8,128)S(1)}, s32[8,256]{1,0:T(8,128)S(1)}, u32[]{:S(2)}, u32[]{:S(2)}) collective-permute-start(s32[8,256]{1,0:T(8,128)S(1)} %get-tuple-element.24), channel_id=1, source_target_pairs={{16,4},{17,5},{18,6},{19,7},{20,8},{21,9},{22,10},{23,11},{24,12},... | collective-permute-start | bytes 24584 | tf_op jit(solution)/shard_map/ppermute | solution.py:558
  7.3 4.3 %copy-start = (s32[2]{0:T(128)S(1)}, s32[2]{0:T(128)}, u32[]{:S(2)}) copy-start(s32[2]{0:T(128)} %rank_ref.3) | copy-start | bytes 28
  7.3 6.4 %collective-permute-start.4 = (s32[2,8,128]{2,1,0:T(8,128)S(1)}, s32[2,8,128]{2,1,0:T(8,128)S(1)}, u32[]{:S(2)}, u32[]{:S(2)}) collective-permute-start(s32[2,8,128]{2,1,0:T(8,128)S(1)} %side_columns.1.ends_ref), channel_id=1, source_target_pairs={{1,2},{3,0},{2,1},{0,3},{5,6},{7,4},{6,5},{4,7},{9,10},{11,8},{10,... | collective-permute-start | bytes 24584 | tf_op jit(solution)/shard_map/ppermute | solution.py:574
  10.9 2.9 %collective-permute-start.3 = (s32[2,8,128]{2,1,0:T(8,128)S(1)}, s32[2,8,128]{2,1,0:T(8,128)S(1)}, u32[]{:S(2)}, u32[]{:S(2)}) collective-permute-start(s32[2,8,128]{2,1,0:T(8,128)S(1)} %side_columns.1.ends_ref), channel_id=1, source_target_pairs={{0,1},{2,3},{1,0},{3,2},{4,5},{6,7},{5,4},{7,6},{8,9},{10,11},{9,8... | collective-permute-start | bytes 24584 | tf_op jit(solution)/shard_map/ppermute | solution.py:573

commit v12 on v8

--- a/solution.py
+++ b/solution.py
@@ -258,14 +258,18 @@
 
 def classify_rows(read_cells, tables, cells_ref, layers, tiles):
     total = float(2 * layers)
-    for z in range(layers):
+
+    def one_layer(z, carry):
         for tile in range(tiles):
             even = cell_values(*read_cells(z, 0, tile), tables, total)
             odd = cell_values(*read_cells(z, 1, tile), tables, total)
             for channel in range(4):
-                base = (z * 4 + channel) * 16
+                base = pl.multiple_of((z * 4 + channel) * 16, 16)
                 block = jnp.concatenate([even[channel], odd[channel]], axis=0)
-                cells_ref[base : base + 16, tile * LANES : (tile + 1) * LANES] = block.astype(jnp.bfloat16)
+                cells_ref[pl.ds(base, 16), tile * LANES : (tile + 1) * LANES] = block.astype(jnp.bfloat16)
+        return carry
+
+    lax.fori_loop(0, layers, one_layer, 0, unroll=2)
 
 
 def rounded(value):
@@ -340,42 +344,42 @@
     top = sub_at == 0
     bottom = sub_at == 7
 
-    def one_slab(position, image):
-        slab = position ^ flip
-        view = along_ref.at[pl.ds(pl.multiple_of(slab * (layers * 64), 64), (layers + 2) * 64), :]
-        lines = lines_ref.at[pl.ds(pl.multiple_of(slab * (layers * 16), 16), layers * 16 + 8), :]
-
-        def layer_rows(layer, channel):
-            base = (layer * 4 + channel) * 16
+    def one_layer(step, image):
+        layer = ((step // layers) ^ flip) * layers + step % layers
+        view = along_ref.at[pl.ds(pl.multiple_of(layer * 64, 64), 3 * 64), :]
+        lines = lines_ref.at[pl.ds(pl.multiple_of(layer * 16, 16), 16 + 8), :]
+
+        def layer_rows(offset, channel):
+            base = (offset * 4 + channel) * 16
             return [view[base + part * 8 : base + part * 8 + 8, :] for part in range(2)]
 
-        for z in range(layers):
-            triple = [[3.0 * value for value in layer_rows(z + 1, channel)] for channel in range(4)]
-            for parity in range(2):
-                clear = [1.0 - value for value in image[3]]
-                updated = []
-                for channel in range(4):
-                    beside = layer_rows(z + 2 * parity, channel)
-                    even, odd = [rounded(beside[part] + triple[channel][part]) for part in range(2)]
-                    line = (z * 2 + parity) * 8 + channel
-                    above = lines[pl.ds(line, 8, stride=0), :]
-                    below = lines[pl.ds(line + 4, 8, stride=0), :]
-                    before_even = jnp.where(top, above, pltpu.roll(odd, 1, 0))
-                    after_odd = jnp.where(bottom, below, pltpu.roll(even, 7, 0))
-                    even_centre = 3.0 * even
-                    odd_centre = 3.0 * odd
-                    samples = [
-                        before_even + even_centre,
-                        even_centre + odd,
-                        even + odd_centre,
-                        odd_centre + after_odd,
-                    ]
-                    updated.append([image[channel][i] + clear[i] * samples[i] for i in range(4)])
-                image = updated
+        triple = [[3.0 * value for value in layer_rows(1, channel)] for channel in range(4)]
+        for parity in range(2):
+            clear = [1.0 - value for value in image[3]]
+            updated = []
+            for channel in range(4):
+                beside = layer_rows(2 * parity, channel)
+                even, odd = [rounded(beside[part] + triple[channel][part]) for part in range(2)]
+                line = parity * 8 + channel
+                above = lines[pl.ds(line, 8, stride=0), :]
+                below = lines[pl.ds(line + 4, 8, stride=0), :]
+                before_even = jnp.where(top, above, pltpu.roll(odd, 1, 0))
+                after_odd = jnp.where(bottom, below, pltpu.roll(even, 7, 0))
+                even_centre = 3.0 * even
+                odd_centre = 3.0 * odd
+                samples = [
+                    before_even + even_centre,
+                    even_centre + odd,
+                    even + odd_centre,
+                    odd_centre + after_odd,
+                ]
+                updated.append([image[channel][i] + clear[i] * samples[i] for i in range(4)])
+            image = updated
         return image
 
     zero = jnp.zeros((8, LANES), jnp.float32)
-    return lax.fori_loop(0, 2, one_slab, [[zero] * 4 for _ in range(4)])
+    image = [[zero] * 4 for _ in range(4)]
+    return lax.fori_loop(0, 2 * layers, one_layer, image, unroll=2)
 
 
 def store_tile(image, mixed_ref, out_ref, lanes):

time: 16.4 us -> 17 us (1.037)
  the two profiles are of different devices: /device:TPU:17 before, /device:TPU:9 now
where the time goes in v12:
time: 17 us; the launch traced here: 16.8 us
  Pallas kernels  8.32 us (49%)
  starting transfers between devices  6.16 us (36%)
  waiting for transfers between devices  2.26 us (13%)
    pallas_call x8, Pallas kernels, run(): pl.pallas_call(kernel, out_shape=out_shape, in_specs=in_specs or [VMEM] *...  8.32 us
    ppermute x1, starting transfers between devices, two_slab_device(): across = lax.ppermute(ends, 'bx', both(cross))  3.53 us
    ppermute x1, waiting for transfers between devices, two_slab_device(): second = lax.ppermute(second, axes, both(diagonal))  1.9 us
    ppermute x1, starting transfers between devices, two_slab_device(): first = lax.ppermute(first, axes, ring)  1.3 us
    ppermute x1, starting transfers between devices, two_slab_device(): bulk = lax.ppermute(bulk, 'bz', [(0, 1), (1, 0)])  1.28 us
    ppermute x1, waiting for transfers between devices, two_slab_device(): first = lax.ppermute(first, axes, ring)  0.35 us
  transfers between devices with their start and end apart: 5, of which 2 were waited for; matrix products, arithmetic and copies ran while one was open for 0% of the time, Pallas kernels for 25%

profile of v12, /device:TPU:9, one launch (start us, length us, event | category | flops | bytes accessed | tf_op | source)
XLA Modules:
  0.0 16.8 jit_solution(18086587265725366913)
XLA Ops:
  0.0 1.2 %stage_block.1 = (s32[8,256]{1,0:T(8,128)S(1)}, s32[8,256]{1,0:T(8,128)S(1)}, s32[8,128]{1,0:T(8,128)S(1)}, f32[8,2,40,128]{3,2,1,0:T(8,128)S(1)}, s32[8,2,40,12...) custom-call(f32[8,32,256]{2,1,0:T(8,128)} %density_ref.1, s32[8,32,256]{2,1,0:T(8,128)} %bins_ref.1, ...), custom_call_target="tpu_custom_call" | custom-call | flops 1200000000 | bytes 4320000 | tf_op jit(solution)/shard_map/stage_block/pallas_call | solution.py:513
  1.2 0.1 pack_block.1
  1.3 1.3 %collective-permute-start = (s32[18,8,256]{2,1,0:T(8,128)S(1)}, s32[18,8,256]{2,1,0:T(8,128)S(1)}, u32[]{:S(2)}, u32[]{:S(2)}) collective-permute-start(s32[18,8,256]{2,1,0:T(8,128)S(1)} %get-tuple-element.22), channel_id=1, source_target_pairs={{0,16},{16,0},{1,17},{17,1},{2,18},{18,2},{3,19},{19,3},{4,20},{20... | collective-permute-start | bytes 442376 | tf_op jit(solution)/shard_map/ppermute | solution.py:561
  2.6 1.3 %collective-permute-start.1 = (s32[8,256]{1,0:T(8,128)S(1)}, s32[8,256]{1,0:T(8,128)S(1)}, u32[]{:S(2)}, u32[]{:S(2)}) collective-permute-start(s32[8,256]{1,0:T(8,128)S(1)} %get-tuple-element.23), channel_id=1, source_target_pairs={{0,4},{1,5},{2,6},{3,7},{4,8},{5,9},{6,10},{7,11},{8,12},{9,13},{1... | collective-permute-start | bytes 24584 | tf_op jit(solution)/shard_map/ppermute | solution.py:562
  3.9 0.1 collective-permute-start.2
  3.9 0.8 %own_cells.1 = (bf16[512,256]{1,0:T(8,128)(2,1)S(1)}, bf16[384,512]{1,0:T(8,128)(2,1)S(1)}) custom-call(f32[8,2,40,128]{3,2,1,0:T(8,128)S(1)} %get-tuple-element.18.dense_ref, s32[8,2,40,128]{3,2,1,0:T(8,128)S(1)} %get-tuple-element.19.index_ref, f32[8,8,128]{2,1,0:T(8,128)S(1)} %get-tuple-element.17.tables_ref), custom_call_target="tpu_custom_call" | custom-call | flops 500000000 | bytes 1800000 | tf_op jit(solution)/shard_map/own_cells/pallas_call | solution.py:513
  4.7 0.3 %own_slab.1.along_ref.own_ref = f32[4,1152,128]{2,1,0:T(8,128)S(1)} custom-call(bf16[512,256]{1,0:T(8,128)(2,1)S(1)} %get-tuple-element.25.cells_ref, bf16[384,512]{1,0:T(8,128)(2,1)S(1)} %get-tuple-element.20.weights_ref), custom_call_target="tpu_custom_call" | custom-call | flops 400000000 | bytes 1440000 | tf_op jit(solution)/shard_map/own_slab/pallas_call | solution.py:513
  5.0 0.4 %collective-permute-done.1.first_ref = s32[8,256]{1,0:T(8,128)S(1)} collective-permute-done((s32[8,256]{1,0:T(8,128)S(1)}, s32[8,256]{1,0:T(8,128)S(1)}, u32[]{:S(2)}, u32[]{:S(2)}) %collective-permute-start.1) | collective-permute-done | bytes 8224 | tf_op jit(solution)/shard_map/ppermute | solution.py:562
  5.4 1.9 %collective-permute-done.2.second_ref = s32[8,256]{1,0:T(8,128)S(1)} collective-permute-done((s32[8,256]{1,0:T(8,128)S(1)}, s32[8,256]{1,0:T(8,128)S(1)}, u32[]{:S(2)}, u32[]{:S(2)}) %collective-permute-start.2) | collective-permute-done | bytes 8224 | tf_op jit(solution)/shard_map/ppermute | solution.py:563
  7.3 0.0 collective-permute-done.bulk_ref
  7.3 0.1 side_columns.1.ends_ref
  7.3 0.0 copy-start
  7.3 3.5 %collective-permute-start.4 = (s32[2,8,128]{2,1,0:T(8,128)S(1)}, s32[2,8,128]{2,1,0:T(8,128)S(1)}, u32[]{:S(2)}, u32[]{:S(2)}) collective-permute-start(s32[2,8,128]{2,1,0:T(8,128)S(1)} %side_columns.1.ends_ref), channel_id=1, source_target_pairs={{1,2},{3,0},{2,1},{0,3},{5,6},{7,4},{6,5},{4,7},{9,10},{11,8},{10,... | collective-permute-start | bytes 24584 | tf_op jit(solution)/shard_map/ppermute | solution.py:579
  10.9 0.0 collective-permute-start.3
  10.9 1.0 %other_slab.1.along_ref = f32[4,1152,128]{2,1,0:T(8,128)S(1)} custom-call(s32[18,8,256]{2,1,0:T(8,128)S(1)} %collective-permute-done.bulk_ref, f32[8,8,128]{2,1,0:T(8,128)S(1)} %get-tuple-element.17.tables_ref, bf16[384,512]{1,0:T(8,128)(2,1)S(1)} %get-tuple-element.20.weights_ref, ...), custom_call_target="tpu_custom_call", output_to_operand_aliasing={{}: (4, {})} | custom-call | flops 800000000 | bytes 2880000 | tf_op jit(solution)/shard_map/other_slab/pallas_call | solution.py:513
  11.9 0.0 copy-done
  11.9 2.1 %inner_tiles.1 = (f32[4,32,256]{2,1,0:T(8,128)S(1)}, f32[2,128,128]{2,1,0:T(8,128)S(1)}) custom-call(s32[2]{0:T(128)S(1)} %copy-done, f32[8,8,128]{2,1,0:T(8,128)S(1)} %get-tuple-element.17.tables_ref, bf16[384,512]{1,0:T(8,128)(2,1)S(1)} %get-tuple-element.20.weights_ref, s32[18,8,256]{2,1,0:T(8,128)S(1)} %collective-permute-done.bulk_ref, ...), custom_call_target="tpu_custom_call" | custom-call | flops 2000000000 | bytes 7200000 | tf_op jit(solution)/shard_map/inner_tiles/pallas_call | solution.py:513
  14.0 0.0 collective-permute-done.4.across_ref
  14.0 0.0 collective-permute-done.3.beside_ref
  14.0 2.8 %outer_tiles.1 = f32[4,32,512]{2,1,0:T(8,128)} custom-call(s32[2]{0:T(128)S(1)} %copy-done, f32[8,8,128]{2,1,0:T(8,128)S(1)} %get-tuple-element.17.tables_ref, bf16[384,512]{1,0:T(8,128)(2,1)S(1)} %get-tuple-element.20.weights_ref, s32[2,8,128]{2,1,0:T(8,128)S(1)} %collective-permute-done.3.beside_ref, s32[2,8,128]{2,1,0:T(8,128)S(1)} %collective-permute-done.4.across_ref, ...), custom_call_target="tpu_custom_call" | custom-call | flops 2000000000 | bytes 7200000 | tf_op jit(solution)/shard_map/outer_tiles/pallas_call | solution.py:513
Async XLA Ops:
  1.3 6.0 %collective-permute-start = (s32[18,8,256]{2,1,0:T(8,128)S(1)}, s32[18,8,256]{2,1,0:T(8,128)S(1)}, u32[]{:S(2)}, u32[]{:S(2)}) collective-permute-start(s32[18,8,256]{2,1,0:T(8,128)S(1)} %get-tuple-element.22), channel_id=1, source_target_pairs={{0,16},{16,0},{1,17},{17,1},{2,18},{18,2},{3,19},{19,3},{4,20},{20... | collective-permute-start | bytes 442376 | tf_op jit(solution)/shard_map/ppermute | solution.py:561
  2.6 2.8 %collective-permute-start.1 = (s32[8,256]{1,0:T(8,128)S(1)}, s32[8,256]{1,0:T(8,128)S(1)}, u32[]{:S(2)}, u32[]{:S(2)}) collective-permute-start(s32[8,256]{1,0:T(8,128)S(1)} %get-tuple-element.23), channel_id=1, source_target_pairs={{0,4},{1,5},{2,6},{3,7},{4,8},{5,9},{6,10},{7,11},{8,12},{9,13},{1... | collective-permute-start | bytes 24584 | tf_op jit(solution)/shard_map/ppermute | solution.py:562
  3.9 3.4 %collective-permute-start.2 = (s32[8,256]{1,0:T(8,128)S(1)}, s32[8,256]{1,0:T(8,128)S(1)}, u32[]{:S(2)}, u32[]{:S(2)}) collective-permute-start(s32[8,256]{1,0:T(8,128)S(1)} %get-tuple-element.24), channel_id=1, source_target_pairs={{16,4},{17,5},{18,6},{19,7},{20,8},{21,9},{22,10},{23,11},{24,12},... | collective-permute-start | bytes 24584 | tf_op jit(solution)/shard_map/ppermute | solution.py:563
  7.3 4.6 %copy-start = (s32[2]{0:T(128)S(1)}, s32[2]{0:T(128)}, u32[]{:S(2)}) copy-start(s32[2]{0:T(128)} %rank_ref.3) | copy-start | bytes 28
  7.3 6.6 %collective-permute-start.4 = (s32[2,8,128]{2,1,0:T(8,128)S(1)}, s32[2,8,128]{2,1,0:T(8,128)S(1)}, u32[]{:S(2)}, u32[]{:S(2)}) collective-permute-start(s32[2,8,128]{2,1,0:T(8,128)S(1)} %side_columns.1.ends_ref), channel_id=1, source_target_pairs={{1,2},{3,0},{2,1},{0,3},{5,6},{7,4},{6,5},{4,7},{9,10},{11,8},{10,... | collective-permute-start | bytes 24584 | tf_op jit(solution)/shard_map/ppermute | solution.py:579
  10.9 3.1 %collective-permute-start.3 = (s32[2,8,128]{2,1,0:T(8,128)S(1)}, s32[2,8,128]{2,1,0:T(8,128)S(1)}, u32[]{:S(2)}, u32[]{:S(2)}) collective-permute-start(s32[2,8,128]{2,1,0:T(8,128)S(1)} %side_columns.1.ends_ref), channel_id=1, source_target_pairs={{0,1},{2,3},{1,0},{3,2},{4,5},{6,7},{5,4},{7,6},{8,9},{10,11},{9,8... | collective-permute-start | bytes 24584 | tf_op jit(solution)/shard_map/ppermute | solution.py:578

commit v13 on v8

--- a/solution.py
+++ b/solution.py
@@ -214,7 +214,7 @@
     return jnp.where(has_near(me == 0), words, 0)
 
 
-def side_kernel(columns_ref, bulk_ref, first_ref, second_ref, along_ref, ends_ref):
+def side_kernel(columns_ref, bulk_ref, second_ref, first_ref, along_ref, ends_ref):
     layers = columns_ref.shape[0]
     front = lax.axis_index("bz") == 0
     lane_at = lax.broadcasted_iota(jnp.int32, (layers, LANES), 1)
@@ -347,16 +347,16 @@
 
         def layer_rows(layer, channel):
             base = (layer * 4 + channel) * 16
-            return [view[base + part * 8 : base + part * 8 + 8, :] for part in range(2)]
+            return view[base : base + 16, :]
 
         for z in range(layers):
-            triple = [[3.0 * value for value in layer_rows(z + 1, channel)] for channel in range(4)]
+            triple = [3.0 * layer_rows(z + 1, channel) for channel in range(4)]
             for parity in range(2):
                 clear = [1.0 - value for value in image[3]]
                 updated = []
                 for channel in range(4):
-                    beside = layer_rows(z + 2 * parity, channel)
-                    even, odd = [rounded(beside[part] + triple[channel][part]) for part in range(2)]
+                    both = rounded(layer_rows(z + 2 * parity, channel) + triple[channel])
+                    even, odd = both[0:8], both[8:16]
                     line = (z * 2 + parity) * 8 + channel
                     above = lines[pl.ds(line, 8, stride=0), :]
                     below = lines[pl.ds(line + 4, 8, stride=0), :]
@@ -386,7 +386,7 @@
 
 
 def inner_kernel(
-    rank_ref, tables_ref, weights_ref, bulk_ref, inside_ref, first_ref, second_ref, along_ref,
+    rank_ref, tables_ref, weights_ref, bulk_ref, inside_ref, second_ref, first_ref, along_ref,
     image_ref, edge_ref, cells_ref, lines_ref, mixed_ref,
 ):
     layers, cols = inside_ref.shape
@@ -567,7 +567,7 @@
     whole = pltpu.VMEM((tiles, 2 * size + 2 * 4 * half, LANES), f32)
     along = call(own_kernel, "own_slab", whole, 0.4)(cells, weights)
     ends = call(side_kernel, "side_columns", pltpu.VMEM((2, layers, LANES), i32), 0.1)(
-        columns, bulk, first, second, along
+        columns, bulk, second, first, along
     )
     pairs = [(x, x + 1) for x in range(0, count_x, 2)]
     cross = [(x, (x + 1) % count_x) for x in range(1, count_x, 2)]
@@ -585,7 +585,7 @@
         2.0,
         [pltpu.VMEM((cols // LANES, 16 * layers + 8, LANES), f32), lines, pltpu.VMEM((4, rows + 8, LANES), f32)],
         [smem] + [VMEM] * 7,
-    )(slab_rank, tables, weights, bulk, inside, first, second, along)
+    )(slab_rank, tables, weights, bulk, inside, second, first, along)
     return call(
         outer_kernel,
         "outer_tiles",

time: 16.4 us -> 16.2 us (0.988)
  the two profiles are of different devices: /device:TPU:17 before, /device:TPU:0 now
where the time goes in v13:
time: 16.2 us; the launch traced here: 16 us
  Pallas kernels  7.49 us (46%)
  starting transfers between devices  6.23 us (38%)
  waiting for transfers between devices  2.24 us (14%)
    pallas_call x8, Pallas kernels, run(): pl.pallas_call(kernel, out_shape=out_shape, in_specs=in_specs or [VMEM] *...  7.49 us
    ppermute x1, starting transfers between devices, two_slab_device(): bulk = lax.ppermute(bulk, 'bz', [(0, 1), (1, 0)])  3 us
    ppermute x1, waiting for transfers between devices, two_slab_device(): first = lax.ppermute(first, axes, ring)  2.23 us
    ppermute x1, starting transfers between devices, two_slab_device(): beside = lax.ppermute(ends, 'bx', both(pairs))  1.62 us
    ppermute x1, starting transfers between devices, two_slab_device(): first = lax.ppermute(first, axes, ring)  1.58 us
  transfers between devices with their start and end apart: 5, of which 1 were waited for; matrix products, arithmetic and copies ran while one was open for 0% of the time, Pallas kernels for 22%

profile of v13, /device:TPU:0, one launch (start us, length us, event | category | flops | bytes accessed | tf_op | source)
XLA Modules:
  0.0 16.0 jit_solution(17611955595844122123)
XLA Ops:
  0.0 1.2 %stage_block.1 = (s32[8,256]{1,0:T(8,128)S(1)}, s32[8,256]{1,0:T(8,128)S(1)}, s32[8,128]{1,0:T(8,128)S(1)}, f32[8,2,40,128]{3,2,1,0:T(8,128)S(1)}, s32[8,2,40,12...) custom-call(f32[8,32,256]{2,1,0:T(8,128)} %density_ref.1, s32[8,32,256]{2,1,0:T(8,128)} %bins_ref.1, ...), custom_call_target="tpu_custom_call" | custom-call | flops 1200000000 | bytes 4320000 | tf_op jit(solution)/shard_map/stage_block/pallas_call | solution.py:509
  1.2 0.1 pack_block.1
  1.3 3.0 %collective-permute-start = (s32[18,8,256]{2,1,0:T(8,128)S(1)}, s32[18,8,256]{2,1,0:T(8,128)S(1)}, u32[]{:S(2)}, u32[]{:S(2)}) collective-permute-start(s32[18,8,256]{2,1,0:T(8,128)S(1)} %get-tuple-element.22), channel_id=1, source_target_pairs={{0,16},{16,0},{1,17},{17,1},{2,18},{18,2},{3,19},{19,3},{4,20},{20... | collective-permute-start | bytes 442376 | tf_op jit(solution)/shard_map/ppermute | solution.py:557
  4.3 0.0 collective-permute-start.1
  4.3 1.6 %collective-permute-start.2 = (s32[8,256]{1,0:T(8,128)S(1)}, s32[8,256]{1,0:T(8,128)S(1)}, u32[]{:S(2)}, u32[]{:S(2)}) collective-permute-start(s32[8,256]{1,0:T(8,128)S(1)} %get-tuple-element.24), channel_id=1, source_target_pairs={{0,4},{1,5},{2,6},{3,7},{4,8},{5,9},{6,10},{7,11},{8,12},{9,13},{1... | collective-permute-start | bytes 24584 | tf_op jit(solution)/shard_map/ppermute | solution.py:558
  5.9 0.5 %own_cells.1 = (bf16[512,256]{1,0:T(8,128)(2,1)S(1)}, bf16[384,512]{1,0:T(8,128)(2,1)S(1)}) custom-call(f32[8,2,40,128]{3,2,1,0:T(8,128)S(1)} %get-tuple-element.18.dense_ref, s32[8,2,40,128]{3,2,1,0:T(8,128)S(1)} %get-tuple-element.19.index_ref, f32[8,8,128]{2,1,0:T(8,128)S(1)} %get-tuple-element.17.tables_ref), custom_call_target="tpu_custom_call" | custom-call | flops 500000000 | bytes 1800000 | tf_op jit(solution)/shard_map/own_cells/pallas_call | solution.py:509
  6.4 0.3 %own_slab.1.along_ref.own_ref = f32[4,1152,128]{2,1,0:T(8,128)S(1)} custom-call(bf16[512,256]{1,0:T(8,128)(2,1)S(1)} %get-tuple-element.25.cells_ref, bf16[384,512]{1,0:T(8,128)(2,1)S(1)} %get-tuple-element.20.weights_ref), custom_call_target="tpu_custom_call" | custom-call | flops 400000000 | bytes 1440000 | tf_op jit(solution)/shard_map/own_slab/pallas_call | solution.py:509
  6.7 0.0 collective-permute-done.1.second_ref
  6.7 2.2 %collective-permute-done.2.first_ref = s32[8,256]{1,0:T(8,128)S(1)} collective-permute-done((s32[8,256]{1,0:T(8,128)S(1)}, s32[8,256]{1,0:T(8,128)S(1)}, u32[]{:S(2)}, u32[]{:S(2)}) %collective-permute-start.2) | collective-permute-done | bytes 8224 | tf_op jit(solution)/shard_map/ppermute | solution.py:558
  9.0 0.0 collective-permute-done.bulk_ref
  9.0 0.1 side_columns.1.ends_ref
  9.0 0.0 copy-start
  9.0 0.0 collective-permute-start.4
  9.1 1.6 %collective-permute-start.3 = (s32[2,8,128]{2,1,0:T(8,128)S(1)}, s32[2,8,128]{2,1,0:T(8,128)S(1)}, u32[]{:S(2)}, u32[]{:S(2)}) collective-permute-start(s32[2,8,128]{2,1,0:T(8,128)S(1)} %side_columns.1.ends_ref), channel_id=1, source_target_pairs={{0,1},{2,3},{1,0},{3,2},{4,5},{6,7},{5,4},{7,6},{8,9},{10,11},{9,8... | collective-permute-start | bytes 24584 | tf_op jit(solution)/shard_map/ppermute | solution.py:574
  10.7 0.8 %other_slab.1.along_ref = f32[4,1152,128]{2,1,0:T(8,128)S(1)} custom-call(s32[18,8,256]{2,1,0:T(8,128)S(1)} %collective-permute-done.bulk_ref, f32[8,8,128]{2,1,0:T(8,128)S(1)} %get-tuple-element.17.tables_ref, bf16[384,512]{1,0:T(8,128)(2,1)S(1)} %get-tuple-element.20.weights_ref, ...), custom_call_target="tpu_custom_call", output_to_operand_aliasing={{}: (4, {})} | custom-call | flops 800000000 | bytes 2880000 | tf_op jit(solution)/shard_map/other_slab/pallas_call | solution.py:509
  11.5 0.0 copy-done
  11.5 1.9 %inner_tiles.1 = (f32[4,32,256]{2,1,0:T(8,128)S(1)}, f32[2,128,128]{2,1,0:T(8,128)S(1)}) custom-call(s32[2]{0:T(128)S(1)} %copy-done, f32[8,8,128]{2,1,0:T(8,128)S(1)} %get-tuple-element.17.tables_ref, bf16[384,512]{1,0:T(8,128)(2,1)S(1)} %get-tuple-element.20.weights_ref, s32[18,8,256]{2,1,0:T(8,128)S(1)} %collective-permute-done.bulk_ref, ...), custom_call_target="tpu_custom_call" | custom-call | flops 2000000000 | bytes 7200000 | tf_op jit(solution)/shard_map/inner_tiles/pallas_call | solution.py:509
  13.4 0.0 collective-permute-done.4.across_ref
  13.4 0.0 collective-permute-done.3.beside_ref
  13.4 2.6 %outer_tiles.1 = f32[4,32,512]{2,1,0:T(8,128)} custom-call(s32[2]{0:T(128)S(1)} %copy-done, f32[8,8,128]{2,1,0:T(8,128)S(1)} %get-tuple-element.17.tables_ref, bf16[384,512]{1,0:T(8,128)(2,1)S(1)} %get-tuple-element.20.weights_ref, s32[2,8,128]{2,1,0:T(8,128)S(1)} %collective-permute-done.3.beside_ref, s32[2,8,128]{2,1,0:T(8,128)S(1)} %collective-permute-done.4.across_ref, ...), custom_call_target="tpu_custom_call" | custom-call | flops 2000000000 | bytes 7200000 | tf_op jit(solution)/shard_map/outer_tiles/pallas_call | solution.py:509
Async XLA Ops:
  1.3 7.7 %collective-permute-start = (s32[18,8,256]{2,1,0:T(8,128)S(1)}, s32[18,8,256]{2,1,0:T(8,128)S(1)}, u32[]{:S(2)}, u32[]{:S(2)}) collective-permute-start(s32[18,8,256]{2,1,0:T(8,128)S(1)} %get-tuple-element.22), channel_id=1, source_target_pairs={{0,16},{16,0},{1,17},{17,1},{2,18},{18,2},{3,19},{19,3},{4,20},{20... | collective-permute-start | bytes 442376 | tf_op jit(solution)/shard_map/ppermute | solution.py:557
  4.3 2.4 %collective-permute-start.1 = (s32[8,256]{1,0:T(8,128)S(1)}, s32[8,256]{1,0:T(8,128)S(1)}, u32[]{:S(2)}, u32[]{:S(2)}) collective-permute-start(s32[8,256]{1,0:T(8,128)S(1)} %get-tuple-element.23), channel_id=1, source_target_pairs={{16,4},{17,5},{18,6},{19,7},{20,8},{21,9},{22,10},{23,11},{24,12},... | collective-permute-start | bytes 24584 | tf_op jit(solution)/shard_map/ppermute | solution.py:559
  4.3 4.7 %collective-permute-start.2 = (s32[8,256]{1,0:T(8,128)S(1)}, s32[8,256]{1,0:T(8,128)S(1)}, u32[]{:S(2)}, u32[]{:S(2)}) collective-permute-start(s32[8,256]{1,0:T(8,128)S(1)} %get-tuple-element.24), channel_id=1, source_target_pairs={{0,4},{1,5},{2,6},{3,7},{4,8},{5,9},{6,10},{7,11},{8,12},{9,13},{1... | collective-permute-start | bytes 24584 | tf_op jit(solution)/shard_map/ppermute | solution.py:558
  9.0 2.5 %copy-start = (s32[2]{0:T(128)S(1)}, s32[2]{0:T(128)}, u32[]{:S(2)}) copy-start(s32[2]{0:T(128)} %rank_ref.3) | copy-start | bytes 28
  9.0 4.3 %collective-permute-start.4 = (s32[2,8,128]{2,1,0:T(8,128)S(1)}, s32[2,8,128]{2,1,0:T(8,128)S(1)}, u32[]{:S(2)}, u32[]{:S(2)}) collective-permute-start(s32[2,8,128]{2,1,0:T(8,128)S(1)} %side_columns.1.ends_ref), channel_id=1, source_target_pairs={{1,2},{3,0},{2,1},{0,3},{5,6},{7,4},{6,5},{4,7},{9,10},{11,8},{10,... | collective-permute-start | bytes 24584 | tf_op jit(solution)/shard_map/ppermute | solution.py:575
  9.1 4.3 %collective-permute-start.3 = (s32[2,8,128]{2,1,0:T(8,128)S(1)}, s32[2,8,128]{2,1,0:T(8,128)S(1)}, u32[]{:S(2)}, u32[]{:S(2)}) collective-permute-start(s32[2,8,128]{2,1,0:T(8,128)S(1)} %side_columns.1.ends_ref), channel_id=1, source_target_pairs={{0,1},{2,3},{1,0},{3,2},{4,5},{6,7},{5,4},{7,6},{8,9},{10,11},{9,8... | collective-permute-start | bytes 24584 | tf_op jit(solution)/shard_map/ppermute | solution.py:574

commit v14 on v13

--- a/solution.py
+++ b/solution.py
@@ -214,7 +214,7 @@
     return jnp.where(has_near(me == 0), words, 0)
 
 
-def side_kernel(columns_ref, bulk_ref, second_ref, first_ref, along_ref, ends_ref):
+def side_kernel(columns_ref, bulk_ref, second_ref, first_ref, part_ref, ends_ref):
     layers = columns_ref.shape[0]
     front = lax.axis_index("bz") == 0
     lane_at = lax.broadcasted_iota(jnp.int32, (layers, LANES), 1)
@@ -324,58 +324,138 @@
     along_columns(cells_ref[...], weights_ref, store)
 
 
-def edge_lines(now, lines_ref, depth):
+def edge_cells(near, inside, tables, cells_ref, front, base, depth):
+    layers, cols = near.shape
+    for side in range(2):
+        use_near = front if side == 0 else jnp.logical_not(front)
+        words = jnp.where(use_near, near, inside)
+        for t in range(cols // LANES):
+            values = cell_values(
+                *unpack_words(words[:, t * LANES : (t + 1) * LANES]), tables, float(depth)
+            )
+            for channel in range(4):
+                at = pl.ds(base + side * 4 + channel, layers, stride=8)
+                cells_ref[t, at, :] = values[channel]
+
+
+def edge_columns(cells_ref, count, weights_ref):
+    return sum(
+        jnp.dot(
+            cells_ref[t, 0:count].astype(jnp.bfloat16),
+            weights_ref[t * LANES : (t + 1) * LANES, :],
+            preferred_element_type=jnp.float32,
+        )
+        for t in range(cells_ref.shape[0])
+    )
+
+
+def edge_lines(now, lines_ref, before=None, after=None):
+    depth = now.shape[0] // 8
     triple = 3.0 * now
     empty = jnp.zeros((8, LANES), jnp.float32)
+    rows = [now[layer * 8 : layer * 8 + 8] for layer in range(depth)]
+    rows = [empty if before is None else before] + rows + [empty if after is None else after]
     for layer in range(depth):
         here = triple[layer * 8 : layer * 8 + 8]
-        before = now[layer * 8 - 8 : layer * 8] if layer > 0 else empty
-        after = now[layer * 8 + 8 : layer * 8 + 16] if layer + 1 < depth else empty
-        lines_ref[layer * 16 : layer * 16 + 8, :] = rounded(before + here)
-        lines_ref[layer * 16 + 8 : layer * 16 + 16, :] = rounded(after + here)
+        for parity in range(2):
+            at = layer * 16 + parity * 8
+            lines_ref[at : at + 8, :] = rounded(rows[layer + 2 * parity] + here)
+
+
+def row_samples(both, above, below):
+    sub_at = lax.broadcasted_iota(jnp.int32, (8, LANES), 0)
+    even, odd = both[0:8], both[8:16]
+    before_even = jnp.where(sub_at == 0, above, pltpu.roll(odd, 1, 0))
+    after_odd = jnp.where(sub_at == 7, below, pltpu.roll(even, 7, 0))
+    even_centre = 3.0 * even
+    odd_centre = 3.0 * odd
+    return [before_even + even_centre, even_centre + odd, even + odd_centre, odd_centre + after_odd]
+
+
+def over_layers(view, lines, layers, image, keep_first=None, keep_last=None):
+    def layer_rows(layer, channel):
+        base = (layer * 4 + channel) * 16
+        return view[base : base + 16, :]
+
+    for z in range(layers):
+        triple = [3.0 * layer_rows(z + 1, channel) for channel in range(4)]
+        for parity in range(2):
+            keep = None
+            if (z, parity) == (0, 0):
+                keep = keep_first
+            if (z, parity) == (layers - 1, 1):
+                keep = keep_last
+            clear = [1.0 - value for value in image[3]]
+            updated = []
+            for channel in range(4):
+                both = rounded(layer_rows(z + 2 * parity, channel) + triple[channel])
+                line = (z * 2 + parity) * 8 + channel
+                above = lines[pl.ds(line, 8, stride=0), :]
+                below = lines[pl.ds(line + 4, 8, stride=0), :]
+                samples = row_samples(both, above, below)
+                if keep is not None:
+                    samples = [jnp.where(keep, sample, 0.0) for sample in samples]
+                updated.append([image[channel][i] + clear[i] * samples[i] for i in range(4)])
+            image = updated
+    return image
+
+
+def empty_image():
+    zero = jnp.zeros((8, LANES), jnp.float32)
+    return [[zero] * 4 for _ in range(4)]
+
+
+def slab_views(along_ref, lines_ref, slab, layers):
+    along_at = pl.multiple_of(slab * (layers * 64), 64)
+    lines_at = pl.multiple_of(slab * (layers * 16), 16)
+    return (
+        along_ref.at[pl.ds(along_at, (layers + 2) * 64), :],
+        lines_ref.at[pl.ds(lines_at, layers * 16 + 8), :],
+    )
 
 
 def render_tile(along_ref, lines_ref, flip, layers):
-    sub_at = lax.broadcasted_iota(jnp.int32, (8, LANES), 0)
-    top = sub_at == 0
-    bottom = sub_at == 7
-
     def one_slab(position, image):
-        slab = position ^ flip
-        view = along_ref.at[pl.ds(pl.multiple_of(slab * (layers * 64), 64), (layers + 2) * 64), :]
-        lines = lines_ref.at[pl.ds(pl.multiple_of(slab * (layers * 16), 16), layers * 16 + 8), :]
-
-        def layer_rows(layer, channel):
-            base = (layer * 4 + channel) * 16
-            return view[base : base + 16, :]
-
-        for z in range(layers):
-            triple = [3.0 * layer_rows(z + 1, channel) for channel in range(4)]
-            for parity in range(2):
-                clear = [1.0 - value for value in image[3]]
-                updated = []
-                for channel in range(4):
-                    both = rounded(layer_rows(z + 2 * parity, channel) + triple[channel])
-                    even, odd = both[0:8], both[8:16]
-                    line = (z * 2 + parity) * 8 + channel
-                    above = lines[pl.ds(line, 8, stride=0), :]
-                    below = lines[pl.ds(line + 4, 8, stride=0), :]
-                    before_even = jnp.where(top, above, pltpu.roll(odd, 1, 0))
-                    after_odd = jnp.where(bottom, below, pltpu.roll(even, 7, 0))
-                    even_centre = 3.0 * even
-                    odd_centre = 3.0 * odd
-                    samples = [
-                        before_even + even_centre,
-                        even_centre + odd,
-                        even + odd_centre,
-                        odd_centre + after_odd,
-                    ]
-                    updated.append([image[channel][i] + clear[i] * samples[i] for i in range(4)])
-                image = updated
-        return image
-
-    zero = jnp.zeros((8, LANES), jnp.float32)
-    return lax.fori_loop(0, 2, one_slab, [[zero] * 4 for _ in range(4)])
+        view, lines = slab_views(along_ref, lines_ref, position ^ flip, layers)
+        return over_layers(view, lines, layers, image)
+
+    return lax.fori_loop(0, 2, one_slab, empty_image())
+
+
+def own_tiles_kernel(
+    tables_ref, weights_ref, inside_ref, first_ref, along_ref,
+    part_ref, edge_ref, cells_ref, lines_ref,
+):
+    layers, cols = inside_ref.shape
+    me = lax.axis_index("bz")
+    front = me == 0
+    near = jnp.where(has_near(front), first_ref[...], 0)
+    edge_cells(near, inside_ref[...], read_tables(tables_ref), cells_ref, front, 0, 2 * layers)
+    edge = edge_columns(cells_ref, 8 * layers, weights_ref)
+    edge_ref[...] = edge
+    edge = rounded(edge)
+    tiles = edge.shape[1] // LANES
+    for index in range(tiles - 2):
+        edge_lines(edge[:, (index + 1) * LANES : (index + 2) * LANES], lines_ref.at[index])
+
+    def one_tile(index, carry):
+        view, _ = slab_views(along_ref.at[index + 1], lines_ref.at[index], me, layers)
+        image = over_layers(
+            view, lines_ref.at[index], layers, empty_image(), front, jnp.logical_not(front)
+        )
+        for channel in range(4):
+            for i in range(4):
+                part_ref[index, channel * 4 + i] = image[channel][i]
+        return carry
+
+    lax.fori_loop(0, tiles - 2, one_tile, 0)
+
+
+def joined(first, in_front, behind):
+    top = [[jnp.where(first, x, y) for x, y in zip(a, b)] for a, b in zip(in_front, behind)]
+    low = [[jnp.where(first, y, x) for x, y in zip(a, b)] for a, b in zip(in_front, behind)]
+    clear = [1.0 - value for value in top[3]]
+    return [[top[c][i] + clear[i] * low[c][i] for i in range(4)] for c in range(4)]
 
 
 def store_tile(image, mixed_ref, out_ref, lanes):
@@ -386,45 +466,52 @@
 
 
 def inner_kernel(
-    rank_ref, tables_ref, weights_ref, bulk_ref, inside_ref, second_ref, first_ref, along_ref,
-    image_ref, edge_ref, cells_ref, lines_ref, mixed_ref,
+    rank_ref, tables_ref, weights_ref, bulk_ref, second_ref, own_edge_ref, part_ref, along_ref,
+    image_ref, edge_ref, cells_ref, lines_ref, between_ref, mixed_ref,
 ):
-    layers, cols = inside_ref.shape
-    depth = 2 * layers
+    cols = bulk_ref.shape[2]
+    layers = (bulk_ref.shape[0] - 2) // 2
     tiles = 2 * cols // LANES
     me = lax.axis_index("bz")
     front = me == 0
-    tables = read_tables(tables_ref)
-    for slab in range(2):
-        inside = jnp.where(me == slab, inside_ref[...], bulk_ref[2 * layers])
-        near = near_words(slab, first_ref, second_ref)
-        for side in range(2):
-            use_near = front if side == 0 else jnp.logical_not(front)
-            words = jnp.where(use_near, near, inside)
-            for t in range(cols // LANES):
-                values = cell_values(
-                    *unpack_words(words[:, t * LANES : (t + 1) * LANES]), tables, float(depth)
-                )
-                for channel in range(4):
-                    at = pl.ds(slab * layers * 8 + side * 4 + channel, layers, stride=8)
-                    cells_ref[t, at, :] = values[channel]
-    edge = sum(
-        jnp.dot(
-            cells_ref[t, 0 : 8 * depth].astype(jnp.bfloat16),
-            weights_ref[t * LANES : (t + 1) * LANES, :],
-            preferred_element_type=jnp.float32,
-        )
-        for t in range(cols // LANES)
-    )
+    near = jnp.where(has_near(front), second_ref[...], 0)
+    edge_cells(near, bulk_ref[2 * layers], read_tables(tables_ref), cells_ref, front, 0, 2 * layers)
+    edge = edge_columns(cells_ref, 8 * layers, weights_ref)
     for tile in range(tiles):
-        now = edge[:, tile * LANES : (tile + 1) * LANES]
+        lanes = slice(tile * LANES, (tile + 1) * LANES)
+        mine, theirs = own_edge_ref[:, lanes], edge[:, lanes]
         if tile in (0, tiles - 1):
-            edge_ref[0 if tile == 0 else 1] = now
+            index = 0 if tile == 0 else 1
+            edge_ref[index, 0 : 8 * layers] = jnp.where(front, mine, theirs)
+            edge_ref[index, 8 * layers : 16 * layers] = jnp.where(front, theirs, mine)
         else:
-            edge_lines(rounded(now), lines_ref.at[tile - 1], depth)
+            mine, theirs = rounded(mine), rounded(theirs)
+            index = tile - 1
+            before = jnp.where(front, mine[8 * layers - 8 :], 0.0)
+            after = jnp.where(front, 0.0, mine[0:8])
+            edge_lines(theirs, lines_ref.at[index], before, after)
+            here = jnp.where(front, mine[8 * layers - 8 :], mine[0:8])
+            beside = jnp.where(front, theirs[0:8], theirs[8 * layers - 8 :])
+            between_ref[index, 0:8] = rounded(beside + 3.0 * here)
+
+    flip = rank_ref[0]
 
     def one_tile(index, carry):
-        image = render_tile(along_ref.at[index + 1], lines_ref.at[index], rank_ref[0], layers)
+        along = along_ref.at[index + 1]
+        view, _ = slab_views(along, lines_ref.at[index], 1 - me, layers)
+        other = over_layers(view, lines_ref.at[index], layers, empty_image())
+        here_at = pl.multiple_of(jnp.where(front, layers, layers + 1) * 64, 64)
+        beside_at = pl.multiple_of(jnp.where(front, layers + 1, layers) * 64, 64)
+        between = []
+        for channel in range(4):
+            here = along[pl.ds(here_at + channel * 16, 16), :]
+            beside = along[pl.ds(beside_at + channel * 16, 16), :]
+            above = between_ref[index, pl.ds(channel, 8, stride=0), :]
+            below = between_ref[index, pl.ds(channel + 4, 8, stride=0), :]
+            between.append(row_samples(rounded(beside + 3.0 * here), above, below))
+        part = [[part_ref[index, channel * 4 + i] for i in range(4)] for channel in range(4)]
+        mine = joined(front, part, between)
+        image = joined((me ^ flip) == 0, mine, other)
         store_tile(image, mixed_ref, image_ref, pl.ds(pl.multiple_of(index * LANES, LANES), LANES))
         return carry
 
@@ -484,7 +571,7 @@
         fixed_ref[index, pad : pad + 2 * size, :] = rounded(
             along_ref[tile, pad : pad + 2 * size, :] + block[0 : 2 * size]
         )
-        edge_lines(rounded(edge_ref[index] + block[2 * size :]), lines_ref.at[index], depth)
+        edge_lines(rounded(edge_ref[index] + block[2 * size :]), lines_ref.at[index])
     out_ref[:, :, LANES : 2 * cols - LANES] = image_ref[...]
 
     def one_tile(index, carry):
@@ -566,8 +653,17 @@
     )(dense, index, tables)
     whole = pltpu.VMEM((tiles, 2 * size + 2 * 4 * half, LANES), f32)
     along = call(own_kernel, "own_slab", whole, 0.4)(cells, weights)
+    lines = pltpu.VMEM((2, 32 * layers + 8, LANES), f32)
+    edge_rows = pltpu.VMEM((cols // LANES, 8 * layers + 8, LANES), f32)
+    part, own_edge = call(
+        own_tiles_kernel,
+        "own_tiles",
+        (pltpu.VMEM((tiles - 2, 16, 8, LANES), f32), pltpu.VMEM((8 * layers, 2 * cols), f32)),
+        0.1,
+        [edge_rows, lines],
+    )(tables, weights, inside, first, along)
     ends = call(side_kernel, "side_columns", pltpu.VMEM((2, layers, LANES), i32), 0.1)(
-        columns, bulk, second, first, along
+        columns, bulk, second, first, part
     )
     pairs = [(x, x + 1) for x in range(0, count_x, 2)]
     cross = [(x, (x + 1) % count_x) for x in range(1, count_x, 2)]
@@ -577,15 +673,19 @@
         bulk, tables, weights, ends, along
     )
     smem = pl.BlockSpec(memory_space=pltpu.SMEM)
-    lines = pltpu.VMEM((2, 32 * layers + 8, LANES), f32)
     image, edge = call(
         inner_kernel,
         "inner_tiles",
         (pltpu.VMEM((4, rows, (tiles - 2) * LANES), f32), pltpu.VMEM((2, 16 * layers, LANES), f32)),
         2.0,
-        [pltpu.VMEM((cols // LANES, 16 * layers + 8, LANES), f32), lines, pltpu.VMEM((4, rows + 8, LANES), f32)],
+        [
+            edge_rows,
+            lines,
+            pltpu.VMEM((tiles - 2, 16, LANES), f32),
+            pltpu.VMEM((4, rows + 8, LANES), f32),
+        ],
         [smem] + [VMEM] * 7,
-    )(slab_rank, tables, weights, bulk, inside, second, first, along)
+    )(slab_rank, tables, weights, bulk, second, own_edge, part, along)
     return call(
         outer_kernel,
         "outer_tiles",

time: 16.2 us -> 16.5 us (1.019)
  Pallas kernels: 7.49 us -> 7.76 us
    pallas_call x8 -> x9, Pallas kernels: 7.49 us -> 7.76 us  [run(): pl.pallas_call(kernel, out_shape=out_shape, in_specs=in_specs or [VMEM] *...]
  transfers between devices with their start and end apart: 5 -> 5, of which waited for: 1 -> 1; matrix products, arithmetic and copies ran while one was open for 0% -> 0% of each run, Pallas kernels for 22% -> 23%
where the time goes in v14:
time: 16.5 us; the launch traced here: 16.3 us
  Pallas kernels  7.76 us (47%)
  starting transfers between devices  6.23 us (38%)
  waiting for transfers between devices  2.25 us (14%)
    pallas_call x9, Pallas kernels, run(): pl.pallas_call(kernel, out_shape=out_shape, in_specs=in_specs or [VMEM] *...  7.76 us
    ppermute x1, starting transfers between devices, two_slab_device(): bulk = lax.ppermute(bulk, 'bz', [(0, 1), (1, 0)])  3 us
    ppermute x1, waiting for transfers between devices, two_slab_device(): first = lax.ppermute(first, axes, ring)  2.24 us
    ppermute x1, starting transfers between devices, two_slab_device(): beside = lax.ppermute(ends, 'bx', both(pairs))  1.62 us
    ppermute x1, starting transfers between devices, two_slab_device(): first = lax.ppermute(first, axes, ring)  1.58 us
  transfers between devices with their start and end apart: 5, of which 1 were waited for; matrix products, arithmetic and copies ran while one was open for 0% of the time, Pallas kernels for 23%

profile of v14, /device:TPU:0, one launch (start us, length us, event | category | flops | bytes accessed | tf_op | source)
XLA Modules:
  0.0 16.3 jit_solution(691647482451011532)
XLA Ops:
  0.0 1.2 %stage_block.1 = (s32[8,256]{1,0:T(8,128)S(1)}, s32[8,256]{1,0:T(8,128)S(1)}, s32[8,128]{1,0:T(8,128)S(1)}, f32[8,2,40,128]{3,2,1,0:T(8,128)S(1)}, s32[8,2,40,12...) custom-call(f32[8,32,256]{2,1,0:T(8,128)} %density_ref.1, s32[8,32,256]{2,1,0:T(8,128)} %bins_ref.1, ...), custom_call_target="tpu_custom_call" | custom-call | flops 1200000000 | bytes 4320000 | tf_op jit(solution)/shard_map/stage_block/pallas_call | solution.py:596
  1.2 0.1 pack_block.1
  1.3 3.0 %collective-permute-start = (s32[18,8,256]{2,1,0:T(8,128)S(1)}, s32[18,8,256]{2,1,0:T(8,128)S(1)}, u32[]{:S(2)}, u32[]{:S(2)}) collective-permute-start(s32[18,8,256]{2,1,0:T(8,128)S(1)} %get-tuple-element.24), channel_id=1, source_target_pairs={{0,16},{16,0},{1,17},{17,1},{2,18},{18,2},{3,19},{19,3},{4,20},{20... | collective-permute-start | bytes 442376 | tf_op jit(solution)/shard_map/ppermute | solution.py:644
  4.3 0.0 collective-permute-start.1
  4.3 1.6 %collective-permute-start.2 = (s32[8,256]{1,0:T(8,128)S(1)}, s32[8,256]{1,0:T(8,128)S(1)}, u32[]{:S(2)}, u32[]{:S(2)}) collective-permute-start(s32[8,256]{1,0:T(8,128)S(1)} %get-tuple-element.26), channel_id=1, source_target_pairs={{0,4},{1,5},{2,6},{3,7},{4,8},{5,9},{6,10},{7,11},{8,12},{9,13},{1... | collective-permute-start | bytes 24584 | tf_op jit(solution)/shard_map/ppermute | solution.py:645
  5.9 0.5 %own_cells.1 = (bf16[512,256]{1,0:T(8,128)(2,1)S(1)}, bf16[384,512]{1,0:T(8,128)(2,1)S(1)}) custom-call(f32[8,2,40,128]{3,2,1,0:T(8,128)S(1)} %get-tuple-element.20.dense_ref, s32[8,2,40,128]{3,2,1,0:T(8,128)S(1)} %get-tuple-element.21.index_ref, f32[8,8,128]{2,1,0:T(8,128)S(1)} %get-tuple-element.19.tables_ref), custom_call_target="tpu_custom_call" | custom-call | flops 500000000 | bytes 1800000 | tf_op jit(solution)/shard_map/own_cells/pallas_call | solution.py:596
  6.4 0.3 %own_slab.1.along_ref.own_ref = f32[4,1152,128]{2,1,0:T(8,128)S(1)} custom-call(bf16[512,256]{1,0:T(8,128)(2,1)S(1)} %get-tuple-element.28.cells_ref, bf16[384,512]{1,0:T(8,128)(2,1)S(1)} %get-tuple-element.22.weights_ref), custom_call_target="tpu_custom_call" | custom-call | flops 400000000 | bytes 1440000 | tf_op jit(solution)/shard_map/own_slab/pallas_call | solution.py:596
  6.7 2.2 %collective-permute-done.2.first_ref = s32[8,256]{1,0:T(8,128)S(1)} collective-permute-done((s32[8,256]{1,0:T(8,128)S(1)}, s32[8,256]{1,0:T(8,128)S(1)}, u32[]{:S(2)}, u32[]{:S(2)}) %collective-permute-start.2) | collective-permute-done | bytes 8224 | tf_op jit(solution)/shard_map/ppermute | solution.py:645
  9.0 0.8 %own_tiles.1 = (f32[2,16,8,128]{3,2,1,0:T(8,128)S(1)}, f32[64,512]{1,0:T(8,128)S(1)}) custom-call(f32[8,8,128]{2,1,0:T(8,128)S(1)} %get-tuple-element.19.tables_ref, bf16[384,512]{1,0:T(8,128)(2,1)S(1)} %get-tuple-element.22.weights_ref, s32[8,256]{1,0:T(8,128)S(1)} %get-tuple-element.27.inside_ref, s32[8,256]{1,0:T(8,128)S(1)} %collective-permute-done.2.first_ref, ...), custom_call_target="tpu_custom_call" | custom-call | flops 100000000 | bytes 360000 | tf_op jit(solution)/shard_map/own_tiles/pallas_call | solution.py:596
  9.8 0.0 collective-permute-done.1.second_ref
  9.8 0.0 collective-permute-done.bulk_ref
  9.8 0.1 side_columns.1.ends_ref
  9.9 0.0 copy-start
  9.9 0.0 collective-permute-start.4
  9.9 1.6 %collective-permute-start.3 = (s32[2,8,128]{2,1,0:T(8,128)S(1)}, s32[2,8,128]{2,1,0:T(8,128)S(1)}, u32[]{:S(2)}, u32[]{:S(2)}) collective-permute-start(s32[2,8,128]{2,1,0:T(8,128)S(1)} %side_columns.1.ends_ref), channel_id=1, source_target_pairs={{0,1},{2,3},{1,0},{3,2},{4,5},{6,7},{5,4},{7,6},{8,9},{10,11},{9,8... | collective-permute-start | bytes 24584 | tf_op jit(solution)/shard_map/ppermute | solution.py:670
  11.5 0.8 %other_slab.1.along_ref = f32[4,1152,128]{2,1,0:T(8,128)S(1)} custom-call(s32[18,8,256]{2,1,0:T(8,128)S(1)} %collective-permute-done.bulk_ref, f32[8,8,128]{2,1,0:T(8,128)S(1)} %get-tuple-element.19.tables_ref, bf16[384,512]{1,0:T(8,128)(2,1)S(1)} %get-tuple-element.22.weights_ref, ...), custom_call_target="tpu_custom_call", output_to_operand_aliasing={{}: (4, {})} | custom-call | flops 800000000 | bytes 2880000 | tf_op jit(solution)/shard_map/other_slab/pallas_call | solution.py:596
  12.3 0.0 copy-done
  12.3 1.3 %inner_tiles.1 = (f32[4,32,256]{2,1,0:T(8,128)S(1)}, f32[2,128,128]{2,1,0:T(8,128)S(1)}) custom-call(s32[2]{0:T(128)S(1)} %copy-done, f32[8,8,128]{2,1,0:T(8,128)S(1)} %get-tuple-element.19.tables_ref, bf16[384,512]{1,0:T(8,128)(2,1)S(1)} %get-tuple-element.22.weights_ref, s32[18,8,256]{2,1,0:T(8,128)S(1)} %collective-permute-done.bulk_ref, ...), custom_call_target="tpu_custom_call" | custom-call | flops 2000000000 | bytes 7200000 | tf_op jit(solution)/shard_map/inner_tiles/pallas_call | solution.py:596
  13.7 0.0 collective-permute-done.4.across_ref
  13.7 0.0 collective-permute-done.3.beside_ref
  13.7 2.6 %outer_tiles.1 = f32[4,32,512]{2,1,0:T(8,128)} custom-call(s32[2]{0:T(128)S(1)} %copy-done, f32[8,8,128]{2,1,0:T(8,128)S(1)} %get-tuple-element.19.tables_ref, bf16[384,512]{1,0:T(8,128)(2,1)S(1)} %get-tuple-element.22.weights_ref, s32[2,8,128]{2,1,0:T(8,128)S(1)} %collective-permute-done.3.beside_ref, s32[2,8,128]{2,1,0:T(8,128)S(1)} %collective-permute-done.4.across_ref, ...), custom_call_target="tpu_custom_call" | custom-call | flops 2000000000 | bytes 7200000 | tf_op jit(solution)/shard_map/outer_tiles/pallas_call | solution.py:596
Async XLA Ops:
  1.3 8.5 %collective-permute-start = (s32[18,8,256]{2,1,0:T(8,128)S(1)}, s32[18,8,256]{2,1,0:T(8,128)S(1)}, u32[]{:S(2)}, u32[]{:S(2)}) collective-permute-start(s32[18,8,256]{2,1,0:T(8,128)S(1)} %get-tuple-element.24), channel_id=1, source_target_pairs={{0,16},{16,0},{1,17},{17,1},{2,18},{18,2},{3,19},{19,3},{4,20},{20... | collective-permute-start | bytes 442376 | tf_op jit(solution)/shard_map/ppermute | solution.py:644
  4.3 5.5 %collective-permute-start.1 = (s32[8,256]{1,0:T(8,128)S(1)}, s32[8,256]{1,0:T(8,128)S(1)}, u32[]{:S(2)}, u32[]{:S(2)}) collective-permute-start(s32[8,256]{1,0:T(8,128)S(1)} %get-tuple-element.25), channel_id=1, source_target_pairs={{16,4},{17,5},{18,6},{19,7},{20,8},{21,9},{22,10},{23,11},{24,12},... | collective-permute-start | bytes 24584 | tf_op jit(solution)/shard_map/ppermute | solution.py:646
  4.3 4.7 %collective-permute-start.2 = (s32[8,256]{1,0:T(8,128)S(1)}, s32[8,256]{1,0:T(8,128)S(1)}, u32[]{:S(2)}, u32[]{:S(2)}) collective-permute-start(s32[8,256]{1,0:T(8,128)S(1)} %get-tuple-element.26), channel_id=1, source_target_pairs={{0,4},{1,5},{2,6},{3,7},{4,8},{5,9},{6,10},{7,11},{8,12},{9,13},{1... | collective-permute-start | bytes 24584 | tf_op jit(solution)/shard_map/ppermute | solution.py:645
  9.9 2.5 %copy-start = (s32[2]{0:T(128)S(1)}, s32[2]{0:T(128)}, u32[]{:S(2)}) copy-start(s32[2]{0:T(128)} %rank_ref.3) | copy-start | bytes 28
  9.9 3.8 %collective-permute-start.4 = (s32[2,8,128]{2,1,0:T(8,128)S(1)}, s32[2,8,128]{2,1,0:T(8,128)S(1)}, u32[]{:S(2)}, u32[]{:S(2)}) collective-permute-start(s32[2,8,128]{2,1,0:T(8,128)S(1)} %side_columns.1.ends_ref), channel_id=1, source_target_pairs={{1,2},{3,0},{2,1},{0,3},{5,6},{7,4},{6,5},{4,7},{9,10},{11,8},{10,... | collective-permute-start | bytes 24584 | tf_op jit(solution)/shard_map/ppermute | solution.py:671
  9.9 3.8 %collective-permute-start.3 = (s32[2,8,128]{2,1,0:T(8,128)S(1)}, s32[2,8,128]{2,1,0:T(8,128)S(1)}, u32[]{:S(2)}, u32[]{:S(2)}) collective-permute-start(s32[2,8,128]{2,1,0:T(8,128)S(1)} %side_columns.1.ends_ref), channel_id=1, source_target_pairs={{0,1},{2,3},{1,0},{3,2},{4,5},{6,7},{5,4},{7,6},{8,9},{10,11},{9,8... | collective-permute-start | bytes 24584 | tf_op jit(solution)/shard_map/ppermute | solution.py:670

commit v15 on v13

--- a/solution.py
+++ b/solution.py
@@ -272,11 +272,12 @@
     return value.astype(jnp.bfloat16).astype(jnp.float32)
 
 
-def cells_kernel(dense_ref, index_ref, tables_ref, cells_ref, weights_ref):
+def cells_kernel(dense_ref, index_ref, tables_ref, cells_ref, weights_ref, mix_ref):
     layers, tiles, rows = dense_ref.shape[0], dense_ref.shape[1], dense_ref.shape[2] - 8
     half = rows // 2
     start = lax.axis_index("bz") * half
     fill_weights(weights_ref, rows)
+    fill_rows(mix_ref)
 
     def read_cells(z, part, tile):
         at = pl.ds(start + part, half // 2, stride=2)
@@ -331,63 +332,77 @@
         here = triple[layer * 8 : layer * 8 + 8]
         before = now[layer * 8 - 8 : layer * 8] if layer > 0 else empty
         after = now[layer * 8 + 8 : layer * 8 + 16] if layer + 1 < depth else empty
-        lines_ref[layer * 16 : layer * 16 + 8, :] = rounded(before + here)
-        lines_ref[layer * 16 + 8 : layer * 16 + 16, :] = rounded(after + here)
-
-
-def render_tile(along_ref, lines_ref, flip, layers):
-    sub_at = lax.broadcasted_iota(jnp.int32, (8, LANES), 0)
-    top = sub_at == 0
-    bottom = sub_at == 7
-
+        for parity, beside in enumerate((before, after)):
+            line = jnp.concatenate([beside + here, empty], axis=0)
+            at = (layer * 2 + parity) * 16
+            lines_ref[at : at + 16, :] = line.astype(jnp.bfloat16)
+
+
+def render_pair(along_refs, lines_refs, rows_ref, flip, layers):
     def one_slab(position, image):
         slab = position ^ flip
-        view = along_ref.at[pl.ds(pl.multiple_of(slab * (layers * 64), 64), (layers + 2) * 64), :]
-        lines = lines_ref.at[pl.ds(pl.multiple_of(slab * (layers * 16), 16), layers * 16 + 8), :]
-
-        def layer_rows(layer, channel):
+        along_at = pl.ds(pl.multiple_of(slab * (layers * 64), 64), (layers + 2) * 64)
+        lines_at = pl.ds(pl.multiple_of(slab * (layers * 32), 32), layers * 32)
+        views = [ref.at[along_at, :] for ref in along_refs]
+        lines = [ref.at[lines_at, :] for ref in lines_refs]
+
+        def layer_rows(view, layer, channel):
             base = (layer * 4 + channel) * 16
             return view[base : base + 16, :]
 
+        def both(pieces):
+            return jnp.concatenate(pieces, axis=1)
+
         for z in range(layers):
-            triple = [3.0 * layer_rows(z + 1, channel) for channel in range(4)]
+            triple = [[3.0 * layer_rows(v, z + 1, channel) for v in views] for channel in range(4)]
+            mixed = []
             for parity in range(2):
-                clear = [1.0 - value for value in image[3]]
-                updated = []
                 for channel in range(4):
-                    both = rounded(layer_rows(z + 2 * parity, channel) + triple[channel])
-                    even, odd = both[0:8], both[8:16]
-                    line = (z * 2 + parity) * 8 + channel
-                    above = lines[pl.ds(line, 8, stride=0), :]
-                    below = lines[pl.ds(line + 4, 8, stride=0), :]
-                    before_even = jnp.where(top, above, pltpu.roll(odd, 1, 0))
-                    after_odd = jnp.where(bottom, below, pltpu.roll(even, 7, 0))
-                    even_centre = 3.0 * even
-                    odd_centre = 3.0 * odd
-                    samples = [
-                        before_even + even_centre,
-                        even_centre + odd,
-                        even + odd_centre,
-                        odd_centre + after_odd,
-                    ]
-                    updated.append([image[channel][i] + clear[i] * samples[i] for i in range(4)])
-                image = updated
+                    mixed.append(
+                        both(
+                            [
+                                (layer_rows(v, z + 2 * parity, channel) + t).astype(jnp.bfloat16)
+                                for v, t in zip(views, triple[channel])
+                            ]
+                        )
+                    )
+                at = (z * 2 + parity) * 16
+                mixed.append(both([line[at : at + 16, :] for line in lines]))
+            samples = jnp.dot(
+                rows_ref[...], jnp.concatenate(mixed, axis=0), preferred_element_type=jnp.float32
+            )
+            for parity in range(2):
+                clear = 1.0 - image[3]
+                base = parity * 128
+                image = [
+                    image[channel] + clear * samples[base + channel * 32 : base + channel * 32 + 32]
+                    for channel in range(4)
+                ]
         return image
 
-    zero = jnp.zeros((8, LANES), jnp.float32)
-    return lax.fori_loop(0, 2, one_slab, [[zero] * 4 for _ in range(4)])
-
-
-def store_tile(image, mixed_ref, out_ref, lanes):
-    for channel in range(4):
-        for i in range(4):
-            mixed_ref[channel, pl.ds(i, 8, stride=4), :] = image[channel][i]
-        out_ref[channel, :, lanes] = mixed_ref[channel, 0:32]
+    return lax.fori_loop(0, 2, one_slab, [jnp.zeros((32, 2 * LANES), jnp.float32)] * 4)
+
+
+def fill_rows(rows_ref):
+    m = lax.broadcasted_iota(jnp.int32, rows_ref.shape, 0)
+    k = lax.broadcasted_iota(jnp.int32, rows_ref.shape, 1)
+    second = k >= 80
+    k = jnp.where(second, k - 80, k)
+    centre = lax.shift_right_logical(m & 31, 1)
+    beside = centre - 1 + 2 * (m & 1)
+    channel = lax.shift_right_logical(m, 5) & 3
+    own = k < 64
+    k_channel = jnp.where(own, lax.shift_right_logical(k, 4), k & 3)
+    k_row = 2 * (k & 7) + (lax.shift_right_logical(k, 3) & 1)
+    k_row = jnp.where(own, k_row, jnp.where(k < 68, -1, jnp.where(k < 72, 16, 99)))
+    same = (k_channel == channel) & (second == (m >= 128))
+    value = jnp.where(k_row == centre, 3.0, jnp.where(k_row == beside, 1.0, 0.0))
+    rows_ref[...] = jnp.where(same, value, 0.0).astype(jnp.bfloat16)
 
 
 def inner_kernel(
-    rank_ref, tables_ref, weights_ref, bulk_ref, inside_ref, second_ref, first_ref, along_ref,
-    image_ref, edge_ref, cells_ref, lines_ref, mixed_ref,
+    rank_ref, tables_ref, weights_ref, bulk_ref, inside_ref, second_ref, first_ref, mix_ref, along_ref,
+    image_ref, edge_ref, cells_ref, lines_ref,
 ):
     layers, cols = inside_ref.shape
     depth = 2 * layers
@@ -423,17 +438,16 @@
         else:
             edge_lines(rounded(now), lines_ref.at[tile - 1], depth)
 
-    def one_tile(index, carry):
-        image = render_tile(along_ref.at[index + 1], lines_ref.at[index], rank_ref[0], layers)
-        store_tile(image, mixed_ref, image_ref, pl.ds(pl.multiple_of(index * LANES, LANES), LANES))
-        return carry
-
-    lax.fori_loop(0, tiles - 2, one_tile, 0)
+    image = render_pair(
+        [along_ref.at[1], along_ref.at[2]], [lines_ref.at[0], lines_ref.at[1]], mix_ref, rank_ref[0], layers
+    )
+    for channel in range(4):
+        image_ref[channel] = image[channel]
 
 
 def outer_kernel(
-    rank_ref, tables_ref, weights_ref, beside_ref, across_ref, along_ref, edge_ref, image_ref,
-    out_ref, ends_ref, values_ref, keep_ref, fixed_ref, lines_ref, mixed_ref,
+    rank_ref, tables_ref, weights_ref, beside_ref, across_ref, mix_ref, along_ref, edge_ref, image_ref,
+    out_ref, ends_ref, values_ref, keep_ref, fixed_ref, lines_ref,
 ):
     rows = out_ref.shape[1]
     cols = out_ref.shape[2] // 2
@@ -487,13 +501,12 @@
         edge_lines(rounded(edge_ref[index] + block[2 * size :]), lines_ref.at[index], depth)
     out_ref[:, :, LANES : 2 * cols - LANES] = image_ref[...]
 
-    def one_tile(index, carry):
-        image = render_tile(fixed_ref.at[index], lines_ref.at[index], rank_ref[0], layers)
-        lanes = pl.ds(pl.multiple_of(index * (2 * cols - LANES), LANES), LANES)
-        store_tile(image, mixed_ref, out_ref, lanes)
-        return carry
-
-    lax.fori_loop(0, 2, one_tile, 0)
+    image = render_pair(
+        [fixed_ref.at[0], fixed_ref.at[1]], [lines_ref.at[0], lines_ref.at[1]], mix_ref, rank_ref[0], layers
+    )
+    for channel in range(4):
+        out_ref[channel, :, 0:LANES] = image[channel][:, 0:LANES]
+        out_ref[channel, :, 2 * cols - LANES : 2 * cols] = image[channel][:, LANES : 2 * LANES]
 
 
 def two_slab_device(density, bin_index, tf_colour, tf_extinction, slab_rank):
@@ -558,10 +571,14 @@
     first = lax.ppermute(first, axes, ring)
     second = lax.ppermute(second, axes, both(diagonal))
 
-    cells, weights = call(
+    cells, weights, mix = call(
         cells_kernel,
         "own_cells",
-        (pltpu.VMEM((size, cols), bf16), pltpu.VMEM((cols + LANES, 2 * cols), bf16)),
+        (
+            pltpu.VMEM((size, cols), bf16),
+            pltpu.VMEM((cols + LANES, 2 * cols), bf16),
+            pltpu.VMEM((256, 160), bf16),
+        ),
         0.5,
     )(dense, index, tables)
     whole = pltpu.VMEM((tiles, 2 * size + 2 * 4 * half, LANES), f32)
@@ -577,15 +594,15 @@
         bulk, tables, weights, ends, along
     )
     smem = pl.BlockSpec(memory_space=pltpu.SMEM)
-    lines = pltpu.VMEM((2, 32 * layers + 8, LANES), f32)
+    lines = pltpu.VMEM((2, 64 * layers, LANES), bf16)
     image, edge = call(
         inner_kernel,
         "inner_tiles",
         (pltpu.VMEM((4, rows, (tiles - 2) * LANES), f32), pltpu.VMEM((2, 16 * layers, LANES), f32)),
         2.0,
-        [pltpu.VMEM((cols // LANES, 16 * layers + 8, LANES), f32), lines, pltpu.VMEM((4, rows + 8, LANES), f32)],
-        [smem] + [VMEM] * 7,
-    )(slab_rank, tables, weights, bulk, inside, second, first, along)
+        [pltpu.VMEM((cols // LANES, 16 * layers + 8, LANES), f32), lines],
+        [smem] + [VMEM] * 8,
+    )(slab_rank, tables, weights, bulk, inside, second, first, mix, along)
     return call(
         outer_kernel,
         "outer_tiles",
@@ -597,10 +614,9 @@
             pltpu.VMEM((16 * layers + 8, LANES), f32),
             pltpu.VMEM((2, 2 * size + 2 * 4 * half, LANES), f32),
             lines,
-            pltpu.VMEM((4, rows + 8, LANES), f32),
         ],
-        [smem] + [VMEM] * 7,
-    )(slab_rank, tables, weights, beside, across, along, edge, image)
+        [smem] + [VMEM] * 8,
+    )(slab_rank, tables, weights, beside, across, mix, along, edge, image)
 
 
 def on_device(density, bin_index, tf_colour, tf_extinction, slab_rank):

time: 16.2 us -> 16.2 us (level)
  transfers between devices with their start and end apart: 5 -> 5, of which waited for: 1 -> 1; matrix products, arithmetic and copies ran while one was open for 0% -> 0% of each run, Pallas kernels for 22% -> 23%
where the time goes in v15:
time: 16.2 us; the launch traced here: 16 us
  Pallas kernels  7.61 us (47%)
  starting transfers between devices  6.23 us (38%)
  waiting for transfers between devices  2.13 us (13%)
    pallas_call x8, Pallas kernels, run(): pl.pallas_call(kernel, out_shape=out_shape, in_specs=in_specs or [VMEM] *...  7.61 us
    ppermute x1, starting transfers between devices, two_slab_device(): bulk = lax.ppermute(bulk, 'bz', [(0, 1), (1, 0)])  3 us
    ppermute x1, waiting for transfers between devices, two_slab_device(): first = lax.ppermute(first, axes, ring)  2.12 us
    ppermute x1, starting transfers between devices, two_slab_device(): beside = lax.ppermute(ends, 'bx', both(pairs))  1.62 us
    ppermute x1, starting transfers between devices, two_slab_device(): first = lax.ppermute(first, axes, ring)  1.58 us
  transfers between devices with their start and end apart: 5, of which 1 were waited for; matrix products, arithmetic and copies ran while one was open for 0% of the time, Pallas kernels for 23%

profile of v15, /device:TPU:0, one launch (start us, length us, event | category | flops | bytes accessed | tf_op | source)
XLA Modules:
  0.0 16.0 jit_solution(16138299798686517390)
XLA Ops:
  0.0 1.2 %stage_block.1 = (s32[8,256]{1,0:T(8,128)S(1)}, s32[8,256]{1,0:T(8,128)S(1)}, s32[8,128]{1,0:T(8,128)S(1)}, f32[8,2,40,128]{3,2,1,0:T(8,128)S(1)}, s32[8,2,40,12...) custom-call(f32[8,32,256]{2,1,0:T(8,128)} %density_ref.1, s32[8,32,256]{2,1,0:T(8,128)} %bins_ref.1, ...), custom_call_target="tpu_custom_call" | custom-call | flops 1200000000 | bytes 4320000 | tf_op jit(solution)/shard_map/stage_block/pallas_call | solution.py:522
  1.2 0.1 pack_block.1
  1.3 3.0 %collective-permute-start = (s32[18,8,256]{2,1,0:T(8,128)S(1)}, s32[18,8,256]{2,1,0:T(8,128)S(1)}, u32[]{:S(2)}, u32[]{:S(2)}) collective-permute-start(s32[18,8,256]{2,1,0:T(8,128)S(1)} %get-tuple-element.23), channel_id=1, source_target_pairs={{0,16},{16,0},{1,17},{17,1},{2,18},{18,2},{3,19},{19,3},{4,20},{20... | collective-permute-start | bytes 442376 | tf_op jit(solution)/shard_map/ppermute | solution.py:570
  4.3 0.0 collective-permute-start.1
  4.3 1.6 %collective-permute-start.2 = (s32[8,256]{1,0:T(8,128)S(1)}, s32[8,256]{1,0:T(8,128)S(1)}, u32[]{:S(2)}, u32[]{:S(2)}) collective-permute-start(s32[8,256]{1,0:T(8,128)S(1)} %get-tuple-element.25), channel_id=1, source_target_pairs={{0,4},{1,5},{2,6},{3,7},{4,8},{5,9},{6,10},{7,11},{8,12},{9,13},{1... | collective-permute-start | bytes 24584 | tf_op jit(solution)/shard_map/ppermute | solution.py:571
  5.9 0.7 %own_cells.1 = (bf16[512,256]{1,0:T(8,128)(2,1)S(1)}, bf16[384,512]{1,0:T(8,128)(2,1)S(1)}, bf16[256,160]{1,0:T(8,128)(2,1)S(1)}) custom-call(f32[8,2,40,128]{3,2,1,0:T(8,128)S(1)} %get-tuple-element.19.dense_ref, s32[8,2,40,128]{3,2,1,0:T(8,128)S(1)} %get-tuple-element.20.index_ref, f32[8,8,128]{2,1,0:T(8,128)S(1)} %get-tuple-element.18.tables_ref), custom_call_target="tpu_custom_call" | custom-call | flops 500000000 | bytes 1800000 | tf_op jit(solution)/shard_map/own_cells/pallas_call | solution.py:522
  6.5 0.3 %own_slab.1.along_ref.own_ref = f32[4,1152,128]{2,1,0:T(8,128)S(1)} custom-call(bf16[512,256]{1,0:T(8,128)(2,1)S(1)} %get-tuple-element.26.cells_ref, bf16[384,512]{1,0:T(8,128)(2,1)S(1)} %get-tuple-element.21.weights_ref), custom_call_target="tpu_custom_call" | custom-call | flops 400000000 | bytes 1440000 | tf_op jit(solution)/shard_map/own_slab/pallas_call | solution.py:522
  6.8 0.0 collective-permute-done.1.second_ref
  6.8 2.1 %collective-permute-done.2.first_ref = s32[8,256]{1,0:T(8,128)S(1)} collective-permute-done((s32[8,256]{1,0:T(8,128)S(1)}, s32[8,256]{1,0:T(8,128)S(1)}, u32[]{:S(2)}, u32[]{:S(2)}) %collective-permute-start.2) | collective-permute-done | bytes 8224 | tf_op jit(solution)/shard_map/ppermute | solution.py:571
  9.0 0.0 collective-permute-done.bulk_ref
  9.0 0.1 side_columns.1.ends_ref
  9.0 0.0 copy-start
  9.0 0.0 collective-permute-start.4
  9.1 1.6 %collective-permute-start.3 = (s32[2,8,128]{2,1,0:T(8,128)S(1)}, s32[2,8,128]{2,1,0:T(8,128)S(1)}, u32[]{:S(2)}, u32[]{:S(2)}) collective-permute-start(s32[2,8,128]{2,1,0:T(8,128)S(1)} %side_columns.1.ends_ref), channel_id=1, source_target_pairs={{0,1},{2,3},{1,0},{3,2},{4,5},{6,7},{5,4},{7,6},{8,9},{10,11},{9,8... | collective-permute-start | bytes 24584 | tf_op jit(solution)/shard_map/ppermute | solution.py:591
  10.7 0.8 %other_slab.1.along_ref = f32[4,1152,128]{2,1,0:T(8,128)S(1)} custom-call(s32[18,8,256]{2,1,0:T(8,128)S(1)} %collective-permute-done.bulk_ref, f32[8,8,128]{2,1,0:T(8,128)S(1)} %get-tuple-element.18.tables_ref, bf16[384,512]{1,0:T(8,128)(2,1)S(1)} %get-tuple-element.21.weights_ref, ...), custom_call_target="tpu_custom_call", output_to_operand_aliasing={{}: (4, {})} | custom-call | flops 800000000 | bytes 2880000 | tf_op jit(solution)/shard_map/other_slab/pallas_call | solution.py:522
  11.5 0.0 copy-done
  11.5 1.9 %inner_tiles.1 = (f32[4,32,256]{2,1,0:T(8,128)S(1)}, f32[2,128,128]{2,1,0:T(8,128)S(1)}) custom-call(s32[2]{0:T(128)S(1)} %copy-done, f32[8,8,128]{2,1,0:T(8,128)S(1)} %get-tuple-element.18.tables_ref, bf16[384,512]{1,0:T(8,128)(2,1)S(1)} %get-tuple-element.21.weights_ref, s32[18,8,256]{2,1,0:T(8,128)S(1)} %collective-permute-done.bulk_ref, ...), custom_call_target="tpu_custom_call" | custom-call | flops 2000000000 | bytes 7200000 | tf_op jit(solution)/shard_map/inner_tiles/pallas_call | solution.py:522
  13.4 0.0 collective-permute-done.4.across_ref
  13.4 0.0 collective-permute-done.3.beside_ref
  13.4 2.6 %outer_tiles.1 = f32[4,32,512]{2,1,0:T(8,128)} custom-call(s32[2]{0:T(128)S(1)} %copy-done, f32[8,8,128]{2,1,0:T(8,128)S(1)} %get-tuple-element.18.tables_ref, bf16[384,512]{1,0:T(8,128)(2,1)S(1)} %get-tuple-element.21.weights_ref, s32[2,8,128]{2,1,0:T(8,128)S(1)} %collective-permute-done.3.beside_ref, s32[2,8,128]{2,1,0:T(8,128)S(1)} %collective-permute-done.4.across_ref, ...), custom_call_target="tpu_custom_call" | custom-call | flops 2000000000 | bytes 7200000 | tf_op jit(solution)/shard_map/outer_tiles/pallas_call | solution.py:522
Async XLA Ops:
  1.3 7.7 %collective-permute-start = (s32[18,8,256]{2,1,0:T(8,128)S(1)}, s32[18,8,256]{2,1,0:T(8,128)S(1)}, u32[]{:S(2)}, u32[]{:S(2)}) collective-permute-start(s32[18,8,256]{2,1,0:T(8,128)S(1)} %get-tuple-element.23), channel_id=1, source_target_pairs={{0,16},{16,0},{1,17},{17,1},{2,18},{18,2},{3,19},{19,3},{4,20},{20... | collective-permute-start | bytes 442376 | tf_op jit(solution)/shard_map/ppermute | solution.py:570
  4.3 2.5 %collective-permute-start.1 = (s32[8,256]{1,0:T(8,128)S(1)}, s32[8,256]{1,0:T(8,128)S(1)}, u32[]{:S(2)}, u32[]{:S(2)}) collective-permute-start(s32[8,256]{1,0:T(8,128)S(1)} %get-tuple-element.24), channel_id=1, source_target_pairs={{16,4},{17,5},{18,6},{19,7},{20,8},{21,9},{22,10},{23,11},{24,12},... | collective-permute-start | bytes 24584 | tf_op jit(solution)/shard_map/ppermute | solution.py:572
  4.3 4.7 %collective-permute-start.2 = (s32[8,256]{1,0:T(8,128)S(1)}, s32[8,256]{1,0:T(8,128)S(1)}, u32[]{:S(2)}, u32[]{:S(2)}) collective-permute-start(s32[8,256]{1,0:T(8,128)S(1)} %get-tuple-element.25), channel_id=1, source_target_pairs={{0,4},{1,5},{2,6},{3,7},{4,8},{5,9},{6,10},{7,11},{8,12},{9,13},{1... | collective-permute-start | bytes 24584 | tf_op jit(solution)/shard_map/ppermute | solution.py:571
  9.0 2.5 %copy-start = (s32[2]{0:T(128)S(1)}, s32[2]{0:T(128)}, u32[]{:S(2)}) copy-start(s32[2]{0:T(128)} %rank_ref.3) | copy-start | bytes 28
  9.0 4.3 %collective-permute-start.4 = (s32[2,8,128]{2,1,0:T(8,128)S(1)}, s32[2,8,128]{2,1,0:T(8,128)S(1)}, u32[]{:S(2)}, u32[]{:S(2)}) collective-permute-start(s32[2,8,128]{2,1,0:T(8,128)S(1)} %side_columns.1.ends_ref), channel_id=1, source_target_pairs={{1,2},{3,0},{2,1},{0,3},{5,6},{7,4},{6,5},{4,7},{9,10},{11,8},{10,... | collective-permute-start | bytes 24584 | tf_op jit(solution)/shard_map/ppermute | solution.py:592
  9.1 4.3 %collective-permute-start.3 = (s32[2,8,128]{2,1,0:T(8,128)S(1)}, s32[2,8,128]{2,1,0:T(8,128)S(1)}, u32[]{:S(2)}, u32[]{:S(2)}) collective-permute-start(s32[2,8,128]{2,1,0:T(8,128)S(1)} %side_columns.1.ends_ref), channel_id=1, source_target_pairs={{0,1},{2,3},{1,0},{3,2},{4,5},{6,7},{5,4},{7,6},{8,9},{10,11},{9,8... | collective-permute-start | bytes 24584 | tf_op jit(solution)/shard_map/ppermute | solution.py:591

commit v16 on v15

--- a/solution.py
+++ b/solution.py
@@ -355,27 +355,30 @@
 
         for z in range(layers):
             triple = [[3.0 * layer_rows(v, z + 1, channel) for v in views] for channel in range(4)]
-            mixed = []
+            samples = []
             for parity in range(2):
-                for channel in range(4):
-                    mixed.append(
-                        both(
-                            [
-                                (layer_rows(v, z + 2 * parity, channel) + t).astype(jnp.bfloat16)
-                                for v, t in zip(views, triple[channel])
-                            ]
-                        )
+                mixed = [
+                    both(
+                        [
+                            (layer_rows(v, z + 2 * parity, channel) + t).astype(jnp.bfloat16)
+                            for v, t in zip(views, triple[channel])
+                        ]
                     )
+                    for channel in range(4)
+                ]
                 at = (z * 2 + parity) * 16
                 mixed.append(both([line[at : at + 16, :] for line in lines]))
-            samples = jnp.dot(
-                rows_ref[...], jnp.concatenate(mixed, axis=0), preferred_element_type=jnp.float32
-            )
-            for parity in range(2):
+                samples.append(
+                    jnp.dot(
+                        rows_ref[...],
+                        jnp.concatenate(mixed, axis=0),
+                        preferred_element_type=jnp.float32,
+                    )
+                )
+            for sample in samples:
                 clear = 1.0 - image[3]
-                base = parity * 128
                 image = [
-                    image[channel] + clear * samples[base + channel * 32 : base + channel * 32 + 32]
+                    image[channel] + clear * sample[channel * 32 : channel * 32 + 32]
                     for channel in range(4)
                 ]
         return image
@@ -386,16 +389,13 @@
 def fill_rows(rows_ref):
     m = lax.broadcasted_iota(jnp.int32, rows_ref.shape, 0)
     k = lax.broadcasted_iota(jnp.int32, rows_ref.shape, 1)
-    second = k >= 80
-    k = jnp.where(second, k - 80, k)
     centre = lax.shift_right_logical(m & 31, 1)
     beside = centre - 1 + 2 * (m & 1)
-    channel = lax.shift_right_logical(m, 5) & 3
     own = k < 64
     k_channel = jnp.where(own, lax.shift_right_logical(k, 4), k & 3)
     k_row = 2 * (k & 7) + (lax.shift_right_logical(k, 3) & 1)
     k_row = jnp.where(own, k_row, jnp.where(k < 68, -1, jnp.where(k < 72, 16, 99)))
-    same = (k_channel == channel) & (second == (m >= 128))
+    same = k_channel == lax.shift_right_logical(m, 5)
     value = jnp.where(k_row == centre, 3.0, jnp.where(k_row == beside, 1.0, 0.0))
     rows_ref[...] = jnp.where(same, value, 0.0).astype(jnp.bfloat16)
 
@@ -577,7 +577,7 @@
         (
             pltpu.VMEM((size, cols), bf16),
             pltpu.VMEM((cols + LANES, 2 * cols), bf16),
-            pltpu.VMEM((256, 160), bf16),
+            pltpu.VMEM((128, 80), bf16),
         ),
         0.5,
     )(dense, index, tables)

time: 16.2 us -> 16.1 us (level)
  Pallas kernels: 7.61 us -> 7.42 us
    pallas_call x8, Pallas kernels: 7.61 us -> 7.42 us  [run(): pl.pallas_call(kernel, out_shape=out_shape, in_specs=in_specs or [VMEM] *...]
  transfers between devices with their start and end apart: 5 -> 5, of which waited for: 1 -> 1; matrix products, arithmetic and copies ran while one was open for 0% -> 0% of each run, Pallas kernels for 23% -> 22%
where the time goes in v16:
time: 16.1 us; the launch traced here: 15.9 us
  Pallas kernels  7.42 us (46%)
  starting transfers between devices  6.23 us (39%)
  waiting for transfers between devices  2.2 us (14%)
    pallas_call x8, Pallas kernels, run(): pl.pallas_call(kernel, out_shape=out_shape, in_specs=in_specs or [VMEM] *...  7.42 us
    ppermute x1, starting transfers between devices, two_slab_device(): bulk = lax.ppermute(bulk, 'bz', [(0, 1), (1, 0)])  3 us
    ppermute x1, waiting for transfers between devices, two_slab_device(): first = lax.ppermute(first, axes, ring)  2.19 us
    ppermute x1, starting transfers between devices, two_slab_device(): beside = lax.ppermute(ends, 'bx', both(pairs))  1.62 us
    ppermute x1, starting transfers between devices, two_slab_device(): first = lax.ppermute(first, axes, ring)  1.58 us
  transfers between devices with their start and end apart: 5, of which 1 were waited for; matrix products, arithmetic and copies ran while one was open for 0% of the time, Pallas kernels for 22%

profile of v16, /device:TPU:0, one launch (start us, length us, event | category | flops | bytes accessed | tf_op | source)
XLA Modules:
  0.0 15.9 jit_solution(4760200624197791906)
XLA Ops:
  0.0 1.2 %stage_block.1 = (s32[8,256]{1,0:T(8,128)S(1)}, s32[8,256]{1,0:T(8,128)S(1)}, s32[8,128]{1,0:T(8,128)S(1)}, f32[8,2,40,128]{3,2,1,0:T(8,128)S(1)}, s32[8,2,40,12...) custom-call(f32[8,32,256]{2,1,0:T(8,128)} %density_ref.1, s32[8,32,256]{2,1,0:T(8,128)} %bins_ref.1, ...), custom_call_target="tpu_custom_call" | custom-call | flops 1200000000 | bytes 4320000 | tf_op jit(solution)/shard_map/stage_block/pallas_call | solution.py:522
  1.2 0.1 pack_block.1
  1.3 3.0 %collective-permute-start = (s32[18,8,256]{2,1,0:T(8,128)S(1)}, s32[18,8,256]{2,1,0:T(8,128)S(1)}, u32[]{:S(2)}, u32[]{:S(2)}) collective-permute-start(s32[18,8,256]{2,1,0:T(8,128)S(1)} %get-tuple-element.23), channel_id=1, source_target_pairs={{0,16},{16,0},{1,17},{17,1},{2,18},{18,2},{3,19},{19,3},{4,20},{20... | collective-permute-start | bytes 442376 | tf_op jit(solution)/shard_map/ppermute | solution.py:570
  4.3 0.0 collective-permute-start.1
  4.3 1.6 %collective-permute-start.2 = (s32[8,256]{1,0:T(8,128)S(1)}, s32[8,256]{1,0:T(8,128)S(1)}, u32[]{:S(2)}, u32[]{:S(2)}) collective-permute-start(s32[8,256]{1,0:T(8,128)S(1)} %get-tuple-element.25), channel_id=1, source_target_pairs={{0,4},{1,5},{2,6},{3,7},{4,8},{5,9},{6,10},{7,11},{8,12},{9,13},{1... | collective-permute-start | bytes 24584 | tf_op jit(solution)/shard_map/ppermute | solution.py:571
  5.9 0.6 %own_cells.1 = (bf16[512,256]{1,0:T(8,128)(2,1)S(1)}, bf16[384,512]{1,0:T(8,128)(2,1)S(1)}, bf16[128,80]{1,0:T(8,128)(2,1)S(1)}) custom-call(f32[8,2,40,128]{3,2,1,0:T(8,128)S(1)} %get-tuple-element.19.dense_ref, s32[8,2,40,128]{3,2,1,0:T(8,128)S(1)} %get-tuple-element.20.index_ref, f32[8,8,128]{2,1,0:T(8,128)S(1)} %get-tuple-element.18.tables_ref), custom_call_target="tpu_custom_call" | custom-call | flops 500000000 | bytes 1800000 | tf_op jit(solution)/shard_map/own_cells/pallas_call | solution.py:522
  6.5 0.3 %own_slab.1.along_ref.own_ref = f32[4,1152,128]{2,1,0:T(8,128)S(1)} custom-call(bf16[512,256]{1,0:T(8,128)(2,1)S(1)} %get-tuple-element.26.cells_ref, bf16[384,512]{1,0:T(8,128)(2,1)S(1)} %get-tuple-element.21.weights_ref), custom_call_target="tpu_custom_call" | custom-call | flops 400000000 | bytes 1440000 | tf_op jit(solution)/shard_map/own_slab/pallas_call | solution.py:522
  6.8 0.0 collective-permute-done.1.second_ref
  6.8 2.2 %collective-permute-done.2.first_ref = s32[8,256]{1,0:T(8,128)S(1)} collective-permute-done((s32[8,256]{1,0:T(8,128)S(1)}, s32[8,256]{1,0:T(8,128)S(1)}, u32[]{:S(2)}, u32[]{:S(2)}) %collective-permute-start.2) | collective-permute-done | bytes 8224 | tf_op jit(solution)/shard_map/ppermute | solution.py:571
  9.0 0.0 collective-permute-done.bulk_ref
  9.0 0.1 side_columns.1.ends_ref
  9.0 0.0 copy-start
  9.0 0.0 collective-permute-start.4
  9.1 1.6 %collective-permute-start.3 = (s32[2,8,128]{2,1,0:T(8,128)S(1)}, s32[2,8,128]{2,1,0:T(8,128)S(1)}, u32[]{:S(2)}, u32[]{:S(2)}) collective-permute-start(s32[2,8,128]{2,1,0:T(8,128)S(1)} %side_columns.1.ends_ref), channel_id=1, source_target_pairs={{0,1},{2,3},{1,0},{3,2},{4,5},{6,7},{5,4},{7,6},{8,9},{10,11},{9,8... | collective-permute-start | bytes 24584 | tf_op jit(solution)/shard_map/ppermute | solution.py:591
  10.7 0.8 %other_slab.1.along_ref = f32[4,1152,128]{2,1,0:T(8,128)S(1)} custom-call(s32[18,8,256]{2,1,0:T(8,128)S(1)} %collective-permute-done.bulk_ref, f32[8,8,128]{2,1,0:T(8,128)S(1)} %get-tuple-element.18.tables_ref, bf16[384,512]{1,0:T(8,128)(2,1)S(1)} %get-tuple-element.21.weights_ref, ...), custom_call_target="tpu_custom_call", output_to_operand_aliasing={{}: (4, {})} | custom-call | flops 800000000 | bytes 2880000 | tf_op jit(solution)/shard_map/other_slab/pallas_call | solution.py:522
  11.5 0.0 copy-done
  11.5 1.8 %inner_tiles.1 = (f32[4,32,256]{2,1,0:T(8,128)S(1)}, f32[2,128,128]{2,1,0:T(8,128)S(1)}) custom-call(s32[2]{0:T(128)S(1)} %copy-done, f32[8,8,128]{2,1,0:T(8,128)S(1)} %get-tuple-element.18.tables_ref, bf16[384,512]{1,0:T(8,128)(2,1)S(1)} %get-tuple-element.21.weights_ref, s32[18,8,256]{2,1,0:T(8,128)S(1)} %collective-permute-done.bulk_ref, ...), custom_call_target="tpu_custom_call" | custom-call | flops 2000000000 | bytes 7200000 | tf_op jit(solution)/shard_map/inner_tiles/pallas_call | solution.py:522
  13.3 0.0 collective-permute-done.4.across_ref
  13.4 0.0 collective-permute-done.3.beside_ref
  13.4 2.6 %outer_tiles.1 = f32[4,32,512]{2,1,0:T(8,128)} custom-call(s32[2]{0:T(128)S(1)} %copy-done, f32[8,8,128]{2,1,0:T(8,128)S(1)} %get-tuple-element.18.tables_ref, bf16[384,512]{1,0:T(8,128)(2,1)S(1)} %get-tuple-element.21.weights_ref, s32[2,8,128]{2,1,0:T(8,128)S(1)} %collective-permute-done.3.beside_ref, s32[2,8,128]{2,1,0:T(8,128)S(1)} %collective-permute-done.4.across_ref, ...), custom_call_target="tpu_custom_call" | custom-call | flops 2000000000 | bytes 7200000 | tf_op jit(solution)/shard_map/outer_tiles/pallas_call | solution.py:522
Async XLA Ops:
  1.3 7.7 %collective-permute-start = (s32[18,8,256]{2,1,0:T(8,128)S(1)}, s32[18,8,256]{2,1,0:T(8,128)S(1)}, u32[]{:S(2)}, u32[]{:S(2)}) collective-permute-start(s32[18,8,256]{2,1,0:T(8,128)S(1)} %get-tuple-element.23), channel_id=1, source_target_pairs={{0,16},{16,0},{1,17},{17,1},{2,18},{18,2},{3,19},{19,3},{4,20},{20... | collective-permute-start | bytes 442376 | tf_op jit(solution)/shard_map/ppermute | solution.py:570
  4.3 2.5 %collective-permute-start.1 = (s32[8,256]{1,0:T(8,128)S(1)}, s32[8,256]{1,0:T(8,128)S(1)}, u32[]{:S(2)}, u32[]{:S(2)}) collective-permute-start(s32[8,256]{1,0:T(8,128)S(1)} %get-tuple-element.24), channel_id=1, source_target_pairs={{16,4},{17,5},{18,6},{19,7},{20,8},{21,9},{22,10},{23,11},{24,12},... | collective-permute-start | bytes 24584 | tf_op jit(solution)/shard_map/ppermute | solution.py:572
  4.3 4.7 %collective-permute-start.2 = (s32[8,256]{1,0:T(8,128)S(1)}, s32[8,256]{1,0:T(8,128)S(1)}, u32[]{:S(2)}, u32[]{:S(2)}) collective-permute-start(s32[8,256]{1,0:T(8,128)S(1)} %get-tuple-element.25), channel_id=1, source_target_pairs={{0,4},{1,5},{2,6},{3,7},{4,8},{5,9},{6,10},{7,11},{8,12},{9,13},{1... | collective-permute-start | bytes 24584 | tf_op jit(solution)/shard_map/ppermute | solution.py:571
  9.0 2.5 %copy-start = (s32[2]{0:T(128)S(1)}, s32[2]{0:T(128)}, u32[]{:S(2)}) copy-start(s32[2]{0:T(128)} %rank_ref.3) | copy-start | bytes 28
  9.0 4.3 %collective-permute-start.4 = (s32[2,8,128]{2,1,0:T(8,128)S(1)}, s32[2,8,128]{2,1,0:T(8,128)S(1)}, u32[]{:S(2)}, u32[]{:S(2)}) collective-permute-start(s32[2,8,128]{2,1,0:T(8,128)S(1)} %side_columns.1.ends_ref), channel_id=1, source_target_pairs={{1,2},{3,0},{2,1},{0,3},{5,6},{7,4},{6,5},{4,7},{9,10},{11,8},{10,... | collective-permute-start | bytes 24584 | tf_op jit(solution)/shard_map/ppermute | solution.py:592
  9.1 4.3 %collective-permute-start.3 = (s32[2,8,128]{2,1,0:T(8,128)S(1)}, s32[2,8,128]{2,1,0:T(8,128)S(1)}, u32[]{:S(2)}, u32[]{:S(2)}) collective-permute-start(s32[2,8,128]{2,1,0:T(8,128)S(1)} %side_columns.1.ends_ref), channel_id=1, source_target_pairs={{0,1},{2,3},{1,0},{3,2},{4,5},{6,7},{5,4},{7,6},{8,9},{10,11},{9,8... | collective-permute-start | bytes 24584 | tf_op jit(solution)/shard_map/ppermute | solution.py:591

commit v17 on v16

--- a/solution.py
+++ b/solution.py
@@ -325,25 +325,31 @@
     along_columns(cells_ref[...], weights_ref, store)
 
 
-def edge_lines(now, lines_ref, depth):
+def edge_lines(now, packed_ref, lines_ref, depth):
     triple = 3.0 * now
     empty = jnp.zeros((8, LANES), jnp.float32)
     for layer in range(depth):
-        here = triple[layer * 8 : layer * 8 + 8]
-        before = now[layer * 8 - 8 : layer * 8] if layer > 0 else empty
-        after = now[layer * 8 + 8 : layer * 8 + 16] if layer + 1 < depth else empty
-        for parity, beside in enumerate((before, after)):
-            line = jnp.concatenate([beside + here, empty], axis=0)
-            at = (layer * 2 + parity) * 16
-            lines_ref[at : at + 16, :] = line.astype(jnp.bfloat16)
-
-
-def render_pair(along_refs, lines_refs, rows_ref, flip, layers):
+        at = layer * 8
+        here = triple[at : at + 8]
+        before = now[at - 8 : at] if layer > 0 else empty
+        after = now[at + 8 : at + 16] if layer + 1 < depth else empty
+        line = jnp.concatenate([before + here, empty], axis=0)
+        packed_ref[2 * at : 2 * at + 16, :] = line.astype(jnp.bfloat16)
+        lines_ref[at : at + 8, :] = rounded(after + here)
+
+
+def render_pair(along_refs, packed_refs, lines_refs, rows_ref, flip, layers):
+    sub_at = lax.broadcasted_iota(jnp.int32, (8, LANES), 0)
+    top = sub_at == 0
+    bottom = sub_at == 7
+
     def one_slab(position, image):
         slab = position ^ flip
         along_at = pl.ds(pl.multiple_of(slab * (layers * 64), 64), (layers + 2) * 64)
-        lines_at = pl.ds(pl.multiple_of(slab * (layers * 32), 32), layers * 32)
+        packed_at = pl.ds(pl.multiple_of(slab * (layers * 16), 16), layers * 16)
+        lines_at = pl.ds(pl.multiple_of(slab * (layers * 8), 8), layers * 8 + 8)
         views = [ref.at[along_at, :] for ref in along_refs]
+        packed = [ref.at[packed_at, :] for ref in packed_refs]
         lines = [ref.at[lines_at, :] for ref in lines_refs]
 
         def layer_rows(view, layer, channel):
@@ -353,44 +359,79 @@
         def both(pieces):
             return jnp.concatenate(pieces, axis=1)
 
+        def blend(image, samples):
+            updated = []
+            for tile in range(2):
+                clear = [1.0 - value for value in image[tile][3]]
+                updated.append(
+                    [
+                        [image[tile][c][i] + clear[i] * samples[tile][c][i] for i in range(4)]
+                        for c in range(4)
+                    ]
+                )
+            return updated
+
         for z in range(layers):
-            triple = [[3.0 * layer_rows(v, z + 1, channel) for v in views] for channel in range(4)]
-            samples = []
-            for parity in range(2):
-                mixed = [
-                    both(
-                        [
-                            (layer_rows(v, z + 2 * parity, channel) + t).astype(jnp.bfloat16)
-                            for v, t in zip(views, triple[channel])
-                        ]
+            triple = [[3.0 * layer_rows(v, z + 1, c) for c in range(4)] for v in views]
+            mixed = [
+                both(
+                    [
+                        (layer_rows(v, z, c) + t[c]).astype(jnp.bfloat16)
+                        for v, t in zip(views, triple)
+                    ]
+                )
+                for c in range(4)
+            ]
+            mixed.append(both([line[z * 16 : z * 16 + 16, :] for line in packed]))
+            even = jnp.dot(
+                rows_ref[...], jnp.concatenate(mixed, axis=0), preferred_element_type=jnp.float32
+            )
+            even = [
+                [
+                    [
+                        even[c * 32 + i * 8 : c * 32 + i * 8 + 8, tile * LANES : (tile + 1) * LANES]
+                        for i in range(4)
+                    ]
+                    for c in range(4)
+                ]
+                for tile in range(2)
+            ]
+            odd = []
+            for tile in range(2):
+                odd.append([])
+                for c in range(4):
+                    value = rounded(layer_rows(views[tile], z + 2, c) + triple[tile][c])
+                    low, high = value[0:8], value[8:16]
+                    above = lines[tile][pl.ds(z * 8 + c, 8, stride=0), :]
+                    below = lines[tile][pl.ds(z * 8 + 4 + c, 8, stride=0), :]
+                    before = jnp.where(top, above, pltpu.roll(high, 1, 0))
+                    after = jnp.where(bottom, below, pltpu.roll(low, 7, 0))
+                    low_centre = 3.0 * low
+                    high_centre = 3.0 * high
+                    odd[tile].append(
+                        [before + low_centre, low_centre + high, low + high_centre, high_centre + after]
                     )
-                    for channel in range(4)
-                ]
-                at = (z * 2 + parity) * 16
-                mixed.append(both([line[at : at + 16, :] for line in lines]))
-                samples.append(
-                    jnp.dot(
-                        rows_ref[...],
-                        jnp.concatenate(mixed, axis=0),
-                        preferred_element_type=jnp.float32,
-                    )
-                )
-            for sample in samples:
-                clear = 1.0 - image[3]
-                image = [
-                    image[channel] + clear * sample[channel * 32 : channel * 32 + 32]
-                    for channel in range(4)
-                ]
+            image = blend(blend(image, even), odd)
         return image
 
-    return lax.fori_loop(0, 2, one_slab, [jnp.zeros((32, 2 * LANES), jnp.float32)] * 4)
+    zero = jnp.zeros((8, LANES), jnp.float32)
+    image = [[[zero] * 4 for _ in range(4)] for _ in range(2)]
+    return lax.fori_loop(0, 2, one_slab, image)
+
+
+def store_tile(image, mixed_ref, out_ref, lanes):
+    for channel in range(4):
+        for i in range(4):
+            mixed_ref[channel, pl.ds(i, 8, stride=4), :] = image[channel][i]
+        out_ref[channel, :, lanes] = mixed_ref[channel, 0:32]
 
 
 def fill_rows(rows_ref):
     m = lax.broadcasted_iota(jnp.int32, rows_ref.shape, 0)
     k = lax.broadcasted_iota(jnp.int32, rows_ref.shape, 1)
-    centre = lax.shift_right_logical(m & 31, 1)
-    beside = centre - 1 + 2 * (m & 1)
+    row = 4 * (m & 7) + (lax.shift_right_logical(m, 3) & 3)
+    centre = lax.shift_right_logical(row, 1)
+    beside = centre - 1 + 2 * (row & 1)
     own = k < 64
     k_channel = jnp.where(own, lax.shift_right_logical(k, 4), k & 3)
     k_row = 2 * (k & 7) + (lax.shift_right_logical(k, 3) & 1)
@@ -402,7 +443,7 @@
 
 def inner_kernel(
     rank_ref, tables_ref, weights_ref, bulk_ref, inside_ref, second_ref, first_ref, mix_ref, along_ref,
-    image_ref, edge_ref, cells_ref, lines_ref,
+    image_ref, edge_ref, cells_ref, packed_ref, lines_ref, mixed_ref,
 ):
     layers, cols = inside_ref.shape
     depth = 2 * layers
@@ -436,18 +477,23 @@
         if tile in (0, tiles - 1):
             edge_ref[0 if tile == 0 else 1] = now
         else:
-            edge_lines(rounded(now), lines_ref.at[tile - 1], depth)
+            edge_lines(rounded(now), packed_ref.at[tile - 1], lines_ref.at[tile - 1], depth)
 
     image = render_pair(
-        [along_ref.at[1], along_ref.at[2]], [lines_ref.at[0], lines_ref.at[1]], mix_ref, rank_ref[0], layers
-    )
-    for channel in range(4):
-        image_ref[channel] = image[channel]
+        [along_ref.at[1], along_ref.at[2]],
+        [packed_ref.at[0], packed_ref.at[1]],
+        [lines_ref.at[0], lines_ref.at[1]],
+        mix_ref,
+        rank_ref[0],
+        layers,
+    )
+    for index in range(2):
+        store_tile(image[index], mixed_ref, image_ref, slice(index * LANES, (index + 1) * LANES))
 
 
 def outer_kernel(
     rank_ref, tables_ref, weights_ref, beside_ref, across_ref, mix_ref, along_ref, edge_ref, image_ref,
-    out_ref, ends_ref, values_ref, keep_ref, fixed_ref, lines_ref,
+    out_ref, ends_ref, values_ref, keep_ref, fixed_ref, packed_ref, lines_ref, mixed_ref,
 ):
     rows = out_ref.shape[1]
     cols = out_ref.shape[2] // 2
@@ -498,15 +544,19 @@
         fixed_ref[index, pad : pad + 2 * size, :] = rounded(
             along_ref[tile, pad : pad + 2 * size, :] + block[0 : 2 * size]
         )
-        edge_lines(rounded(edge_ref[index] + block[2 * size :]), lines_ref.at[index], depth)
+        edge_lines(rounded(edge_ref[index] + block[2 * size :]), packed_ref.at[index], lines_ref.at[index], depth)
     out_ref[:, :, LANES : 2 * cols - LANES] = image_ref[...]
 
     image = render_pair(
-        [fixed_ref.at[0], fixed_ref.at[1]], [lines_ref.at[0], lines_ref.at[1]], mix_ref, rank_ref[0], layers
-    )
-    for channel in range(4):
-        out_ref[channel, :, 0:LANES] = image[channel][:, 0:LANES]
-        out_ref[channel, :, 2 * cols - LANES : 2 * cols] = image[channel][:, LANES : 2 * LANES]
+        [fixed_ref.at[0], fixed_ref.at[1]],
+        [packed_ref.at[0], packed_ref.at[1]],
+        [lines_ref.at[0], lines_ref.at[1]],
+        mix_ref,
+        rank_ref[0],
+        layers,
+    )
+    for index, start in enumerate((0, 2 * cols - LANES)):
+        store_tile(image[index], mixed_ref, out_ref, slice(start, start + LANES))
 
 
 def two_slab_device(density, bin_index, tf_colour, tf_extinction, slab_rank):
@@ -594,13 +644,17 @@
         bulk, tables, weights, ends, along
     )
     smem = pl.BlockSpec(memory_space=pltpu.SMEM)
-    lines = pltpu.VMEM((2, 64 * layers, LANES), bf16)
+    lines = [
+        pltpu.VMEM((2, 32 * layers, LANES), bf16),
+        pltpu.VMEM((2, 16 * layers + 8, LANES), f32),
+        pltpu.VMEM((4, rows + 8, LANES), f32),
+    ]
     image, edge = call(
         inner_kernel,
         "inner_tiles",
         (pltpu.VMEM((4, rows, (tiles - 2) * LANES), f32), pltpu.VMEM((2, 16 * layers, LANES), f32)),
         2.0,
-        [pltpu.VMEM((cols // LANES, 16 * layers + 8, LANES), f32), lines],
+        [pltpu.VMEM((cols // LANES, 16 * layers + 8, LANES), f32)] + lines,
         [smem] + [VMEM] * 8,
     )(slab_rank, tables, weights, bulk, inside, second, first, mix, along)
     return call(
@@ -613,8 +667,8 @@
             pltpu.VMEM((8, 2 * layers, LANES), f32),
             pltpu.VMEM((16 * layers + 8, LANES), f32),
             pltpu.VMEM((2, 2 * size + 2 * 4 * half, LANES), f32),
-            lines,
-        ],
+        ]
+        + lines,
         [smem] + [VMEM] * 8,
     )(slab_rank, tables, weights, beside, across, mix, along, edge, image)
 

time: 16.1 us -> 16 us (level)
  no operation moved by 1% of the time
where the time goes in v17:
time: 16 us; the launch traced here: 15.8 us
  Pallas kernels  7.32 us (46%)
  starting transfers between devices  6.23 us (39%)
  waiting for transfers between devices  2.2 us (14%)
    pallas_call x8, Pallas kernels, run(): pl.pallas_call(kernel, out_shape=out_shape, in_specs=in_specs or [VMEM] *...  7.32 us
    ppermute x1, starting transfers between devices, two_slab_device(): bulk = lax.ppermute(bulk, 'bz', [(0, 1), (1, 0)])  3 us
    ppermute x1, waiting for transfers between devices, two_slab_device(): first = lax.ppermute(first, axes, ring)  2.19 us
    ppermute x1, starting transfers between devices, two_slab_device(): beside = lax.ppermute(ends, 'bx', both(pairs))  1.62 us
    ppermute x1, starting transfers between devices, two_slab_device(): first = lax.ppermute(first, axes, ring)  1.58 us
  transfers between devices with their start and end apart: 5, of which 1 were waited for; matrix products, arithmetic and copies ran while one was open for 0% of the time, Pallas kernels for 22%

profile of v17, /device:TPU:0, one launch (start us, length us, event | category | flops | bytes accessed | tf_op | source)
XLA Modules:
  0.0 15.8 jit_solution(5371542787525123493)
XLA Ops:
  0.0 1.2 %stage_block.1 = (s32[8,256]{1,0:T(8,128)S(1)}, s32[8,256]{1,0:T(8,128)S(1)}, s32[8,128]{1,0:T(8,128)S(1)}, f32[8,2,40,128]{3,2,1,0:T(8,128)S(1)}, s32[8,2,40,12...) custom-call(f32[8,32,256]{2,1,0:T(8,128)} %density_ref.1, s32[8,32,256]{2,1,0:T(8,128)} %bins_ref.1, ...), custom_call_target="tpu_custom_call" | custom-call | flops 1200000000 | bytes 4320000 | tf_op jit(solution)/shard_map/stage_block/pallas_call | solution.py:572
  1.2 0.1 pack_block.1
  1.3 3.0 %collective-permute-start = (s32[18,8,256]{2,1,0:T(8,128)S(1)}, s32[18,8,256]{2,1,0:T(8,128)S(1)}, u32[]{:S(2)}, u32[]{:S(2)}) collective-permute-start(s32[18,8,256]{2,1,0:T(8,128)S(1)} %get-tuple-element.23), channel_id=1, source_target_pairs={{0,16},{16,0},{1,17},{17,1},{2,18},{18,2},{3,19},{19,3},{4,20},{20... | collective-permute-start | bytes 442376 | tf_op jit(solution)/shard_map/ppermute | solution.py:620
  4.3 0.0 collective-permute-start.1
  4.3 1.6 %collective-permute-start.2 = (s32[8,256]{1,0:T(8,128)S(1)}, s32[8,256]{1,0:T(8,128)S(1)}, u32[]{:S(2)}, u32[]{:S(2)}) collective-permute-start(s32[8,256]{1,0:T(8,128)S(1)} %get-tuple-element.25), channel_id=1, source_target_pairs={{0,4},{1,5},{2,6},{3,7},{4,8},{5,9},{6,10},{7,11},{8,12},{9,13},{1... | collective-permute-start | bytes 24584 | tf_op jit(solution)/shard_map/ppermute | solution.py:621
  5.9 0.6 %own_cells.1 = (bf16[512,256]{1,0:T(8,128)(2,1)S(1)}, bf16[384,512]{1,0:T(8,128)(2,1)S(1)}, bf16[128,80]{1,0:T(8,128)(2,1)S(1)}) custom-call(f32[8,2,40,128]{3,2,1,0:T(8,128)S(1)} %get-tuple-element.19.dense_ref, s32[8,2,40,128]{3,2,1,0:T(8,128)S(1)} %get-tuple-element.20.index_ref, f32[8,8,128]{2,1,0:T(8,128)S(1)} %get-tuple-element.18.tables_ref), custom_call_target="tpu_custom_call" | custom-call | flops 500000000 | bytes 1800000 | tf_op jit(solution)/shard_map/own_cells/pallas_call | solution.py:572
  6.5 0.3 %own_slab.1.along_ref.own_ref = f32[4,1152,128]{2,1,0:T(8,128)S(1)} custom-call(bf16[512,256]{1,0:T(8,128)(2,1)S(1)} %get-tuple-element.26.cells_ref, bf16[384,512]{1,0:T(8,128)(2,1)S(1)} %get-tuple-element.21.weights_ref), custom_call_target="tpu_custom_call" | custom-call | flops 400000000 | bytes 1440000 | tf_op jit(solution)/shard_map/own_slab/pallas_call | solution.py:572
  6.8 0.0 collective-permute-done.1.second_ref
  6.8 2.2 %collective-permute-done.2.first_ref = s32[8,256]{1,0:T(8,128)S(1)} collective-permute-done((s32[8,256]{1,0:T(8,128)S(1)}, s32[8,256]{1,0:T(8,128)S(1)}, u32[]{:S(2)}, u32[]{:S(2)}) %collective-permute-start.2) | collective-permute-done | bytes 8224 | tf_op jit(solution)/shard_map/ppermute | solution.py:621
  9.0 0.0 collective-permute-done.bulk_ref
  9.0 0.1 side_columns.1.ends_ref
  9.0 0.0 copy-start
  9.0 0.0 collective-permute-start.4
  9.1 1.6 %collective-permute-start.3 = (s32[2,8,128]{2,1,0:T(8,128)S(1)}, s32[2,8,128]{2,1,0:T(8,128)S(1)}, u32[]{:S(2)}, u32[]{:S(2)}) collective-permute-start(s32[2,8,128]{2,1,0:T(8,128)S(1)} %side_columns.1.ends_ref), channel_id=1, source_target_pairs={{0,1},{2,3},{1,0},{3,2},{4,5},{6,7},{5,4},{7,6},{8,9},{10,11},{9,8... | collective-permute-start | bytes 24584 | tf_op jit(solution)/shard_map/ppermute | solution.py:641
  10.7 0.8 %other_slab.1.along_ref = f32[4,1152,128]{2,1,0:T(8,128)S(1)} custom-call(s32[18,8,256]{2,1,0:T(8,128)S(1)} %collective-permute-done.bulk_ref, f32[8,8,128]{2,1,0:T(8,128)S(1)} %get-tuple-element.18.tables_ref, bf16[384,512]{1,0:T(8,128)(2,1)S(1)} %get-tuple-element.21.weights_ref, ...), custom_call_target="tpu_custom_call", output_to_operand_aliasing={{}: (4, {})} | custom-call | flops 800000000 | bytes 2880000 | tf_op jit(solution)/shard_map/other_slab/pallas_call | solution.py:572
  11.5 0.0 copy-done
  11.5 1.8 %inner_tiles.1 = (f32[4,32,256]{2,1,0:T(8,128)S(1)}, f32[2,128,128]{2,1,0:T(8,128)S(1)}) custom-call(s32[2]{0:T(128)S(1)} %copy-done, f32[8,8,128]{2,1,0:T(8,128)S(1)} %get-tuple-element.18.tables_ref, bf16[384,512]{1,0:T(8,128)(2,1)S(1)} %get-tuple-element.21.weights_ref, s32[18,8,256]{2,1,0:T(8,128)S(1)} %collective-permute-done.bulk_ref, ...), custom_call_target="tpu_custom_call" | custom-call | flops 2000000000 | bytes 7200000 | tf_op jit(solution)/shard_map/inner_tiles/pallas_call | solution.py:572
  13.3 0.0 collective-permute-done.4.across_ref
  13.3 0.0 collective-permute-done.3.beside_ref
  13.3 2.5 %outer_tiles.1 = f32[4,32,512]{2,1,0:T(8,128)} custom-call(s32[2]{0:T(128)S(1)} %copy-done, f32[8,8,128]{2,1,0:T(8,128)S(1)} %get-tuple-element.18.tables_ref, bf16[384,512]{1,0:T(8,128)(2,1)S(1)} %get-tuple-element.21.weights_ref, s32[2,8,128]{2,1,0:T(8,128)S(1)} %collective-permute-done.3.beside_ref, s32[2,8,128]{2,1,0:T(8,128)S(1)} %collective-permute-done.4.across_ref, ...), custom_call_target="tpu_custom_call" | custom-call | flops 2000000000 | bytes 7200000 | tf_op jit(solution)/shard_map/outer_tiles/pallas_call | solution.py:572
Async XLA Ops:
  1.3 7.7 %collective-permute-start = (s32[18,8,256]{2,1,0:T(8,128)S(1)}, s32[18,8,256]{2,1,0:T(8,128)S(1)}, u32[]{:S(2)}, u32[]{:S(2)}) collective-permute-start(s32[18,8,256]{2,1,0:T(8,128)S(1)} %get-tuple-element.23), channel_id=1, source_target_pairs={{0,16},{16,0},{1,17},{17,1},{2,18},{18,2},{3,19},{19,3},{4,20},{20... | collective-permute-start | bytes 442376 | tf_op jit(solution)/shard_map/ppermute | solution.py:620
  4.3 2.5 %collective-permute-start.1 = (s32[8,256]{1,0:T(8,128)S(1)}, s32[8,256]{1,0:T(8,128)S(1)}, u32[]{:S(2)}, u32[]{:S(2)}) collective-permute-start(s32[8,256]{1,0:T(8,128)S(1)} %get-tuple-element.24), channel_id=1, source_target_pairs={{16,4},{17,5},{18,6},{19,7},{20,8},{21,9},{22,10},{23,11},{24,12},... | collective-permute-start | bytes 24584 | tf_op jit(solution)/shard_map/ppermute | solution.py:622
  4.3 4.7 %collective-permute-start.2 = (s32[8,256]{1,0:T(8,128)S(1)}, s32[8,256]{1,0:T(8,128)S(1)}, u32[]{:S(2)}, u32[]{:S(2)}) collective-permute-start(s32[8,256]{1,0:T(8,128)S(1)} %get-tuple-element.25), channel_id=1, source_target_pairs={{0,4},{1,5},{2,6},{3,7},{4,8},{5,9},{6,10},{7,11},{8,12},{9,13},{1... | collective-permute-start | bytes 24584 | tf_op jit(solution)/shard_map/ppermute | solution.py:621
  9.0 2.5 %copy-start = (s32[2]{0:T(128)S(1)}, s32[2]{0:T(128)}, u32[]{:S(2)}) copy-start(s32[2]{0:T(128)} %rank_ref.3) | copy-start | bytes 28
  9.0 4.2 %collective-permute-start.4 = (s32[2,8,128]{2,1,0:T(8,128)S(1)}, s32[2,8,128]{2,1,0:T(8,128)S(1)}, u32[]{:S(2)}, u32[]{:S(2)}) collective-permute-start(s32[2,8,128]{2,1,0:T(8,128)S(1)} %side_columns.1.ends_ref), channel_id=1, source_target_pairs={{1,2},{3,0},{2,1},{0,3},{5,6},{7,4},{6,5},{4,7},{9,10},{11,8},{10,... | collective-permute-start | bytes 24584 | tf_op jit(solution)/shard_map/ppermute | solution.py:642
  9.1 4.2 %collective-permute-start.3 = (s32[2,8,128]{2,1,0:T(8,128)S(1)}, s32[2,8,128]{2,1,0:T(8,128)S(1)}, u32[]{:S(2)}, u32[]{:S(2)}) collective-permute-start(s32[2,8,128]{2,1,0:T(8,128)S(1)} %side_columns.1.ends_ref), channel_id=1, source_target_pairs={{0,1},{2,3},{1,0},{3,2},{4,5},{6,7},{5,4},{7,6},{8,9},{10,11},{9,8... | collective-permute-start | bytes 24584 | tf_op jit(solution)/shard_map/ppermute | solution.py:641

commit v18 on v17

--- a/solution.py
+++ b/solution.py
@@ -155,9 +155,10 @@
 
 
 def stage_kernel(
-    density_ref, bins_ref, colour_ref, extinction_ref,
-    first_ref, second_ref, columns_ref, dense_ref, index_ref, tables_ref,
+    rank_ref, density_ref, bins_ref, colour_ref, extinction_ref,
+    flip_ref, first_ref, second_ref, columns_ref, dense_ref, index_ref, tables_ref,
 ):
+    flip_ref[0] = rank_ref[0]
     layers, rows, cols = density_ref.shape
     front = lax.axis_index("bz") == 0
     row_at = lax.broadcasted_iota(jnp.int32, (rows, LANES), 0)
@@ -442,7 +443,7 @@
 
 
 def inner_kernel(
-    rank_ref, tables_ref, weights_ref, bulk_ref, inside_ref, second_ref, first_ref, mix_ref, along_ref,
+    flip_ref, tables_ref, weights_ref, bulk_ref, inside_ref, second_ref, first_ref, mix_ref, along_ref,
     image_ref, edge_ref, cells_ref, packed_ref, lines_ref, mixed_ref,
 ):
     layers, cols = inside_ref.shape
@@ -484,7 +485,7 @@
         [packed_ref.at[0], packed_ref.at[1]],
         [lines_ref.at[0], lines_ref.at[1]],
         mix_ref,
-        rank_ref[0],
+        flip_ref[0],
         layers,
     )
     for index in range(2):
@@ -492,7 +493,7 @@
 
 
 def outer_kernel(
-    rank_ref, tables_ref, weights_ref, beside_ref, across_ref, mix_ref, along_ref, edge_ref, image_ref,
+    flip_ref, tables_ref, weights_ref, beside_ref, across_ref, mix_ref, along_ref, edge_ref, image_ref,
     out_ref, ends_ref, values_ref, keep_ref, fixed_ref, packed_ref, lines_ref, mixed_ref,
 ):
     rows = out_ref.shape[1]
@@ -552,7 +553,7 @@
         [packed_ref.at[0], packed_ref.at[1]],
         [lines_ref.at[0], lines_ref.at[1]],
         mix_ref,
-        rank_ref[0],
+        flip_ref[0],
         layers,
     )
     for index, start in enumerate((0, 2 * cols - LANES)):
@@ -567,13 +568,14 @@
     count_y, count_x = lax.axis_size("by"), lax.axis_size("bx")
     f32, bf16, i32 = jnp.float32, jnp.bfloat16, jnp.int32
 
-    def call(kernel, name, out_shape, time, scratch_shapes=(), in_specs=None, aliases={}):
+    def call(kernel, name, out_shape, time, scratch_shapes=(), in_specs=None, out_specs=None, aliases={}):
         def run(*operands):
             return pl.pallas_call(
                 kernel,
                 out_shape=out_shape,
                 in_specs=in_specs or [VMEM] * len(operands),
-                out_specs=(VMEM,) * len(out_shape) if isinstance(out_shape, tuple) else VMEM,
+                out_specs=out_specs
+                or ((VMEM,) * len(out_shape) if isinstance(out_shape, tuple) else VMEM),
                 scratch_shapes=scratch_shapes,
                 input_output_aliases=aliases,
                 compiler_params=pltpu.CompilerParams(vmem_limit_bytes=16 * 1024 * 1024),
@@ -588,10 +590,16 @@
 
     blocks = (layers, cols // LANES, rows + 8, LANES)
     row = pltpu.VMEM((layers, cols), i32)
-    first, second, columns, dense, index, tables = call(
+    smem = pl.BlockSpec(memory_space=pltpu.SMEM)
+    inputs = [
+        pltpu.with_memory_space_constraint(x, pltpu.HBM)
+        for x in (slab_rank, density, bin_index, tf_colour, tf_extinction)
+    ]
+    flip, first, second, columns, dense, index, tables = call(
         stage_kernel,
         "stage_block",
         (
+            pltpu.SMEM((1,), i32),
             row,
             row,
             pltpu.VMEM((layers, LANES), i32),
@@ -600,7 +608,9 @@
             pltpu.VMEM((8, 8, LANES), f32),
         ),
         1.2,
-    )(*[pltpu.with_memory_space_constraint(x, pltpu.HBM) for x in (density, bin_index, tf_colour, tf_extinction)])
+        in_specs=[smem] + [VMEM] * 4,
+        out_specs=(smem,) + (VMEM,) * 6,
+    )(*inputs)
     bulk, inside = call(
         pack_kernel, "pack_block", (pltpu.VMEM((2 * layers + 2, 8, cols), i32), row), 0.1
     )(dense, index, columns)
@@ -643,7 +653,6 @@
     along = call(other_kernel, "other_slab", whole, 0.8, [pltpu.VMEM((size, cols), bf16)], aliases={4: 0})(
         bulk, tables, weights, ends, along
     )
-    smem = pl.BlockSpec(memory_space=pltpu.SMEM)
     lines = [
         pltpu.VMEM((2, 32 * layers, LANES), bf16),
         pltpu.VMEM((2, 16 * layers + 8, LANES), f32),
@@ -656,7 +665,7 @@
         2.0,
         [pltpu.VMEM((cols // LANES, 16 * layers + 8, LANES), f32)] + lines,
         [smem] + [VMEM] * 8,
-    )(slab_rank, tables, weights, bulk, inside, second, first, mix, along)
+    )(flip, tables, weights, bulk, inside, second, first, mix, along)
     return call(
         outer_kernel,
         "outer_tiles",
@@ -670,7 +679,7 @@
         ]
         + lines,
         [smem] + [VMEM] * 8,
-    )(slab_rank, tables, weights, beside, across, mix, along, edge, image)
+    )(flip, tables, weights, beside, across, mix, along, edge, image)
 
 
 def on_device(density, bin_index, tf_colour, tf_extinction, slab_rank):

time: 16 us -> 14.9 us (0.931)
  Pallas kernels: 7.32 us -> 6.25 us
    pallas_call x8, Pallas kernels: 7.32 us -> 6.25 us  [run(): pl.pallas_call(kernel, out_shape=out_shape, in_specs=in_specs or [VMEM] *...]
  transfers between devices with their start and end apart: 5 -> 5, of which waited for: 1 -> 1; matrix products, arithmetic and copies ran while one was open for 0% -> 0% of each run, Pallas kernels for 22% -> 20%
where the time goes in v18:
time: 14.9 us; the launch traced here: 14.7 us
  Pallas kernels  6.25 us (42%)
  starting transfers between devices  6.22 us (42%)
  waiting for transfers between devices  2.2 us (15%)
    pallas_call x8, Pallas kernels, run(): pl.pallas_call(kernel, out_shape=out_shape, in_specs=in_specs or [VMEM] *...  6.25 us
    ppermute x1, starting transfers between devices, two_slab_device(): bulk = lax.ppermute(bulk, 'bz', [(0, 1), (1, 0)])  3 us
    ppermute x1, waiting for transfers between devices, two_slab_device(): first = lax.ppermute(first, axes, ring)  2.19 us
    ppermute x1, starting transfers between devices, two_slab_device(): beside = lax.ppermute(ends, 'bx', both(pairs))  1.62 us
    ppermute x1, starting transfers between devices, two_slab_device(): first = lax.ppermute(first, axes, ring)  1.58 us
  transfers between devices with their start and end apart: 5, of which 1 were waited for; matrix products, arithmetic and copies ran while one was open for 0% of the time, Pallas kernels for 20%

profile of v18, /device:TPU:0, one launch (start us, length us, event | category | flops | bytes accessed | tf_op | source)
XLA Modules:
  0.0 14.7 jit_solution(1147244968486702226)
XLA Ops:
  0.0 1.2 %stage_block.1 = (s32[1]{0:T(128)S(4)}, s32[8,256]{1,0:T(8,128)S(1)}, s32[8,256]{1,0:T(8,128)S(1)}, s32[8,128]{1,0:T(8,128)S(1)}, f32[8,2,40,128]{3,2,1,0:T(8,12...) custom-call(s32[2]{0:T(128)} %rank_ref.1, f32[8,32,256]{2,1,0:T(8,128)} %density_ref.1, ...), custom_call_target="tpu_custom_call" | custom-call | flops 1200000000 | bytes 4320000 | tf_op jit(solution)/shard_map/stage_block/pallas_call | solution.py:573
  1.2 0.1 pack_block.1
  1.3 3.0 %collective-permute-start = (s32[18,8,256]{2,1,0:T(8,128)S(1)}, s32[18,8,256]{2,1,0:T(8,128)S(1)}, u32[]{:S(2)}, u32[]{:S(2)}) collective-permute-start(s32[18,8,256]{2,1,0:T(8,128)S(1)} %get-tuple-element.25), channel_id=1, source_target_pairs={{0,16},{16,0},{1,17},{17,1},{2,18},{18,2},{3,19},{19,3},{4,20},{20... | collective-permute-start | bytes 442376 | tf_op jit(solution)/shard_map/ppermute | solution.py:630
  4.3 0.0 collective-permute-start.1
  4.3 1.6 %collective-permute-start.2 = (s32[8,256]{1,0:T(8,128)S(1)}, s32[8,256]{1,0:T(8,128)S(1)}, u32[]{:S(2)}, u32[]{:S(2)}) collective-permute-start(s32[8,256]{1,0:T(8,128)S(1)} %get-tuple-element.27), channel_id=1, source_target_pairs={{0,4},{1,5},{2,6},{3,7},{4,8},{5,9},{6,10},{7,11},{8,12},{9,13},{1... | collective-permute-start | bytes 24584 | tf_op jit(solution)/shard_map/ppermute | solution.py:631
  5.9 0.6 %own_cells.1 = (bf16[512,256]{1,0:T(8,128)(2,1)S(1)}, bf16[384,512]{1,0:T(8,128)(2,1)S(1)}, bf16[128,80]{1,0:T(8,128)(2,1)S(1)}) custom-call(f32[8,2,40,128]{3,2,1,0:T(8,128)S(1)} %get-tuple-element.21.dense_ref, s32[8,2,40,128]{3,2,1,0:T(8,128)S(1)} %get-tuple-element.22.index_ref, f32[8,8,128]{2,1,0:T(8,128)S(1)} %get-tuple-element.20.tables_ref), custom_call_target="tpu_custom_call" | custom-call | flops 500000000 | bytes 1800000 | tf_op jit(solution)/shard_map/own_cells/pallas_call | solution.py:573
  6.5 0.3 %own_slab.1.along_ref.own_ref = f32[4,1152,128]{2,1,0:T(8,128)S(1)} custom-call(bf16[512,256]{1,0:T(8,128)(2,1)S(1)} %get-tuple-element.28.cells_ref, bf16[384,512]{1,0:T(8,128)(2,1)S(1)} %get-tuple-element.23.weights_ref), custom_call_target="tpu_custom_call" | custom-call | flops 400000000 | bytes 1440000 | tf_op jit(solution)/shard_map/own_slab/pallas_call | solution.py:573
  6.8 0.0 collective-permute-done.1.second_ref
  6.8 2.2 %collective-permute-done.2.first_ref = s32[8,256]{1,0:T(8,128)S(1)} collective-permute-done((s32[8,256]{1,0:T(8,128)S(1)}, s32[8,256]{1,0:T(8,128)S(1)}, u32[]{:S(2)}, u32[]{:S(2)}) %collective-permute-start.2) | collective-permute-done | bytes 8224 | tf_op jit(solution)/shard_map/ppermute | solution.py:631
  9.0 0.0 collective-permute-done.bulk_ref
  9.0 0.1 side_columns.1.ends_ref
  9.0 0.0 collective-permute-start.4
  9.1 1.6 %collective-permute-start.3 = (s32[2,8,128]{2,1,0:T(8,128)S(1)}, s32[2,8,128]{2,1,0:T(8,128)S(1)}, u32[]{:S(2)}, u32[]{:S(2)}) collective-permute-start(s32[2,8,128]{2,1,0:T(8,128)S(1)} %side_columns.1.ends_ref), channel_id=1, source_target_pairs={{0,1},{2,3},{1,0},{3,2},{4,5},{6,7},{5,4},{7,6},{8,9},{10,11},{9,8... | collective-permute-start | bytes 24584 | tf_op jit(solution)/shard_map/ppermute | solution.py:651
  10.7 0.8 %other_slab.1.along_ref = f32[4,1152,128]{2,1,0:T(8,128)S(1)} custom-call(s32[18,8,256]{2,1,0:T(8,128)S(1)} %collective-permute-done.bulk_ref, f32[8,8,128]{2,1,0:T(8,128)S(1)} %get-tuple-element.20.tables_ref, bf16[384,512]{1,0:T(8,128)(2,1)S(1)} %get-tuple-element.23.weights_ref, ...), custom_call_target="tpu_custom_call", output_to_operand_aliasing={{}: (4, {})} | custom-call | flops 800000000 | bytes 2880000 | tf_op jit(solution)/shard_map/other_slab/pallas_call | solution.py:573
  11.5 1.2 %inner_tiles.1 = (f32[4,32,256]{2,1,0:T(8,128)S(1)}, f32[2,128,128]{2,1,0:T(8,128)S(1)}) custom-call(s32[1]{0:T(128)S(4)} %get-tuple-element.19.flip_ref, f32[8,8,128]{2,1,0:T(8,128)S(1)} %get-tuple-element.20.tables_ref, bf16[384,512]{1,0:T(8,128)(2,1)S(1)} %get-tuple-element.23.weights_ref, s32[18,8,256]{2,1,0:T(8,128)S(1)} %collective-permute-done.bulk_ref, ...), custom_call_target="tpu_custom_call" | custom-call | flops 2000000000 | bytes 7200000 | tf_op jit(solution)/shard_map/inner_tiles/pallas_call | solution.py:573
  12.7 0.0 collective-permute-done.4.across_ref
  12.7 0.0 collective-permute-done.3.beside_ref
  12.8 2.0 %outer_tiles.1 = f32[4,32,512]{2,1,0:T(8,128)} custom-call(s32[1]{0:T(128)S(4)} %get-tuple-element.19.flip_ref, f32[8,8,128]{2,1,0:T(8,128)S(1)} %get-tuple-element.20.tables_ref, bf16[384,512]{1,0:T(8,128)(2,1)S(1)} %get-tuple-element.23.weights_ref, s32[2,8,128]{2,1,0:T(8,128)S(1)} %collective-permute-done.3.beside_ref, ...), custom_call_target="tpu_custom_call" | custom-call | flops 2000000000 | bytes 7200000 | tf_op jit(solution)/shard_map/outer_tiles/pallas_call | solution.py:573
Async XLA Ops:
  1.3 7.7 %collective-permute-start = (s32[18,8,256]{2,1,0:T(8,128)S(1)}, s32[18,8,256]{2,1,0:T(8,128)S(1)}, u32[]{:S(2)}, u32[]{:S(2)}) collective-permute-start(s32[18,8,256]{2,1,0:T(8,128)S(1)} %get-tuple-element.25), channel_id=1, source_target_pairs={{0,16},{16,0},{1,17},{17,1},{2,18},{18,2},{3,19},{19,3},{4,20},{20... | collective-permute-start | bytes 442376 | tf_op jit(solution)/shard_map/ppermute | solution.py:630
  4.3 2.5 %collective-permute-start.1 = (s32[8,256]{1,0:T(8,128)S(1)}, s32[8,256]{1,0:T(8,128)S(1)}, u32[]{:S(2)}, u32[]{:S(2)}) collective-permute-start(s32[8,256]{1,0:T(8,128)S(1)} %get-tuple-element.26), channel_id=1, source_target_pairs={{16,4},{17,5},{18,6},{19,7},{20,8},{21,9},{22,10},{23,11},{24,12},... | collective-permute-start | bytes 24584 | tf_op jit(solution)/shard_map/ppermute | solution.py:632
  4.3 4.7 %collective-permute-start.2 = (s32[8,256]{1,0:T(8,128)S(1)}, s32[8,256]{1,0:T(8,128)S(1)}, u32[]{:S(2)}, u32[]{:S(2)}) collective-permute-start(s32[8,256]{1,0:T(8,128)S(1)} %get-tuple-element.27), channel_id=1, source_target_pairs={{0,4},{1,5},{2,6},{3,7},{4,8},{5,9},{6,10},{7,11},{8,12},{9,13},{1... | collective-permute-start | bytes 24584 | tf_op jit(solution)/shard_map/ppermute | solution.py:631
  9.0 3.7 %collective-permute-start.4 = (s32[2,8,128]{2,1,0:T(8,128)S(1)}, s32[2,8,128]{2,1,0:T(8,128)S(1)}, u32[]{:S(2)}, u32[]{:S(2)}) collective-permute-start(s32[2,8,128]{2,1,0:T(8,128)S(1)} %side_columns.1.ends_ref), channel_id=1, source_target_pairs={{1,2},{3,0},{2,1},{0,3},{5,6},{7,4},{6,5},{4,7},{9,10},{11,8},{10,... | collective-permute-start | bytes 24584 | tf_op jit(solution)/shard_map/ppermute | solution.py:652
  9.1 3.7 %collective-permute-start.3 = (s32[2,8,128]{2,1,0:T(8,128)S(1)}, s32[2,8,128]{2,1,0:T(8,128)S(1)}, u32[]{:S(2)}, u32[]{:S(2)}) collective-permute-start(s32[2,8,128]{2,1,0:T(8,128)S(1)} %side_columns.1.ends_ref), channel_id=1, source_target_pairs={{0,1},{2,3},{1,0},{3,2},{4,5},{6,7},{5,4},{7,6},{8,9},{10,11},{9,8... | collective-permute-start | bytes 24584 | tf_op jit(solution)/shard_map/ppermute | solution.py:651

commit v19 on v18

--- a/solution.py
+++ b/solution.py
@@ -1,3 +1,5 @@
+import functools
+
 import jax
 import jax.numpy as jnp
 from jax import lax
@@ -166,7 +168,7 @@
     for z in range(layers):
         first = pack_words(density_ref[z, :, 0:1], bins_ref[z, :, 0:1])
         last = pack_words(density_ref[z, :, cols - 1 : cols], bins_ref[z, :, cols - 1 : cols])
-        line = jnp.where(lane_at == row_at, first, 0) + jnp.where(lane_at == row_at + rows, last, 0)
+        line = jnp.where(lane_at == row_at, first, 0) + jnp.where(lane_at == row_at + LANES // 2, last, 0)
         columns_ref[z : z + 1, :] = jnp.sum(line, axis=0, keepdims=True)
         top, bottom = [
             pack_words(density_ref[z, r : r + 1, :], bins_ref[z, r : r + 1, :]) for r in (0, rows - 1)
@@ -215,7 +217,7 @@
     return jnp.where(has_near(me == 0), words, 0)
 
 
-def side_kernel(columns_ref, bulk_ref, second_ref, first_ref, along_ref, ends_ref):
+def side_kernel(rows, columns_ref, bulk_ref, second_ref, first_ref, along_ref, ends_ref):
     layers = columns_ref.shape[0]
     front = lax.axis_index("bz") == 0
     lane_at = lax.broadcasted_iota(jnp.int32, (layers, LANES), 1)
@@ -224,8 +226,10 @@
         columns = jnp.where(mine, columns_ref[...], bulk_ref[2 * layers + 1, :, 0:LANES])
         near = near_words(slab, first_ref, second_ref)
         cols = near.shape[1]
-        columns = jnp.where(lane_at == 64, near[:, 0:1], columns)
-        ends_ref[slab] = jnp.where(lane_at == 65, near[:, cols - 1 : cols], columns)
+        columns = jnp.where(lane_at == rows, near[:, 0:1], columns)
+        ends_ref[slab] = jnp.where(
+            lane_at == LANES // 2 + rows, near[:, cols - 1 : cols], columns
+        )
 
 
 def has_near(front):
@@ -233,28 +237,15 @@
     return jnp.where(front, me_y > 0, me_y + 1 < lax.axis_size("by"))
 
 
-def fill_weights(weights_ref, rows):
-    cols = weights_ref.shape[0] - LANES
+def fill_weights(weights_ref):
+    cols = weights_ref.shape[0]
     row = lax.broadcasted_iota(jnp.int32, (cols, 2 * cols), 0)
     at = lax.broadcasted_iota(jnp.int32, (cols, 2 * cols), 1)
     centre = lax.shift_right_logical(at, 1)
     beside = centre - 1 + 2 * (at & 1)
-    weights_ref[0:cols, :] = jnp.where(
-        row == centre, 3.0, jnp.where(row == beside, 1.0, 0.0)
-    ).astype(jnp.bfloat16)
-    row = lax.broadcasted_iota(jnp.int32, (LANES, 2 * LANES), 0)
-    at = lax.broadcasted_iota(jnp.int32, (LANES, 2 * LANES), 1)
-    right = ((row < rows) | (row == 64)) & (at == 2 * LANES - 1)
-    left = (((row >= rows) & (row < 2 * rows)) | (row == 65)) & (at == 0)
-    weights_ref[cols : cols + LANES, 0 : 2 * LANES] = jnp.where(right | left, 1.0, 0.0).astype(
+    weights_ref[...] = jnp.where(row == centre, 3.0, jnp.where(row == beside, 1.0, 0.0)).astype(
         jnp.bfloat16
     )
-
-
-def lane_maps(rows):
-    lane_at = lax.broadcasted_iota(jnp.int32, (8, LANES), 1)
-    sub_at = lax.broadcasted_iota(jnp.int32, (8, LANES), 0)
-    return lane_at & (rows - 1), lane_at < 2 * rows, sub_at
 
 
 def classify_rows(read_cells, tables, cells_ref, layers, tiles):
@@ -277,7 +268,7 @@
     layers, tiles, rows = dense_ref.shape[0], dense_ref.shape[1], dense_ref.shape[2] - 8
     half = rows // 2
     start = lax.axis_index("bz") * half
-    fill_weights(weights_ref, rows)
+    fill_weights(weights_ref)
     fill_rows(mix_ref)
 
     def read_cells(z, part, tile):
@@ -288,12 +279,9 @@
 
 
 def along_columns(cells, weights_ref, store):
-    cols = cells.shape[1]
-    tiles = 2 * cols // LANES
-    result = jnp.dot(cells, weights_ref[0:cols, :], preferred_element_type=jnp.float32)
-    for tile in range(tiles):
-        block = result[:, tile * LANES : (tile + 1) * LANES]
-        store(tile, block if tile in (0, tiles - 1) else rounded(block))
+    result = rounded(jnp.dot(cells, weights_ref[...], preferred_element_type=jnp.float32))
+    for tile in range(result.shape[1] // LANES):
+        store(tile, result[:, tile * LANES : (tile + 1) * LANES])
 
 
 def own_kernel(cells_ref, weights_ref, along_ref):
@@ -420,13 +408,6 @@
     return lax.fori_loop(0, 2, one_slab, image)
 
 
-def store_tile(image, mixed_ref, out_ref, lanes):
-    for channel in range(4):
-        for i in range(4):
-            mixed_ref[channel, pl.ds(i, 8, stride=4), :] = image[channel][i]
-        out_ref[channel, :, lanes] = mixed_ref[channel, 0:32]
-
-
 def fill_rows(rows_ref):
     m = lax.broadcasted_iota(jnp.int32, rows_ref.shape, 0)
     k = lax.broadcasted_iota(jnp.int32, rows_ref.shape, 1)
@@ -442,9 +423,9 @@
     rows_ref[...] = jnp.where(same, value, 0.0).astype(jnp.bfloat16)
 
 
-def inner_kernel(
-    flip_ref, tables_ref, weights_ref, bulk_ref, inside_ref, second_ref, first_ref, mix_ref, along_ref,
-    image_ref, edge_ref, cells_ref, packed_ref, lines_ref, mixed_ref,
+def tiles_kernel(
+    flip_ref, tables_ref, weights_ref, bulk_ref, inside_ref, second_ref, first_ref, ends_ref, mix_ref,
+    along_ref, image_ref, mine_ref, cells_ref, packed_ref, lines_ref,
 ):
     layers, cols = inside_ref.shape
     depth = 2 * layers
@@ -465,99 +446,129 @@
                 for channel in range(4):
                     at = pl.ds(slab * layers * 8 + side * 4 + channel, layers, stride=8)
                     cells_ref[t, at, :] = values[channel]
-    edge = sum(
-        jnp.dot(
-            cells_ref[t, 0 : 8 * depth].astype(jnp.bfloat16),
-            weights_ref[t * LANES : (t + 1) * LANES, :],
-            preferred_element_type=jnp.float32,
+        values = cell_values(*unpack_words(ends_ref[slab]), tables, float(depth))
+        for channel in range(4):
+            mine_ref[slab * 4 + channel] = 3.0 * rounded(values[channel])
+    edge = rounded(
+        sum(
+            jnp.dot(
+                cells_ref[t, 0 : 8 * depth].astype(jnp.bfloat16),
+                weights_ref[t * LANES : (t + 1) * LANES, :],
+                preferred_element_type=jnp.float32,
+            )
+            for t in range(cols // LANES)
         )
-        for t in range(cols // LANES)
     )
     for tile in range(tiles):
         now = edge[:, tile * LANES : (tile + 1) * LANES]
-        if tile in (0, tiles - 1):
-            edge_ref[0 if tile == 0 else 1] = now
-        else:
-            edge_lines(rounded(now), packed_ref.at[tile - 1], lines_ref.at[tile - 1], depth)
-
-    image = render_pair(
-        [along_ref.at[1], along_ref.at[2]],
-        [packed_ref.at[0], packed_ref.at[1]],
-        [lines_ref.at[0], lines_ref.at[1]],
-        mix_ref,
-        flip_ref[0],
-        layers,
-    )
-    for index in range(2):
-        store_tile(image[index], mixed_ref, image_ref, slice(index * LANES, (index + 1) * LANES))
-
-
-def outer_kernel(
-    flip_ref, tables_ref, weights_ref, beside_ref, across_ref, mix_ref, along_ref, edge_ref, image_ref,
-    out_ref, ends_ref, values_ref, keep_ref, fixed_ref, packed_ref, lines_ref, mixed_ref,
+        edge_lines(now, packed_ref.at[tile], lines_ref.at[tile], depth)
+
+    def one_pair(pair, carry):
+        at = [2 * pair, 2 * pair + 1]
+        image = render_pair(
+            [along_ref.at[tile] for tile in at],
+            [packed_ref.at[tile] for tile in at],
+            [lines_ref.at[tile] for tile in at],
+            mix_ref,
+            flip_ref[0],
+            layers,
+        )
+        for index, tile in enumerate(at):
+            for channel in range(4):
+                for i in range(4):
+                    image_ref[tile, channel, pl.ds(i, 8, stride=4), :] = image[index][channel][i]
+        return carry
+
+    lax.fori_loop(0, tiles // 2, one_pair, 0)
+
+
+def edge_kernel(
+    flip_ref, tables_ref, beside_ref, across_ref, mine_ref, image_ref,
+    out_ref, samples_ref, final_ref, turned_ref, fixed_ref,
 ):
     rows = out_ref.shape[1]
     cols = out_ref.shape[2] // 2
+    half = rows // 2
     layers = beside_ref.shape[1]
-    depth = 2 * layers
     tiles = 2 * cols // LANES
-    pad = 64
-    size = layers * pad
+    middle = LANES // 2
     front = lax.axis_index("bz") == 0
-    start = lax.axis_index("bz") * (rows // 2)
+    start = pl.multiple_of(lax.axis_index("bz") * half, half)
     me_x = lax.axis_index("bx")
     even_x = lax.rem(me_x, 2) == 0
     tables = read_tables(tables_ref)
-    side_lane, has_side, sub_at = lane_maps(rows)
-    masks = [has_side & (side_lane == start + 2 * sub_at + part) for part in range(2)]
     lane_at = lax.broadcasted_iota(jnp.int32, (layers, LANES), 1)
-    is_right = (lane_at < rows) | (lane_at == 64)
+    layer_at = lax.broadcasted_iota(jnp.int32, (layers, LANES), 0)
+    first_lane = (lane_at & (middle - 1)) == 0
+    along = [[], []]
     for slab in range(2):
         right = jnp.where(even_x, beside_ref[slab], across_ref[slab])
         left = jnp.where(even_x, across_ref[slab], beside_ref[slab])
         right = jnp.where(me_x + 1 < lax.axis_size("bx"), right, 0)
         left = jnp.where(me_x > 0, left, 0)
-        words = jnp.where(is_right, right, left)
-        values = cell_values(*unpack_words(words), tables, float(depth))
+        words = pltpu.roll(jnp.where(lane_at < middle, right, left), middle, 1)
+        halo = cell_values(*unpack_words(words), tables, float(2 * layers))
         for channel in range(4):
-            values_ref[slab * 4 + channel, 0:layers] = values[channel]
+            along[slab].append(rounded(mine_ref[slab * 4 + channel] + rounded(halo[channel])))
+    for channel in range(4):
+        front_part, back_part = along[0][channel], along[1][channel]
+        down = [pltpu.roll(front_part, 1, 0), pltpu.roll(back_part, 1, 0)]
+        up = [pltpu.roll(front_part, layers - 1, 0), pltpu.roll(back_part, layers - 1, 0)]
+        is_first, is_last = layer_at == 0, layer_at == layers - 1
+        before = [jnp.where(is_first, 0.0, down[0]), jnp.where(is_first, down[0], down[1])]
+        after = [jnp.where(is_last, up[1], up[0]), jnp.where(is_last, 0.0, up[1])]
+        for slab in range(2):
+            triple = 3.0 * along[slab][channel]
+            for parity, other in enumerate((before[slab], after[slab])):
+                mixed = rounded(other + triple)
+                centre = 3.0 * mixed
+                above = pltpu.roll(mixed, 1, 1)
+                near = pltpu.roll(mixed, LANES - rows, 1)
+                above = jnp.where(first_lane, jnp.where(front, near, above), above)
+                below = pltpu.roll(mixed, LANES - 1, 1)
+                for odd, value in enumerate((above + centre, centre + below)):
+                    at = (parity * 2 + odd) * 4 + channel
+                    samples_ref[slab, at, 0:layers, :] = value
+
+    def one_slab(position, image):
+        slab = position ^ flip_ref[0]
         for z in range(layers):
-            for channel in range(4):
-                line = values_ref[slab * 4 + channel, pl.ds(z, 8, stride=0), :]
-                block = jnp.concatenate([jnp.where(mask, line, 0.0) for mask in masks], axis=0)
-                at = slab * size + (z * 4 + channel) * 16
-                ends_ref[at : at + 16, :] = block.astype(jnp.bfloat16)
-        for side in range(2):
-            row = jnp.where(front, 64, rows // 2 - 1) if side == 0 else jnp.where(front, rows // 2, 64)
-            twin = jnp.where(row == 64, 65, row + rows)
-            keep = (lane_at == row) | (lane_at == twin)
-            for channel in range(4):
-                at = pl.ds(slab * layers * 8 + side * 4 + channel, layers, stride=8)
-                keep_ref[at, :] = jnp.where(keep, values[channel], 0.0)
-    ends_ref[2 * size :, :] = keep_ref[0 : 8 * depth].astype(jnp.bfloat16)
-    added = jnp.dot(
-        ends_ref[...], weights_ref[cols : cols + LANES, 0 : 2 * LANES], preferred_element_type=jnp.float32
-    )
+            for parity in range(2):
+                clear = [1.0 - image[odd][3] for odd in range(2)]
+                image = [
+                    [
+                        image[odd][channel]
+                        + clear[odd]
+                        * samples_ref[slab, (parity * 2 + odd) * 4 + channel, pl.ds(z, 8, stride=0), :]
+                        for channel in range(4)
+                    ]
+                    for odd in range(2)
+                ]
+        return image
+
+    zero = jnp.zeros((8, LANES), jnp.float32)
+    image = lax.fori_loop(0, 2, one_slab, [[zero] * 4 for _ in range(2)])
+    final_ref[8:, :] = jnp.zeros((LANES - 8, LANES), jnp.float32)
+    for odd in range(2):
+        for channel in range(4):
+            at = odd * 4 + channel
+            final_ref[at : at + 1, :] = image[odd][channel][0:1]
+    turned_ref[...] = final_ref[...].T
+    wide = lax.broadcasted_iota(jnp.int32, (half, LANES), 1)
     for index, tile in enumerate((0, tiles - 1)):
-        block = added[:, index * LANES : (index + 1) * LANES]
-        fixed_ref[index, 0:pad, :] = jnp.zeros((pad, LANES), jnp.float32)
-        fixed_ref[index, pad + 2 * size :, :] = jnp.zeros((pad, LANES), jnp.float32)
-        fixed_ref[index, pad : pad + 2 * size, :] = rounded(
-            along_ref[tile, pad : pad + 2 * size, :] + block[0 : 2 * size]
-        )
-        edge_lines(rounded(edge_ref[index] + block[2 * size :]), packed_ref.at[index], lines_ref.at[index], depth)
-    out_ref[:, :, LANES : 2 * cols - LANES] = image_ref[...]
-
-    image = render_pair(
-        [fixed_ref.at[0], fixed_ref.at[1]],
-        [packed_ref.at[0], packed_ref.at[1]],
-        [lines_ref.at[0], lines_ref.at[1]],
-        mix_ref,
-        flip_ref[0],
-        layers,
-    )
-    for index, start in enumerate((0, 2 * cols - LANES)):
-        store_tile(image[index], mixed_ref, out_ref, slice(start, start + LANES))
+        place = wide == index * (LANES - 1)
+        turned = turned_ref[pl.ds(start + index * middle, half), :]
+        for channel in range(4):
+            for odd in range(2):
+                at = pl.ds(odd, half, stride=2)
+                column = odd * 4 + channel
+                fixed_ref[index, channel, at, :] = jnp.where(
+                    place, turned[:, column : column + 1], image_ref[tile, channel, at, :]
+                )
+            out_ref[channel, :, tile * LANES : (tile + 1) * LANES] = fixed_ref[index, channel, 0:rows]
+    for tile in range(1, tiles - 1):
+        for channel in range(4):
+            out_ref[channel, :, tile * LANES : (tile + 1) * LANES] = image_ref[tile, channel, 0:rows]
 
 
 def two_slab_device(density, bin_index, tf_colour, tf_extinction, slab_rank):
@@ -636,14 +647,14 @@
         "own_cells",
         (
             pltpu.VMEM((size, cols), bf16),
-            pltpu.VMEM((cols + LANES, 2 * cols), bf16),
+            pltpu.VMEM((cols, 2 * cols), bf16),
             pltpu.VMEM((128, 80), bf16),
         ),
         0.5,
     )(dense, index, tables)
     whole = pltpu.VMEM((tiles, 2 * size + 2 * 4 * half, LANES), f32)
     along = call(own_kernel, "own_slab", whole, 0.4)(cells, weights)
-    ends = call(side_kernel, "side_columns", pltpu.VMEM((2, layers, LANES), i32), 0.1)(
+    ends = call(functools.partial(side_kernel, rows), "side_columns", pltpu.VMEM((2, layers, LANES), i32), 0.1)(
         columns, bulk, second, first, along
     )
     pairs = [(x, x + 1) for x in range(0, count_x, 2)]
@@ -653,33 +664,31 @@
     along = call(other_kernel, "other_slab", whole, 0.8, [pltpu.VMEM((size, cols), bf16)], aliases={4: 0})(
         bulk, tables, weights, ends, along
     )
-    lines = [
-        pltpu.VMEM((2, 32 * layers, LANES), bf16),
-        pltpu.VMEM((2, 16 * layers + 8, LANES), f32),
-        pltpu.VMEM((4, rows + 8, LANES), f32),
-    ]
-    image, edge = call(
-        inner_kernel,
-        "inner_tiles",
-        (pltpu.VMEM((4, rows, (tiles - 2) * LANES), f32), pltpu.VMEM((2, 16 * layers, LANES), f32)),
-        2.0,
-        [pltpu.VMEM((cols // LANES, 16 * layers + 8, LANES), f32)] + lines,
-        [smem] + [VMEM] * 8,
-    )(flip, tables, weights, bulk, inside, second, first, mix, along)
-    return call(
-        outer_kernel,
-        "outer_tiles",
-        jax.ShapeDtypeStruct((4, rows, 2 * cols), f32),
+    image, mine = call(
+        tiles_kernel,
+        "render_tiles",
+        (pltpu.VMEM((tiles, 4, rows + 8, LANES), f32), pltpu.VMEM((8, layers, LANES), f32)),
         2.0,
         [
-            pltpu.VMEM((2 * size + 16 * layers, LANES), bf16),
-            pltpu.VMEM((8, 2 * layers, LANES), f32),
-            pltpu.VMEM((16 * layers + 8, LANES), f32),
-            pltpu.VMEM((2, 2 * size + 2 * 4 * half, LANES), f32),
-        ]
-        + lines,
-        [smem] + [VMEM] * 8,
-    )(flip, tables, weights, beside, across, mix, along, edge, image)
+            pltpu.VMEM((cols // LANES, 16 * layers + 8, LANES), f32),
+            pltpu.VMEM((tiles, 32 * layers, LANES), bf16),
+            pltpu.VMEM((tiles, 16 * layers + 8, LANES), f32),
+        ],
+        [smem] + [VMEM] * 9,
+    )(flip, tables, weights, bulk, inside, second, first, ends, mix, along)
+    return call(
+        edge_kernel,
+        "edge_columns",
+        jax.ShapeDtypeStruct((4, rows, 2 * cols), f32),
+        1.0,
+        [
+            pltpu.VMEM((2, 16, 2 * layers, LANES), f32),
+            pltpu.VMEM((LANES, LANES), f32),
+            pltpu.VMEM((LANES, LANES), f32),
+            pltpu.VMEM((2, 4, rows + 8, LANES), f32),
+        ],
+        [smem] + [VMEM] * 5,
+    )(flip, tables, beside, across, mine, image)
 
 
 def on_device(density, bin_index, tf_colour, tf_extinction, slab_rank):

time: 14.9 us -> 15 us (level)
  Pallas kernels: 6.25 us -> 6.4 us
    pallas_call x8, Pallas kernels: 6.25 us -> 6.4 us  [run(): pl.pallas_call(kernel, out_shape=out_shape, in_specs=in_specs or [VMEM] *...]
  transfers between devices with their start and end apart: 5 -> 5, of which waited for: 1 -> 1; matrix products, arithmetic and copies ran while one was open for 0% -> 0% of each run, Pallas kernels for 20% -> 25%
where the time goes in v19:
time: 15 us; the launch traced here: 14.9 us
  Pallas kernels  6.4 us (43%)
  starting transfers between devices  6.22 us (41%)
  waiting for transfers between devices  2.2 us (15%)
    pallas_call x8, Pallas kernels, run(): pl.pallas_call(kernel, out_shape=out_shape, in_specs=in_specs or [VMEM] *...  6.4 us
    ppermute x1, starting transfers between devices, two_slab_device(): bulk = lax.ppermute(bulk, 'bz', [(0, 1), (1, 0)])  3 us
    ppermute x1, waiting for transfers between devices, two_slab_device(): first = lax.ppermute(first, axes, ring)  2.19 us
    ppermute x1, starting transfers between devices, two_slab_device(): beside = lax.ppermute(ends, 'bx', both(pairs))  1.62 us
    ppermute x1, starting transfers between devices, two_slab_device(): first = lax.ppermute(first, axes, ring)  1.58 us
  transfers between devices with their start and end apart: 5, of which 1 were waited for; matrix products, arithmetic and copies ran while one was open for 0% of the time, Pallas kernels for 25%

profile of v19, /device:TPU:0, one launch (start us, length us, event | category | flops | bytes accessed | tf_op | source)
XLA Modules:
  0.0 14.9 jit_solution(16154124232118703703)
XLA Ops:
  0.0 1.2 %stage_block.1 = (s32[1]{0:T(128)S(4)}, s32[8,256]{1,0:T(8,128)S(1)}, s32[8,256]{1,0:T(8,128)S(1)}, s32[8,128]{1,0:T(8,128)S(1)}, f32[8,2,40,128]{3,2,1,0:T(8,12...) custom-call(s32[2]{0:T(128)} %rank_ref.1, f32[8,32,256]{2,1,0:T(8,128)} %density_ref.1, ...), custom_call_target="tpu_custom_call" | custom-call | flops 1200000000 | bytes 4320000 | tf_op jit(solution)/shard_map/stage_block/pallas_call | solution.py:584
  1.2 0.1 pack_block.1
  1.3 3.0 %collective-permute-start = (s32[18,8,256]{2,1,0:T(8,128)S(1)}, s32[18,8,256]{2,1,0:T(8,128)S(1)}, u32[]{:S(2)}, u32[]{:S(2)}) collective-permute-start(s32[18,8,256]{2,1,0:T(8,128)S(1)} %get-tuple-element.24), channel_id=1, source_target_pairs={{0,16},{16,0},{1,17},{17,1},{2,18},{18,2},{3,19},{19,3},{4,20},{20... | collective-permute-start | bytes 442376 | tf_op jit(solution)/shard_map/ppermute | solution.py:641
  4.3 0.0 collective-permute-start.1
  4.3 1.6 %collective-permute-start.2 = (s32[8,256]{1,0:T(8,128)S(1)}, s32[8,256]{1,0:T(8,128)S(1)}, u32[]{:S(2)}, u32[]{:S(2)}) collective-permute-start(s32[8,256]{1,0:T(8,128)S(1)} %get-tuple-element.26), channel_id=1, source_target_pairs={{0,4},{1,5},{2,6},{3,7},{4,8},{5,9},{6,10},{7,11},{8,12},{9,13},{1... | collective-permute-start | bytes 24584 | tf_op jit(solution)/shard_map/ppermute | solution.py:642
  5.9 0.6 %own_cells.1 = (bf16[512,256]{1,0:T(8,128)(2,1)S(1)}, bf16[256,512]{1,0:T(8,128)(2,1)S(1)}, bf16[128,80]{1,0:T(8,128)(2,1)S(1)}) custom-call(f32[8,2,40,128]{3,2,1,0:T(8,128)S(1)} %get-tuple-element.22.dense_ref, s32[8,2,40,128]{3,2,1,0:T(8,128)S(1)} %get-tuple-element.23.index_ref, f32[8,8,128]{2,1,0:T(8,128)S(1)} %get-tuple-element.20.tables_ref), custom_call_target="tpu_custom_call" | custom-call | flops 500000000 | bytes 1800000 | tf_op jit(solution)/shard_map/own_cells/pallas_call | solution.py:584
  6.5 0.3 %own_slab.1.along_ref.own_ref = f32[4,1152,128]{2,1,0:T(8,128)S(1)} custom-call(bf16[512,256]{1,0:T(8,128)(2,1)S(1)} %get-tuple-element.27.cells_ref, bf16[256,512]{1,0:T(8,128)(2,1)S(1)} %get-tuple-element.28.weights_ref), custom_call_target="tpu_custom_call" | custom-call | flops 400000000 | bytes 1440000 | tf_op jit(solution)/shard_map/own_slab/pallas_call | solution.py:584
  6.8 0.0 collective-permute-done.1.second_ref
  6.8 2.2 %collective-permute-done.2.first_ref = s32[8,256]{1,0:T(8,128)S(1)} collective-permute-done((s32[8,256]{1,0:T(8,128)S(1)}, s32[8,256]{1,0:T(8,128)S(1)}, u32[]{:S(2)}, u32[]{:S(2)}) %collective-permute-start.2) | collective-permute-done | bytes 8224 | tf_op jit(solution)/shard_map/ppermute | solution.py:642
  9.0 0.0 collective-permute-done.bulk_ref
  9.0 0.1 side_columns.1.ends_ref
  9.0 0.0 collective-permute-start.4
  9.1 1.6 %collective-permute-start.3 = (s32[2,8,128]{2,1,0:T(8,128)S(1)}, s32[2,8,128]{2,1,0:T(8,128)S(1)}, u32[]{:S(2)}, u32[]{:S(2)}) collective-permute-start(s32[2,8,128]{2,1,0:T(8,128)S(1)} %side_columns.1.ends_ref), channel_id=1, source_target_pairs={{0,1},{2,3},{1,0},{3,2},{4,5},{6,7},{5,4},{7,6},{8,9},{10,11},{9,8... | collective-permute-start | bytes 24584 | tf_op jit(solution)/shard_map/ppermute | solution.py:662
  10.7 0.8 %other_slab.1.along_ref = f32[4,1152,128]{2,1,0:T(8,128)S(1)} custom-call(s32[18,8,256]{2,1,0:T(8,128)S(1)} %collective-permute-done.bulk_ref, f32[8,8,128]{2,1,0:T(8,128)S(1)} %get-tuple-element.20.tables_ref, bf16[256,512]{1,0:T(8,128)(2,1)S(1)} %get-tuple-element.28.weights_ref, ...), custom_call_target="tpu_custom_call", output_to_operand_aliasing={{}: (4, {})} | custom-call | flops 800000000 | bytes 2880000 | tf_op jit(solution)/shard_map/other_slab/pallas_call | solution.py:584
  11.5 2.0 %render_tiles.1 = (f32[4,4,40,128]{3,2,1,0:T(8,128)S(1)}, f32[8,8,128]{2,1,0:T(8,128)S(1)}) custom-call(s32[1]{0:T(128)S(4)} %get-tuple-element.19.flip_ref, f32[8,8,128]{2,1,0:T(8,128)S(1)} %get-tuple-element.20.tables_ref, bf16[256,512]{1,0:T(8,128)(2,1)S(1)} %get-tuple-element.28.weights_ref, s32[18,8,256]{2,1,0:T(8,128)S(1)} %collective-permute-done.bulk_ref, ...), custom_call_target="tpu_custom_call" | custom-call | flops 2000000000 | bytes 7200000 | tf_op jit(solution)/shard_map/render_tiles/pallas_call | solution.py:584
  13.5 0.0 collective-permute-done.4.across_ref
  13.5 0.0 collective-permute-done.3.beside_ref
  13.5 1.3 %edge_columns.1 = f32[4,32,512]{2,1,0:T(8,128)} custom-call(s32[1]{0:T(128)S(4)} %get-tuple-element.19.flip_ref, f32[8,8,128]{2,1,0:T(8,128)S(1)} %get-tuple-element.20.tables_ref, s32[2,8,128]{2,1,0:T(8,128)S(1)} %collective-permute-done.3.beside_ref, s32[2,8,128]{2,1,0:T(8,128)S(1)} %collective-permute-done.4.across_ref, ...), custom_call_target="tpu_custom_call" | custom-call | flops 1000000000 | bytes 3600000 | tf_op jit(solution)/shard_map/edge_columns/pallas_call | solution.py:584
Async XLA Ops:
  1.3 7.7 %collective-permute-start = (s32[18,8,256]{2,1,0:T(8,128)S(1)}, s32[18,8,256]{2,1,0:T(8,128)S(1)}, u32[]{:S(2)}, u32[]{:S(2)}) collective-permute-start(s32[18,8,256]{2,1,0:T(8,128)S(1)} %get-tuple-element.24), channel_id=1, source_target_pairs={{0,16},{16,0},{1,17},{17,1},{2,18},{18,2},{3,19},{19,3},{4,20},{20... | collective-permute-start | bytes 442376 | tf_op jit(solution)/shard_map/ppermute | solution.py:641
  4.3 2.5 %collective-permute-start.1 = (s32[8,256]{1,0:T(8,128)S(1)}, s32[8,256]{1,0:T(8,128)S(1)}, u32[]{:S(2)}, u32[]{:S(2)}) collective-permute-start(s32[8,256]{1,0:T(8,128)S(1)} %get-tuple-element.25), channel_id=1, source_target_pairs={{16,4},{17,5},{18,6},{19,7},{20,8},{21,9},{22,10},{23,11},{24,12},... | collective-permute-start | bytes 24584 | tf_op jit(solution)/shard_map/ppermute | solution.py:643
  4.3 4.7 %collective-permute-start.2 = (s32[8,256]{1,0:T(8,128)S(1)}, s32[8,256]{1,0:T(8,128)S(1)}, u32[]{:S(2)}, u32[]{:S(2)}) collective-permute-start(s32[8,256]{1,0:T(8,128)S(1)} %get-tuple-element.26), channel_id=1, source_target_pairs={{0,4},{1,5},{2,6},{3,7},{4,8},{5,9},{6,10},{7,11},{8,12},{9,13},{1... | collective-permute-start | bytes 24584 | tf_op jit(solution)/shard_map/ppermute | solution.py:642
  9.0 4.5 %collective-permute-start.4 = (s32[2,8,128]{2,1,0:T(8,128)S(1)}, s32[2,8,128]{2,1,0:T(8,128)S(1)}, u32[]{:S(2)}, u32[]{:S(2)}) collective-permute-start(s32[2,8,128]{2,1,0:T(8,128)S(1)} %side_columns.1.ends_ref), channel_id=1, source_target_pairs={{1,2},{3,0},{2,1},{0,3},{5,6},{7,4},{6,5},{4,7},{9,10},{11,8},{10,... | collective-permute-start | bytes 24584 | tf_op jit(solution)/shard_map/ppermute | solution.py:663
  9.1 4.5 %collective-permute-start.3 = (s32[2,8,128]{2,1,0:T(8,128)S(1)}, s32[2,8,128]{2,1,0:T(8,128)S(1)}, u32[]{:S(2)}, u32[]{:S(2)}) collective-permute-start(s32[2,8,128]{2,1,0:T(8,128)S(1)} %side_columns.1.ends_ref), channel_id=1, source_target_pairs={{0,1},{2,3},{1,0},{3,2},{4,5},{6,7},{5,4},{7,6},{8,9},{10,11},{9,8... | collective-permute-start | bytes 24584 | tf_op jit(solution)/shard_map/ppermute | solution.py:662

commit v20 on v19

--- a/solution.py
+++ b/solution.py
@@ -158,18 +158,12 @@
 
 def stage_kernel(
     rank_ref, density_ref, bins_ref, colour_ref, extinction_ref,
-    flip_ref, first_ref, second_ref, columns_ref, dense_ref, index_ref, tables_ref,
+    flip_ref, first_ref, second_ref, dense_ref, index_ref, tables_ref,
 ):
     flip_ref[0] = rank_ref[0]
     layers, rows, cols = density_ref.shape
     front = lax.axis_index("bz") == 0
-    row_at = lax.broadcasted_iota(jnp.int32, (rows, LANES), 0)
-    lane_at = lax.broadcasted_iota(jnp.int32, (rows, LANES), 1)
     for z in range(layers):
-        first = pack_words(density_ref[z, :, 0:1], bins_ref[z, :, 0:1])
-        last = pack_words(density_ref[z, :, cols - 1 : cols], bins_ref[z, :, cols - 1 : cols])
-        line = jnp.where(lane_at == row_at, first, 0) + jnp.where(lane_at == row_at + LANES // 2, last, 0)
-        columns_ref[z : z + 1, :] = jnp.sum(line, axis=0, keepdims=True)
         top, bottom = [
             pack_words(density_ref[z, r : r + 1, :], bins_ref[z, r : r + 1, :]) for r in (0, rows - 1)
         ]
@@ -189,14 +183,13 @@
             )
 
 
-def pack_kernel(dense_ref, index_ref, columns_ref, bulk_ref, inside_ref):
+def pack_kernel(dense_ref, index_ref, bulk_ref, inside_ref):
     layers, tiles, rows = dense_ref.shape[0], dense_ref.shape[1], dense_ref.shape[2] - 8
     half = rows // 2
     front = lax.axis_index("bz") == 0
     start = jnp.where(front, half, 0)
     for tile in range(tiles):
         lanes = slice(tile * LANES, (tile + 1) * LANES)
-        bulk_ref[2 * layers + 1, :, lanes] = columns_ref[...]
         for z in range(layers):
             for part in range(2):
                 at = pl.ds(start + part, half // 2, stride=2)
@@ -217,13 +210,33 @@
     return jnp.where(has_near(me == 0), words, 0)
 
 
-def side_kernel(rows, columns_ref, bulk_ref, second_ref, first_ref, along_ref, ends_ref):
+def column_lines(read_words, inside, lines_ref, rows):
+    layers, cols = inside.shape
+    front = lax.axis_index("bz") == 0
+    start = lax.axis_index("bz") * (rows // 2)
+    middle = LANES // 2
+    lane_at = lax.broadcasted_iota(jnp.int32, (8, LANES), 1)
+    row_at = start + 2 * lax.broadcasted_iota(jnp.int32, (8, LANES), 0)
+    for z in range(layers):
+        line = jnp.zeros((8, LANES), jnp.int32)
+        for part in range(2):
+            first = read_words(z, part, 0)[:, 0:1]
+            last = read_words(z, part, cols // LANES - 1)[:, LANES - 1 : LANES]
+            line += jnp.where(lane_at == row_at + part, first, 0)
+            line += jnp.where(lane_at == row_at + part + middle, last, 0)
+        lines_ref[z : z + 1, :] = jnp.sum(line, axis=0, keepdims=True)
+    beside = jnp.where(front, rows // 2, rows // 2 - 1)
+    lines = jnp.where(lane_at == beside, inside[:, 0:1], lines_ref[...])
+    lines_ref[...] = jnp.where(lane_at == beside + middle, inside[:, cols - 1 : cols], lines)
+
+
+def side_kernel(rows, columns_ref, other_ref, second_ref, first_ref, ends_ref):
     layers = columns_ref.shape[0]
     front = lax.axis_index("bz") == 0
     lane_at = lax.broadcasted_iota(jnp.int32, (layers, LANES), 1)
     for slab in range(2):
         mine = front if slab == 0 else jnp.logical_not(front)
-        columns = jnp.where(mine, columns_ref[...], bulk_ref[2 * layers + 1, :, 0:LANES])
+        columns = jnp.where(mine, columns_ref[...], other_ref[...])
         near = near_words(slab, first_ref, second_ref)
         cols = near.shape[1]
         columns = jnp.where(lane_at == rows, near[:, 0:1], columns)
@@ -264,7 +277,7 @@
     return value.astype(jnp.bfloat16).astype(jnp.float32)
 
 
-def cells_kernel(dense_ref, index_ref, tables_ref, cells_ref, weights_ref, mix_ref):
+def cells_kernel(dense_ref, index_ref, inside_ref, tables_ref, cells_ref, weights_ref, mix_ref, lines_ref):
     layers, tiles, rows = dense_ref.shape[0], dense_ref.shape[1], dense_ref.shape[2] - 8
     half = rows // 2
     start = lax.axis_index("bz") * half
@@ -276,6 +289,7 @@
         return dense_ref[z, tile, at, :], index_ref[z, tile, at, :]
 
     classify_rows(read_cells, read_tables(tables_ref), cells_ref, layers, tiles)
+    column_lines(lambda *at: pack_words(*read_cells(*at)), inside_ref[...], lines_ref, rows)
 
 
 def along_columns(cells, weights_ref, store):
@@ -297,19 +311,25 @@
     along_columns(cells_ref[...], weights_ref, store)
 
 
-def other_kernel(bulk_ref, tables_ref, weights_ref, ends_ref, own_ref, along_ref, cells_ref):
-    layers = (bulk_ref.shape[0] - 2) // 2
+def other_kernel(
+    rows, bulk_ref, tables_ref, weights_ref, own_ref, along_ref, columns_ref, cells_ref
+):
+    layers = (bulk_ref.shape[0] - 1) // 2
     cols = bulk_ref.shape[2]
     size = cells_ref.shape[0]
     pad = along_ref.shape[1] // 2 - size
     theirs = pl.multiple_of(pad + (1 - lax.axis_index("bz")) * size, pad)
 
+    def read_words(z, part, tile):
+        return bulk_ref[2 * z + part, :, tile * LANES : (tile + 1) * LANES]
+
     def read_cells(z, part, tile):
-        return unpack_words(bulk_ref[2 * z + part, :, tile * LANES : (tile + 1) * LANES])
+        return unpack_words(read_words(z, part, tile))
 
     def store(tile, block):
         along_ref[tile, pl.ds(theirs, size), :] = block
 
+    column_lines(read_words, bulk_ref[2 * layers], columns_ref, rows)
     classify_rows(read_cells, read_tables(tables_ref), cells_ref, layers, cols // LANES)
     along_columns(cells_ref[...], weights_ref, store)
 
@@ -530,9 +550,10 @@
                     at = (parity * 2 + odd) * 4 + channel
                     samples_ref[slab, at, 0:layers, :] = value
 
-    def one_slab(position, image):
-        slab = position ^ flip_ref[0]
-        for z in range(layers):
+    def over_some(slab, layers_at):
+        zero = jnp.zeros((8, LANES), jnp.float32)
+        image = [[zero] * 4 for _ in range(2)]
+        for z in layers_at:
             for parity in range(2):
                 clear = [1.0 - image[odd][3] for odd in range(2)]
                 image = [
@@ -546,8 +567,28 @@
                 ]
         return image
 
-    zero = jnp.zeros((8, LANES), jnp.float32)
-    image = lax.fori_loop(0, 2, one_slab, [[zero] * 4 for _ in range(2)])
+    def over(in_front, behind):
+        return [
+            [top + (1.0 - tops[3]) * low for top, low in zip(tops, lows)]
+            for tops, lows in zip(in_front, behind)
+        ]
+
+    slabs = [
+        over(
+            over_some(slab, range(layers // 2)), over_some(slab, range(layers // 2, layers))
+        )
+        for slab in range(2)
+    ]
+    in_order = flip_ref[0] == 0
+    image = over(
+        *[
+            [
+                [jnp.where(in_order, x, y) for x, y in zip(xs, ys)]
+                for xs, ys in zip(slabs[at], slabs[1 - at])
+            ]
+            for at in range(2)
+        ]
+    )
     final_ref[8:, :] = jnp.zeros((LANES - 8, LANES), jnp.float32)
     for odd in range(2):
         for channel in range(4):
@@ -606,25 +647,24 @@
         pltpu.with_memory_space_constraint(x, pltpu.HBM)
         for x in (slab_rank, density, bin_index, tf_colour, tf_extinction)
     ]
-    flip, first, second, columns, dense, index, tables = call(
+    flip, first, second, dense, index, tables = call(
         stage_kernel,
         "stage_block",
         (
             pltpu.SMEM((1,), i32),
             row,
             row,
-            pltpu.VMEM((layers, LANES), i32),
             pltpu.VMEM(blocks, f32),
             pltpu.VMEM(blocks, i32),
             pltpu.VMEM((8, 8, LANES), f32),
         ),
         1.2,
         in_specs=[smem] + [VMEM] * 4,
-        out_specs=(smem,) + (VMEM,) * 6,
+        out_specs=(smem,) + (VMEM,) * 5,
     )(*inputs)
     bulk, inside = call(
-        pack_kernel, "pack_block", (pltpu.VMEM((2 * layers + 2, 8, cols), i32), row), 0.1
-    )(dense, index, columns)
+        pack_kernel, "pack_block", (pltpu.VMEM((2 * layers + 1, 8, cols), i32), row), 0.1
+    )(dense, index)
 
     def place(z, y, x):
         return (z * count_y + y) * count_x + x
@@ -642,28 +682,34 @@
     first = lax.ppermute(first, axes, ring)
     second = lax.ppermute(second, axes, both(diagonal))
 
-    cells, weights, mix = call(
+    cells, weights, mix, columns = call(
         cells_kernel,
         "own_cells",
         (
             pltpu.VMEM((size, cols), bf16),
             pltpu.VMEM((cols, 2 * cols), bf16),
             pltpu.VMEM((128, 80), bf16),
+            pltpu.VMEM((layers, LANES), i32),
         ),
         0.5,
-    )(dense, index, tables)
+    )(dense, index, inside, tables)
     whole = pltpu.VMEM((tiles, 2 * size + 2 * 4 * half, LANES), f32)
     along = call(own_kernel, "own_slab", whole, 0.4)(cells, weights)
-    ends = call(functools.partial(side_kernel, rows), "side_columns", pltpu.VMEM((2, layers, LANES), i32), 0.1)(
-        columns, bulk, second, first, along
-    )
+    along, other_columns = call(
+        functools.partial(other_kernel, rows),
+        "other_slab",
+        (whole, pltpu.VMEM((layers, LANES), i32)),
+        0.8,
+        [pltpu.VMEM((size, cols), bf16)],
+        aliases={3: 0},
+    )(bulk, tables, weights, along)
+    ends = call(
+        functools.partial(side_kernel, rows), "side_columns", pltpu.VMEM((2, layers, LANES), i32), 0.1
+    )(columns, other_columns, second, first)
     pairs = [(x, x + 1) for x in range(0, count_x, 2)]
     cross = [(x, (x + 1) % count_x) for x in range(1, count_x, 2)]
     beside = lax.ppermute(ends, "bx", both(pairs))
     across = lax.ppermute(ends, "bx", both(cross))
-    along = call(other_kernel, "other_slab", whole, 0.8, [pltpu.VMEM((size, cols), bf16)], aliases={4: 0})(
-        bulk, tables, weights, ends, along
-    )
     image, mine = call(
         tiles_kernel,
         "render_tiles",

time: 15 us -> 14.3 us (0.953)
  waiting for transfers between devices: 2.2 us -> 1.32 us
  starting transfers between devices: 6.22 us -> 6.45 us
    ppermute x1, waiting for transfers between devices: 2.19 us -> 0.05 us  [two_slab_device(): first = lax.ppermute(first, axes, ring)]
    ppermute x1, waiting for transfers between devices: 0.01 us -> 1.26 us  [two_slab_device(): bulk = lax.ppermute(bulk, 'bz', [(0, 1), (1, 0)])]
    ppermute x1, starting transfers between devices: 0.01 us -> 0.23 us  [two_slab_device(): across = lax.ppermute(ends, 'bx', both(cross))]
  transfers between devices with their start and end apart: 5 -> 5, of which waited for: 1 -> 2; matrix products, arithmetic and copies ran while one was open for 0% -> 0% of each run, Pallas kernels for 25% -> 27%
where the time goes in v20:
time: 14.3 us; the launch traced here: 14.2 us
  starting transfers between devices  6.45 us (45%)
  Pallas kernels  6.32 us (44%)
  waiting for transfers between devices  1.32 us (9%)
    pallas_call x8, Pallas kernels, run(): pl.pallas_call(kernel, out_shape=out_shape, in_specs=in_specs or [VMEM] *...  6.32 us
    ppermute x1, starting transfers between devices, two_slab_device(): bulk = lax.ppermute(bulk, 'bz', [(0, 1), (1, 0)])  3 us
    ppermute x1, starting transfers between devices, two_slab_device(): beside = lax.ppermute(ends, 'bx', both(pairs))  1.64 us
    ppermute x1, starting transfers between devices, two_slab_device(): first = lax.ppermute(first, axes, ring)  1.58 us
    ppermute x1, waiting for transfers between devices, two_slab_device(): bulk = lax.ppermute(bulk, 'bz', [(0, 1), (1, 0)])  1.26 us
  transfers between devices with their start and end apart: 5, of which 2 were waited for; matrix products, arithmetic and copies ran while one was open for 0% of the time, Pallas kernels for 27%

profile of v20, /device:TPU:0, one launch (start us, length us, event | category | flops | bytes accessed | tf_op | source)
XLA Modules:
  0.0 14.2 jit_solution(14857265577389616526)
XLA Ops:
  0.0 1.1 %stage_block.1 = (s32[1]{0:T(128)S(4)}, s32[8,256]{1,0:T(8,128)S(1)}, s32[8,256]{1,0:T(8,128)S(1)}, f32[8,2,40,128]{3,2,1,0:T(8,128)S(1)}, s32[8,2,40,128]{3,2,1,0:T(8,128)S(1)}, /*index=5*/f32[8,8,128]{2,1,0:T(8,128)S(1)}) custom-call(s32[2]{0:T(128)} %rank_ref.1, f32[8,32,256]{2,1,0:T(8,128)} %density_ref.1, s32[8,32,256]{2,1,0:T(8,128)} %bins_ref.1, ...), custom_call_target="tpu_custom_call" | custom-call | flops 1200000000 | bytes 4320000 | tf_op jit(solution)/shard_map/stage_block/pallas_call | solution.py:625
  1.1 0.1 pack_block.1
  1.2 3.0 %collective-permute-start = (s32[17,8,256]{2,1,0:T(8,128)S(1)}, s32[17,8,256]{2,1,0:T(8,128)S(1)}, u32[]{:S(2)}, u32[]{:S(2)}) collective-permute-start(s32[17,8,256]{2,1,0:T(8,128)S(1)} %get-tuple-element.27), channel_id=1, source_target_pairs={{0,16},{16,0},{1,17},{17,1},{2,18},{18,2},{3,19},{19,3},{4,20},{20... | collective-permute-start | bytes 417800 | tf_op jit(solution)/shard_map/ppermute | solution.py:681
  4.2 0.0 collective-permute-start.1
  4.2 1.6 %collective-permute-start.2 = (s32[8,256]{1,0:T(8,128)S(1)}, s32[8,256]{1,0:T(8,128)S(1)}, u32[]{:S(2)}, u32[]{:S(2)}) collective-permute-start(s32[8,256]{1,0:T(8,128)S(1)} %get-tuple-element.32), channel_id=1, source_target_pairs={{0,4},{1,5},{2,6},{3,7},{4,8},{5,9},{6,10},{7,11},{8,12},{9,13},{1... | collective-permute-start | bytes 24584 | tf_op jit(solution)/shard_map/ppermute | solution.py:682
  5.8 0.6 %own_cells.1 = (bf16[512,256]{1,0:T(8,128)(2,1)S(1)}, bf16[256,512]{1,0:T(8,128)(2,1)S(1)}, bf16[128,80]{1,0:T(8,128)(2,1)S(1)}, s32[8,128]{1,0:T(8,128)S(1)}) custom-call(f32[8,2,40,128]{3,2,1,0:T(8,128)S(1)} %get-tuple-element.23.dense_ref, s32[8,2,40,128]{3,2,1,0:T(8,128)S(1)} %get-tuple-element.24.index_ref, s32[8,256]{1,0:T(8,128)S(1)} %get-tuple-element.25.inside_ref, ...), custom_call_target="tpu_custom_call" | custom-call | flops 500000000 | bytes 1800000 | tf_op jit(solution)/shard_map/own_cells/pallas_call | solution.py:625
  6.4 0.3 %own_slab.1.own_ref = f32[4,1152,128]{2,1,0:T(8,128)S(1)} custom-call(bf16[512,256]{1,0:T(8,128)(2,1)S(1)} %get-tuple-element.29.cells_ref, bf16[256,512]{1,0:T(8,128)(2,1)S(1)} %get-tuple-element.28.weights_ref), custom_call_target="tpu_custom_call" | custom-call | flops 400000000 | bytes 1440000 | tf_op jit(solution)/shard_map/own_slab/pallas_call | solution.py:625
  6.7 1.3 %collective-permute-done.bulk_ref = s32[17,8,256]{2,1,0:T(8,128)S(1)} collective-permute-done((s32[17,8,256]{2,1,0:T(8,128)S(1)}, s32[17,8,256]{2,1,0:T(8,128)S(1)}, u32[]{:S(2)}, u32[]{:S(2)}) %collective-permute-start) | collective-permute-done | bytes 139296 | tf_op jit(solution)/shard_map/ppermute | solution.py:681
  7.9 0.8 %other_slab.1 = (f32[4,1152,128]{2,1,0:T(8,128)S(1)}, s32[8,128]{1,0:T(8,128)S(1)}) custom-call(s32[17,8,256]{2,1,0:T(8,128)S(1)} %collective-permute-done.bulk_ref, f32[8,8,128]{2,1,0:T(8,128)S(1)} %get-tuple-element.22.tables_ref, bf16[256,512]{1,0:T(8,128)(2,1)S(1)} %get-tuple-element.28.weights_ref, ...), custom_call_target="tpu_custom_call", output_to_operand_aliasing={{0}: (3, {})} | custom-call | flops 800000000 | bytes 2880000 | tf_op jit(solution)/shard_map/other_slab/pallas_call | solution.py:625
  8.8 0.0 collective-permute-done.1.second_ref
  8.8 0.1 collective-permute-done.2.first_ref
  8.8 0.1 side_columns.1.ends_ref
  8.9 0.2 %collective-permute-start.4 = (s32[2,8,128]{2,1,0:T(8,128)S(1)}, s32[2,8,128]{2,1,0:T(8,128)S(1)}, u32[]{:S(2)}, u32[]{:S(2)}) collective-permute-start(s32[2,8,128]{2,1,0:T(8,128)S(1)} %side_columns.1.ends_ref), channel_id=1, source_target_pairs={{1,2},{3,0},{2,1},{0,3},{5,6},{7,4},{6,5},{4,7},{9,10},{11,8},{10,... | collective-permute-start | bytes 24584 | tf_op jit(solution)/shard_map/ppermute | solution.py:712
  9.2 1.6 %collective-permute-start.3 = (s32[2,8,128]{2,1,0:T(8,128)S(1)}, s32[2,8,128]{2,1,0:T(8,128)S(1)}, u32[]{:S(2)}, u32[]{:S(2)}) collective-permute-start(s32[2,8,128]{2,1,0:T(8,128)S(1)} %side_columns.1.ends_ref), channel_id=1, source_target_pairs={{0,1},{2,3},{1,0},{3,2},{4,5},{6,7},{5,4},{7,6},{8,9},{10,11},{9,8... | collective-permute-start | bytes 24584 | tf_op jit(solution)/shard_map/ppermute | solution.py:711
  10.8 2.0 %render_tiles.1 = (f32[4,4,40,128]{3,2,1,0:T(8,128)S(1)}, f32[8,8,128]{2,1,0:T(8,128)S(1)}) custom-call(s32[1]{0:T(128)S(4)} %get-tuple-element.21.flip_ref, f32[8,8,128]{2,1,0:T(8,128)S(1)} %get-tuple-element.22.tables_ref, bf16[256,512]{1,0:T(8,128)(2,1)S(1)} %get-tuple-element.28.weights_ref, s32[17,8,256]{2,1,0:T(8,128)S(1)} %collective-permute-done.bulk_ref, ...), custom_call_target="tpu_custom_call" | custom-call | flops 2000000000 | bytes 7200000 | tf_op jit(solution)/shard_map/render_tiles/pallas_call | solution.py:625
  12.8 0.0 collective-permute-done.4.across_ref
  12.8 0.0 collective-permute-done.3.beside_ref
  12.8 1.3 %edge_columns.1 = f32[4,32,512]{2,1,0:T(8,128)} custom-call(s32[1]{0:T(128)S(4)} %get-tuple-element.21.flip_ref, f32[8,8,128]{2,1,0:T(8,128)S(1)} %get-tuple-element.22.tables_ref, s32[2,8,128]{2,1,0:T(8,128)S(1)} %collective-permute-done.3.beside_ref, s32[2,8,128]{2,1,0:T(8,128)S(1)} %collective-permute-done.4.across_ref, ...), custom_call_target="tpu_custom_call" | custom-call | flops 1000000000 | bytes 3600000 | tf_op jit(solution)/shard_map/edge_columns/pallas_call | solution.py:625
Async XLA Ops:
  1.2 6.8 %collective-permute-start = (s32[17,8,256]{2,1,0:T(8,128)S(1)}, s32[17,8,256]{2,1,0:T(8,128)S(1)}, u32[]{:S(2)}, u32[]{:S(2)}) collective-permute-start(s32[17,8,256]{2,1,0:T(8,128)S(1)} %get-tuple-element.27), channel_id=1, source_target_pairs={{0,16},{16,0},{1,17},{17,1},{2,18},{18,2},{3,19},{19,3},{4,20},{20... | collective-permute-start | bytes 417800 | tf_op jit(solution)/shard_map/ppermute | solution.py:681
  4.2 4.6 %collective-permute-start.1 = (s32[8,256]{1,0:T(8,128)S(1)}, s32[8,256]{1,0:T(8,128)S(1)}, u32[]{:S(2)}, u32[]{:S(2)}) collective-permute-start(s32[8,256]{1,0:T(8,128)S(1)} %get-tuple-element.31), channel_id=1, source_target_pairs={{16,4},{17,5},{18,6},{19,7},{20,8},{21,9},{22,10},{23,11},{24,12},... | collective-permute-start | bytes 24584 | tf_op jit(solution)/shard_map/ppermute | solution.py:683
  4.2 4.7 %collective-permute-start.2 = (s32[8,256]{1,0:T(8,128)S(1)}, s32[8,256]{1,0:T(8,128)S(1)}, u32[]{:S(2)}, u32[]{:S(2)}) collective-permute-start(s32[8,256]{1,0:T(8,128)S(1)} %get-tuple-element.32), channel_id=1, source_target_pairs={{0,4},{1,5},{2,6},{3,7},{4,8},{5,9},{6,10},{7,11},{8,12},{9,13},{1... | collective-permute-start | bytes 24584 | tf_op jit(solution)/shard_map/ppermute | solution.py:682
  8.9 3.9 %collective-permute-start.4 = (s32[2,8,128]{2,1,0:T(8,128)S(1)}, s32[2,8,128]{2,1,0:T(8,128)S(1)}, u32[]{:S(2)}, u32[]{:S(2)}) collective-permute-start(s32[2,8,128]{2,1,0:T(8,128)S(1)} %side_columns.1.ends_ref), channel_id=1, source_target_pairs={{1,2},{3,0},{2,1},{0,3},{5,6},{7,4},{6,5},{4,7},{9,10},{11,8},{10,... | collective-permute-start | bytes 24584 | tf_op jit(solution)/shard_map/ppermute | solution.py:712
  9.2 3.7 %collective-permute-start.3 = (s32[2,8,128]{2,1,0:T(8,128)S(1)}, s32[2,8,128]{2,1,0:T(8,128)S(1)}, u32[]{:S(2)}, u32[]{:S(2)}) collective-permute-start(s32[2,8,128]{2,1,0:T(8,128)S(1)} %side_columns.1.ends_ref), channel_id=1, source_target_pairs={{0,1},{2,3},{1,0},{3,2},{4,5},{6,7},{5,4},{7,6},{8,9},{10,11},{9,8... | collective-permute-start | bytes 24584 | tf_op jit(solution)/shard_map/ppermute | solution.py:711

commit v21 on v20

--- a/solution.py
+++ b/solution.py
@@ -158,7 +158,7 @@
 
 def stage_kernel(
     rank_ref, density_ref, bins_ref, colour_ref, extinction_ref,
-    flip_ref, first_ref, second_ref, dense_ref, index_ref, tables_ref,
+    flip_ref, first_ref, second_ref, bulk_ref, inside_ref, dense_ref, index_ref, tables_ref,
 ):
     flip_ref[0] = rank_ref[0]
     layers, rows, cols = density_ref.shape
@@ -173,6 +173,7 @@
             lanes = slice(tile * LANES, (tile + 1) * LANES)
             dense_ref[z, tile, 0:rows] = density_ref[z, :, lanes]
             index_ref[z, tile, 0:rows] = bins_ref[z, :, lanes]
+    pack_block(dense_ref, index_ref, bulk_ref, inside_ref)
     colour = colour_ref[...].astype(jnp.float32)
     extinction = extinction_ref[...].astype(jnp.float32).reshape(1, 2 * LANES)
     for channel in range(4):
@@ -183,7 +184,7 @@
             )
 
 
-def pack_kernel(dense_ref, index_ref, bulk_ref, inside_ref):
+def pack_block(dense_ref, index_ref, bulk_ref, inside_ref):
     layers, tiles, rows = dense_ref.shape[0], dense_ref.shape[1], dense_ref.shape[2] - 8
     half = rows // 2
     front = lax.axis_index("bz") == 0
@@ -504,7 +505,7 @@
 
 def edge_kernel(
     flip_ref, tables_ref, beside_ref, across_ref, mine_ref, image_ref,
-    out_ref, samples_ref, final_ref, turned_ref, fixed_ref,
+    out_ref, samples_ref, final_ref, turned_ref, fixed_ref, sems,
 ):
     rows = out_ref.shape[1]
     cols = out_ref.shape[2] // 2
@@ -517,6 +518,16 @@
     me_x = lax.axis_index("bx")
     even_x = lax.rem(me_x, 2) == 0
     tables = read_tables(tables_ref)
+
+    def to_out(tile, source):
+        lanes = pl.ds(tile * LANES, LANES)
+        return pltpu.make_async_copy(
+            source.at[:, pl.ds(0, rows), :], out_ref.at[:, :, lanes], sems.at[tile]
+        )
+
+    copies = [to_out(tile, image_ref.at[tile]) for tile in range(1, tiles - 1)]
+    for copy in copies:
+        copy.start()
     lane_at = lax.broadcasted_iota(jnp.int32, (layers, LANES), 1)
     layer_at = lax.broadcasted_iota(jnp.int32, (layers, LANES), 0)
     first_lane = (lane_at & (middle - 1)) == 0
@@ -589,12 +600,11 @@
             for at in range(2)
         ]
     )
-    final_ref[8:, :] = jnp.zeros((LANES - 8, LANES), jnp.float32)
     for odd in range(2):
         for channel in range(4):
             at = odd * 4 + channel
             final_ref[at : at + 1, :] = image[odd][channel][0:1]
-    turned_ref[...] = final_ref[...].T
+    turned_ref[:, 0:8] = final_ref[...].T
     wide = lax.broadcasted_iota(jnp.int32, (half, LANES), 1)
     for index, tile in enumerate((0, tiles - 1)):
         place = wide == index * (LANES - 1)
@@ -606,10 +616,10 @@
                 fixed_ref[index, channel, at, :] = jnp.where(
                     place, turned[:, column : column + 1], image_ref[tile, channel, at, :]
                 )
-            out_ref[channel, :, tile * LANES : (tile + 1) * LANES] = fixed_ref[index, channel, 0:rows]
-    for tile in range(1, tiles - 1):
-        for channel in range(4):
-            out_ref[channel, :, tile * LANES : (tile + 1) * LANES] = image_ref[tile, channel, 0:rows]
+        copies.append(to_out(tile, fixed_ref.at[index]))
+        copies[-1].start()
+    for copy in copies:
+        copy.wait()
 
 
 def two_slab_device(density, bin_index, tf_colour, tf_extinction, slab_rank):
@@ -647,12 +657,14 @@
         pltpu.with_memory_space_constraint(x, pltpu.HBM)
         for x in (slab_rank, density, bin_index, tf_colour, tf_extinction)
     ]
-    flip, first, second, dense, index, tables = call(
+    flip, first, second, bulk, inside, dense, index, tables = call(
         stage_kernel,
         "stage_block",
         (
             pltpu.SMEM((1,), i32),
             row,
+            row,
+            pltpu.VMEM((2 * layers + 1, 8, cols), i32),
             row,
             pltpu.VMEM(blocks, f32),
             pltpu.VMEM(blocks, i32),
@@ -660,12 +672,8 @@
         ),
         1.2,
         in_specs=[smem] + [VMEM] * 4,
-        out_specs=(smem,) + (VMEM,) * 5,
+        out_specs=(smem,) + (VMEM,) * 7,
     )(*inputs)
-    bulk, inside = call(
-        pack_kernel, "pack_block", (pltpu.VMEM((2 * layers + 1, 8, cols), i32), row), 0.1
-    )(dense, index)
-
     def place(z, y, x):
         return (z * count_y + y) * count_x + x
 
@@ -729,11 +737,13 @@
         1.0,
         [
             pltpu.VMEM((2, 16, 2 * layers, LANES), f32),
-            pltpu.VMEM((LANES, LANES), f32),
+            pltpu.VMEM((8, LANES), f32),
             pltpu.VMEM((LANES, LANES), f32),
             pltpu.VMEM((2, 4, rows + 8, LANES), f32),
+            pltpu.SemaphoreType.DMA((tiles,)),
         ],
         [smem] + [VMEM] * 5,
+        pl.BlockSpec(memory_space=pltpu.HBM),
     )(flip, tables, beside, across, mine, image)
 
 

time: 14.3 us -> 14.3 us (level)
    pallas_call x8 -> x7, Pallas kernels: 6.32 us -> 6.32 us  [run(): pl.pallas_call(kernel, out_shape=out_shape, in_specs=in_specs or [VMEM] *...]
  transfers between devices with their start and end apart: 5 -> 5, of which waited for: 2 -> 2; matrix products, arithmetic and copies ran while one was open for 0% -> 0% of each run, Pallas kernels for 27% -> 26%
where the time goes in v21:
time: 14.3 us; the launch traced here: 14.2 us
  starting transfers between devices  6.44 us (45%)
  Pallas kernels  6.32 us (44%)
  waiting for transfers between devices  1.33 us (9%)
    pallas_call x7, Pallas kernels, run(): pl.pallas_call(kernel, out_shape=out_shape, in_specs=in_specs or [VMEM] *...  6.32 us
    ppermute x1, starting transfers between devices, two_slab_device(): bulk = lax.ppermute(bulk, 'bz', [(0, 1), (1, 0)])  3 us
    ppermute x1, starting transfers between devices, two_slab_device(): beside = lax.ppermute(ends, 'bx', both(pairs))  1.63 us
    ppermute x1, starting transfers between devices, two_slab_device(): first = lax.ppermute(first, axes, ring)  1.58 us
    ppermute x1, waiting for transfers between devices, two_slab_device(): bulk = lax.ppermute(bulk, 'bz', [(0, 1), (1, 0)])  1.27 us
  transfers between devices with their start and end apart: 5, of which 2 were waited for; matrix products, arithmetic and copies ran while one was open for 0% of the time, Pallas kernels for 26%

profile of v21, /device:TPU:0, one launch (start us, length us, event | category | flops | bytes accessed | tf_op | source)
XLA Modules:
  0.0 14.2 jit_solution(17327768599797058520)
XLA Ops:
  0.0 1.2 %stage_block.1 = (s32[1]{0:T(128)S(4)}, s32[8,256]{1,0:T(8,128)S(1)}, s32[8,256]{1,0:T(8,128)S(1)}, s32[17,8,256]{2,1,0:T(8,128)S(1)}, s32[8,256]{1,0:T(8,128)S(...) custom-call(s32[2]{0:T(128)} %rank_ref.1, f32[8,32,256]{2,1,0:T(8,128)} %density_ref.1, ...), custom_call_target="tpu_custom_call" | custom-call | flops 1200000000 | bytes 4320000 | tf_op jit(solution)/shard_map/stage_block/pallas_call | solution.py:635
  1.2 3.0 %collective-permute-start = (s32[17,8,256]{2,1,0:T(8,128)S(1)}, s32[17,8,256]{2,1,0:T(8,128)S(1)}, u32[]{:S(2)}, u32[]{:S(2)}) collective-permute-start(s32[17,8,256]{2,1,0:T(8,128)S(1)} %get-tuple-element.27), channel_id=1, source_target_pairs={{0,16},{16,0},{1,17},{17,1},{2,18},{18,2},{3,19},{19,3},{4,20},{20... | collective-permute-start | bytes 417800 | tf_op jit(solution)/shard_map/ppermute | solution.py:689
  4.2 0.0 collective-permute-start.1
  4.2 1.6 %collective-permute-start.2 = (s32[8,256]{1,0:T(8,128)S(1)}, s32[8,256]{1,0:T(8,128)S(1)}, u32[]{:S(2)}, u32[]{:S(2)}) collective-permute-start(s32[8,256]{1,0:T(8,128)S(1)} %get-tuple-element.32), channel_id=1, source_target_pairs={{0,4},{1,5},{2,6},{3,7},{4,8},{5,9},{6,10},{7,11},{8,12},{9,13},{1... | collective-permute-start | bytes 24584 | tf_op jit(solution)/shard_map/ppermute | solution.py:690
  5.7 0.6 %own_cells.1 = (bf16[512,256]{1,0:T(8,128)(2,1)S(1)}, bf16[256,512]{1,0:T(8,128)(2,1)S(1)}, bf16[128,80]{1,0:T(8,128)(2,1)S(1)}, s32[8,128]{1,0:T(8,128)S(1)}) custom-call(f32[8,2,40,128]{3,2,1,0:T(8,128)S(1)} %get-tuple-element.23.dense_ref, s32[8,2,40,128]{3,2,1,0:T(8,128)S(1)} %get-tuple-element.24.index_ref, s32[8,256]{1,0:T(8,128)S(1)} %get-tuple-element.25.inside_ref, ...), custom_call_target="tpu_custom_call" | custom-call | flops 500000000 | bytes 1800000 | tf_op jit(solution)/shard_map/own_cells/pallas_call | solution.py:635
  6.3 0.3 %own_slab.1.own_ref = f32[4,1152,128]{2,1,0:T(8,128)S(1)} custom-call(bf16[512,256]{1,0:T(8,128)(2,1)S(1)} %get-tuple-element.29.cells_ref, bf16[256,512]{1,0:T(8,128)(2,1)S(1)} %get-tuple-element.28.weights_ref), custom_call_target="tpu_custom_call" | custom-call | flops 400000000 | bytes 1440000 | tf_op jit(solution)/shard_map/own_slab/pallas_call | solution.py:635
  6.7 1.3 %collective-permute-done.bulk_ref = s32[17,8,256]{2,1,0:T(8,128)S(1)} collective-permute-done((s32[17,8,256]{2,1,0:T(8,128)S(1)}, s32[17,8,256]{2,1,0:T(8,128)S(1)}, u32[]{:S(2)}, u32[]{:S(2)}) %collective-permute-start) | collective-permute-done | bytes 139296 | tf_op jit(solution)/shard_map/ppermute | solution.py:689
  7.9 0.8 %other_slab.1 = (f32[4,1152,128]{2,1,0:T(8,128)S(1)}, s32[8,128]{1,0:T(8,128)S(1)}) custom-call(s32[17,8,256]{2,1,0:T(8,128)S(1)} %collective-permute-done.bulk_ref, f32[8,8,128]{2,1,0:T(8,128)S(1)} %get-tuple-element.22.tables_ref, bf16[256,512]{1,0:T(8,128)(2,1)S(1)} %get-tuple-element.28.weights_ref, ...), custom_call_target="tpu_custom_call", output_to_operand_aliasing={{0}: (3, {})} | custom-call | flops 800000000 | bytes 2880000 | tf_op jit(solution)/shard_map/other_slab/pallas_call | solution.py:635
  8.8 0.0 collective-permute-done.1.second_ref
  8.8 0.1 collective-permute-done.2.first_ref
  8.8 0.1 side_columns.1.ends_ref
  8.9 0.2 %collective-permute-start.4 = (s32[2,8,128]{2,1,0:T(8,128)S(1)}, s32[2,8,128]{2,1,0:T(8,128)S(1)}, u32[]{:S(2)}, u32[]{:S(2)}) collective-permute-start(s32[2,8,128]{2,1,0:T(8,128)S(1)} %side_columns.1.ends_ref), channel_id=1, source_target_pairs={{1,2},{3,0},{2,1},{0,3},{5,6},{7,4},{6,5},{4,7},{9,10},{11,8},{10,... | collective-permute-start | bytes 24584 | tf_op jit(solution)/shard_map/ppermute | solution.py:720
  9.1 1.6 %collective-permute-start.3 = (s32[2,8,128]{2,1,0:T(8,128)S(1)}, s32[2,8,128]{2,1,0:T(8,128)S(1)}, u32[]{:S(2)}, u32[]{:S(2)}) collective-permute-start(s32[2,8,128]{2,1,0:T(8,128)S(1)} %side_columns.1.ends_ref), channel_id=1, source_target_pairs={{0,1},{2,3},{1,0},{3,2},{4,5},{6,7},{5,4},{7,6},{8,9},{10,11},{9,8... | collective-permute-start | bytes 24584 | tf_op jit(solution)/shard_map/ppermute | solution.py:719
  10.8 2.0 %render_tiles.1 = (f32[4,4,40,128]{3,2,1,0:T(8,128)S(1)}, f32[8,8,128]{2,1,0:T(8,128)S(1)}) custom-call(s32[1]{0:T(128)S(4)} %get-tuple-element.21.flip_ref, f32[8,8,128]{2,1,0:T(8,128)S(1)} %get-tuple-element.22.tables_ref, bf16[256,512]{1,0:T(8,128)(2,1)S(1)} %get-tuple-element.28.weights_ref, s32[17,8,256]{2,1,0:T(8,128)S(1)} %collective-permute-done.bulk_ref, ...), custom_call_target="tpu_custom_call" | custom-call | flops 2000000000 | bytes 7200000 | tf_op jit(solution)/shard_map/render_tiles/pallas_call | solution.py:635
  12.8 0.0 collective-permute-done.4.across_ref
  12.8 0.0 collective-permute-done.3.beside_ref
  12.8 1.3 %edge_columns.1 = f32[4,32,512]{2,1,0:T(8,128)} custom-call(s32[1]{0:T(128)S(4)} %get-tuple-element.21.flip_ref, f32[8,8,128]{2,1,0:T(8,128)S(1)} %get-tuple-element.22.tables_ref, s32[2,8,128]{2,1,0:T(8,128)S(1)} %collective-permute-done.3.beside_ref, s32[2,8,128]{2,1,0:T(8,128)S(1)} %collective-permute-done.4.across_ref, ...), custom_call_target="tpu_custom_call" | custom-call | flops 1000000000 | bytes 3600000 | tf_op jit(solution)/shard_map/edge_columns/pallas_call | solution.py:635
Async XLA Ops:
  1.2 6.8 %collective-permute-start = (s32[17,8,256]{2,1,0:T(8,128)S(1)}, s32[17,8,256]{2,1,0:T(8,128)S(1)}, u32[]{:S(2)}, u32[]{:S(2)}) collective-permute-start(s32[17,8,256]{2,1,0:T(8,128)S(1)} %get-tuple-element.27), channel_id=1, source_target_pairs={{0,16},{16,0},{1,17},{17,1},{2,18},{18,2},{3,19},{19,3},{4,20},{20... | collective-permute-start | bytes 417800 | tf_op jit(solution)/shard_map/ppermute | solution.py:689
  4.2 4.6 %collective-permute-start.1 = (s32[8,256]{1,0:T(8,128)S(1)}, s32[8,256]{1,0:T(8,128)S(1)}, u32[]{:S(2)}, u32[]{:S(2)}) collective-permute-start(s32[8,256]{1,0:T(8,128)S(1)} %get-tuple-element.31), channel_id=1, source_target_pairs={{16,4},{17,5},{18,6},{19,7},{20,8},{21,9},{22,10},{23,11},{24,12},... | collective-permute-start | bytes 24584 | tf_op jit(solution)/shard_map/ppermute | solution.py:691
  4.2 4.7 %collective-permute-start.2 = (s32[8,256]{1,0:T(8,128)S(1)}, s32[8,256]{1,0:T(8,128)S(1)}, u32[]{:S(2)}, u32[]{:S(2)}) collective-permute-start(s32[8,256]{1,0:T(8,128)S(1)} %get-tuple-element.32), channel_id=1, source_target_pairs={{0,4},{1,5},{2,6},{3,7},{4,8},{5,9},{6,10},{7,11},{8,12},{9,13},{1... | collective-permute-start | bytes 24584 | tf_op jit(solution)/shard_map/ppermute | solution.py:690
  8.9 3.9 %collective-permute-start.4 = (s32[2,8,128]{2,1,0:T(8,128)S(1)}, s32[2,8,128]{2,1,0:T(8,128)S(1)}, u32[]{:S(2)}, u32[]{:S(2)}) collective-permute-start(s32[2,8,128]{2,1,0:T(8,128)S(1)} %side_columns.1.ends_ref), channel_id=1, source_target_pairs={{1,2},{3,0},{2,1},{0,3},{5,6},{7,4},{6,5},{4,7},{9,10},{11,8},{10,... | collective-permute-start | bytes 24584 | tf_op jit(solution)/shard_map/ppermute | solution.py:720
  9.1 3.7 %collective-permute-start.3 = (s32[2,8,128]{2,1,0:T(8,128)S(1)}, s32[2,8,128]{2,1,0:T(8,128)S(1)}, u32[]{:S(2)}, u32[]{:S(2)}) collective-permute-start(s32[2,8,128]{2,1,0:T(8,128)S(1)} %side_columns.1.ends_ref), channel_id=1, source_target_pairs={{0,1},{2,3},{1,0},{3,2},{4,5},{6,7},{5,4},{7,6},{8,9},{10,11},{9,8... | collective-permute-start | bytes 24584 | tf_op jit(solution)/shard_map/ppermute | solution.py:719

commit v22 on v21

--- a/solution.py
+++ b/solution.py
@@ -231,10 +231,17 @@
     lines_ref[...] = jnp.where(lane_at == beside + middle, inside[:, cols - 1 : cols], lines)
 
 
-def side_kernel(rows, columns_ref, other_ref, second_ref, first_ref, ends_ref):
-    layers = columns_ref.shape[0]
+def side_kernel(
+    rows, columns_ref, bulk_ref, second_ref, first_ref, part_ref, ends_ref, other_ref
+):
+    layers, _ = columns_ref.shape
     front = lax.axis_index("bz") == 0
     lane_at = lax.broadcasted_iota(jnp.int32, (layers, LANES), 1)
+
+    def read_words(z, part, tile):
+        return bulk_ref[2 * z + part, :, tile * LANES : (tile + 1) * LANES]
+
+    column_lines(read_words, bulk_ref[2 * layers], other_ref, rows)
     for slab in range(2):
         mine = front if slab == 0 else jnp.logical_not(front)
         columns = jnp.where(mine, columns_ref[...], other_ref[...])
@@ -301,38 +308,59 @@
 
 def own_kernel(cells_ref, weights_ref, along_ref):
     size = cells_ref.shape[0]
-    pad = along_ref.shape[1] // 2 - size
+    pad = 64
     mine = pl.multiple_of(pad + lax.axis_index("bz") * size, pad)
 
     def store(tile, block):
         along_ref[tile, 0:pad, :] = jnp.zeros((pad, LANES), jnp.float32)
-        along_ref[tile, pad + 2 * size :, :] = jnp.zeros((pad, LANES), jnp.float32)
+        along_ref[tile, pad + 2 * size : 2 * pad + 2 * size, :] = jnp.zeros((pad, LANES), jnp.float32)
         along_ref[tile, pl.ds(mine, size), :] = block
 
     along_columns(cells_ref[...], weights_ref, store)
 
 
-def other_kernel(
-    rows, bulk_ref, tables_ref, weights_ref, own_ref, along_ref, columns_ref, cells_ref
-):
+def other_kernel(bulk_ref, tables_ref, weights_ref, ends_ref, own_ref, along_ref, cells_ref):
     layers = (bulk_ref.shape[0] - 1) // 2
     cols = bulk_ref.shape[2]
     size = cells_ref.shape[0]
-    pad = along_ref.shape[1] // 2 - size
+    pad = 64
     theirs = pl.multiple_of(pad + (1 - lax.axis_index("bz")) * size, pad)
 
-    def read_words(z, part, tile):
-        return bulk_ref[2 * z + part, :, tile * LANES : (tile + 1) * LANES]
-
     def read_cells(z, part, tile):
-        return unpack_words(read_words(z, part, tile))
+        return unpack_words(bulk_ref[2 * z + part, :, tile * LANES : (tile + 1) * LANES])
 
     def store(tile, block):
         along_ref[tile, pl.ds(theirs, size), :] = block
 
-    column_lines(read_words, bulk_ref[2 * layers], columns_ref, rows)
     classify_rows(read_cells, read_tables(tables_ref), cells_ref, layers, cols // LANES)
     along_columns(cells_ref[...], weights_ref, store)
+
+
+def edge_cells(near, inside, tables, cells_ref, front, base):
+    layers, cols = near.shape
+    for side in range(2):
+        use_near = front if side == 0 else jnp.logical_not(front)
+        words = jnp.where(use_near, near, inside)
+        for t in range(cols // LANES):
+            values = cell_values(
+                *unpack_words(words[:, t * LANES : (t + 1) * LANES]), tables, float(2 * layers)
+            )
+            for channel in range(4):
+                at = pl.ds(base + side * 4 + channel, layers, stride=8)
+                cells_ref[t, at, :] = values[channel]
+
+
+def edge_along(cells_ref, count, weights_ref):
+    return rounded(
+        sum(
+            jnp.dot(
+                cells_ref[t, 0:count].astype(jnp.bfloat16),
+                weights_ref[t * LANES : (t + 1) * LANES, :],
+                preferred_element_type=jnp.float32,
+            )
+            for t in range(cells_ref.shape[0])
+        )
+    )
 
 
 def edge_lines(now, packed_ref, lines_ref, depth):
@@ -348,85 +376,114 @@
         lines_ref[at : at + 8, :] = rounded(after + here)
 
 
-def render_pair(along_refs, packed_refs, lines_refs, rows_ref, flip, layers):
+def row_samples(value, above, below):
     sub_at = lax.broadcasted_iota(jnp.int32, (8, LANES), 0)
-    top = sub_at == 0
-    bottom = sub_at == 7
-
-    def one_slab(position, image):
-        slab = position ^ flip
-        along_at = pl.ds(pl.multiple_of(slab * (layers * 64), 64), (layers + 2) * 64)
-        packed_at = pl.ds(pl.multiple_of(slab * (layers * 16), 16), layers * 16)
-        lines_at = pl.ds(pl.multiple_of(slab * (layers * 8), 8), layers * 8 + 8)
-        views = [ref.at[along_at, :] for ref in along_refs]
-        packed = [ref.at[packed_at, :] for ref in packed_refs]
-        lines = [ref.at[lines_at, :] for ref in lines_refs]
-
-        def layer_rows(view, layer, channel):
-            base = (layer * 4 + channel) * 16
-            return view[base : base + 16, :]
-
-        def both(pieces):
-            return jnp.concatenate(pieces, axis=1)
-
-        def blend(image, samples):
-            updated = []
-            for tile in range(2):
-                clear = [1.0 - value for value in image[tile][3]]
-                updated.append(
-                    [
-                        [image[tile][c][i] + clear[i] * samples[tile][c][i] for i in range(4)]
-                        for c in range(4)
-                    ]
-                )
-            return updated
-
-        for z in range(layers):
-            triple = [[3.0 * layer_rows(v, z + 1, c) for c in range(4)] for v in views]
-            mixed = [
-                both(
-                    [
-                        (layer_rows(v, z, c) + t[c]).astype(jnp.bfloat16)
-                        for v, t in zip(views, triple)
-                    ]
-                )
-                for c in range(4)
-            ]
-            mixed.append(both([line[z * 16 : z * 16 + 16, :] for line in packed]))
-            even = jnp.dot(
-                rows_ref[...], jnp.concatenate(mixed, axis=0), preferred_element_type=jnp.float32
-            )
-            even = [
+    low, high = value[0:8], value[8:16]
+    before = jnp.where(sub_at == 0, above, pltpu.roll(high, 1, 0))
+    after = jnp.where(sub_at == 7, below, pltpu.roll(low, 7, 0))
+    low_centre = 3.0 * low
+    high_centre = 3.0 * high
+    return [before + low_centre, low_centre + high, low + high_centre, high_centre + after]
+
+
+def slab_pair(
+    along_refs, packed_refs, lines_refs, rows_ref, slab, lines_slab, layers, keep_first=None, keep_last=None
+):
+    along_at = pl.ds(pl.multiple_of(slab * (layers * 64), 64), (layers + 2) * 64)
+    packed_at = pl.ds(pl.multiple_of(lines_slab * (layers * 16), 16), layers * 16)
+    lines_at = pl.ds(pl.multiple_of(lines_slab * (layers * 8), 8), layers * 8 + 8)
+    views = [ref.at[along_at, :] for ref in along_refs]
+    packed = [ref.at[packed_at, :] for ref in packed_refs]
+    lines = [ref.at[lines_at, :] for ref in lines_refs]
+
+    def layer_rows(view, layer, channel):
+        base = (layer * 4 + channel) * 16
+        return view[base : base + 16, :]
+
+    def both(pieces):
+        return jnp.concatenate(pieces, axis=1)
+
+    def blend(image, samples, keep):
+        updated = []
+        for tile in range(2):
+            clear = [1.0 - value for value in image[tile][3]]
+            updated.append([])
+            for c in range(4):
+                values = samples[tile][c]
+                if keep is not None:
+                    values = [jnp.where(keep, value, 0.0) for value in values]
+                updated[tile].append([image[tile][c][i] + clear[i] * values[i] for i in range(4)])
+        return updated
+
+    zero = jnp.zeros((8, LANES), jnp.float32)
+    image = [[[zero] * 4 for _ in range(4)] for _ in range(2)]
+    for z in range(layers):
+        triple = [[3.0 * layer_rows(v, z + 1, c) for c in range(4)] for v in views]
+        mixed = [
+            both([(layer_rows(v, z, c) + t[c]).astype(jnp.bfloat16) for v, t in zip(views, triple)])
+            for c in range(4)
+        ]
+        mixed.append(both([line[z * 16 : z * 16 + 16, :] for line in packed]))
+        product = jnp.dot(
+            rows_ref[...], jnp.concatenate(mixed, axis=0), preferred_element_type=jnp.float32
+        )
+        even, odd = [], []
+        for tile in range(2):
+            lanes = slice(tile * LANES, (tile + 1) * LANES)
+            even.append(
                 [
-                    [
-                        even[c * 32 + i * 8 : c * 32 + i * 8 + 8, tile * LANES : (tile + 1) * LANES]
-                        for i in range(4)
-                    ]
+                    [product[c * 32 + i * 8 : c * 32 + i * 8 + 8, lanes] for i in range(4)]
                     for c in range(4)
                 ]
-                for tile in range(2)
-            ]
-            odd = []
-            for tile in range(2):
-                odd.append([])
-                for c in range(4):
-                    value = rounded(layer_rows(views[tile], z + 2, c) + triple[tile][c])
-                    low, high = value[0:8], value[8:16]
-                    above = lines[tile][pl.ds(z * 8 + c, 8, stride=0), :]
-                    below = lines[tile][pl.ds(z * 8 + 4 + c, 8, stride=0), :]
-                    before = jnp.where(top, above, pltpu.roll(high, 1, 0))
-                    after = jnp.where(bottom, below, pltpu.roll(low, 7, 0))
-                    low_centre = 3.0 * low
-                    high_centre = 3.0 * high
-                    odd[tile].append(
-                        [before + low_centre, low_centre + high, low + high_centre, high_centre + after]
-                    )
-            image = blend(blend(image, even), odd)
-        return image
-
-    zero = jnp.zeros((8, LANES), jnp.float32)
-    image = [[[zero] * 4 for _ in range(4)] for _ in range(2)]
-    return lax.fori_loop(0, 2, one_slab, image)
+            )
+            odd.append([])
+            for c in range(4):
+                value = rounded(layer_rows(views[tile], z + 2, c) + triple[tile][c])
+                above = lines[tile][pl.ds(z * 8 + c, 8, stride=0), :]
+                below = lines[tile][pl.ds(z * 8 + 4 + c, 8, stride=0), :]
+                odd[tile].append(row_samples(value, above, below))
+        image = blend(image, even, keep_first if z == 0 else None)
+        image = blend(image, odd, keep_last if z == layers - 1 else None)
+    return image
+
+
+def joined(first, in_front, behind):
+    top = [[jnp.where(first, x, y) for x, y in zip(a, b)] for a, b in zip(in_front, behind)]
+    low = [[jnp.where(first, y, x) for x, y in zip(a, b)] for a, b in zip(in_front, behind)]
+    clear = [1.0 - value for value in top[3]]
+    return [[top[c][i] + clear[i] * low[c][i] for i in range(4)] for c in range(4)]
+
+
+def own_tiles_kernel(
+    tables_ref, weights_ref, inside_ref, mix_ref, along_ref, part_ref, cells_ref, packed_ref, lines_ref
+):
+    layers, cols = inside_ref.shape
+    me = lax.axis_index("bz")
+    front = me == 0
+    inside = inside_ref[...]
+    edge_cells(jnp.zeros_like(inside), inside, read_tables(tables_ref), cells_ref, front, 0)
+    edge = edge_along(cells_ref, 8 * layers, weights_ref)
+    tiles = 2 * cols // LANES
+    for tile in range(tiles):
+        now = edge[:, tile * LANES : (tile + 1) * LANES]
+        edge_lines(now, packed_ref.at[tile], lines_ref.at[tile], layers)
+    for pair in range(tiles // 2):
+        at = [2 * pair, 2 * pair + 1]
+        image = slab_pair(
+            [along_ref.at[tile] for tile in at],
+            [packed_ref.at[tile] for tile in at],
+            [lines_ref.at[tile] for tile in at],
+            mix_ref,
+            me,
+            0,
+            layers,
+            front,
+            jnp.logical_not(front),
+        )
+        for index, tile in enumerate(at):
+            for channel in range(4):
+                for i in range(4):
+                    part_ref[tile, channel * 4 + i] = image[index][channel][i]
 
 
 def fill_rows(rows_ref):
@@ -446,7 +503,7 @@
 
 def tiles_kernel(
     flip_ref, tables_ref, weights_ref, bulk_ref, inside_ref, second_ref, first_ref, ends_ref, mix_ref,
-    along_ref, image_ref, mine_ref, cells_ref, packed_ref, lines_ref,
+    part_ref, along_ref, image_ref, mine_ref, cells_ref, packed_ref, lines_ref, edge_ref, between_ref,
 ):
     layers, cols = inside_ref.shape
     depth = 2 * layers
@@ -457,50 +514,82 @@
     for slab in range(2):
         inside = jnp.where(me == slab, inside_ref[...], bulk_ref[2 * layers])
         near = near_words(slab, first_ref, second_ref)
-        for side in range(2):
-            use_near = front if side == 0 else jnp.logical_not(front)
-            words = jnp.where(use_near, near, inside)
-            for t in range(cols // LANES):
-                values = cell_values(
-                    *unpack_words(words[:, t * LANES : (t + 1) * LANES]), tables, float(depth)
-                )
-                for channel in range(4):
-                    at = pl.ds(slab * layers * 8 + side * 4 + channel, layers, stride=8)
-                    cells_ref[t, at, :] = values[channel]
+        edge_cells(near, inside, tables, cells_ref, front, slab * layers * 8)
         values = cell_values(*unpack_words(ends_ref[slab]), tables, float(depth))
         for channel in range(4):
             mine_ref[slab * 4 + channel] = 3.0 * rounded(values[channel])
-    edge = rounded(
-        sum(
-            jnp.dot(
-                cells_ref[t, 0 : 8 * depth].astype(jnp.bfloat16),
-                weights_ref[t * LANES : (t + 1) * LANES, :],
-                preferred_element_type=jnp.float32,
-            )
-            for t in range(cols // LANES)
-        )
-    )
+    edge = edge_along(cells_ref, 8 * depth, weights_ref)
+    here_at, beside_at = layers * 8 - 8, layers * 8
+    empty = jnp.zeros((8, LANES), jnp.float32)
     for tile in range(tiles):
         now = edge[:, tile * LANES : (tile + 1) * LANES]
         edge_lines(now, packed_ref.at[tile], lines_ref.at[tile], depth)
-
-    def one_pair(pair, carry):
+        upper, lower = now[here_at : here_at + 8], now[beside_at : beside_at + 8]
+        between_ref[tile, 0:8] = rounded(
+            jnp.where(front, lower, upper) + 3.0 * jnp.where(front, upper, lower)
+        )
+        edge_ref[tile, 0:8] = empty
+        edge_ref[tile, 8 : 8 * depth + 8] = now
+        edge_ref[tile, 8 * depth + 8 :] = empty
+
+    row = jnp.where(front, 0, 15)
+    first_layer = me * layers
+    replaced = []
+    for tile in range(tiles):
+        inner, outer = [], []
+        for z in range(layers + 2):
+            at = (first_layer + z) * 64 + row
+            inner.append(along_ref[tile, pl.ds(at, 4, stride=16), :])
+            both = edge_ref[tile, pl.ds(pl.multiple_of((first_layer + z) * 8, 8), 8), :]
+            outer.append(jnp.where(front, both[0:4], both[4:8]))
+        image = jnp.zeros((4, LANES), jnp.float32)
+        for z in range(layers):
+            for parity in range(2):
+                beside = z + 2 * parity
+                sample = rounded(outer[beside] + 3.0 * outer[z + 1]) + 3.0 * rounded(
+                    inner[beside] + 3.0 * inner[z + 1]
+                )
+                if (z, parity) == (0, 0):
+                    sample = jnp.where(front, sample, 0.0)
+                if (z, parity) == (layers - 1, 1):
+                    sample = jnp.where(front, 0.0, sample)
+                image = image + (1.0 - image[3:4]) * sample
+        replaced.append(image)
+
+    sub_at = lax.broadcasted_iota(jnp.int32, (8, LANES), 0)
+    for pair in range(tiles // 2):
         at = [2 * pair, 2 * pair + 1]
-        image = render_pair(
+        other = slab_pair(
             [along_ref.at[tile] for tile in at],
             [packed_ref.at[tile] for tile in at],
             [lines_ref.at[tile] for tile in at],
             mix_ref,
-            flip_ref[0],
+            1 - me,
+            1 - me,
             layers,
         )
         for index, tile in enumerate(at):
-            for channel in range(4):
+            here = pl.multiple_of(jnp.where(front, layers, layers + 1) * 64, 64)
+            beside = pl.multiple_of(jnp.where(front, layers + 1, layers) * 64, 64)
+            between, part = [], []
+            for c in range(4):
+                value = rounded(
+                    along_ref[tile, pl.ds(beside + c * 16, 16), :]
+                    + 3.0 * along_ref[tile, pl.ds(here + c * 16, 16), :]
+                )
+                above = between_ref[tile, pl.ds(c, 8, stride=0), :]
+                below = between_ref[tile, pl.ds(c + 4, 8, stride=0), :]
+                between.append(row_samples(value, above, below))
+                values = [part_ref[tile, c * 4 + i] for i in range(4)]
+                line = replaced[tile][c : c + 1]
+                values[0] = jnp.where(sub_at == 0, jnp.where(front, line, values[0]), values[0])
+                values[3] = jnp.where(sub_at == 7, jnp.where(front, values[3], line), values[3])
+                part.append(values)
+            mine = joined(front, part, between)
+            image = joined((me ^ flip_ref[0]) == 0, mine, other[index])
+            for c in range(4):
                 for i in range(4):
-                    image_ref[tile, channel, pl.ds(i, 8, stride=4), :] = image[index][channel][i]
-        return carry
-
-    lax.fori_loop(0, tiles // 2, one_pair, 0)
+                    image_ref[tile, c, pl.ds(i, 8, stride=4), :] = image[c][i]
 
 
 def edge_kernel(
@@ -701,35 +790,46 @@
         ),
         0.5,
     )(dense, index, inside, tables)
-    whole = pltpu.VMEM((tiles, 2 * size + 2 * 4 * half, LANES), f32)
+    whole = pltpu.VMEM((tiles, 2 * size + 3 * 4 * half, LANES), f32)
     along = call(own_kernel, "own_slab", whole, 0.4)(cells, weights)
-    along, other_columns = call(
-        functools.partial(other_kernel, rows),
-        "other_slab",
-        (whole, pltpu.VMEM((layers, LANES), i32)),
-        0.8,
-        [pltpu.VMEM((size, cols), bf16)],
-        aliases={3: 0},
-    )(bulk, tables, weights, along)
+    edges = pltpu.VMEM((cols // LANES, 16 * layers + 8, LANES), f32)
+    packed = pltpu.VMEM((tiles, 32 * layers, LANES), bf16)
+    lines = pltpu.VMEM((tiles, 16 * layers + 8, LANES), f32)
+    part = call(
+        own_tiles_kernel,
+        "own_tiles",
+        pltpu.VMEM((tiles, 16, 8, LANES), f32),
+        0.1,
+        [edges, packed, lines],
+    )(tables, weights, inside, mix, along)
     ends = call(
-        functools.partial(side_kernel, rows), "side_columns", pltpu.VMEM((2, layers, LANES), i32), 0.1
-    )(columns, other_columns, second, first)
+        functools.partial(side_kernel, rows),
+        "side_columns",
+        pltpu.VMEM((2, layers, LANES), i32),
+        0.1,
+        [pltpu.VMEM((layers, LANES), i32)],
+    )(columns, bulk, second, first, part)
     pairs = [(x, x + 1) for x in range(0, count_x, 2)]
     cross = [(x, (x + 1) % count_x) for x in range(1, count_x, 2)]
     beside = lax.ppermute(ends, "bx", both(pairs))
     across = lax.ppermute(ends, "bx", both(cross))
+    along = call(other_kernel, "other_slab", whole, 0.8, [pltpu.VMEM((size, cols), bf16)], aliases={4: 0})(
+        bulk, tables, weights, ends, along
+    )
     image, mine = call(
         tiles_kernel,
         "render_tiles",
         (pltpu.VMEM((tiles, 4, rows + 8, LANES), f32), pltpu.VMEM((8, layers, LANES), f32)),
         2.0,
         [
-            pltpu.VMEM((cols // LANES, 16 * layers + 8, LANES), f32),
-            pltpu.VMEM((tiles, 32 * layers, LANES), bf16),
-            pltpu.VMEM((tiles, 16 * layers + 8, LANES), f32),
+            edges,
+            packed,
+            lines,
+            pltpu.VMEM((tiles, 16 * layers + 16, LANES), f32),
+            pltpu.VMEM((tiles, 16, LANES), f32),
         ],
-        [smem] + [VMEM] * 9,
-    )(flip, tables, weights, bulk, inside, second, first, ends, mix, along)
+        [smem] + [VMEM] * 10,
+    )(flip, tables, weights, bulk, inside, second, first, ends, mix, part, along)
     return call(
         edge_kernel,
         "edge_columns",

time: 14.3 us -> 14.3 us (level)
  Pallas kernels: 6.32 us -> 6.68 us
  starting transfers between devices: 6.44 us -> 6.28 us
  waiting for transfers between devices: 1.33 us -> 1.18 us
    ppermute x1, waiting for transfers between devices: 1.27 us -> 0.01 us  [two_slab_device(): bulk = lax.ppermute(bulk, 'bz', [(0, 1), (1, 0)])]
    ppermute x1, waiting for transfers between devices: 0.05 us -> 1.17 us  [two_slab_device(): first = lax.ppermute(first, axes, ring)]
    pallas_call x7 -> x8, Pallas kernels: 6.32 us -> 6.68 us  [run(): pl.pallas_call(kernel, out_shape=out_shape, in_specs=in_specs or [VMEM] *...]
    ppermute x1, starting transfers between devices: 0.23 us -> 0.07 us  [two_slab_device(): across = lax.ppermute(ends, 'bx', both(cross))]
  transfers between devices with their start and end apart: 5 -> 5, of which waited for: 2 -> 1; matrix products, arithmetic and copies ran while one was open for 0% -> 0% of each run, Pallas kernels for 26% -> 29%
where the time goes in v22:
time: 14.3 us; the launch traced here: 14.2 us
  Pallas kernels  6.68 us (47%)
  starting transfers between devices  6.28 us (44%)
  waiting for transfers between devices  1.18 us (8%)
    pallas_call x8, Pallas kernels, run(): pl.pallas_call(kernel, out_shape=out_shape, in_specs=in_specs or [VMEM] *...  6.68 us
    ppermute x1, starting transfers between devices, two_slab_device(): bulk = lax.ppermute(bulk, 'bz', [(0, 1), (1, 0)])  3 us
    ppermute x1, starting transfers between devices, two_slab_device(): beside = lax.ppermute(ends, 'bx', both(pairs))  1.62 us
    ppermute x1, starting transfers between devices, two_slab_device(): first = lax.ppermute(first, axes, ring)  1.58 us
    ppermute x1, waiting for transfers between devices, two_slab_device(): first = lax.ppermute(first, axes, ring)  1.17 us
  transfers between devices with their start and end apart: 5, of which 1 were waited for; matrix products, arithmetic and copies ran while one was open for 0% of the time, Pallas kernels for 29%

profile of v22, /device:TPU:0, one launch (start us, length us, event | category | flops | bytes accessed | tf_op | source)
XLA Modules:
  0.0 14.2 jit_solution(4941369810511788658)
XLA Ops:
  0.0 1.2 %stage_block.1 = (s32[1]{0:T(128)S(4)}, s32[8,256]{1,0:T(8,128)S(1)}, s32[8,256]{1,0:T(8,128)S(1)}, s32[17,8,256]{2,1,0:T(8,128)S(1)}, s32[8,256]{1,0:T(8,128)S(...) custom-call(s32[2]{0:T(128)} %rank_ref.1, f32[8,32,256]{2,1,0:T(8,128)} %density_ref.1, ...), custom_call_target="tpu_custom_call" | custom-call | flops 1200000000 | bytes 4320000 | tf_op jit(solution)/shard_map/stage_block/pallas_call | solution.py:724
  1.2 3.0 %collective-permute-start = (s32[17,8,256]{2,1,0:T(8,128)S(1)}, s32[17,8,256]{2,1,0:T(8,128)S(1)}, u32[]{:S(2)}, u32[]{:S(2)}) collective-permute-start(s32[17,8,256]{2,1,0:T(8,128)S(1)} %get-tuple-element.25), channel_id=1, source_target_pairs={{0,16},{16,0},{1,17},{17,1},{2,18},{18,2},{3,19},{19,3},{4,20},{20... | collective-permute-start | bytes 417800 | tf_op jit(solution)/shard_map/ppermute | solution.py:778
  4.2 0.0 collective-permute-start.1
  4.2 1.6 %collective-permute-start.2 = (s32[8,256]{1,0:T(8,128)S(1)}, s32[8,256]{1,0:T(8,128)S(1)}, u32[]{:S(2)}, u32[]{:S(2)}) collective-permute-start(s32[8,256]{1,0:T(8,128)S(1)} %get-tuple-element.27), channel_id=1, source_target_pairs={{0,4},{1,5},{2,6},{3,7},{4,8},{5,9},{6,10},{7,11},{8,12},{9,13},{1... | collective-permute-start | bytes 24584 | tf_op jit(solution)/shard_map/ppermute | solution.py:779
  5.7 0.6 %own_cells.1 = (bf16[512,256]{1,0:T(8,128)(2,1)S(1)}, bf16[256,512]{1,0:T(8,128)(2,1)S(1)}, bf16[128,80]{1,0:T(8,128)(2,1)S(1)}, s32[8,128]{1,0:T(8,128)S(1)}) custom-call(f32[8,2,40,128]{3,2,1,0:T(8,128)S(1)} %get-tuple-element.21.dense_ref, s32[8,2,40,128]{3,2,1,0:T(8,128)S(1)} %get-tuple-element.22.index_ref, s32[8,256]{1,0:T(8,128)S(1)} %get-tuple-element.23.inside_ref, ...), custom_call_target="tpu_custom_call" | custom-call | flops 500000000 | bytes 1800000 | tf_op jit(solution)/shard_map/own_cells/pallas_call | solution.py:724
  6.3 0.3 %own_slab.1.along_ref.own_ref = f32[4,1216,128]{2,1,0:T(8,128)S(1)} custom-call(bf16[512,256]{1,0:T(8,128)(2,1)S(1)} %get-tuple-element.30.cells_ref, bf16[256,512]{1,0:T(8,128)(2,1)S(1)} %get-tuple-element.28.weights_ref), custom_call_target="tpu_custom_call" | custom-call | flops 400000000 | bytes 1440000 | tf_op jit(solution)/shard_map/own_slab/pallas_call | solution.py:724
  6.6 1.0 %own_tiles.1.part_ref = f32[4,16,8,128]{3,2,1,0:T(8,128)S(1)} custom-call(f32[8,8,128]{2,1,0:T(8,128)S(1)} %get-tuple-element.20.tables_ref, bf16[256,512]{1,0:T(8,128)(2,1)S(1)} %get-tuple-element.28.weights_ref, s32[8,256]{1,0:T(8,128)S(1)} %get-tuple-element.23.inside_ref, bf16[128,80]{1,0:T(8,128)(2,1)S(1)} %get-tuple-element.29.mix_ref, ...), custom_call_target="tpu_custom_call" | custom-call | flops 100000000 | bytes 360000 | tf_op jit(solution)/shard_map/own_tiles/pallas_call | solution.py:724
  7.7 0.0 collective-permute-done.1.second_ref
  7.7 1.2 %collective-permute-done.2.first_ref = s32[8,256]{1,0:T(8,128)S(1)} collective-permute-done((s32[8,256]{1,0:T(8,128)S(1)}, s32[8,256]{1,0:T(8,128)S(1)}, u32[]{:S(2)}, u32[]{:S(2)}) %collective-permute-start.2) | collective-permute-done | bytes 8224 | tf_op jit(solution)/shard_map/ppermute | solution.py:779
  8.8 0.0 collective-permute-done.bulk_ref
  8.8 0.1 side_columns.1.ends_ref
  9.0 0.1 collective-permute-start.4
  9.0 1.6 %collective-permute-start.3 = (s32[2,8,128]{2,1,0:T(8,128)S(1)}, s32[2,8,128]{2,1,0:T(8,128)S(1)}, u32[]{:S(2)}, u32[]{:S(2)}) collective-permute-start(s32[2,8,128]{2,1,0:T(8,128)S(1)} %side_columns.1.ends_ref), channel_id=1, source_target_pairs={{0,1},{2,3},{1,0},{3,2},{4,5},{6,7},{5,4},{7,6},{8,9},{10,11},{9,8... | collective-permute-start | bytes 24584 | tf_op jit(solution)/shard_map/ppermute | solution.py:814
  10.7 0.8 %other_slab.1.along_ref = f32[4,1216,128]{2,1,0:T(8,128)S(1)} custom-call(s32[17,8,256]{2,1,0:T(8,128)S(1)} %collective-permute-done.bulk_ref, f32[8,8,128]{2,1,0:T(8,128)S(1)} %get-tuple-element.20.tables_ref, bf16[256,512]{1,0:T(8,128)(2,1)S(1)} %get-tuple-element.28.weights_ref, ...), custom_call_target="tpu_custom_call", output_to_operand_aliasing={{}: (4, {})} | custom-call | flops 800000000 | bytes 2880000 | tf_op jit(solution)/shard_map/other_slab/pallas_call | solution.py:724
  11.5 1.4 %render_tiles.1 = (f32[4,4,40,128]{3,2,1,0:T(8,128)S(1)}, f32[8,8,128]{2,1,0:T(8,128)S(1)}) custom-call(s32[1]{0:T(128)S(4)} %get-tuple-element.19.flip_ref, f32[8,8,128]{2,1,0:T(8,128)S(1)} %get-tuple-element.20.tables_ref, bf16[256,512]{1,0:T(8,128)(2,1)S(1)} %get-tuple-element.28.weights_ref, s32[17,8,256]{2,1,0:T(8,128)S(1)} %collective-permute-done.bulk_ref, ...), custom_call_target="tpu_custom_call" | custom-call | flops 2000000000 | bytes 7200000 | tf_op jit(solution)/shard_map/render_tiles/pallas_call | solution.py:724
  12.9 0.0 collective-permute-done.4.across_ref
  12.9 0.0 collective-permute-done.3.beside_ref
  12.9 1.3 %edge_columns.1 = f32[4,32,512]{2,1,0:T(8,128)} custom-call(s32[1]{0:T(128)S(4)} %get-tuple-element.19.flip_ref, f32[8,8,128]{2,1,0:T(8,128)S(1)} %get-tuple-element.20.tables_ref, s32[2,8,128]{2,1,0:T(8,128)S(1)} %collective-permute-done.3.beside_ref, s32[2,8,128]{2,1,0:T(8,128)S(1)} %collective-permute-done.4.across_ref, ...), custom_call_target="tpu_custom_call" | custom-call | flops 1000000000 | bytes 3600000 | tf_op jit(solution)/shard_map/edge_columns/pallas_call | solution.py:724
Async XLA Ops:
  1.2 7.7 %collective-permute-start = (s32[17,8,256]{2,1,0:T(8,128)S(1)}, s32[17,8,256]{2,1,0:T(8,128)S(1)}, u32[]{:S(2)}, u32[]{:S(2)}) collective-permute-start(s32[17,8,256]{2,1,0:T(8,128)S(1)} %get-tuple-element.25), channel_id=1, source_target_pairs={{0,16},{16,0},{1,17},{17,1},{2,18},{18,2},{3,19},{19,3},{4,20},{20... | collective-permute-start | bytes 417800 | tf_op jit(solution)/shard_map/ppermute | solution.py:778
  4.2 3.5 %collective-permute-start.1 = (s32[8,256]{1,0:T(8,128)S(1)}, s32[8,256]{1,0:T(8,128)S(1)}, u32[]{:S(2)}, u32[]{:S(2)}) collective-permute-start(s32[8,256]{1,0:T(8,128)S(1)} %get-tuple-element.26), channel_id=1, source_target_pairs={{16,4},{17,5},{18,6},{19,7},{20,8},{21,9},{22,10},{23,11},{24,12},... | collective-permute-start | bytes 24584 | tf_op jit(solution)/shard_map/ppermute | solution.py:780
  4.2 4.7 %collective-permute-start.2 = (s32[8,256]{1,0:T(8,128)S(1)}, s32[8,256]{1,0:T(8,128)S(1)}, u32[]{:S(2)}, u32[]{:S(2)}) collective-permute-start(s32[8,256]{1,0:T(8,128)S(1)} %get-tuple-element.27), channel_id=1, source_target_pairs={{0,4},{1,5},{2,6},{3,7},{4,8},{5,9},{6,10},{7,11},{8,12},{9,13},{1... | collective-permute-start | bytes 24584 | tf_op jit(solution)/shard_map/ppermute | solution.py:779
  9.0 3.9 %collective-permute-start.4 = (s32[2,8,128]{2,1,0:T(8,128)S(1)}, s32[2,8,128]{2,1,0:T(8,128)S(1)}, u32[]{:S(2)}, u32[]{:S(2)}) collective-permute-start(s32[2,8,128]{2,1,0:T(8,128)S(1)} %side_columns.1.ends_ref), channel_id=1, source_target_pairs={{1,2},{3,0},{2,1},{0,3},{5,6},{7,4},{6,5},{4,7},{9,10},{11,8},{10,... | collective-permute-start | bytes 24584 | tf_op jit(solution)/shard_map/ppermute | solution.py:815
  9.0 3.8 %collective-permute-start.3 = (s32[2,8,128]{2,1,0:T(8,128)S(1)}, s32[2,8,128]{2,1,0:T(8,128)S(1)}, u32[]{:S(2)}, u32[]{:S(2)}) collective-permute-start(s32[2,8,128]{2,1,0:T(8,128)S(1)} %side_columns.1.ends_ref), channel_id=1, source_target_pairs={{0,1},{2,3},{1,0},{3,2},{4,5},{6,7},{5,4},{7,6},{8,9},{10,11},{9,8... | collective-permute-start | bytes 24584 | tf_op jit(solution)/shard_map/ppermute | solution.py:814

commit v23 on v22

--- a/solution.py
+++ b/solution.py
@@ -163,12 +163,13 @@
     flip_ref[0] = rank_ref[0]
     layers, rows, cols = density_ref.shape
     front = lax.axis_index("bz") == 0
+    inner = lax.axis_index("by") > 0
     for z in range(layers):
         top, bottom = [
             pack_words(density_ref[z, r : r + 1, :], bins_ref[z, r : r + 1, :]) for r in (0, rows - 1)
         ]
-        first_ref[z : z + 1, :] = jnp.where(front, bottom, top)
-        second_ref[z : z + 1, :] = jnp.where(front, top, bottom)
+        first_ref[z : z + 1, :] = jnp.where(jnp.logical_not(front) & inner, top, bottom)
+        second_ref[z : z + 1, :] = jnp.where(front & inner, top, bottom)
         for tile in range(cols // LANES):
             lanes = slice(tile * LANES, (tile + 1) * LANES)
             dense_ref[z, tile, 0:rows] = density_ref[z, :, lanes]
@@ -207,7 +208,8 @@
 
 def near_words(slab, first_ref, second_ref):
     me = lax.axis_index("bz")
-    words = jnp.where(me == slab, first_ref[...], second_ref[...])
+    turned = (me == 0) & (lax.axis_index("by") == 1)
+    words = jnp.where((me == slab) != turned, first_ref[...], second_ref[...])
     return jnp.where(has_near(me == 0), words, 0)
 
 
@@ -766,18 +768,24 @@
     def place(z, y, x):
         return (z * count_y + y) * count_x + x
 
-    steps = range(count_y - 1)
-    ring = [(place(0, y, 0), place(0, y + 1, 0)) for y in steps]
-    ring += [(place(1, y + 1, 0), place(1, y, 0)) for y in steps]
-    ring += [(place(0, count_y - 1, 0), place(1, count_y - 1, 0)), (place(1, 0, 0), place(0, 0, 0))]
-    ring = [(source + x, target + x) for source, target in ring for x in range(count_x)]
-    diagonal = [(place(1, y, x), place(0, y + 1, x)) for y in steps for x in range(count_x)]
-    for z, y in ((0, 0), (1, count_y - 1)):
-        diagonal += [(place(z, y, x), place(z, y, x + 1)) for x in range(0, count_x, 2)]
+    def lanes(route):
+        return [(place(*source, x), place(*target, x)) for source, target in route for x in range(count_x)]
+
+    def twins(z, y):
+        return both([(place(z, y, x), place(z, y, x + 1)) for x in range(0, count_x, 2)])
+
+    last = count_y - 1
+    ring = [((1, 0), (0, 1)), ((0, last), (1, last))]
+    ring += [((0, y), (0, y + 1)) for y in range(1, last)] + [((1, y + 1), (1, y)) for y in range(last)]
+    ring = lanes(ring) + twins(0, 0)
+    diagonal = [((1, 0), (0, 0)), ((0, 0), (0, 1)), ((0, 1), (1, 0))]
+    for y in range(1, last):
+        diagonal += both([((1, y), (0, y + 1))])
+    diagonal = lanes(diagonal) + twins(1, last)
     axes = ("bz", "by", "bx")
     bulk = lax.ppermute(bulk, "bz", [(0, 1), (1, 0)])
     first = lax.ppermute(first, axes, ring)
-    second = lax.ppermute(second, axes, both(diagonal))
+    second = lax.ppermute(second, axes, diagonal)
 
     cells, weights, mix, columns = call(
         cells_kernel,

time: 14.3 us -> 13.8 us (0.965)
  waiting for transfers between devices: 1.18 us -> 0.37 us
  starting transfers between devices: 6.28 us -> 6.53 us
    ppermute x1, starting transfers between devices: 0.01 us -> 1.58 us  [two_slab_device(): second = lax.ppermute(second, axes, diagonal)]
    ppermute x1, starting transfers between devices: 1.58 us -> 0.01 us  [two_slab_device(): first = lax.ppermute(first, axes, ring)]
    ppermute x1, starting transfers between devices: 0.07 us -> 1.37 us  [two_slab_device(): across = lax.ppermute(ends, 'bx', both(cross))]
    ppermute x1, waiting for transfers between devices: 1.17 us -> 0.01 us  [two_slab_device(): first = lax.ppermute(first, axes, ring)]
    ppermute x1, starting transfers between devices: 1.62 us -> 0.58 us  [two_slab_device(): beside = lax.ppermute(ends, 'bx', both(pairs))]
    ppermute x1, waiting for transfers between devices: 0.01 us -> 0.36 us  [two_slab_device(): second = lax.ppermute(second, axes, diagonal)]
  transfers between devices with their start and end apart: 5 -> 5, of which waited for: 1 -> 1; matrix products, arithmetic and copies ran while one was open for 0% -> 0% of each run, Pallas kernels for 29% -> 30%
where the time goes in v23:
time: 13.8 us; the launch traced here: 13.6 us
  Pallas kernels  6.69 us (48%)
  starting transfers between devices  6.53 us (47%)
  waiting for transfers between devices  0.37 us (3%)
    pallas_call x8, Pallas kernels, run(): pl.pallas_call(kernel, out_shape=out_shape, in_specs=in_specs or [VMEM] *...  6.69 us
    ppermute x1, starting transfers between devices, two_slab_device(): bulk = lax.ppermute(bulk, 'bz', [(0, 1), (1, 0)])  3 us
    ppermute x1, starting transfers between devices, two_slab_device(): second = lax.ppermute(second, axes, diagonal)  1.58 us
    ppermute x1, starting transfers between devices, two_slab_device(): across = lax.ppermute(ends, 'bx', both(cross))  1.37 us
    ppermute x1, starting transfers between devices, two_slab_device(): beside = lax.ppermute(ends, 'bx', both(pairs))  0.58 us
    ppermute x1, waiting for transfers between devices, two_slab_device(): second = lax.ppermute(second, axes, diagonal)  0.36 us
  transfers between devices with their start and end apart: 5, of which 1 were waited for; matrix products, arithmetic and copies ran while one was open for 0% of the time, Pallas kernels for 30%

profile of v23, /device:TPU:0, one launch (start us, length us, event | category | flops | bytes accessed | tf_op | source)
XLA Modules:
  0.0 13.6 jit_solution(2238709719433974595)
XLA Ops:
  0.0 1.2 %stage_block.1 = (s32[1]{0:T(128)S(4)}, s32[8,256]{1,0:T(8,128)S(1)}, s32[8,256]{1,0:T(8,128)S(1)}, s32[17,8,256]{2,1,0:T(8,128)S(1)}, s32[8,256]{1,0:T(8,128)S(...) custom-call(s32[2]{0:T(128)} %rank_ref.1, f32[8,32,256]{2,1,0:T(8,128)} %density_ref.1, ...), custom_call_target="tpu_custom_call" | custom-call | flops 1200000000 | bytes 4320000 | tf_op jit(solution)/shard_map/stage_block/pallas_call | solution.py:726
  1.2 3.0 %collective-permute-start = (s32[17,8,256]{2,1,0:T(8,128)S(1)}, s32[17,8,256]{2,1,0:T(8,128)S(1)}, u32[]{:S(2)}, u32[]{:S(2)}) collective-permute-start(s32[17,8,256]{2,1,0:T(8,128)S(1)} %get-tuple-element.25), channel_id=1, source_target_pairs={{0,16},{16,0},{1,17},{17,1},{2,18},{18,2},{3,19},{19,3},{4,20},{20... | collective-permute-start | bytes 417800 | tf_op jit(solution)/shard_map/ppermute | solution.py:786
  4.2 1.6 %collective-permute-start.1 = (s32[8,256]{1,0:T(8,128)S(1)}, s32[8,256]{1,0:T(8,128)S(1)}, u32[]{:S(2)}, u32[]{:S(2)}) collective-permute-start(s32[8,256]{1,0:T(8,128)S(1)} %get-tuple-element.26), channel_id=1, source_target_pairs={{16,0},{17,1},{18,2},{19,3},{0,4},{1,5},{2,6},{3,7},{4,16},{5,17},... | collective-permute-start | bytes 24584 | tf_op jit(solution)/shard_map/ppermute | solution.py:788
  5.7 0.0 collective-permute-start.2
  5.7 0.6 %own_cells.1 = (bf16[512,256]{1,0:T(8,128)(2,1)S(1)}, bf16[256,512]{1,0:T(8,128)(2,1)S(1)}, bf16[128,80]{1,0:T(8,128)(2,1)S(1)}, s32[8,128]{1,0:T(8,128)S(1)}) custom-call(f32[8,2,40,128]{3,2,1,0:T(8,128)S(1)} %get-tuple-element.21.dense_ref, s32[8,2,40,128]{3,2,1,0:T(8,128)S(1)} %get-tuple-element.22.index_ref, s32[8,256]{1,0:T(8,128)S(1)} %get-tuple-element.23.inside_ref, ...), custom_call_target="tpu_custom_call" | custom-call | flops 500000000 | bytes 1800000 | tf_op jit(solution)/shard_map/own_cells/pallas_call | solution.py:726
  6.3 0.3 %own_slab.1.along_ref.own_ref = f32[4,1216,128]{2,1,0:T(8,128)S(1)} custom-call(bf16[512,256]{1,0:T(8,128)(2,1)S(1)} %get-tuple-element.30.cells_ref, bf16[256,512]{1,0:T(8,128)(2,1)S(1)} %get-tuple-element.28.weights_ref), custom_call_target="tpu_custom_call" | custom-call | flops 400000000 | bytes 1440000 | tf_op jit(solution)/shard_map/own_slab/pallas_call | solution.py:726
  6.6 1.0 %own_tiles.1.part_ref = f32[4,16,8,128]{3,2,1,0:T(8,128)S(1)} custom-call(f32[8,8,128]{2,1,0:T(8,128)S(1)} %get-tuple-element.20.tables_ref, bf16[256,512]{1,0:T(8,128)(2,1)S(1)} %get-tuple-element.28.weights_ref, s32[8,256]{1,0:T(8,128)S(1)} %get-tuple-element.23.inside_ref, bf16[128,80]{1,0:T(8,128)(2,1)S(1)} %get-tuple-element.29.mix_ref, ...), custom_call_target="tpu_custom_call" | custom-call | flops 100000000 | bytes 360000 | tf_op jit(solution)/shard_map/own_tiles/pallas_call | solution.py:726
  7.7 0.4 %collective-permute-done.1.second_ref = s32[8,256]{1,0:T(8,128)S(1)} collective-permute-done((s32[8,256]{1,0:T(8,128)S(1)}, s32[8,256]{1,0:T(8,128)S(1)}, u32[]{:S(2)}, u32[]{:S(2)}) %collective-permute-start.1) | collective-permute-done | bytes 8224 | tf_op jit(solution)/shard_map/ppermute | solution.py:788
  8.0 0.0 collective-permute-done.2.first_ref
  8.0 0.0 collective-permute-done.bulk_ref
  8.0 0.1 side_columns.1.ends_ref
  8.1 1.4 %collective-permute-start.4 = (s32[2,8,128]{2,1,0:T(8,128)S(1)}, s32[2,8,128]{2,1,0:T(8,128)S(1)}, u32[]{:S(2)}, u32[]{:S(2)}) collective-permute-start(s32[2,8,128]{2,1,0:T(8,128)S(1)} %side_columns.1.ends_ref), channel_id=1, source_target_pairs={{1,2},{3,0},{2,1},{0,3},{5,6},{7,4},{6,5},{4,7},{9,10},{11,8},{10,... | collective-permute-start | bytes 24584 | tf_op jit(solution)/shard_map/ppermute | solution.py:823
  9.5 0.6 %collective-permute-start.3 = (s32[2,8,128]{2,1,0:T(8,128)S(1)}, s32[2,8,128]{2,1,0:T(8,128)S(1)}, u32[]{:S(2)}, u32[]{:S(2)}) collective-permute-start(s32[2,8,128]{2,1,0:T(8,128)S(1)} %side_columns.1.ends_ref), channel_id=1, source_target_pairs={{0,1},{2,3},{1,0},{3,2},{4,5},{6,7},{5,4},{7,6},{8,9},{10,11},{9,8... | collective-permute-start | bytes 24584 | tf_op jit(solution)/shard_map/ppermute | solution.py:822
  10.1 0.8 %other_slab.1.along_ref = f32[4,1216,128]{2,1,0:T(8,128)S(1)} custom-call(s32[17,8,256]{2,1,0:T(8,128)S(1)} %collective-permute-done.bulk_ref, f32[8,8,128]{2,1,0:T(8,128)S(1)} %get-tuple-element.20.tables_ref, bf16[256,512]{1,0:T(8,128)(2,1)S(1)} %get-tuple-element.28.weights_ref, ...), custom_call_target="tpu_custom_call", output_to_operand_aliasing={{}: (4, {})} | custom-call | flops 800000000 | bytes 2880000 | tf_op jit(solution)/shard_map/other_slab/pallas_call | solution.py:726
  10.9 1.4 %render_tiles.1 = (f32[4,4,40,128]{3,2,1,0:T(8,128)S(1)}, f32[8,8,128]{2,1,0:T(8,128)S(1)}) custom-call(s32[1]{0:T(128)S(4)} %get-tuple-element.19.flip_ref, f32[8,8,128]{2,1,0:T(8,128)S(1)} %get-tuple-element.20.tables_ref, bf16[256,512]{1,0:T(8,128)(2,1)S(1)} %get-tuple-element.28.weights_ref, s32[17,8,256]{2,1,0:T(8,128)S(1)} %collective-permute-done.bulk_ref, ...), custom_call_target="tpu_custom_call" | custom-call | flops 2000000000 | bytes 7200000 | tf_op jit(solution)/shard_map/render_tiles/pallas_call | solution.py:726
  12.3 0.0 collective-permute-done.4.across_ref
  12.3 0.0 collective-permute-done.3.beside_ref
  12.3 1.3 %edge_columns.1 = f32[4,32,512]{2,1,0:T(8,128)} custom-call(s32[1]{0:T(128)S(4)} %get-tuple-element.19.flip_ref, f32[8,8,128]{2,1,0:T(8,128)S(1)} %get-tuple-element.20.tables_ref, s32[2,8,128]{2,1,0:T(8,128)S(1)} %collective-permute-done.3.beside_ref, s32[2,8,128]{2,1,0:T(8,128)S(1)} %collective-permute-done.4.across_ref, ...), custom_call_target="tpu_custom_call" | custom-call | flops 1000000000 | bytes 3600000 | tf_op jit(solution)/shard_map/edge_columns/pallas_call | solution.py:726
Async XLA Ops:
  1.2 6.9 %collective-permute-start = (s32[17,8,256]{2,1,0:T(8,128)S(1)}, s32[17,8,256]{2,1,0:T(8,128)S(1)}, u32[]{:S(2)}, u32[]{:S(2)}) collective-permute-start(s32[17,8,256]{2,1,0:T(8,128)S(1)} %get-tuple-element.25), channel_id=1, source_target_pairs={{0,16},{16,0},{1,17},{17,1},{2,18},{18,2},{3,19},{19,3},{4,20},{20... | collective-permute-start | bytes 417800 | tf_op jit(solution)/shard_map/ppermute | solution.py:786
  4.2 3.8 %collective-permute-start.1 = (s32[8,256]{1,0:T(8,128)S(1)}, s32[8,256]{1,0:T(8,128)S(1)}, u32[]{:S(2)}, u32[]{:S(2)}) collective-permute-start(s32[8,256]{1,0:T(8,128)S(1)} %get-tuple-element.26), channel_id=1, source_target_pairs={{16,0},{17,1},{18,2},{19,3},{0,4},{1,5},{2,6},{3,7},{4,16},{5,17},... | collective-permute-start | bytes 24584 | tf_op jit(solution)/shard_map/ppermute | solution.py:788
  5.7 2.3 %collective-permute-start.2 = (s32[8,256]{1,0:T(8,128)S(1)}, s32[8,256]{1,0:T(8,128)S(1)}, u32[]{:S(2)}, u32[]{:S(2)}) collective-permute-start(s32[8,256]{1,0:T(8,128)S(1)} %get-tuple-element.27), channel_id=1, source_target_pairs={{16,4},{17,5},{18,6},{19,7},{12,28},{13,29},{14,30},{15,31},{4,8},... | collective-permute-start | bytes 24584 | tf_op jit(solution)/shard_map/ppermute | solution.py:787
  8.1 4.2 %collective-permute-start.4 = (s32[2,8,128]{2,1,0:T(8,128)S(1)}, s32[2,8,128]{2,1,0:T(8,128)S(1)}, u32[]{:S(2)}, u32[]{:S(2)}) collective-permute-start(s32[2,8,128]{2,1,0:T(8,128)S(1)} %side_columns.1.ends_ref), channel_id=1, source_target_pairs={{1,2},{3,0},{2,1},{0,3},{5,6},{7,4},{6,5},{4,7},{9,10},{11,8},{10,... | collective-permute-start | bytes 24584 | tf_op jit(solution)/shard_map/ppermute | solution.py:823
  9.5 2.8 %collective-permute-start.3 = (s32[2,8,128]{2,1,0:T(8,128)S(1)}, s32[2,8,128]{2,1,0:T(8,128)S(1)}, u32[]{:S(2)}, u32[]{:S(2)}) collective-permute-start(s32[2,8,128]{2,1,0:T(8,128)S(1)} %side_columns.1.ends_ref), channel_id=1, source_target_pairs={{0,1},{2,3},{1,0},{3,2},{4,5},{6,7},{5,4},{7,6},{8,9},{10,11},{9,8... | collective-permute-start | bytes 24584 | tf_op jit(solution)/shard_map/ppermute | solution.py:822

commit v24 on v23

--- a/solution.py
+++ b/solution.py
@@ -118,6 +118,8 @@
 LANES = 128
 LEVELS = 65535.0
 VMEM = pl.BlockSpec(memory_space=pltpu.VMEM)
+SMEM = pl.BlockSpec(memory_space=pltpu.SMEM)
+FLIP, ME, HAS_NEAR, TURNED, ODD_X, HAS_RIGHT, HAS_LEFT = range(7)
 
 
 def pack_words(density, bins):
@@ -158,12 +160,25 @@
 
 def stage_kernel(
     rank_ref, density_ref, bins_ref, colour_ref, extinction_ref,
-    flip_ref, first_ref, second_ref, bulk_ref, inside_ref, dense_ref, index_ref, tables_ref,
+    place_ref, first_ref, second_ref, bulk_ref, inside_ref, dense_ref, index_ref, tables_ref,
 ):
-    flip_ref[0] = rank_ref[0]
+    me, me_y, me_x = lax.axis_index("bz"), lax.axis_index("by"), lax.axis_index("bx")
+    past = jnp.where(me == 0, me_y, lax.axis_size("by") - 1 - me_y)
+    for at, value in enumerate(
+        (
+            rank_ref[0],
+            me,
+            jnp.minimum(past, 1),
+            jnp.where((me == 0) & (me_y == 1), 1, 0),
+            lax.rem(me_x, 2),
+            jnp.where(me_x + 1 < lax.axis_size("bx"), 1, 0),
+            jnp.minimum(me_x, 1),
+        )
+    ):
+        place_ref[at] = value
     layers, rows, cols = density_ref.shape
-    front = lax.axis_index("bz") == 0
-    inner = lax.axis_index("by") > 0
+    front = me == 0
+    inner = me_y > 0
     for z in range(layers):
         top, bottom = [
             pack_words(density_ref[z, r : r + 1, :], bins_ref[z, r : r + 1, :]) for r in (0, rows - 1)
@@ -174,7 +189,7 @@
             lanes = slice(tile * LANES, (tile + 1) * LANES)
             dense_ref[z, tile, 0:rows] = density_ref[z, :, lanes]
             index_ref[z, tile, 0:rows] = bins_ref[z, :, lanes]
-    pack_block(dense_ref, index_ref, bulk_ref, inside_ref)
+    pack_block(front, dense_ref, index_ref, bulk_ref, inside_ref)
     colour = colour_ref[...].astype(jnp.float32)
     extinction = extinction_ref[...].astype(jnp.float32).reshape(1, 2 * LANES)
     for channel in range(4):
@@ -185,10 +200,9 @@
             )
 
 
-def pack_block(dense_ref, index_ref, bulk_ref, inside_ref):
+def pack_block(front, dense_ref, index_ref, bulk_ref, inside_ref):
     layers, tiles, rows = dense_ref.shape[0], dense_ref.shape[1], dense_ref.shape[2] - 8
     half = rows // 2
-    front = lax.axis_index("bz") == 0
     start = jnp.where(front, half, 0)
     for tile in range(tiles):
         lanes = slice(tile * LANES, (tile + 1) * LANES)
@@ -206,17 +220,16 @@
             inside_ref[z : z + 1, lanes] = jnp.where(front, line[1], line[0])
 
 
-def near_words(slab, first_ref, second_ref):
-    me = lax.axis_index("bz")
-    turned = (me == 0) & (lax.axis_index("by") == 1)
-    words = jnp.where((me == slab) != turned, first_ref[...], second_ref[...])
-    return jnp.where(has_near(me == 0), words, 0)
-
-
-def column_lines(read_words, inside, lines_ref, rows):
+def near_words(slab, place_ref, first_ref, second_ref):
+    own = (place_ref[ME] == slab) != (place_ref[TURNED] == 1)
+    words = jnp.where(own, first_ref[...], second_ref[...])
+    return jnp.where(place_ref[HAS_NEAR] == 1, words, 0)
+
+
+def column_lines(me, read_words, inside, lines_ref, rows):
     layers, cols = inside.shape
-    front = lax.axis_index("bz") == 0
-    start = lax.axis_index("bz") * (rows // 2)
+    front = me == 0
+    start = me * (rows // 2)
     middle = LANES // 2
     lane_at = lax.broadcasted_iota(jnp.int32, (8, LANES), 1)
     row_at = start + 2 * lax.broadcasted_iota(jnp.int32, (8, LANES), 0)
@@ -234,20 +247,21 @@
 
 
 def side_kernel(
-    rows, columns_ref, bulk_ref, second_ref, first_ref, part_ref, ends_ref, other_ref
+    rows, place_ref, columns_ref, bulk_ref, second_ref, first_ref, part_ref, ends_ref, other_ref
 ):
     layers, _ = columns_ref.shape
-    front = lax.axis_index("bz") == 0
+    me = place_ref[ME]
+    front = me == 0
     lane_at = lax.broadcasted_iota(jnp.int32, (layers, LANES), 1)
 
     def read_words(z, part, tile):
         return bulk_ref[2 * z + part, :, tile * LANES : (tile + 1) * LANES]
 
-    column_lines(read_words, bulk_ref[2 * layers], other_ref, rows)
+    column_lines(me, read_words, bulk_ref[2 * layers], other_ref, rows)
     for slab in range(2):
         mine = front if slab == 0 else jnp.logical_not(front)
         columns = jnp.where(mine, columns_ref[...], other_ref[...])
-        near = near_words(slab, first_ref, second_ref)
+        near = near_words(slab, place_ref, first_ref, second_ref)
         cols = near.shape[1]
         columns = jnp.where(lane_at == rows, near[:, 0:1], columns)
         ends_ref[slab] = jnp.where(
@@ -255,20 +269,23 @@
         )
 
 
-def has_near(front):
-    me_y = lax.axis_index("by")
-    return jnp.where(front, me_y > 0, me_y + 1 < lax.axis_size("by"))
-
-
 def fill_weights(weights_ref):
     cols = weights_ref.shape[0]
-    row = lax.broadcasted_iota(jnp.int32, (cols, 2 * cols), 0)
-    at = lax.broadcasted_iota(jnp.int32, (cols, 2 * cols), 1)
-    centre = lax.shift_right_logical(at, 1)
-    beside = centre - 1 + 2 * (at & 1)
-    weights_ref[...] = jnp.where(row == centre, 3.0, jnp.where(row == beside, 1.0, 0.0)).astype(
-        jnp.bfloat16
-    )
+    row = lax.broadcasted_iota(jnp.int32, (LANES, 2 * LANES), 0)
+    at = lax.broadcasted_iota(jnp.int32, (LANES, 2 * LANES), 1)
+    place = at - 2 * row
+    block = jnp.where(
+        (place == 0) | (place == 1), 3.0, jnp.where((place == -1) | (place == 2), 1.0, 0.0)
+    ).astype(jnp.bfloat16)
+    after = jnp.where((row == LANES - 1) & (at == 0), 1.0, 0.0).astype(jnp.bfloat16)
+    before = jnp.where((row == 0) & (at == 2 * LANES - 1), 1.0, 0.0).astype(jnp.bfloat16)
+    count = cols // LANES
+    for i in range(count):
+        for j in range(count):
+            piece = block if i == j else after if j == i + 1 else before if j == i - 1 else None
+            if piece is None:
+                piece = jnp.zeros((LANES, 2 * LANES), jnp.bfloat16)
+            weights_ref[i * LANES : (i + 1) * LANES, 2 * j * LANES : 2 * (j + 1) * LANES] = piece
 
 
 def classify_rows(read_cells, tables, cells_ref, layers, tiles):
@@ -287,10 +304,12 @@
     return value.astype(jnp.bfloat16).astype(jnp.float32)
 
 
-def cells_kernel(dense_ref, index_ref, inside_ref, tables_ref, cells_ref, weights_ref, mix_ref, lines_ref):
+def cells_kernel(
+    place_ref, dense_ref, index_ref, inside_ref, tables_ref, cells_ref, weights_ref, mix_ref, lines_ref
+):
     layers, tiles, rows = dense_ref.shape[0], dense_ref.shape[1], dense_ref.shape[2] - 8
     half = rows // 2
-    start = lax.axis_index("bz") * half
+    start = place_ref[ME] * half
     fill_weights(weights_ref)
     fill_rows(mix_ref)
 
@@ -299,7 +318,7 @@
         return dense_ref[z, tile, at, :], index_ref[z, tile, at, :]
 
     classify_rows(read_cells, read_tables(tables_ref), cells_ref, layers, tiles)
-    column_lines(lambda *at: pack_words(*read_cells(*at)), inside_ref[...], lines_ref, rows)
+    column_lines(place_ref[ME], lambda *at: pack_words(*read_cells(*at)), inside_ref[...], lines_ref, rows)
 
 
 def along_columns(cells, weights_ref, store):
@@ -308,10 +327,10 @@
         store(tile, result[:, tile * LANES : (tile + 1) * LANES])
 
 
-def own_kernel(cells_ref, weights_ref, along_ref):
+def own_kernel(place_ref, cells_ref, weights_ref, along_ref):
     size = cells_ref.shape[0]
     pad = 64
-    mine = pl.multiple_of(pad + lax.axis_index("bz") * size, pad)
+    mine = pl.multiple_of(pad + place_ref[ME] * size, pad)
 
     def store(tile, block):
         along_ref[tile, 0:pad, :] = jnp.zeros((pad, LANES), jnp.float32)
@@ -321,12 +340,14 @@
     along_columns(cells_ref[...], weights_ref, store)
 
 
-def other_kernel(bulk_ref, tables_ref, weights_ref, ends_ref, own_ref, along_ref, cells_ref):
+def other_kernel(
+    place_ref, bulk_ref, tables_ref, weights_ref, ends_ref, own_ref, along_ref, cells_ref
+):
     layers = (bulk_ref.shape[0] - 1) // 2
     cols = bulk_ref.shape[2]
     size = cells_ref.shape[0]
     pad = 64
-    theirs = pl.multiple_of(pad + (1 - lax.axis_index("bz")) * size, pad)
+    theirs = pl.multiple_of(pad + (1 - place_ref[ME]) * size, pad)
 
     def read_cells(z, part, tile):
         return unpack_words(bulk_ref[2 * z + part, :, tile * LANES : (tile + 1) * LANES])
@@ -457,10 +478,10 @@
 
 
 def own_tiles_kernel(
-    tables_ref, weights_ref, inside_ref, mix_ref, along_ref, part_ref, cells_ref, packed_ref, lines_ref
+    place_ref, tables_ref, weights_ref, inside_ref, mix_ref, along_ref, part_ref, cells_ref, packed_ref, lines_ref
 ):
     layers, cols = inside_ref.shape
-    me = lax.axis_index("bz")
+    me = place_ref[ME]
     front = me == 0
     inside = inside_ref[...]
     edge_cells(jnp.zeros_like(inside), inside, read_tables(tables_ref), cells_ref, front, 0)
@@ -504,18 +525,18 @@
 
 
 def tiles_kernel(
-    flip_ref, tables_ref, weights_ref, bulk_ref, inside_ref, second_ref, first_ref, ends_ref, mix_ref,
+    place_ref, tables_ref, weights_ref, bulk_ref, inside_ref, second_ref, first_ref, ends_ref, mix_ref,
     part_ref, along_ref, image_ref, mine_ref, cells_ref, packed_ref, lines_ref, edge_ref, between_ref,
 ):
     layers, cols = inside_ref.shape
     depth = 2 * layers
     tiles = 2 * cols // LANES
-    me = lax.axis_index("bz")
+    me = place_ref[ME]
     front = me == 0
     tables = read_tables(tables_ref)
     for slab in range(2):
         inside = jnp.where(me == slab, inside_ref[...], bulk_ref[2 * layers])
-        near = near_words(slab, first_ref, second_ref)
+        near = near_words(slab, place_ref, first_ref, second_ref)
         edge_cells(near, inside, tables, cells_ref, front, slab * layers * 8)
         values = cell_values(*unpack_words(ends_ref[slab]), tables, float(depth))
         for channel in range(4):
@@ -588,14 +609,14 @@
                 values[3] = jnp.where(sub_at == 7, jnp.where(front, values[3], line), values[3])
                 part.append(values)
             mine = joined(front, part, between)
-            image = joined((me ^ flip_ref[0]) == 0, mine, other[index])
+            image = joined((me ^ place_ref[FLIP]) == 0, mine, other[index])
             for c in range(4):
                 for i in range(4):
                     image_ref[tile, c, pl.ds(i, 8, stride=4), :] = image[c][i]
 
 
 def edge_kernel(
-    flip_ref, tables_ref, beside_ref, across_ref, mine_ref, image_ref,
+    place_ref, tables_ref, beside_ref, across_ref, mine_ref, image_ref,
     out_ref, samples_ref, final_ref, turned_ref, fixed_ref, sems,
 ):
     rows = out_ref.shape[1]
@@ -604,10 +625,9 @@
     layers = beside_ref.shape[1]
     tiles = 2 * cols // LANES
     middle = LANES // 2
-    front = lax.axis_index("bz") == 0
-    start = pl.multiple_of(lax.axis_index("bz") * half, half)
-    me_x = lax.axis_index("bx")
-    even_x = lax.rem(me_x, 2) == 0
+    front = place_ref[ME] == 0
+    start = pl.multiple_of(place_ref[ME] * half, half)
+    even_x = place_ref[ODD_X] == 0
     tables = read_tables(tables_ref)
 
     def to_out(tile, source):
@@ -626,8 +646,8 @@
     for slab in range(2):
         right = jnp.where(even_x, beside_ref[slab], across_ref[slab])
         left = jnp.where(even_x, across_ref[slab], beside_ref[slab])
-        right = jnp.where(me_x + 1 < lax.axis_size("bx"), right, 0)
-        left = jnp.where(me_x > 0, left, 0)
+        right = jnp.where(place_ref[HAS_RIGHT] == 1, right, 0)
+        left = jnp.where(place_ref[HAS_LEFT] == 1, left, 0)
         words = pltpu.roll(jnp.where(lane_at < middle, right, left), middle, 1)
         halo = cell_values(*unpack_words(words), tables, float(2 * layers))
         for channel in range(4):
@@ -681,7 +701,7 @@
         )
         for slab in range(2)
     ]
-    in_order = flip_ref[0] == 0
+    in_order = place_ref[FLIP] == 0
     image = over(
         *[
             [
@@ -726,7 +746,7 @@
             return pl.pallas_call(
                 kernel,
                 out_shape=out_shape,
-                in_specs=in_specs or [VMEM] * len(operands),
+                in_specs=in_specs or [SMEM] + [VMEM] * (len(operands) - 1),
                 out_specs=out_specs
                 or ((VMEM,) * len(out_shape) if isinstance(out_shape, tuple) else VMEM),
                 scratch_shapes=scratch_shapes,
@@ -743,16 +763,15 @@
 
     blocks = (layers, cols // LANES, rows + 8, LANES)
     row = pltpu.VMEM((layers, cols), i32)
-    smem = pl.BlockSpec(memory_space=pltpu.SMEM)
     inputs = [
         pltpu.with_memory_space_constraint(x, pltpu.HBM)
         for x in (slab_rank, density, bin_index, tf_colour, tf_extinction)
     ]
-    flip, first, second, bulk, inside, dense, index, tables = call(
+    place, first, second, bulk, inside, dense, index, tables = call(
         stage_kernel,
         "stage_block",
         (
-            pltpu.SMEM((1,), i32),
+            pltpu.SMEM((7,), i32),
             row,
             row,
             pltpu.VMEM((2 * layers + 1, 8, cols), i32),
@@ -762,17 +781,17 @@
             pltpu.VMEM((8, 8, LANES), f32),
         ),
         1.2,
-        in_specs=[smem] + [VMEM] * 4,
-        out_specs=(smem,) + (VMEM,) * 7,
+        in_specs=[SMEM] + [VMEM] * 4,
+        out_specs=(SMEM,) + (VMEM,) * 7,
     )(*inputs)
-    def place(z, y, x):
+    def device(z, y, x):
         return (z * count_y + y) * count_x + x
 
     def lanes(route):
-        return [(place(*source, x), place(*target, x)) for source, target in route for x in range(count_x)]
+        return [(device(*source, x), device(*target, x)) for source, target in route for x in range(count_x)]
 
     def twins(z, y):
-        return both([(place(z, y, x), place(z, y, x + 1)) for x in range(0, count_x, 2)])
+        return both([(device(z, y, x), device(z, y, x + 1)) for x in range(0, count_x, 2)])
 
     last = count_y - 1
     ring = [((1, 0), (0, 1)), ((0, last), (1, last))]
@@ -797,9 +816,9 @@
             pltpu.VMEM((layers, LANES), i32),
         ),
         0.5,
-    )(dense, index, inside, tables)
+    )(place, dense, index, inside, tables)
     whole = pltpu.VMEM((tiles, 2 * size + 3 * 4 * half, LANES), f32)
-    along = call(own_kernel, "own_slab", whole, 0.4)(cells, weights)
+    along = call(own_kernel, "own_slab", whole, 0.4)(place, cells, weights)
     edges = pltpu.VMEM((cols // LANES, 16 * layers + 8, LANES), f32)
     packed = pltpu.VMEM((tiles, 32 * layers, LANES), bf16)
     lines = pltpu.VMEM((tiles, 16 * layers + 8, LANES), f32)
@@ -809,20 +828,20 @@
         pltpu.VMEM((tiles, 16, 8, LANES), f32),
         0.1,
         [edges, packed, lines],
-    )(tables, weights, inside, mix, along)
+    )(place, tables, weights, inside, mix, along)
     ends = call(
         functools.partial(side_kernel, rows),
         "side_columns",
         pltpu.VMEM((2, layers, LANES), i32),
         0.1,
         [pltpu.VMEM((layers, LANES), i32)],
-    )(columns, bulk, second, first, part)
+    )(place, columns, bulk, second, first, part)
     pairs = [(x, x + 1) for x in range(0, count_x, 2)]
     cross = [(x, (x + 1) % count_x) for x in range(1, count_x, 2)]
     beside = lax.ppermute(ends, "bx", both(pairs))
     across = lax.ppermute(ends, "bx", both(cross))
-    along = call(other_kernel, "other_slab", whole, 0.8, [pltpu.VMEM((size, cols), bf16)], aliases={4: 0})(
-        bulk, tables, weights, ends, along
+    along = call(other_kernel, "other_slab", whole, 0.8, [pltpu.VMEM((size, cols), bf16)], aliases={5: 0})(
+        place, bulk, tables, weights, ends, along
     )
     image, mine = call(
         tiles_kernel,
@@ -836,8 +855,7 @@
             pltpu.VMEM((tiles, 16 * layers + 16, LANES), f32),
             pltpu.VMEM((tiles, 16, LANES), f32),
         ],
-        [smem] + [VMEM] * 10,
-    )(flip, tables, weights, bulk, inside, second, first, ends, mix, part, along)
+    )(place, tables, weights, bulk, inside, second, first, ends, mix, part, along)
     return call(
         edge_kernel,
         "edge_columns",
@@ -850,9 +868,8 @@
             pltpu.VMEM((2, 4, rows + 8, LANES), f32),
             pltpu.SemaphoreType.DMA((tiles,)),
         ],
-        [smem] + [VMEM] * 5,
-        pl.BlockSpec(memory_space=pltpu.HBM),
-    )(flip, tables, beside, across, mine, image)
+        out_specs=pl.BlockSpec(memory_space=pltpu.HBM),
+    )(place, tables, beside, across, mine, image)
 
 
 def on_device(density, bin_index, tf_colour, tf_extinction, slab_rank):

time: 13.8 us -> 13.8 us (level)
  no operation moved by 1% of the time
where the time goes in v24:
time: 13.8 us; the launch traced here: 13.7 us
  Pallas kernels  6.71 us (49%)
  starting transfers between devices  6.53 us (47%)
  waiting for transfers between devices  0.39 us (3%)
    pallas_call x8, Pallas kernels, run(): pl.pallas_call(kernel, out_shape=out_shape, in_specs=in_specs or [SMEM] +...  6.71 us
    ppermute x1, starting transfers between devices, two_slab_device(): bulk = lax.ppermute(bulk, 'bz', [(0, 1), (1, 0)])  3 us
    ppermute x1, starting transfers between devices, two_slab_device(): second = lax.ppermute(second, axes, diagonal)  1.58 us
    ppermute x1, starting transfers between devices, two_slab_device(): across = lax.ppermute(ends, 'bx', both(cross))  1.35 us
    ppermute x1, starting transfers between devices, two_slab_device(): beside = lax.ppermute(ends, 'bx', both(pairs))  0.6 us
    ppermute x1, waiting for transfers between devices, two_slab_device(): second = lax.ppermute(second, axes, diagonal)  0.38 us
  transfers between devices with their start and end apart: 5, of which 1 were waited for; matrix products, arithmetic and copies ran while one was open for 0% of the time, Pallas kernels for 30%

profile of v24, /device:TPU:0, one launch (start us, length us, event | category | flops | bytes accessed | tf_op | source)
XLA Modules:
  0.0 13.7 jit_solution(13250869076143445500)
XLA Ops:
  0.0 1.2 %stage_block.1 = (s32[7]{0:T(128)S(4)}, s32[8,256]{1,0:T(8,128)S(1)}, s32[8,256]{1,0:T(8,128)S(1)}, s32[17,8,256]{2,1,0:T(8,128)S(1)}, s32[8,256]{1,0:T(8,128)S(...) custom-call(s32[2]{0:T(128)} %rank_ref.1, f32[8,32,256]{2,1,0:T(8,128)} %density_ref.1, ...), custom_call_target="tpu_custom_call" | custom-call | flops 1200000000 | bytes 4320000 | tf_op jit(solution)/shard_map/stage_block/pallas_call | solution.py:746
  1.2 3.0 %collective-permute-start = (s32[17,8,256]{2,1,0:T(8,128)S(1)}, s32[17,8,256]{2,1,0:T(8,128)S(1)}, u32[]{:S(2)}, u32[]{:S(2)}) collective-permute-start(s32[17,8,256]{2,1,0:T(8,128)S(1)} %get-tuple-element.25), channel_id=1, source_target_pairs={{0,16},{16,0},{1,17},{17,1},{2,18},{18,2},{3,19},{19,3},{4,20},{20... | collective-permute-start | bytes 417800 | tf_op jit(solution)/shard_map/ppermute | solution.py:805
  4.2 1.6 %collective-permute-start.1 = (s32[8,256]{1,0:T(8,128)S(1)}, s32[8,256]{1,0:T(8,128)S(1)}, u32[]{:S(2)}, u32[]{:S(2)}) collective-permute-start(s32[8,256]{1,0:T(8,128)S(1)} %get-tuple-element.26), channel_id=1, source_target_pairs={{16,0},{17,1},{18,2},{19,3},{0,4},{1,5},{2,6},{3,7},{4,16},{5,17},... | collective-permute-start | bytes 24584 | tf_op jit(solution)/shard_map/ppermute | solution.py:807
  5.7 0.0 collective-permute-start.2
  5.7 0.5 %own_cells.1 = (bf16[512,256]{1,0:T(8,128)(2,1)S(1)}, bf16[256,512]{1,0:T(8,128)(2,1)S(1)}, bf16[128,80]{1,0:T(8,128)(2,1)S(1)}, s32[8,128]{1,0:T(8,128)S(1)}) custom-call(s32[7]{0:T(128)S(4)} %get-tuple-element.19.place_ref, f32[8,2,40,128]{3,2,1,0:T(8,128)S(1)} %get-tuple-element.21.dense_ref, s32[8,2,40,128]{3,2,1,0:T(8,128)S(1)} %get-tuple-element.22.index_ref, ...), custom_call_target="tpu_custom_call" | custom-call | flops 500000000 | bytes 1800000 | tf_op jit(solution)/shard_map/own_cells/pallas_call | solution.py:746
  6.3 0.4 %own_slab.1.along_ref.own_ref = f32[4,1216,128]{2,1,0:T(8,128)S(1)} custom-call(s32[7]{0:T(128)S(4)} %get-tuple-element.19.place_ref, bf16[512,256]{1,0:T(8,128)(2,1)S(1)} %get-tuple-element.30.cells_ref, bf16[256,512]{1,0:T(8,128)(2,1)S(1)} %get-tuple-element.28.weights_ref), custom_call_target="tpu_custom_call" | custom-call | flops 400000000 | bytes 1440000 | tf_op jit(solution)/shard_map/own_slab/pallas_call | solution.py:746
  6.6 1.0 %own_tiles.1.part_ref = f32[4,16,8,128]{3,2,1,0:T(8,128)S(1)} custom-call(s32[7]{0:T(128)S(4)} %get-tuple-element.19.place_ref, f32[8,8,128]{2,1,0:T(8,128)S(1)} %get-tuple-element.20.tables_ref, bf16[256,512]{1,0:T(8,128)(2,1)S(1)} %get-tuple-element.28.weights_ref, s32[8,256]{1,0:T(8,128)S(1)} %get-tuple-element.23.inside_ref, ...), custom_call_target="tpu_custom_call" | custom-call | flops 100000000 | bytes 360000 | tf_op jit(solution)/shard_map/own_tiles/pallas_call | solution.py:746
  7.6 0.4 %collective-permute-done.1.second_ref = s32[8,256]{1,0:T(8,128)S(1)} collective-permute-done((s32[8,256]{1,0:T(8,128)S(1)}, s32[8,256]{1,0:T(8,128)S(1)}, u32[]{:S(2)}, u32[]{:S(2)}) %collective-permute-start.1) | collective-permute-done | bytes 8224 | tf_op jit(solution)/shard_map/ppermute | solution.py:807
  8.0 0.0 collective-permute-done.2.first_ref
  8.0 0.0 collective-permute-done.bulk_ref
  8.0 0.1 side_columns.1.ends_ref
  8.1 1.3 %collective-permute-start.4 = (s32[2,8,128]{2,1,0:T(8,128)S(1)}, s32[2,8,128]{2,1,0:T(8,128)S(1)}, u32[]{:S(2)}, u32[]{:S(2)}) collective-permute-start(s32[2,8,128]{2,1,0:T(8,128)S(1)} %side_columns.1.ends_ref), channel_id=1, source_target_pairs={{1,2},{3,0},{2,1},{0,3},{5,6},{7,4},{6,5},{4,7},{9,10},{11,8},{10,... | collective-permute-start | bytes 24584 | tf_op jit(solution)/shard_map/ppermute | solution.py:842
  9.5 0.6 %collective-permute-start.3 = (s32[2,8,128]{2,1,0:T(8,128)S(1)}, s32[2,8,128]{2,1,0:T(8,128)S(1)}, u32[]{:S(2)}, u32[]{:S(2)}) collective-permute-start(s32[2,8,128]{2,1,0:T(8,128)S(1)} %side_columns.1.ends_ref), channel_id=1, source_target_pairs={{0,1},{2,3},{1,0},{3,2},{4,5},{6,7},{5,4},{7,6},{8,9},{10,11},{9,8... | collective-permute-start | bytes 24584 | tf_op jit(solution)/shard_map/ppermute | solution.py:841
  10.1 0.8 %other_slab.1.along_ref = f32[4,1216,128]{2,1,0:T(8,128)S(1)} custom-call(s32[7]{0:T(128)S(4)} %get-tuple-element.19.place_ref, s32[17,8,256]{2,1,0:T(8,128)S(1)} %collective-permute-done.bulk_ref, f32[8,8,128]{2,1,0:T(8,128)S(1)} %get-tuple-element.20.tables_ref, ...), custom_call_target="tpu_custom_call", output_to_operand_aliasing={{}: (5, {})} | custom-call | flops 800000000 | bytes 2880000 | tf_op jit(solution)/shard_map/other_slab/pallas_call | solution.py:746
  10.9 1.4 %render_tiles.1 = (f32[4,4,40,128]{3,2,1,0:T(8,128)S(1)}, f32[8,8,128]{2,1,0:T(8,128)S(1)}) custom-call(s32[7]{0:T(128)S(4)} %get-tuple-element.19.place_ref, f32[8,8,128]{2,1,0:T(8,128)S(1)} %get-tuple-element.20.tables_ref, bf16[256,512]{1,0:T(8,128)(2,1)S(1)} %get-tuple-element.28.weights_ref, s32[17,8,256]{2,1,0:T(8,128)S(1)} %collective-permute-done.bulk_ref, ...), custom_call_target="tpu_custom_call" | custom-call | flops 2000000000 | bytes 7200000 | tf_op jit(solution)/shard_map/render_tiles/pallas_call | solution.py:746
  12.3 0.0 collective-permute-done.4.across_ref
  12.3 0.0 collective-permute-done.3.beside_ref
  12.3 1.3 %edge_columns.1 = f32[4,32,512]{2,1,0:T(8,128)} custom-call(s32[7]{0:T(128)S(4)} %get-tuple-element.19.place_ref, f32[8,8,128]{2,1,0:T(8,128)S(1)} %get-tuple-element.20.tables_ref, s32[2,8,128]{2,1,0:T(8,128)S(1)} %collective-permute-done.3.beside_ref, s32[2,8,128]{2,1,0:T(8,128)S(1)} %collective-permute-done.4.across_ref, ...), custom_call_target="tpu_custom_call" | custom-call | flops 1000000000 | bytes 3600000 | tf_op jit(solution)/shard_map/edge_columns/pallas_call | solution.py:746
Async XLA Ops:
  1.2 6.9 %collective-permute-start = (s32[17,8,256]{2,1,0:T(8,128)S(1)}, s32[17,8,256]{2,1,0:T(8,128)S(1)}, u32[]{:S(2)}, u32[]{:S(2)}) collective-permute-start(s32[17,8,256]{2,1,0:T(8,128)S(1)} %get-tuple-element.25), channel_id=1, source_target_pairs={{0,16},{16,0},{1,17},{17,1},{2,18},{18,2},{3,19},{19,3},{4,20},{20... | collective-permute-start | bytes 417800 | tf_op jit(solution)/shard_map/ppermute | solution.py:805
  4.2 3.8 %collective-permute-start.1 = (s32[8,256]{1,0:T(8,128)S(1)}, s32[8,256]{1,0:T(8,128)S(1)}, u32[]{:S(2)}, u32[]{:S(2)}) collective-permute-start(s32[8,256]{1,0:T(8,128)S(1)} %get-tuple-element.26), channel_id=1, source_target_pairs={{16,0},{17,1},{18,2},{19,3},{0,4},{1,5},{2,6},{3,7},{4,16},{5,17},... | collective-permute-start | bytes 24584 | tf_op jit(solution)/shard_map/ppermute | solution.py:807
  5.7 2.3 %collective-permute-start.2 = (s32[8,256]{1,0:T(8,128)S(1)}, s32[8,256]{1,0:T(8,128)S(1)}, u32[]{:S(2)}, u32[]{:S(2)}) collective-permute-start(s32[8,256]{1,0:T(8,128)S(1)} %get-tuple-element.27), channel_id=1, source_target_pairs={{16,4},{17,5},{18,6},{19,7},{12,28},{13,29},{14,30},{15,31},{4,8},... | collective-permute-start | bytes 24584 | tf_op jit(solution)/shard_map/ppermute | solution.py:806
  8.1 4.2 %collective-permute-start.4 = (s32[2,8,128]{2,1,0:T(8,128)S(1)}, s32[2,8,128]{2,1,0:T(8,128)S(1)}, u32[]{:S(2)}, u32[]{:S(2)}) collective-permute-start(s32[2,8,128]{2,1,0:T(8,128)S(1)} %side_columns.1.ends_ref), channel_id=1, source_target_pairs={{1,2},{3,0},{2,1},{0,3},{5,6},{7,4},{6,5},{4,7},{9,10},{11,8},{10,... | collective-permute-start | bytes 24584 | tf_op jit(solution)/shard_map/ppermute | solution.py:842
  9.5 2.8 %collective-permute-start.3 = (s32[2,8,128]{2,1,0:T(8,128)S(1)}, s32[2,8,128]{2,1,0:T(8,128)S(1)}, u32[]{:S(2)}, u32[]{:S(2)}) collective-permute-start(s32[2,8,128]{2,1,0:T(8,128)S(1)} %side_columns.1.ends_ref), channel_id=1, source_target_pairs={{0,1},{2,3},{1,0},{3,2},{4,5},{6,7},{5,4},{7,6},{8,9},{10,11},{9,8... | collective-permute-start | bytes 24584 | tf_op jit(solution)/shard_map/ppermute | solution.py:841

commit v25 on v24

--- a/solution.py
+++ b/solution.py
@@ -617,7 +617,7 @@
 
 def edge_kernel(
     place_ref, tables_ref, beside_ref, across_ref, mine_ref, image_ref,
-    out_ref, samples_ref, final_ref, turned_ref, fixed_ref, sems,
+    out_ref, final_ref, turned_ref, fixed_ref, sems,
 ):
     rows = out_ref.shape[1]
     cols = out_ref.shape[2] // 2
@@ -643,6 +643,7 @@
     layer_at = lax.broadcasted_iota(jnp.int32, (layers, LANES), 0)
     first_lane = (lane_at & (middle - 1)) == 0
     along = [[], []]
+    samples = {}
     for slab in range(2):
         right = jnp.where(even_x, beside_ref[slab], across_ref[slab])
         left = jnp.where(even_x, across_ref[slab], beside_ref[slab])
@@ -668,49 +669,35 @@
                 near = pltpu.roll(mixed, LANES - rows, 1)
                 above = jnp.where(first_lane, jnp.where(front, near, above), above)
                 below = pltpu.roll(mixed, LANES - 1, 1)
-                for odd, value in enumerate((above + centre, centre + below)):
-                    at = (parity * 2 + odd) * 4 + channel
-                    samples_ref[slab, at, 0:layers, :] = value
-
-    def over_some(slab, layers_at):
-        zero = jnp.zeros((8, LANES), jnp.float32)
-        image = [[zero] * 4 for _ in range(2)]
-        for z in layers_at:
-            for parity in range(2):
-                clear = [1.0 - image[odd][3] for odd in range(2)]
-                image = [
-                    [
-                        image[odd][channel]
-                        + clear[odd]
-                        * samples_ref[slab, (parity * 2 + odd) * 4 + channel, pl.ds(z, 8, stride=0), :]
-                        for channel in range(4)
-                    ]
-                    for odd in range(2)
-                ]
-        return image
+                samples[slab, parity, 0, channel] = above + centre
+                samples[slab, parity, 1, channel] = centre + below
 
     def over(in_front, behind):
-        return [
-            [top + (1.0 - tops[3]) * low for top, low in zip(tops, lows)]
-            for tops, lows in zip(in_front, behind)
-        ]
-
-    slabs = [
+        clear = 1.0 - in_front[3]
+        return [top + clear * low for top, low in zip(in_front, behind)]
+
+    slabs = []
+    for slab in range(2):
+        slabs.append([])
+        for odd in range(2):
+            image = over(
+                *[[samples[slab, parity, odd, channel] for channel in range(4)] for parity in range(2)]
+            )
+            step = 1
+            while step < layers:
+                image = over(image, [pltpu.roll(value, layers - step, 0) for value in image])
+                step *= 2
+            slabs[slab].append(image)
+    in_order = place_ref[FLIP] == 0
+    image = [
         over(
-            over_some(slab, range(layers // 2)), over_some(slab, range(layers // 2, layers))
-        )
-        for slab in range(2)
+            *[
+                [jnp.where(in_order, x, y) for x, y in zip(slabs[at][odd], slabs[1 - at][odd])]
+                for at in range(2)
+            ]
+        )
+        for odd in range(2)
     ]
-    in_order = place_ref[FLIP] == 0
-    image = over(
-        *[
-            [
-                [jnp.where(in_order, x, y) for x, y in zip(xs, ys)]
-                for xs, ys in zip(slabs[at], slabs[1 - at])
-            ]
-            for at in range(2)
-        ]
-    )
     for odd in range(2):
         for channel in range(4):
             at = odd * 4 + channel
@@ -862,7 +849,6 @@
         jax.ShapeDtypeStruct((4, rows, 2 * cols), f32),
         1.0,
         [
-            pltpu.VMEM((2, 16, 2 * layers, LANES), f32),
             pltpu.VMEM((8, LANES), f32),
             pltpu.VMEM((LANES, LANES), f32),
             pltpu.VMEM((2, 4, rows + 8, LANES), f32),

time: 13.8 us -> 13.8 us (level)
  no operation moved by 1% of the time
where the time goes in v25:
time: 13.8 us; the launch traced here: 13.6 us
  Pallas kernels  6.64 us (48%)
  starting transfers between devices  6.53 us (47%)
  waiting for transfers between devices  0.39 us (3%)
    pallas_call x8, Pallas kernels, run(): pl.pallas_call(kernel, out_shape=out_shape, in_specs=in_specs or [SMEM] +...  6.64 us
    ppermute x1, starting transfers between devices, two_slab_device(): bulk = lax.ppermute(bulk, 'bz', [(0, 1), (1, 0)])  3 us
    ppermute x1, starting transfers between devices, two_slab_device(): second = lax.ppermute(second, axes, diagonal)  1.58 us
    ppermute x1, starting transfers between devices, two_slab_device(): across = lax.ppermute(ends, 'bx', both(cross))  1.35 us
    ppermute x1, starting transfers between devices, two_slab_device(): beside = lax.ppermute(ends, 'bx', both(pairs))  0.6 us
    ppermute x1, waiting for transfers between devices, two_slab_device(): second = lax.ppermute(second, axes, diagonal)  0.38 us
  transfers between devices with their start and end apart: 5, of which 1 were waited for; matrix products, arithmetic and copies ran while one was open for 0% of the time, Pallas kernels for 30%

profile of v25, /device:TPU:0, one launch (start us, length us, event | category | flops | bytes accessed | tf_op | source)
XLA Modules:
  0.0 13.6 jit_solution(4771502830694184941)
XLA Ops:
  0.0 1.2 %stage_block.1 = (s32[7]{0:T(128)S(4)}, s32[8,256]{1,0:T(8,128)S(1)}, s32[8,256]{1,0:T(8,128)S(1)}, s32[17,8,256]{2,1,0:T(8,128)S(1)}, s32[8,256]{1,0:T(8,128)S(...) custom-call(s32[2]{0:T(128)} %rank_ref.1, f32[8,32,256]{2,1,0:T(8,128)} %density_ref.1, ...), custom_call_target="tpu_custom_call" | custom-call | flops 1200000000 | bytes 4320000 | tf_op jit(solution)/shard_map/stage_block/pallas_call | solution.py:733
  1.2 3.0 %collective-permute-start = (s32[17,8,256]{2,1,0:T(8,128)S(1)}, s32[17,8,256]{2,1,0:T(8,128)S(1)}, u32[]{:S(2)}, u32[]{:S(2)}) collective-permute-start(s32[17,8,256]{2,1,0:T(8,128)S(1)} %get-tuple-element.25), channel_id=1, source_target_pairs={{0,16},{16,0},{1,17},{17,1},{2,18},{18,2},{3,19},{19,3},{4,20},{20... | collective-permute-start | bytes 417800 | tf_op jit(solution)/shard_map/ppermute | solution.py:792
  4.2 1.6 %collective-permute-start.1 = (s32[8,256]{1,0:T(8,128)S(1)}, s32[8,256]{1,0:T(8,128)S(1)}, u32[]{:S(2)}, u32[]{:S(2)}) collective-permute-start(s32[8,256]{1,0:T(8,128)S(1)} %get-tuple-element.26), channel_id=1, source_target_pairs={{16,0},{17,1},{18,2},{19,3},{0,4},{1,5},{2,6},{3,7},{4,16},{5,17},... | collective-permute-start | bytes 24584 | tf_op jit(solution)/shard_map/ppermute | solution.py:794
  5.7 0.0 collective-permute-start.2
  5.7 0.5 %own_cells.1 = (bf16[512,256]{1,0:T(8,128)(2,1)S(1)}, bf16[256,512]{1,0:T(8,128)(2,1)S(1)}, bf16[128,80]{1,0:T(8,128)(2,1)S(1)}, s32[8,128]{1,0:T(8,128)S(1)}) custom-call(s32[7]{0:T(128)S(4)} %get-tuple-element.19.place_ref, f32[8,2,40,128]{3,2,1,0:T(8,128)S(1)} %get-tuple-element.21.dense_ref, s32[8,2,40,128]{3,2,1,0:T(8,128)S(1)} %get-tuple-element.22.index_ref, ...), custom_call_target="tpu_custom_call" | custom-call | flops 500000000 | bytes 1800000 | tf_op jit(solution)/shard_map/own_cells/pallas_call | solution.py:733
  6.3 0.4 %own_slab.1.along_ref.own_ref = f32[4,1216,128]{2,1,0:T(8,128)S(1)} custom-call(s32[7]{0:T(128)S(4)} %get-tuple-element.19.place_ref, bf16[512,256]{1,0:T(8,128)(2,1)S(1)} %get-tuple-element.30.cells_ref, bf16[256,512]{1,0:T(8,128)(2,1)S(1)} %get-tuple-element.28.weights_ref), custom_call_target="tpu_custom_call" | custom-call | flops 400000000 | bytes 1440000 | tf_op jit(solution)/shard_map/own_slab/pallas_call | solution.py:733
  6.6 1.0 %own_tiles.1.part_ref = f32[4,16,8,128]{3,2,1,0:T(8,128)S(1)} custom-call(s32[7]{0:T(128)S(4)} %get-tuple-element.19.place_ref, f32[8,8,128]{2,1,0:T(8,128)S(1)} %get-tuple-element.20.tables_ref, bf16[256,512]{1,0:T(8,128)(2,1)S(1)} %get-tuple-element.28.weights_ref, s32[8,256]{1,0:T(8,128)S(1)} %get-tuple-element.23.inside_ref, ...), custom_call_target="tpu_custom_call" | custom-call | flops 100000000 | bytes 360000 | tf_op jit(solution)/shard_map/own_tiles/pallas_call | solution.py:733
  7.6 0.4 %collective-permute-done.1.second_ref = s32[8,256]{1,0:T(8,128)S(1)} collective-permute-done((s32[8,256]{1,0:T(8,128)S(1)}, s32[8,256]{1,0:T(8,128)S(1)}, u32[]{:S(2)}, u32[]{:S(2)}) %collective-permute-start.1) | collective-permute-done | bytes 8224 | tf_op jit(solution)/shard_map/ppermute | solution.py:794
  8.0 0.0 collective-permute-done.2.first_ref
  8.0 0.0 collective-permute-done.bulk_ref
  8.0 0.1 side_columns.1.ends_ref
  8.1 1.3 %collective-permute-start.4 = (s32[2,8,128]{2,1,0:T(8,128)S(1)}, s32[2,8,128]{2,1,0:T(8,128)S(1)}, u32[]{:S(2)}, u32[]{:S(2)}) collective-permute-start(s32[2,8,128]{2,1,0:T(8,128)S(1)} %side_columns.1.ends_ref), channel_id=1, source_target_pairs={{1,2},{3,0},{2,1},{0,3},{5,6},{7,4},{6,5},{4,7},{9,10},{11,8},{10,... | collective-permute-start | bytes 24584 | tf_op jit(solution)/shard_map/ppermute | solution.py:829
  9.5 0.6 %collective-permute-start.3 = (s32[2,8,128]{2,1,0:T(8,128)S(1)}, s32[2,8,128]{2,1,0:T(8,128)S(1)}, u32[]{:S(2)}, u32[]{:S(2)}) collective-permute-start(s32[2,8,128]{2,1,0:T(8,128)S(1)} %side_columns.1.ends_ref), channel_id=1, source_target_pairs={{0,1},{2,3},{1,0},{3,2},{4,5},{6,7},{5,4},{7,6},{8,9},{10,11},{9,8... | collective-permute-start | bytes 24584 | tf_op jit(solution)/shard_map/ppermute | solution.py:828
  10.1 0.8 %other_slab.1.along_ref = f32[4,1216,128]{2,1,0:T(8,128)S(1)} custom-call(s32[7]{0:T(128)S(4)} %get-tuple-element.19.place_ref, s32[17,8,256]{2,1,0:T(8,128)S(1)} %collective-permute-done.bulk_ref, f32[8,8,128]{2,1,0:T(8,128)S(1)} %get-tuple-element.20.tables_ref, ...), custom_call_target="tpu_custom_call", output_to_operand_aliasing={{}: (5, {})} | custom-call | flops 800000000 | bytes 2880000 | tf_op jit(solution)/shard_map/other_slab/pallas_call | solution.py:733
  10.9 1.4 %render_tiles.1 = (f32[4,4,40,128]{3,2,1,0:T(8,128)S(1)}, f32[8,8,128]{2,1,0:T(8,128)S(1)}) custom-call(s32[7]{0:T(128)S(4)} %get-tuple-element.19.place_ref, f32[8,8,128]{2,1,0:T(8,128)S(1)} %get-tuple-element.20.tables_ref, bf16[256,512]{1,0:T(8,128)(2,1)S(1)} %get-tuple-element.28.weights_ref, s32[17,8,256]{2,1,0:T(8,128)S(1)} %collective-permute-done.bulk_ref, ...), custom_call_target="tpu_custom_call" | custom-call | flops 2000000000 | bytes 7200000 | tf_op jit(solution)/shard_map/render_tiles/pallas_call | solution.py:733
  12.3 0.0 collective-permute-done.4.across_ref
  12.3 0.0 collective-permute-done.3.beside_ref
  12.3 1.3 %edge_columns.1 = f32[4,32,512]{2,1,0:T(8,128)} custom-call(s32[7]{0:T(128)S(4)} %get-tuple-element.19.place_ref, f32[8,8,128]{2,1,0:T(8,128)S(1)} %get-tuple-element.20.tables_ref, s32[2,8,128]{2,1,0:T(8,128)S(1)} %collective-permute-done.3.beside_ref, s32[2,8,128]{2,1,0:T(8,128)S(1)} %collective-permute-done.4.across_ref, ...), custom_call_target="tpu_custom_call" | custom-call | flops 1000000000 | bytes 3600000 | tf_op jit(solution)/shard_map/edge_columns/pallas_call | solution.py:733
Async XLA Ops:
  1.2 6.9 %collective-permute-start = (s32[17,8,256]{2,1,0:T(8,128)S(1)}, s32[17,8,256]{2,1,0:T(8,128)S(1)}, u32[]{:S(2)}, u32[]{:S(2)}) collective-permute-start(s32[17,8,256]{2,1,0:T(8,128)S(1)} %get-tuple-element.25), channel_id=1, source_target_pairs={{0,16},{16,0},{1,17},{17,1},{2,18},{18,2},{3,19},{19,3},{4,20},{20... | collective-permute-start | bytes 417800 | tf_op jit(solution)/shard_map/ppermute | solution.py:792
  4.2 3.8 %collective-permute-start.1 = (s32[8,256]{1,0:T(8,128)S(1)}, s32[8,256]{1,0:T(8,128)S(1)}, u32[]{:S(2)}, u32[]{:S(2)}) collective-permute-start(s32[8,256]{1,0:T(8,128)S(1)} %get-tuple-element.26), channel_id=1, source_target_pairs={{16,0},{17,1},{18,2},{19,3},{0,4},{1,5},{2,6},{3,7},{4,16},{5,17},... | collective-permute-start | bytes 24584 | tf_op jit(solution)/shard_map/ppermute | solution.py:794
  5.7 2.3 %collective-permute-start.2 = (s32[8,256]{1,0:T(8,128)S(1)}, s32[8,256]{1,0:T(8,128)S(1)}, u32[]{:S(2)}, u32[]{:S(2)}) collective-permute-start(s32[8,256]{1,0:T(8,128)S(1)} %get-tuple-element.27), channel_id=1, source_target_pairs={{16,4},{17,5},{18,6},{19,7},{12,28},{13,29},{14,30},{15,31},{4,8},... | collective-permute-start | bytes 24584 | tf_op jit(solution)/shard_map/ppermute | solution.py:793
  8.1 4.2 %collective-permute-start.4 = (s32[2,8,128]{2,1,0:T(8,128)S(1)}, s32[2,8,128]{2,1,0:T(8,128)S(1)}, u32[]{:S(2)}, u32[]{:S(2)}) collective-permute-start(s32[2,8,128]{2,1,0:T(8,128)S(1)} %side_columns.1.ends_ref), channel_id=1, source_target_pairs={{1,2},{3,0},{2,1},{0,3},{5,6},{7,4},{6,5},{4,7},{9,10},{11,8},{10,... | collective-permute-start | bytes 24584 | tf_op jit(solution)/shard_map/ppermute | solution.py:829
  9.5 2.8 %collective-permute-start.3 = (s32[2,8,128]{2,1,0:T(8,128)S(1)}, s32[2,8,128]{2,1,0:T(8,128)S(1)}, u32[]{:S(2)}, u32[]{:S(2)}) collective-permute-start(s32[2,8,128]{2,1,0:T(8,128)S(1)} %side_columns.1.ends_ref), channel_id=1, source_target_pairs={{0,1},{2,3},{1,0},{3,2},{4,5},{6,7},{5,4},{7,6},{8,9},{10,11},{9,8... | collective-permute-start | bytes 24584 | tf_op jit(solution)/shard_map/ppermute | solution.py:828

commit v26 on v25

--- a/solution.py
+++ b/solution.py
@@ -247,7 +247,7 @@
 
 
 def side_kernel(
-    rows, place_ref, columns_ref, bulk_ref, second_ref, first_ref, part_ref, ends_ref, other_ref
+    rows, place_ref, columns_ref, bulk_ref, second_ref, first_ref, part_ref, cells_ref, ends_ref, other_ref
 ):
     layers, _ = columns_ref.shape
     me = place_ref[ME]
@@ -340,23 +340,14 @@
     along_columns(cells_ref[...], weights_ref, store)
 
 
-def other_kernel(
-    place_ref, bulk_ref, tables_ref, weights_ref, ends_ref, own_ref, along_ref, cells_ref
-):
+def other_cells_kernel(bulk_ref, tables_ref, cells_ref):
     layers = (bulk_ref.shape[0] - 1) // 2
     cols = bulk_ref.shape[2]
-    size = cells_ref.shape[0]
-    pad = 64
-    theirs = pl.multiple_of(pad + (1 - place_ref[ME]) * size, pad)
 
     def read_cells(z, part, tile):
         return unpack_words(bulk_ref[2 * z + part, :, tile * LANES : (tile + 1) * LANES])
 
-    def store(tile, block):
-        along_ref[tile, pl.ds(theirs, size), :] = block
-
     classify_rows(read_cells, read_tables(tables_ref), cells_ref, layers, cols // LANES)
-    along_columns(cells_ref[...], weights_ref, store)
 
 
 def edge_cells(near, inside, tables, cells_ref, front, base):
@@ -526,7 +517,7 @@
 
 def tiles_kernel(
     place_ref, tables_ref, weights_ref, bulk_ref, inside_ref, second_ref, first_ref, ends_ref, mix_ref,
-    part_ref, along_ref, image_ref, mine_ref, cells_ref, packed_ref, lines_ref, edge_ref, between_ref,
+    part_ref, other_ref, own_ref, image_ref, mine_ref, along_ref, cells_ref, packed_ref, lines_ref, edge_ref, between_ref,
 ):
     layers, cols = inside_ref.shape
     depth = 2 * layers
@@ -534,6 +525,13 @@
     me = place_ref[ME]
     front = me == 0
     tables = read_tables(tables_ref)
+    size = other_ref.shape[0]
+    theirs = pl.multiple_of(64 + (1 - me) * size, 64)
+
+    def store(tile, block):
+        along_ref[tile, pl.ds(theirs, size), :] = block
+
+    along_columns(other_ref[...], weights_ref, store)
     for slab in range(2):
         inside = jnp.where(me == slab, inside_ref[...], bulk_ref[2 * layers])
         near = near_words(slab, place_ref, first_ref, second_ref)
@@ -816,24 +814,24 @@
         0.1,
         [edges, packed, lines],
     )(place, tables, weights, inside, mix, along)
+    other_cells = call(
+        other_cells_kernel, "other_cells", pltpu.VMEM((size, cols), bf16), 0.1, in_specs=[VMEM] * 2
+    )(bulk, tables)
     ends = call(
         functools.partial(side_kernel, rows),
         "side_columns",
         pltpu.VMEM((2, layers, LANES), i32),
         0.1,
         [pltpu.VMEM((layers, LANES), i32)],
-    )(place, columns, bulk, second, first, part)
+    )(place, columns, bulk, second, first, part, other_cells)
     pairs = [(x, x + 1) for x in range(0, count_x, 2)]
     cross = [(x, (x + 1) % count_x) for x in range(1, count_x, 2)]
     beside = lax.ppermute(ends, "bx", both(pairs))
     across = lax.ppermute(ends, "bx", both(cross))
-    along = call(other_kernel, "other_slab", whole, 0.8, [pltpu.VMEM((size, cols), bf16)], aliases={5: 0})(
-        place, bulk, tables, weights, ends, along
-    )
-    image, mine = call(
+    image, mine, _ = call(
         tiles_kernel,
         "render_tiles",
-        (pltpu.VMEM((tiles, 4, rows + 8, LANES), f32), pltpu.VMEM((8, layers, LANES), f32)),
+        (pltpu.VMEM((tiles, 4, rows + 8, LANES), f32), pltpu.VMEM((8, layers, LANES), f32), whole),
         2.0,
         [
             edges,
@@ -842,7 +840,8 @@
             pltpu.VMEM((tiles, 16 * layers + 16, LANES), f32),
             pltpu.VMEM((tiles, 16, LANES), f32),
         ],
-    )(place, tables, weights, bulk, inside, second, first, ends, mix, part, along)
+        aliases={11: 2},
+    )(place, tables, weights, bulk, inside, second, first, ends, mix, part, other_cells, along)
     return call(
         edge_kernel,
         "edge_columns",

time: 13.8 us -> 13.3 us (0.964)
  Pallas kernels: 6.64 us -> 6.3 us
    ppermute x1, waiting for transfers between devices: 0.38 us -> 0.01 us  [two_slab_device(): second = lax.ppermute(second, axes, diagonal)]
    pallas_call x8, Pallas kernels: 6.64 us -> 6.3 us  [run(): pl.pallas_call(kernel, out_shape=out_shape, in_specs=in_specs or [SMEM] +...]
    ppermute x1, waiting for transfers between devices: 0.01 us -> 0.29 us  [two_slab_device(): bulk = lax.ppermute(bulk, 'bz', [(0, 1), (1, 0)])]
  transfers between devices with their start and end apart: 5 -> 5, of which waited for: 1 -> 1; matrix products, arithmetic and copies ran while one was open for 0% -> 0% of each run, Pallas kernels for 30% -> 28%
where the time goes in v26:
time: 13.3 us; the launch traced here: 13.2 us
  starting transfers between devices  6.53 us (49%)
  Pallas kernels  6.3 us (47%)
  waiting for transfers between devices  0.3 us (2%)
    pallas_call x8, Pallas kernels, run(): pl.pallas_call(kernel, out_shape=out_shape, in_specs=in_specs or [SMEM] +...  6.3 us
    ppermute x1, starting transfers between devices, two_slab_device(): bulk = lax.ppermute(bulk, 'bz', [(0, 1), (1, 0)])  3 us
    ppermute x1, starting transfers between devices, two_slab_device(): second = lax.ppermute(second, axes, diagonal)  1.58 us
    ppermute x1, starting transfers between devices, two_slab_device(): across = lax.ppermute(ends, 'bx', both(cross))  1.43 us
    ppermute x1, starting transfers between devices, two_slab_device(): beside = lax.ppermute(ends, 'bx', both(pairs))  0.53 us
    ppermute x1, waiting for transfers between devices, two_slab_device(): bulk = lax.ppermute(bulk, 'bz', [(0, 1), (1, 0)])  0.29 us
  transfers between devices with their start and end apart: 5, of which 1 were waited for; matrix products, arithmetic and copies ran while one was open for 0% of the time, Pallas kernels for 28%

profile of v26, /device:TPU:0, one launch (start us, length us, event | category | flops | bytes accessed | tf_op | source)
XLA Modules:
  0.0 13.2 jit_solution(3034813483417730301)
XLA Ops:
  0.0 1.2 %stage_block.1 = (s32[7]{0:T(128)S(4)}, s32[8,256]{1,0:T(8,128)S(1)}, s32[8,256]{1,0:T(8,128)S(1)}, s32[17,8,256]{2,1,0:T(8,128)S(1)}, s32[8,256]{1,0:T(8,128)S(...) custom-call(s32[2]{0:T(128)} %rank_ref.1, f32[8,32,256]{2,1,0:T(8,128)} %density_ref.1, ...), custom_call_target="tpu_custom_call" | custom-call | flops 1200000000 | bytes 4320000 | tf_op jit(solution)/shard_map/stage_block/pallas_call | solution.py:731
  1.2 3.0 %collective-permute-start = (s32[17,8,256]{2,1,0:T(8,128)S(1)}, s32[17,8,256]{2,1,0:T(8,128)S(1)}, u32[]{:S(2)}, u32[]{:S(2)}) collective-permute-start(s32[17,8,256]{2,1,0:T(8,128)S(1)} %get-tuple-element.25), channel_id=1, source_target_pairs={{0,16},{16,0},{1,17},{17,1},{2,18},{18,2},{3,19},{19,3},{4,20},{20... | collective-permute-start | bytes 417800 | tf_op jit(solution)/shard_map/ppermute | solution.py:790
  4.2 1.6 %collective-permute-start.1 = (s32[8,256]{1,0:T(8,128)S(1)}, s32[8,256]{1,0:T(8,128)S(1)}, u32[]{:S(2)}, u32[]{:S(2)}) collective-permute-start(s32[8,256]{1,0:T(8,128)S(1)} %get-tuple-element.26), channel_id=1, source_target_pairs={{16,0},{17,1},{18,2},{19,3},{0,4},{1,5},{2,6},{3,7},{4,16},{5,17},... | collective-permute-start | bytes 24584 | tf_op jit(solution)/shard_map/ppermute | solution.py:792
  5.7 0.0 collective-permute-start.2
  5.7 0.5 %own_cells.1 = (bf16[512,256]{1,0:T(8,128)(2,1)S(1)}, bf16[256,512]{1,0:T(8,128)(2,1)S(1)}, bf16[128,80]{1,0:T(8,128)(2,1)S(1)}, s32[8,128]{1,0:T(8,128)S(1)}) custom-call(s32[7]{0:T(128)S(4)} %get-tuple-element.19.place_ref, f32[8,2,40,128]{3,2,1,0:T(8,128)S(1)} %get-tuple-element.21.dense_ref, s32[8,2,40,128]{3,2,1,0:T(8,128)S(1)} %get-tuple-element.22.index_ref, ...), custom_call_target="tpu_custom_call" | custom-call | flops 500000000 | bytes 1800000 | tf_op jit(solution)/shard_map/own_cells/pallas_call | solution.py:731
  6.3 0.4 %own_slab.1.along_ref.own_ref = f32[4,1216,128]{2,1,0:T(8,128)S(1)} custom-call(s32[7]{0:T(128)S(4)} %get-tuple-element.19.place_ref, bf16[512,256]{1,0:T(8,128)(2,1)S(1)} %get-tuple-element.30.cells_ref, bf16[256,512]{1,0:T(8,128)(2,1)S(1)} %get-tuple-element.28.weights_ref), custom_call_target="tpu_custom_call" | custom-call | flops 400000000 | bytes 1440000 | tf_op jit(solution)/shard_map/own_slab/pallas_call | solution.py:731
  6.6 1.0 %own_tiles.1.part_ref = f32[4,16,8,128]{3,2,1,0:T(8,128)S(1)} custom-call(s32[7]{0:T(128)S(4)} %get-tuple-element.19.place_ref, f32[8,8,128]{2,1,0:T(8,128)S(1)} %get-tuple-element.20.tables_ref, bf16[256,512]{1,0:T(8,128)(2,1)S(1)} %get-tuple-element.28.weights_ref, s32[8,256]{1,0:T(8,128)S(1)} %get-tuple-element.23.inside_ref, ...), custom_call_target="tpu_custom_call" | custom-call | flops 100000000 | bytes 360000 | tf_op jit(solution)/shard_map/own_tiles/pallas_call | solution.py:731
  7.6 0.3 %collective-permute-done.bulk_ref = s32[17,8,256]{2,1,0:T(8,128)S(1)} collective-permute-done((s32[17,8,256]{2,1,0:T(8,128)S(1)}, s32[17,8,256]{2,1,0:T(8,128)S(1)}, u32[]{:S(2)}, u32[]{:S(2)}) %collective-permute-start) | collective-permute-done | bytes 139296 | tf_op jit(solution)/shard_map/ppermute | solution.py:790
  7.9 0.4 %other_cells.1.cells_ref.other_ref = bf16[512,256]{1,0:T(8,128)(2,1)S(1)} custom-call(s32[17,8,256]{2,1,0:T(8,128)S(1)} %collective-permute-done.bulk_ref, f32[8,8,128]{2,1,0:T(8,128)S(1)} %get-tuple-element.20.tables_ref), custom_call_target="tpu_custom_call" | custom-call | flops 100000000 | bytes 360000 | tf_op jit(solution)/shard_map/other_cells/pallas_call | solution.py:731
  8.4 0.0 collective-permute-done.1.second_ref
  8.4 0.0 collective-permute-done.2.first_ref
  8.4 0.1 side_columns.1.ends_ref
  8.5 1.4 %collective-permute-start.4 = (s32[2,8,128]{2,1,0:T(8,128)S(1)}, s32[2,8,128]{2,1,0:T(8,128)S(1)}, u32[]{:S(2)}, u32[]{:S(2)}) collective-permute-start(s32[2,8,128]{2,1,0:T(8,128)S(1)} %side_columns.1.ends_ref), channel_id=1, source_target_pairs={{1,2},{3,0},{2,1},{0,3},{5,6},{7,4},{6,5},{4,7},{9,10},{11,8},{10,... | collective-permute-start | bytes 24584 | tf_op jit(solution)/shard_map/ppermute | solution.py:830
  9.9 0.5 %collective-permute-start.3 = (s32[2,8,128]{2,1,0:T(8,128)S(1)}, s32[2,8,128]{2,1,0:T(8,128)S(1)}, u32[]{:S(2)}, u32[]{:S(2)}) collective-permute-start(s32[2,8,128]{2,1,0:T(8,128)S(1)} %side_columns.1.ends_ref), channel_id=1, source_target_pairs={{0,1},{2,3},{1,0},{3,2},{4,5},{6,7},{5,4},{7,6},{8,9},{10,11},{9,8... | collective-permute-start | bytes 24584 | tf_op jit(solution)/shard_map/ppermute | solution.py:829
  10.5 1.4 %render_tiles.1 = (f32[4,4,40,128]{3,2,1,0:T(8,128)S(1)}, f32[8,8,128]{2,1,0:T(8,128)S(1)}, f32[4,1216,128]{2,1,0:T(8,128)S(1)}) custom-call(s32[7]{0:T(128)S(4)} %get-tuple-element.19.place_ref, f32[8,8,128]{2,1,0:T(8,128)S(1)} %get-tuple-element.20.tables_ref, ...), custom_call_target="tpu_custom_call", output_to_operand_aliasing={{2}: (11, {})} | custom-call | flops 2000000000 | bytes 7200000 | tf_op jit(solution)/shard_map/render_tiles/pallas_call | solution.py:731
  11.9 0.0 collective-permute-done.4.across_ref
  11.9 0.0 collective-permute-done.3.beside_ref
  11.9 1.3 %edge_columns.1 = f32[4,32,512]{2,1,0:T(8,128)} custom-call(s32[7]{0:T(128)S(4)} %get-tuple-element.19.place_ref, f32[8,8,128]{2,1,0:T(8,128)S(1)} %get-tuple-element.20.tables_ref, s32[2,8,128]{2,1,0:T(8,128)S(1)} %collective-permute-done.3.beside_ref, s32[2,8,128]{2,1,0:T(8,128)S(1)} %collective-permute-done.4.across_ref, ...), custom_call_target="tpu_custom_call" | custom-call | flops 1000000000 | bytes 3600000 | tf_op jit(solution)/shard_map/edge_columns/pallas_call | solution.py:731
Async XLA Ops:
  1.2 6.8 %collective-permute-start = (s32[17,8,256]{2,1,0:T(8,128)S(1)}, s32[17,8,256]{2,1,0:T(8,128)S(1)}, u32[]{:S(2)}, u32[]{:S(2)}) collective-permute-start(s32[17,8,256]{2,1,0:T(8,128)S(1)} %get-tuple-element.25), channel_id=1, source_target_pairs={{0,16},{16,0},{1,17},{17,1},{2,18},{18,2},{3,19},{19,3},{4,20},{20... | collective-permute-start | bytes 417800 | tf_op jit(solution)/shard_map/ppermute | solution.py:790
  4.2 4.2 %collective-permute-start.1 = (s32[8,256]{1,0:T(8,128)S(1)}, s32[8,256]{1,0:T(8,128)S(1)}, u32[]{:S(2)}, u32[]{:S(2)}) collective-permute-start(s32[8,256]{1,0:T(8,128)S(1)} %get-tuple-element.26), channel_id=1, source_target_pairs={{16,0},{17,1},{18,2},{19,3},{0,4},{1,5},{2,6},{3,7},{4,16},{5,17},... | collective-permute-start | bytes 24584 | tf_op jit(solution)/shard_map/ppermute | solution.py:792
  5.7 2.6 %collective-permute-start.2 = (s32[8,256]{1,0:T(8,128)S(1)}, s32[8,256]{1,0:T(8,128)S(1)}, u32[]{:S(2)}, u32[]{:S(2)}) collective-permute-start(s32[8,256]{1,0:T(8,128)S(1)} %get-tuple-element.27), channel_id=1, source_target_pairs={{16,4},{17,5},{18,6},{19,7},{12,28},{13,29},{14,30},{15,31},{4,8},... | collective-permute-start | bytes 24584 | tf_op jit(solution)/shard_map/ppermute | solution.py:791
  8.5 3.4 %collective-permute-start.4 = (s32[2,8,128]{2,1,0:T(8,128)S(1)}, s32[2,8,128]{2,1,0:T(8,128)S(1)}, u32[]{:S(2)}, u32[]{:S(2)}) collective-permute-start(s32[2,8,128]{2,1,0:T(8,128)S(1)} %side_columns.1.ends_ref), channel_id=1, source_target_pairs={{1,2},{3,0},{2,1},{0,3},{5,6},{7,4},{6,5},{4,7},{9,10},{11,8},{10,... | collective-permute-start | bytes 24584 | tf_op jit(solution)/shard_map/ppermute | solution.py:830
  9.9 2.0 %collective-permute-start.3 = (s32[2,8,128]{2,1,0:T(8,128)S(1)}, s32[2,8,128]{2,1,0:T(8,128)S(1)}, u32[]{:S(2)}, u32[]{:S(2)}) collective-permute-start(s32[2,8,128]{2,1,0:T(8,128)S(1)} %side_columns.1.ends_ref), channel_id=1, source_target_pairs={{0,1},{2,3},{1,0},{3,2},{4,5},{6,7},{5,4},{7,6},{8,9},{10,11},{9,8... | collective-permute-start | bytes 24584 | tf_op jit(solution)/shard_map/ppermute | solution.py:829

commit v27 on v26

--- a/solution.py
+++ b/solution.py
@@ -247,7 +247,7 @@
 
 
 def side_kernel(
-    rows, place_ref, columns_ref, bulk_ref, second_ref, first_ref, part_ref, cells_ref, ends_ref, other_ref
+    rows, place_ref, columns_ref, bulk_ref, second_ref, first_ref, part_ref, ends_ref, other_ref
 ):
     layers, _ = columns_ref.shape
     me = place_ref[ME]
@@ -304,50 +304,10 @@
     return value.astype(jnp.bfloat16).astype(jnp.float32)
 
 
-def cells_kernel(
-    place_ref, dense_ref, index_ref, inside_ref, tables_ref, cells_ref, weights_ref, mix_ref, lines_ref
-):
-    layers, tiles, rows = dense_ref.shape[0], dense_ref.shape[1], dense_ref.shape[2] - 8
-    half = rows // 2
-    start = place_ref[ME] * half
-    fill_weights(weights_ref)
-    fill_rows(mix_ref)
-
-    def read_cells(z, part, tile):
-        at = pl.ds(start + part, half // 2, stride=2)
-        return dense_ref[z, tile, at, :], index_ref[z, tile, at, :]
-
-    classify_rows(read_cells, read_tables(tables_ref), cells_ref, layers, tiles)
-    column_lines(place_ref[ME], lambda *at: pack_words(*read_cells(*at)), inside_ref[...], lines_ref, rows)
-
-
 def along_columns(cells, weights_ref, store):
     result = rounded(jnp.dot(cells, weights_ref[...], preferred_element_type=jnp.float32))
     for tile in range(result.shape[1] // LANES):
         store(tile, result[:, tile * LANES : (tile + 1) * LANES])
-
-
-def own_kernel(place_ref, cells_ref, weights_ref, along_ref):
-    size = cells_ref.shape[0]
-    pad = 64
-    mine = pl.multiple_of(pad + place_ref[ME] * size, pad)
-
-    def store(tile, block):
-        along_ref[tile, 0:pad, :] = jnp.zeros((pad, LANES), jnp.float32)
-        along_ref[tile, pad + 2 * size : 2 * pad + 2 * size, :] = jnp.zeros((pad, LANES), jnp.float32)
-        along_ref[tile, pl.ds(mine, size), :] = block
-
-    along_columns(cells_ref[...], weights_ref, store)
-
-
-def other_cells_kernel(bulk_ref, tables_ref, cells_ref):
-    layers = (bulk_ref.shape[0] - 1) // 2
-    cols = bulk_ref.shape[2]
-
-    def read_cells(z, part, tile):
-        return unpack_words(bulk_ref[2 * z + part, :, tile * LANES : (tile + 1) * LANES])
-
-    classify_rows(read_cells, read_tables(tables_ref), cells_ref, layers, cols // LANES)
 
 
 def edge_cells(near, inside, tables, cells_ref, front, base):
@@ -468,11 +428,34 @@
     return [[top[c][i] + clear[i] * low[c][i] for i in range(4)] for c in range(4)]
 
 
-def own_tiles_kernel(
-    place_ref, tables_ref, weights_ref, inside_ref, mix_ref, along_ref, part_ref, cells_ref, packed_ref, lines_ref
+def own_kernel(
+    place_ref, dense_ref, index_ref, inside_ref, tables_ref,
+    weights_ref, mix_ref, columns_ref, along_ref, part_ref,
+    own_ref, cells_ref, packed_ref, lines_ref,
 ):
     layers, cols = inside_ref.shape
     me = place_ref[ME]
+    rows = dense_ref.shape[2] - 8
+    half = rows // 2
+    size = own_ref.shape[0]
+    pad = 64
+    start = me * half
+    mine = pl.multiple_of(pad + me * size, pad)
+    fill_weights(weights_ref)
+    fill_rows(mix_ref)
+
+    def read_cells(z, part, tile):
+        at = pl.ds(start + part, half // 2, stride=2)
+        return dense_ref[z, tile, at, :], index_ref[z, tile, at, :]
+
+    def store(tile, block):
+        along_ref[tile, 0:pad, :] = jnp.zeros((pad, LANES), jnp.float32)
+        along_ref[tile, pad + 2 * size : 2 * pad + 2 * size, :] = jnp.zeros((pad, LANES), jnp.float32)
+        along_ref[tile, pl.ds(mine, size), :] = block
+
+    classify_rows(read_cells, read_tables(tables_ref), own_ref, layers, cols // LANES)
+    along_columns(own_ref[...], weights_ref, store)
+    column_lines(me, lambda *at: pack_words(*read_cells(*at)), inside_ref[...], columns_ref, rows)
     front = me == 0
     inside = inside_ref[...]
     edge_cells(jnp.zeros_like(inside), inside, read_tables(tables_ref), cells_ref, front, 0)
@@ -517,7 +500,7 @@
 
 def tiles_kernel(
     place_ref, tables_ref, weights_ref, bulk_ref, inside_ref, second_ref, first_ref, ends_ref, mix_ref,
-    part_ref, other_ref, own_ref, image_ref, mine_ref, along_ref, cells_ref, packed_ref, lines_ref, edge_ref, between_ref,
+    part_ref, own_ref, image_ref, mine_ref, along_ref, other_ref, cells_ref, packed_ref, lines_ref, edge_ref, between_ref,
 ):
     layers, cols = inside_ref.shape
     depth = 2 * layers
@@ -531,6 +514,10 @@
     def store(tile, block):
         along_ref[tile, pl.ds(theirs, size), :] = block
 
+    def read_cells(z, part, tile):
+        return unpack_words(bulk_ref[2 * z + part, :, tile * LANES : (tile + 1) * LANES])
+
+    classify_rows(read_cells, tables, other_ref, layers, cols // LANES)
     along_columns(other_ref[...], weights_ref, store)
     for slab in range(2):
         inside = jnp.where(me == slab, inside_ref[...], bulk_ref[2 * layers])
@@ -791,39 +778,30 @@
     first = lax.ppermute(first, axes, ring)
     second = lax.ppermute(second, axes, diagonal)
 
-    cells, weights, mix, columns = call(
-        cells_kernel,
-        "own_cells",
+    whole = pltpu.VMEM((tiles, 2 * size + 3 * 4 * half, LANES), f32)
+    edges = pltpu.VMEM((cols // LANES, 16 * layers + 8, LANES), f32)
+    packed = pltpu.VMEM((tiles, 32 * layers, LANES), bf16)
+    lines = pltpu.VMEM((tiles, 16 * layers + 8, LANES), f32)
+    weights, mix, columns, along, part = call(
+        own_kernel,
+        "own_slab",
         (
-            pltpu.VMEM((size, cols), bf16),
             pltpu.VMEM((cols, 2 * cols), bf16),
             pltpu.VMEM((128, 80), bf16),
             pltpu.VMEM((layers, LANES), i32),
+            whole,
+            pltpu.VMEM((tiles, 16, 8, LANES), f32),
         ),
-        0.5,
+        0.4,
+        [pltpu.VMEM((size, cols), bf16), edges, packed, lines],
     )(place, dense, index, inside, tables)
-    whole = pltpu.VMEM((tiles, 2 * size + 3 * 4 * half, LANES), f32)
-    along = call(own_kernel, "own_slab", whole, 0.4)(place, cells, weights)
-    edges = pltpu.VMEM((cols // LANES, 16 * layers + 8, LANES), f32)
-    packed = pltpu.VMEM((tiles, 32 * layers, LANES), bf16)
-    lines = pltpu.VMEM((tiles, 16 * layers + 8, LANES), f32)
-    part = call(
-        own_tiles_kernel,
-        "own_tiles",
-        pltpu.VMEM((tiles, 16, 8, LANES), f32),
-        0.1,
-        [edges, packed, lines],
-    )(place, tables, weights, inside, mix, along)
-    other_cells = call(
-        other_cells_kernel, "other_cells", pltpu.VMEM((size, cols), bf16), 0.1, in_specs=[VMEM] * 2
-    )(bulk, tables)
     ends = call(
         functools.partial(side_kernel, rows),
         "side_columns",
         pltpu.VMEM((2, layers, LANES), i32),
         0.1,
         [pltpu.VMEM((layers, LANES), i32)],
-    )(place, columns, bulk, second, first, part, other_cells)
+    )(place, columns, bulk, second, first, part)
     pairs = [(x, x + 1) for x in range(0, count_x, 2)]
     cross = [(x, (x + 1) % count_x) for x in range(1, count_x, 2)]
     beside = lax.ppermute(ends, "bx", both(pairs))
@@ -834,14 +812,15 @@
         (pltpu.VMEM((tiles, 4, rows + 8, LANES), f32), pltpu.VMEM((8, layers, LANES), f32), whole),
         2.0,
         [
+            pltpu.VMEM((size, cols), bf16),
             edges,
             packed,
             lines,
             pltpu.VMEM((tiles, 16 * layers + 16, LANES), f32),
             pltpu.VMEM((tiles, 16, LANES), f32),
         ],
-        aliases={11: 2},
-    )(place, tables, weights, bulk, inside, second, first, ends, mix, part, other_cells, along)
+        aliases={10: 2},
+    )(place, tables, weights, bulk, inside, second, first, ends, mix, part, along)
     return call(
         edge_kernel,
         "edge_columns",

time: 13.3 us -> 13.6 us (1.023)
  Pallas kernels: 6.3 us -> 6.58 us
    ppermute x1, waiting for transfers between devices: 0.01 us -> 0.33 us  [two_slab_device(): second = lax.ppermute(second, axes, diagonal)]
    ppermute x1, waiting for transfers between devices: 0.29 us -> 0.01 us  [two_slab_device(): bulk = lax.ppermute(bulk, 'bz', [(0, 1), (1, 0)])]
    pallas_call x8 -> x5, Pallas kernels: 6.3 us -> 6.58 us  [run(): pl.pallas_call(kernel, out_shape=out_shape, in_specs=in_specs or [SMEM] +...]
  transfers between devices with their start and end apart: 5 -> 5, of which waited for: 1 -> 1; matrix products, arithmetic and copies ran while one was open for 0% -> 0% of each run, Pallas kernels for 28% -> 30%
where the time goes in v27:
time: 13.6 us; the launch traced here: 13.5 us
  Pallas kernels  6.58 us (48%)
  starting transfers between devices  6.53 us (48%)
  waiting for transfers between devices  0.34 us (2%)
    pallas_call x5, Pallas kernels, run(): pl.pallas_call(kernel, out_shape=out_shape, in_specs=in_specs or [SMEM] +...  6.58 us
    ppermute x1, starting transfers between devices, two_slab_device(): bulk = lax.ppermute(bulk, 'bz', [(0, 1), (1, 0)])  3 us
    ppermute x1, starting transfers between devices, two_slab_device(): second = lax.ppermute(second, axes, diagonal)  1.58 us
    ppermute x1, starting transfers between devices, two_slab_device(): across = lax.ppermute(ends, 'bx', both(cross))  1.39 us
    ppermute x1, starting transfers between devices, two_slab_device(): beside = lax.ppermute(ends, 'bx', both(pairs))  0.56 us
    ppermute x1, waiting for transfers between devices, two_slab_device(): second = lax.ppermute(second, axes, diagonal)  0.33 us
  transfers between devices with their start and end apart: 5, of which 1 were waited for; matrix products, arithmetic and copies ran while one was open for 0% of the time, Pallas kernels for 30%

profile of v27, /device:TPU:0, one launch (start us, length us, event | category | flops | bytes accessed | tf_op | source)
XLA Modules:
  0.0 13.5 jit_solution(4152451134754953649)
XLA Ops:
  0.0 1.2 %stage_block.1 = (s32[7]{0:T(128)S(4)}, s32[8,256]{1,0:T(8,128)S(1)}, s32[8,256]{1,0:T(8,128)S(1)}, s32[17,8,256]{2,1,0:T(8,128)S(1)}, s32[8,256]{1,0:T(8,128)S(...) custom-call(s32[2]{0:T(128)} %rank_ref.1, f32[8,32,256]{2,1,0:T(8,128)} %density_ref.1, ...), custom_call_target="tpu_custom_call" | custom-call | flops 1200000000 | bytes 4320000 | tf_op jit(solution)/shard_map/stage_block/pallas_call | solution.py:718
  1.2 3.0 %collective-permute-start = (s32[17,8,256]{2,1,0:T(8,128)S(1)}, s32[17,8,256]{2,1,0:T(8,128)S(1)}, u32[]{:S(2)}, u32[]{:S(2)}) collective-permute-start(s32[17,8,256]{2,1,0:T(8,128)S(1)} %get-tuple-element.26), channel_id=1, source_target_pairs={{0,16},{16,0},{1,17},{17,1},{2,18},{18,2},{3,19},{19,3},{4,20},{20... | collective-permute-start | bytes 417800 | tf_op jit(solution)/shard_map/ppermute | solution.py:777
  4.2 1.6 %collective-permute-start.1 = (s32[8,256]{1,0:T(8,128)S(1)}, s32[8,256]{1,0:T(8,128)S(1)}, u32[]{:S(2)}, u32[]{:S(2)}) collective-permute-start(s32[8,256]{1,0:T(8,128)S(1)} %get-tuple-element.27), channel_id=1, source_target_pairs={{16,0},{17,1},{18,2},{19,3},{0,4},{1,5},{2,6},{3,7},{4,16},{5,17},... | collective-permute-start | bytes 24584 | tf_op jit(solution)/shard_map/ppermute | solution.py:779
  5.7 0.0 collective-permute-start.2
  5.7 1.9 %own_slab.1 = (bf16[256,512]{1,0:T(8,128)(2,1)S(1)}, bf16[128,80]{1,0:T(8,128)(2,1)S(1)}, s32[8,128]{1,0:T(8,128)S(1)}, f32[4,1216,128]{2,1,0:T(8,128)S(1)}, f32[4,16,8,128]{3,2,1,0:T(8,128)S(1)}) custom-call(s32[7]{0:T(128)S(4)} %get-tuple-element.20.place_ref, f32[8,2,40,128]{3,2,1,0:T(8,128)S(1)} %get-tuple-element.22.dense_ref, ...), custom_call_target="tpu_custom_call" | custom-call | flops 400000000 | bytes 1440000 | tf_op jit(solution)/shard_map/own_slab/pallas_call | solution.py:718
  7.7 0.3 %collective-permute-done.1.second_ref = s32[8,256]{1,0:T(8,128)S(1)} collective-permute-done((s32[8,256]{1,0:T(8,128)S(1)}, s32[8,256]{1,0:T(8,128)S(1)}, u32[]{:S(2)}, u32[]{:S(2)}) %collective-permute-start.1) | collective-permute-done | bytes 8224 | tf_op jit(solution)/shard_map/ppermute | solution.py:779
  8.0 0.0 collective-permute-done.2.first_ref
  8.0 0.0 collective-permute-done.bulk_ref
  8.0 0.1 side_columns.1.ends_ref
  8.1 1.4 %collective-permute-start.4 = (s32[2,8,128]{2,1,0:T(8,128)S(1)}, s32[2,8,128]{2,1,0:T(8,128)S(1)}, u32[]{:S(2)}, u32[]{:S(2)}) collective-permute-start(s32[2,8,128]{2,1,0:T(8,128)S(1)} %side_columns.1.ends_ref), channel_id=1, source_target_pairs={{1,2},{3,0},{2,1},{0,3},{5,6},{7,4},{6,5},{4,7},{9,10},{11,8},{10,... | collective-permute-start | bytes 24584 | tf_op jit(solution)/shard_map/ppermute | solution.py:808
  9.5 0.6 %collective-permute-start.3 = (s32[2,8,128]{2,1,0:T(8,128)S(1)}, s32[2,8,128]{2,1,0:T(8,128)S(1)}, u32[]{:S(2)}, u32[]{:S(2)}) collective-permute-start(s32[2,8,128]{2,1,0:T(8,128)S(1)} %side_columns.1.ends_ref), channel_id=1, source_target_pairs={{0,1},{2,3},{1,0},{3,2},{4,5},{6,7},{5,4},{7,6},{8,9},{10,11},{9,8... | collective-permute-start | bytes 24584 | tf_op jit(solution)/shard_map/ppermute | solution.py:807
  10.1 2.1 %render_tiles.1 = (f32[4,4,40,128]{3,2,1,0:T(8,128)S(1)}, f32[8,8,128]{2,1,0:T(8,128)S(1)}, f32[4,1216,128]{2,1,0:T(8,128)S(1)}) custom-call(s32[7]{0:T(128)S(4)} %get-tuple-element.20.place_ref, f32[8,8,128]{2,1,0:T(8,128)S(1)} %get-tuple-element.21.tables_ref, ...), custom_call_target="tpu_custom_call", output_to_operand_aliasing={{2}: (10, {})} | custom-call | flops 2000000000 | bytes 7200000 | tf_op jit(solution)/shard_map/render_tiles/pallas_call | solution.py:718
  12.2 0.0 collective-permute-done.4.across_ref
  12.2 0.0 collective-permute-done.3.beside_ref
  12.2 1.3 %edge_columns.1 = f32[4,32,512]{2,1,0:T(8,128)} custom-call(s32[7]{0:T(128)S(4)} %get-tuple-element.20.place_ref, f32[8,8,128]{2,1,0:T(8,128)S(1)} %get-tuple-element.21.tables_ref, s32[2,8,128]{2,1,0:T(8,128)S(1)} %collective-permute-done.3.beside_ref, s32[2,8,128]{2,1,0:T(8,128)S(1)} %collective-permute-done.4.across_ref, ...), custom_call_target="tpu_custom_call" | custom-call | flops 1000000000 | bytes 3600000 | tf_op jit(solution)/shard_map/edge_columns/pallas_call | solution.py:718
Async XLA Ops:
  1.2 6.9 %collective-permute-start = (s32[17,8,256]{2,1,0:T(8,128)S(1)}, s32[17,8,256]{2,1,0:T(8,128)S(1)}, u32[]{:S(2)}, u32[]{:S(2)}) collective-permute-start(s32[17,8,256]{2,1,0:T(8,128)S(1)} %get-tuple-element.26), channel_id=1, source_target_pairs={{0,16},{16,0},{1,17},{17,1},{2,18},{18,2},{3,19},{19,3},{4,20},{20... | collective-permute-start | bytes 417800 | tf_op jit(solution)/shard_map/ppermute | solution.py:777
  4.2 3.8 %collective-permute-start.1 = (s32[8,256]{1,0:T(8,128)S(1)}, s32[8,256]{1,0:T(8,128)S(1)}, u32[]{:S(2)}, u32[]{:S(2)}) collective-permute-start(s32[8,256]{1,0:T(8,128)S(1)} %get-tuple-element.27), channel_id=1, source_target_pairs={{16,0},{17,1},{18,2},{19,3},{0,4},{1,5},{2,6},{3,7},{4,16},{5,17},... | collective-permute-start | bytes 24584 | tf_op jit(solution)/shard_map/ppermute | solution.py:779
  5.7 2.3 %collective-permute-start.2 = (s32[8,256]{1,0:T(8,128)S(1)}, s32[8,256]{1,0:T(8,128)S(1)}, u32[]{:S(2)}, u32[]{:S(2)}) collective-permute-start(s32[8,256]{1,0:T(8,128)S(1)} %get-tuple-element.28), channel_id=1, source_target_pairs={{16,4},{17,5},{18,6},{19,7},{12,28},{13,29},{14,30},{15,31},{4,8},... | collective-permute-start | bytes 24584 | tf_op jit(solution)/shard_map/ppermute | solution.py:778
  8.1 4.1 %collective-permute-start.4 = (s32[2,8,128]{2,1,0:T(8,128)S(1)}, s32[2,8,128]{2,1,0:T(8,128)S(1)}, u32[]{:S(2)}, u32[]{:S(2)}) collective-permute-start(s32[2,8,128]{2,1,0:T(8,128)S(1)} %side_columns.1.ends_ref), channel_id=1, source_target_pairs={{1,2},{3,0},{2,1},{0,3},{5,6},{7,4},{6,5},{4,7},{9,10},{11,8},{10,... | collective-permute-start | bytes 24584 | tf_op jit(solution)/shard_map/ppermute | solution.py:808
  9.5 2.7 %collective-permute-start.3 = (s32[2,8,128]{2,1,0:T(8,128)S(1)}, s32[2,8,128]{2,1,0:T(8,128)S(1)}, u32[]{:S(2)}, u32[]{:S(2)}) collective-permute-start(s32[2,8,128]{2,1,0:T(8,128)S(1)} %side_columns.1.ends_ref), channel_id=1, source_target_pairs={{0,1},{2,3},{1,0},{3,2},{4,5},{6,7},{5,4},{7,6},{8,9},{10,11},{9,8... | collective-permute-start | bytes 24584 | tf_op jit(solution)/shard_map/ppermute | solution.py:807

commit v28 on v26

--- a/solution.py
+++ b/solution.py
@@ -515,6 +515,20 @@
     rows_ref[...] = jnp.where(same, value, 0.0).astype(jnp.bfloat16)
 
 
+def over(in_front, behind):
+    clear = 1.0 - in_front[3]
+    return [top + clear * low for top, low in zip(in_front, behind)]
+
+
+def through_layers(samples, layers):
+    image = over(*samples)
+    step = 1
+    while step < layers:
+        image = over(image, [pltpu.roll(value, layers - step, 0) for value in image])
+        step *= 2
+    return image
+
+
 def tiles_kernel(
     place_ref, tables_ref, weights_ref, bulk_ref, inside_ref, second_ref, first_ref, ends_ref, mix_ref,
     part_ref, other_ref, own_ref, image_ref, mine_ref, along_ref, cells_ref, packed_ref, lines_ref, edge_ref, between_ref,
@@ -551,31 +565,34 @@
         )
         edge_ref[tile, 0:8] = empty
         edge_ref[tile, 8 : 8 * depth + 8] = now
-        edge_ref[tile, 8 * depth + 8 :] = empty
+        edge_ref[tile, 8 * depth + 8 : 8 * depth + 16] = empty
 
     row = jnp.where(front, 0, 15)
+    line = jnp.where(front, 0, 4)
     first_layer = me * layers
+    layer_at = lax.broadcasted_iota(jnp.int32, (layers, LANES), 0)
     replaced = []
     for tile in range(tiles):
-        inner, outer = [], []
-        for z in range(layers + 2):
-            at = (first_layer + z) * 64 + row
-            inner.append(along_ref[tile, pl.ds(at, 4, stride=16), :])
-            both = edge_ref[tile, pl.ds(pl.multiple_of((first_layer + z) * 8, 8), 8), :]
-            outer.append(jnp.where(front, both[0:4], both[4:8]))
-        image = jnp.zeros((4, LANES), jnp.float32)
-        for z in range(layers):
+        samples = [[], []]
+        for channel in range(4):
+            inner, outer = [], []
+            for z in range(3):
+                at = (first_layer + z) * 64 + channel * 16 + row
+                inner.append(along_ref[tile, pl.ds(at, layers, stride=64), :])
+                at = (first_layer + z) * 8 + channel + line
+                outer.append(edge_ref[tile, pl.ds(at, layers, stride=8), :])
             for parity in range(2):
-                beside = z + 2 * parity
-                sample = rounded(outer[beside] + 3.0 * outer[z + 1]) + 3.0 * rounded(
-                    inner[beside] + 3.0 * inner[z + 1]
+                sample = rounded(outer[2 * parity] + 3.0 * outer[1]) + 3.0 * rounded(
+                    inner[2 * parity] + 3.0 * inner[1]
                 )
-                if (z, parity) == (0, 0):
-                    sample = jnp.where(front, sample, 0.0)
-                if (z, parity) == (layers - 1, 1):
-                    sample = jnp.where(front, 0.0, sample)
-                image = image + (1.0 - image[3:4]) * sample
-        replaced.append(image)
+                if parity == 0:
+                    kept = jnp.where(front, sample, 0.0)
+                    sample = jnp.where(layer_at == 0, kept, sample)
+                else:
+                    kept = jnp.where(front, 0.0, sample)
+                    sample = jnp.where(layer_at == layers - 1, kept, sample)
+                samples[parity].append(sample)
+        replaced.append(through_layers(samples, layers))
 
     sub_at = lax.broadcasted_iota(jnp.int32, (8, LANES), 0)
     for pair in range(tiles // 2):
@@ -602,7 +619,7 @@
                 below = between_ref[tile, pl.ds(c + 4, 8, stride=0), :]
                 between.append(row_samples(value, above, below))
                 values = [part_ref[tile, c * 4 + i] for i in range(4)]
-                line = replaced[tile][c : c + 1]
+                line = replaced[tile][c][0:1]
                 values[0] = jnp.where(sub_at == 0, jnp.where(front, line, values[0]), values[0])
                 values[3] = jnp.where(sub_at == 7, jnp.where(front, values[3], line), values[3])
                 part.append(values)
@@ -670,21 +687,14 @@
                 samples[slab, parity, 0, channel] = above + centre
                 samples[slab, parity, 1, channel] = centre + below
 
-    def over(in_front, behind):
-        clear = 1.0 - in_front[3]
-        return [top + clear * low for top, low in zip(in_front, behind)]
-
     slabs = []
     for slab in range(2):
         slabs.append([])
         for odd in range(2):
-            image = over(
-                *[[samples[slab, parity, odd, channel] for channel in range(4)] for parity in range(2)]
+            image = through_layers(
+                [[samples[slab, parity, odd, channel] for channel in range(4)] for parity in range(2)],
+                layers,
             )
-            step = 1
-            while step < layers:
-                image = over(image, [pltpu.roll(value, layers - step, 0) for value in image])
-                step *= 2
             slabs[slab].append(image)
     in_order = place_ref[FLIP] == 0
     image = [
@@ -802,7 +812,7 @@
         ),
         0.5,
     )(place, dense, index, inside, tables)
-    whole = pltpu.VMEM((tiles, 2 * size + 3 * 4 * half, LANES), f32)
+    whole = pltpu.VMEM((tiles, 2 * size + 4 * 4 * half, LANES), f32)
     along = call(own_kernel, "own_slab", whole, 0.4)(place, cells, weights)
     edges = pltpu.VMEM((cols // LANES, 16 * layers + 8, LANES), f32)
     packed = pltpu.VMEM((tiles, 32 * layers, LANES), bf16)
@@ -837,7 +847,7 @@
             edges,
             packed,
             lines,
-            pltpu.VMEM((tiles, 16 * layers + 16, LANES), f32),
+            pltpu.VMEM((tiles, 16 * layers + 32, LANES), f32),
             pltpu.VMEM((tiles, 16, LANES), f32),
         ],
         aliases={11: 2},

time: 13.3 us -> 13.4 us (level)
  transfers between devices with their start and end apart: 5 -> 5, of which waited for: 1 -> 1; matrix products, arithmetic and copies ran while one was open for 0% -> 0% of each run, Pallas kernels for 28% -> 29%
where the time goes in v28:
time: 13.4 us; the launch traced here: 13.3 us
  starting transfers between devices  6.53 us (49%)
  Pallas kernels  6.37 us (48%)
  waiting for transfers between devices  0.3 us (2%)
    pallas_call x8, Pallas kernels, run(): pl.pallas_call(kernel, out_shape=out_shape, in_specs=in_specs or [SMEM] +...  6.37 us
    ppermute x1, starting transfers between devices, two_slab_device(): bulk = lax.ppermute(bulk, 'bz', [(0, 1), (1, 0)])  3 us
    ppermute x1, starting transfers between devices, two_slab_device(): second = lax.ppermute(second, axes, diagonal)  1.58 us
    ppermute x1, starting transfers between devices, two_slab_device(): across = lax.ppermute(ends, 'bx', both(cross))  1.42 us
    ppermute x1, starting transfers between devices, two_slab_device(): beside = lax.ppermute(ends, 'bx', both(pairs))  0.53 us
    ppermute x1, waiting for transfers between devices, two_slab_device(): bulk = lax.ppermute(bulk, 'bz', [(0, 1), (1, 0)])  0.28 us
  transfers between devices with their start and end apart: 5, of which 1 were waited for; matrix products, arithmetic and copies ran while one was open for 0% of the time, Pallas kernels for 29%

profile of v28, /device:TPU:0, one launch (start us, length us, event | category | flops | bytes accessed | tf_op | source)
XLA Modules:
  0.0 13.3 jit_solution(17158892565356356818)
XLA Ops:
  0.0 1.2 %stage_block.1 = (s32[7]{0:T(128)S(4)}, s32[8,256]{1,0:T(8,128)S(1)}, s32[8,256]{1,0:T(8,128)S(1)}, s32[17,8,256]{2,1,0:T(8,128)S(1)}, s32[8,256]{1,0:T(8,128)S(...) custom-call(s32[2]{0:T(128)} %rank_ref.1, f32[8,32,256]{2,1,0:T(8,128)} %density_ref.1, ...), custom_call_target="tpu_custom_call" | custom-call | flops 1200000000 | bytes 4320000 | tf_op jit(solution)/shard_map/stage_block/pallas_call | solution.py:741
  1.2 3.0 %collective-permute-start = (s32[17,8,256]{2,1,0:T(8,128)S(1)}, s32[17,8,256]{2,1,0:T(8,128)S(1)}, u32[]{:S(2)}, u32[]{:S(2)}) collective-permute-start(s32[17,8,256]{2,1,0:T(8,128)S(1)} %get-tuple-element.25), channel_id=1, source_target_pairs={{0,16},{16,0},{1,17},{17,1},{2,18},{18,2},{3,19},{19,3},{4,20},{20... | collective-permute-start | bytes 417800 | tf_op jit(solution)/shard_map/ppermute | solution.py:800
  4.2 1.6 %collective-permute-start.1 = (s32[8,256]{1,0:T(8,128)S(1)}, s32[8,256]{1,0:T(8,128)S(1)}, u32[]{:S(2)}, u32[]{:S(2)}) collective-permute-start(s32[8,256]{1,0:T(8,128)S(1)} %get-tuple-element.26), channel_id=1, source_target_pairs={{16,0},{17,1},{18,2},{19,3},{0,4},{1,5},{2,6},{3,7},{4,16},{5,17},... | collective-permute-start | bytes 24584 | tf_op jit(solution)/shard_map/ppermute | solution.py:802
  5.7 0.0 collective-permute-start.2
  5.7 0.5 %own_cells.1 = (bf16[512,256]{1,0:T(8,128)(2,1)S(1)}, bf16[256,512]{1,0:T(8,128)(2,1)S(1)}, bf16[128,80]{1,0:T(8,128)(2,1)S(1)}, s32[8,128]{1,0:T(8,128)S(1)}) custom-call(s32[7]{0:T(128)S(4)} %get-tuple-element.19.place_ref, f32[8,2,40,128]{3,2,1,0:T(8,128)S(1)} %get-tuple-element.21.dense_ref, s32[8,2,40,128]{3,2,1,0:T(8,128)S(1)} %get-tuple-element.22.index_ref, ...), custom_call_target="tpu_custom_call" | custom-call | flops 500000000 | bytes 1800000 | tf_op jit(solution)/shard_map/own_cells/pallas_call | solution.py:741
  6.3 0.4 %own_slab.1.along_ref.own_ref = f32[4,1280,128]{2,1,0:T(8,128)S(1)} custom-call(s32[7]{0:T(128)S(4)} %get-tuple-element.19.place_ref, bf16[512,256]{1,0:T(8,128)(2,1)S(1)} %get-tuple-element.30.cells_ref, bf16[256,512]{1,0:T(8,128)(2,1)S(1)} %get-tuple-element.28.weights_ref), custom_call_target="tpu_custom_call" | custom-call | flops 400000000 | bytes 1440000 | tf_op jit(solution)/shard_map/own_slab/pallas_call | solution.py:741
  6.6 1.0 %own_tiles.1.part_ref = f32[4,16,8,128]{3,2,1,0:T(8,128)S(1)} custom-call(s32[7]{0:T(128)S(4)} %get-tuple-element.19.place_ref, f32[8,8,128]{2,1,0:T(8,128)S(1)} %get-tuple-element.20.tables_ref, bf16[256,512]{1,0:T(8,128)(2,1)S(1)} %get-tuple-element.28.weights_ref, s32[8,256]{1,0:T(8,128)S(1)} %get-tuple-element.23.inside_ref, ...), custom_call_target="tpu_custom_call" | custom-call | flops 100000000 | bytes 360000 | tf_op jit(solution)/shard_map/own_tiles/pallas_call | solution.py:741
  7.6 0.3 %collective-permute-done.bulk_ref = s32[17,8,256]{2,1,0:T(8,128)S(1)} collective-permute-done((s32[17,8,256]{2,1,0:T(8,128)S(1)}, s32[17,8,256]{2,1,0:T(8,128)S(1)}, u32[]{:S(2)}, u32[]{:S(2)}) %collective-permute-start) | collective-permute-done | bytes 139296 | tf_op jit(solution)/shard_map/ppermute | solution.py:800
  7.9 0.4 %other_cells.1.cells_ref.other_ref = bf16[512,256]{1,0:T(8,128)(2,1)S(1)} custom-call(s32[17,8,256]{2,1,0:T(8,128)S(1)} %collective-permute-done.bulk_ref, f32[8,8,128]{2,1,0:T(8,128)S(1)} %get-tuple-element.20.tables_ref), custom_call_target="tpu_custom_call" | custom-call | flops 100000000 | bytes 360000 | tf_op jit(solution)/shard_map/other_cells/pallas_call | solution.py:741
  8.4 0.0 collective-permute-done.1.second_ref
  8.4 0.0 collective-permute-done.2.first_ref
  8.4 0.1 side_columns.1.ends_ref
  8.5 1.4 %collective-permute-start.4 = (s32[2,8,128]{2,1,0:T(8,128)S(1)}, s32[2,8,128]{2,1,0:T(8,128)S(1)}, u32[]{:S(2)}, u32[]{:S(2)}) collective-permute-start(s32[2,8,128]{2,1,0:T(8,128)S(1)} %side_columns.1.ends_ref), channel_id=1, source_target_pairs={{1,2},{3,0},{2,1},{0,3},{5,6},{7,4},{6,5},{4,7},{9,10},{11,8},{10,... | collective-permute-start | bytes 24584 | tf_op jit(solution)/shard_map/ppermute | solution.py:840
  9.9 0.5 %collective-permute-start.3 = (s32[2,8,128]{2,1,0:T(8,128)S(1)}, s32[2,8,128]{2,1,0:T(8,128)S(1)}, u32[]{:S(2)}, u32[]{:S(2)}) collective-permute-start(s32[2,8,128]{2,1,0:T(8,128)S(1)} %side_columns.1.ends_ref), channel_id=1, source_target_pairs={{0,1},{2,3},{1,0},{3,2},{4,5},{6,7},{5,4},{7,6},{8,9},{10,11},{9,8... | collective-permute-start | bytes 24584 | tf_op jit(solution)/shard_map/ppermute | solution.py:839
  10.5 1.5 %render_tiles.1 = (f32[4,4,40,128]{3,2,1,0:T(8,128)S(1)}, f32[8,8,128]{2,1,0:T(8,128)S(1)}, f32[4,1280,128]{2,1,0:T(8,128)S(1)}) custom-call(s32[7]{0:T(128)S(4)} %get-tuple-element.19.place_ref, f32[8,8,128]{2,1,0:T(8,128)S(1)} %get-tuple-element.20.tables_ref, ...), custom_call_target="tpu_custom_call", output_to_operand_aliasing={{2}: (11, {})} | custom-call | flops 2000000000 | bytes 7200000 | tf_op jit(solution)/shard_map/render_tiles/pallas_call | solution.py:741
  12.0 0.0 collective-permute-done.4.across_ref
  12.0 0.0 collective-permute-done.3.beside_ref
  12.0 1.3 %edge_columns.1 = f32[4,32,512]{2,1,0:T(8,128)} custom-call(s32[7]{0:T(128)S(4)} %get-tuple-element.19.place_ref, f32[8,8,128]{2,1,0:T(8,128)S(1)} %get-tuple-element.20.tables_ref, s32[2,8,128]{2,1,0:T(8,128)S(1)} %collective-permute-done.3.beside_ref, s32[2,8,128]{2,1,0:T(8,128)S(1)} %collective-permute-done.4.across_ref, ...), custom_call_target="tpu_custom_call" | custom-call | flops 1000000000 | bytes 3600000 | tf_op jit(solution)/shard_map/edge_columns/pallas_call | solution.py:741
Async XLA Ops:
  1.2 6.8 %collective-permute-start = (s32[17,8,256]{2,1,0:T(8,128)S(1)}, s32[17,8,256]{2,1,0:T(8,128)S(1)}, u32[]{:S(2)}, u32[]{:S(2)}) collective-permute-start(s32[17,8,256]{2,1,0:T(8,128)S(1)} %get-tuple-element.25), channel_id=1, source_target_pairs={{0,16},{16,0},{1,17},{17,1},{2,18},{18,2},{3,19},{19,3},{4,20},{20... | collective-permute-start | bytes 417800 | tf_op jit(solution)/shard_map/ppermute | solution.py:800
  4.2 4.2 %collective-permute-start.1 = (s32[8,256]{1,0:T(8,128)S(1)}, s32[8,256]{1,0:T(8,128)S(1)}, u32[]{:S(2)}, u32[]{:S(2)}) collective-permute-start(s32[8,256]{1,0:T(8,128)S(1)} %get-tuple-element.26), channel_id=1, source_target_pairs={{16,0},{17,1},{18,2},{19,3},{0,4},{1,5},{2,6},{3,7},{4,16},{5,17},... | collective-permute-start | bytes 24584 | tf_op jit(solution)/shard_map/ppermute | solution.py:802
  5.7 2.6 %collective-permute-start.2 = (s32[8,256]{1,0:T(8,128)S(1)}, s32[8,256]{1,0:T(8,128)S(1)}, u32[]{:S(2)}, u32[]{:S(2)}) collective-permute-start(s32[8,256]{1,0:T(8,128)S(1)} %get-tuple-element.27), channel_id=1, source_target_pairs={{16,4},{17,5},{18,6},{19,7},{12,28},{13,29},{14,30},{15,31},{4,8},... | collective-permute-start | bytes 24584 | tf_op jit(solution)/shard_map/ppermute | solution.py:801
  8.5 3.5 %collective-permute-start.4 = (s32[2,8,128]{2,1,0:T(8,128)S(1)}, s32[2,8,128]{2,1,0:T(8,128)S(1)}, u32[]{:S(2)}, u32[]{:S(2)}) collective-permute-start(s32[2,8,128]{2,1,0:T(8,128)S(1)} %side_columns.1.ends_ref), channel_id=1, source_target_pairs={{1,2},{3,0},{2,1},{0,3},{5,6},{7,4},{6,5},{4,7},{9,10},{11,8},{10,... | collective-permute-start | bytes 24584 | tf_op jit(solution)/shard_map/ppermute | solution.py:840
  9.9 2.0 %collective-permute-start.3 = (s32[2,8,128]{2,1,0:T(8,128)S(1)}, s32[2,8,128]{2,1,0:T(8,128)S(1)}, u32[]{:S(2)}, u32[]{:S(2)}) collective-permute-start(s32[2,8,128]{2,1,0:T(8,128)S(1)} %side_columns.1.ends_ref), channel_id=1, source_target_pairs={{0,1},{2,3},{1,0},{3,2},{4,5},{6,7},{5,4},{7,6},{8,9},{10,11},{9,8... | collective-permute-start | bytes 24584 | tf_op jit(solution)/shard_map/ppermute | solution.py:839

commit v29 on v26

--- a/solution.py
+++ b/solution.py
@@ -451,11 +451,10 @@
                 ]
             )
             odd.append([])
+            line = lines[tile][z * 8 : z * 8 + 8, :]
             for c in range(4):
                 value = rounded(layer_rows(views[tile], z + 2, c) + triple[tile][c])
-                above = lines[tile][pl.ds(z * 8 + c, 8, stride=0), :]
-                below = lines[tile][pl.ds(z * 8 + 4 + c, 8, stride=0), :]
-                odd[tile].append(row_samples(value, above, below))
+                odd[tile].append(row_samples(value, line[c : c + 1], line[4 + c : 5 + c]))
         image = blend(image, even, keep_first if z == 0 else None)
         image = blend(image, odd, keep_last if z == layers - 1 else None)
     return image

time: 13.3 us -> 13.3 us (level)
  transfers between devices with their start and end apart: 5 -> 5, of which waited for: 1 -> 1; matrix products, arithmetic and copies ran while one was open for 0% -> 0% of each run, Pallas kernels for 28% -> 29%
where the time goes in v29:
time: 13.3 us; the launch traced here: 13.2 us
  starting transfers between devices  6.53 us (49%)
  Pallas kernels  6.34 us (48%)
  waiting for transfers between devices  0.26 us (2%)
    pallas_call x8, Pallas kernels, run(): pl.pallas_call(kernel, out_shape=out_shape, in_specs=in_specs or [SMEM] +...  6.34 us
    ppermute x1, starting transfers between devices, two_slab_device(): bulk = lax.ppermute(bulk, 'bz', [(0, 1), (1, 0)])  3 us
    ppermute x1, starting transfers between devices, two_slab_device(): second = lax.ppermute(second, axes, diagonal)  1.58 us
    ppermute x1, starting transfers between devices, two_slab_device(): across = lax.ppermute(ends, 'bx', both(cross))  1.46 us
    ppermute x1, starting transfers between devices, two_slab_device(): beside = lax.ppermute(ends, 'bx', both(pairs))  0.49 us
  transfers between devices with their start and end apart: 5, of which 1 were waited for; matrix products, arithmetic and copies ran while one was open for 0% of the time, Pallas kernels for 29%

profile of v29, /device:TPU:0, one launch (start us, length us, event | category | flops | bytes accessed | tf_op | source)
XLA Modules:
  0.0 13.2 jit_solution(1569492607599282074)
XLA Ops:
  0.0 1.2 %stage_block.1 = (s32[7]{0:T(128)S(4)}, s32[8,256]{1,0:T(8,128)S(1)}, s32[8,256]{1,0:T(8,128)S(1)}, s32[17,8,256]{2,1,0:T(8,128)S(1)}, s32[8,256]{1,0:T(8,128)S(...) custom-call(s32[2]{0:T(128)} %rank_ref.1, f32[8,32,256]{2,1,0:T(8,128)} %density_ref.1, ...), custom_call_target="tpu_custom_call" | custom-call | flops 1200000000 | bytes 4320000 | tf_op jit(solution)/shard_map/stage_block/pallas_call | solution.py:730
  1.2 3.0 %collective-permute-start = (s32[17,8,256]{2,1,0:T(8,128)S(1)}, s32[17,8,256]{2,1,0:T(8,128)S(1)}, u32[]{:S(2)}, u32[]{:S(2)}) collective-permute-start(s32[17,8,256]{2,1,0:T(8,128)S(1)} %get-tuple-element.25), channel_id=1, source_target_pairs={{0,16},{16,0},{1,17},{17,1},{2,18},{18,2},{3,19},{19,3},{4,20},{20... | collective-permute-start | bytes 417800 | tf_op jit(solution)/shard_map/ppermute | solution.py:789
  4.2 1.6 %collective-permute-start.1 = (s32[8,256]{1,0:T(8,128)S(1)}, s32[8,256]{1,0:T(8,128)S(1)}, u32[]{:S(2)}, u32[]{:S(2)}) collective-permute-start(s32[8,256]{1,0:T(8,128)S(1)} %get-tuple-element.26), channel_id=1, source_target_pairs={{16,0},{17,1},{18,2},{19,3},{0,4},{1,5},{2,6},{3,7},{4,16},{5,17},... | collective-permute-start | bytes 24584 | tf_op jit(solution)/shard_map/ppermute | solution.py:791
  5.7 0.0 collective-permute-start.2
  5.7 0.5 %own_cells.1 = (bf16[512,256]{1,0:T(8,128)(2,1)S(1)}, bf16[256,512]{1,0:T(8,128)(2,1)S(1)}, bf16[128,80]{1,0:T(8,128)(2,1)S(1)}, s32[8,128]{1,0:T(8,128)S(1)}) custom-call(s32[7]{0:T(128)S(4)} %get-tuple-element.19.place_ref, f32[8,2,40,128]{3,2,1,0:T(8,128)S(1)} %get-tuple-element.21.dense_ref, s32[8,2,40,128]{3,2,1,0:T(8,128)S(1)} %get-tuple-element.22.index_ref, ...), custom_call_target="tpu_custom_call" | custom-call | flops 500000000 | bytes 1800000 | tf_op jit(solution)/shard_map/own_cells/pallas_call | solution.py:730
  6.3 0.4 %own_slab.1.along_ref.own_ref = f32[4,1216,128]{2,1,0:T(8,128)S(1)} custom-call(s32[7]{0:T(128)S(4)} %get-tuple-element.19.place_ref, bf16[512,256]{1,0:T(8,128)(2,1)S(1)} %get-tuple-element.30.cells_ref, bf16[256,512]{1,0:T(8,128)(2,1)S(1)} %get-tuple-element.28.weights_ref), custom_call_target="tpu_custom_call" | custom-call | flops 400000000 | bytes 1440000 | tf_op jit(solution)/shard_map/own_slab/pallas_call | solution.py:730
  6.6 1.0 %own_tiles.1.part_ref = f32[4,16,8,128]{3,2,1,0:T(8,128)S(1)} custom-call(s32[7]{0:T(128)S(4)} %get-tuple-element.19.place_ref, f32[8,8,128]{2,1,0:T(8,128)S(1)} %get-tuple-element.20.tables_ref, bf16[256,512]{1,0:T(8,128)(2,1)S(1)} %get-tuple-element.28.weights_ref, s32[8,256]{1,0:T(8,128)S(1)} %get-tuple-element.23.inside_ref, ...), custom_call_target="tpu_custom_call" | custom-call | flops 100000000 | bytes 360000 | tf_op jit(solution)/shard_map/own_tiles/pallas_call | solution.py:730
  7.7 0.3 %collective-permute-done.bulk_ref = s32[17,8,256]{2,1,0:T(8,128)S(1)} collective-permute-done((s32[17,8,256]{2,1,0:T(8,128)S(1)}, s32[17,8,256]{2,1,0:T(8,128)S(1)}, u32[]{:S(2)}, u32[]{:S(2)}) %collective-permute-start) | collective-permute-done | bytes 139296 | tf_op jit(solution)/shard_map/ppermute | solution.py:789
  7.9 0.4 %other_cells.1.cells_ref.other_ref = bf16[512,256]{1,0:T(8,128)(2,1)S(1)} custom-call(s32[17,8,256]{2,1,0:T(8,128)S(1)} %collective-permute-done.bulk_ref, f32[8,8,128]{2,1,0:T(8,128)S(1)} %get-tuple-element.20.tables_ref), custom_call_target="tpu_custom_call" | custom-call | flops 100000000 | bytes 360000 | tf_op jit(solution)/shard_map/other_cells/pallas_call | solution.py:730
  8.4 0.0 collective-permute-done.1.second_ref
  8.4 0.0 collective-permute-done.2.first_ref
  8.4 0.1 side_columns.1.ends_ref
  8.5 1.5 %collective-permute-start.4 = (s32[2,8,128]{2,1,0:T(8,128)S(1)}, s32[2,8,128]{2,1,0:T(8,128)S(1)}, u32[]{:S(2)}, u32[]{:S(2)}) collective-permute-start(s32[2,8,128]{2,1,0:T(8,128)S(1)} %side_columns.1.ends_ref), channel_id=1, source_target_pairs={{1,2},{3,0},{2,1},{0,3},{5,6},{7,4},{6,5},{4,7},{9,10},{11,8},{10,... | collective-permute-start | bytes 24584 | tf_op jit(solution)/shard_map/ppermute | solution.py:829
  10.0 0.5 %collective-permute-start.3 = (s32[2,8,128]{2,1,0:T(8,128)S(1)}, s32[2,8,128]{2,1,0:T(8,128)S(1)}, u32[]{:S(2)}, u32[]{:S(2)}) collective-permute-start(s32[2,8,128]{2,1,0:T(8,128)S(1)} %side_columns.1.ends_ref), channel_id=1, source_target_pairs={{0,1},{2,3},{1,0},{3,2},{4,5},{6,7},{5,4},{7,6},{8,9},{10,11},{9,8... | collective-permute-start | bytes 24584 | tf_op jit(solution)/shard_map/ppermute | solution.py:828
  10.5 1.4 %render_tiles.1 = (f32[4,4,40,128]{3,2,1,0:T(8,128)S(1)}, f32[8,8,128]{2,1,0:T(8,128)S(1)}, f32[4,1216,128]{2,1,0:T(8,128)S(1)}) custom-call(s32[7]{0:T(128)S(4)} %get-tuple-element.19.place_ref, f32[8,8,128]{2,1,0:T(8,128)S(1)} %get-tuple-element.20.tables_ref, ...), custom_call_target="tpu_custom_call", output_to_operand_aliasing={{2}: (11, {})} | custom-call | flops 2000000000 | bytes 7200000 | tf_op jit(solution)/shard_map/render_tiles/pallas_call | solution.py:730
  11.9 0.0 collective-permute-done.4.across_ref
  11.9 0.0 collective-permute-done.3.beside_ref
  11.9 1.3 %edge_columns.1 = f32[4,32,512]{2,1,0:T(8,128)} custom-call(s32[7]{0:T(128)S(4)} %get-tuple-element.19.place_ref, f32[8,8,128]{2,1,0:T(8,128)S(1)} %get-tuple-element.20.tables_ref, s32[2,8,128]{2,1,0:T(8,128)S(1)} %collective-permute-done.3.beside_ref, s32[2,8,128]{2,1,0:T(8,128)S(1)} %collective-permute-done.4.across_ref, ...), custom_call_target="tpu_custom_call" | custom-call | flops 1000000000 | bytes 3600000 | tf_op jit(solution)/shard_map/edge_columns/pallas_call | solution.py:730
Async XLA Ops:
  1.2 6.8 %collective-permute-start = (s32[17,8,256]{2,1,0:T(8,128)S(1)}, s32[17,8,256]{2,1,0:T(8,128)S(1)}, u32[]{:S(2)}, u32[]{:S(2)}) collective-permute-start(s32[17,8,256]{2,1,0:T(8,128)S(1)} %get-tuple-element.25), channel_id=1, source_target_pairs={{0,16},{16,0},{1,17},{17,1},{2,18},{18,2},{3,19},{19,3},{4,20},{20... | collective-permute-start | bytes 417800 | tf_op jit(solution)/shard_map/ppermute | solution.py:789
  4.2 4.2 %collective-permute-start.1 = (s32[8,256]{1,0:T(8,128)S(1)}, s32[8,256]{1,0:T(8,128)S(1)}, u32[]{:S(2)}, u32[]{:S(2)}) collective-permute-start(s32[8,256]{1,0:T(8,128)S(1)} %get-tuple-element.26), channel_id=1, source_target_pairs={{16,0},{17,1},{18,2},{19,3},{0,4},{1,5},{2,6},{3,7},{4,16},{5,17},... | collective-permute-start | bytes 24584 | tf_op jit(solution)/shard_map/ppermute | solution.py:791
  5.7 2.6 %collective-permute-start.2 = (s32[8,256]{1,0:T(8,128)S(1)}, s32[8,256]{1,0:T(8,128)S(1)}, u32[]{:S(2)}, u32[]{:S(2)}) collective-permute-start(s32[8,256]{1,0:T(8,128)S(1)} %get-tuple-element.27), channel_id=1, source_target_pairs={{16,4},{17,5},{18,6},{19,7},{12,28},{13,29},{14,30},{15,31},{4,8},... | collective-permute-start | bytes 24584 | tf_op jit(solution)/shard_map/ppermute | solution.py:790
  8.5 3.4 %collective-permute-start.4 = (s32[2,8,128]{2,1,0:T(8,128)S(1)}, s32[2,8,128]{2,1,0:T(8,128)S(1)}, u32[]{:S(2)}, u32[]{:S(2)}) collective-permute-start(s32[2,8,128]{2,1,0:T(8,128)S(1)} %side_columns.1.ends_ref), channel_id=1, source_target_pairs={{1,2},{3,0},{2,1},{0,3},{5,6},{7,4},{6,5},{4,7},{9,10},{11,8},{10,... | collective-permute-start | bytes 24584 | tf_op jit(solution)/shard_map/ppermute | solution.py:829
  10.0 1.9 %collective-permute-start.3 = (s32[2,8,128]{2,1,0:T(8,128)S(1)}, s32[2,8,128]{2,1,0:T(8,128)S(1)}, u32[]{:S(2)}, u32[]{:S(2)}) collective-permute-start(s32[2,8,128]{2,1,0:T(8,128)S(1)} %side_columns.1.ends_ref), channel_id=1, source_target_pairs={{0,1},{2,3},{1,0},{3,2},{4,5},{6,7},{5,4},{7,6},{8,9},{10,11},{9,8... | collective-permute-start | bytes 24584 | tf_op jit(solution)/shard_map/ppermute | solution.py:828
